TPU v7x, 32 devices: a whole 2x2x4 slice. The times are simulated.
32 devices in a mesh: mats: 2 (over y), col: 4 (over x, core), row: 4 (over z).
Axes of the slice: x: 2, y: 2, z: 4, core: 2. Of those that a mesh axis runs over, the one named last changes fastest.
Arguments:
- iterate: float32 [7168, 8192], P(('mats', 'row'), 'col'), parts along dimension 0, may hold values from -0.0390625 to 0.0390625
Outputs:
- update: float32 [7168, 8192], P(('mats', 'row'), 'col'), parts along dimension 0
There are 2 independent parts, one for each index of `mats`. A program takes and returns all parts, laid end to end along the dimension named above; each array names one. Nothing has to cross between parts.
All inputs are finite; a program needn't handle non-finite values.
Results may differ from a plain program's by a relative error of at most 0.0043.
Values may be sent and summed in bfloat16 or wider, within the bound.
No kernel may reach another device: no remote copies, remote signals or barrier semaphores. Data moves between devices by JAX's collectives and lax.ppermute only.
A program may use at most 128 MiB of HBM per device.

v0:
```python
import math

import jax
import jax.numpy as jnp
from jax import lax
from jax.sharding import PartitionSpec as P

ORDER = 3584
COLS = 8192


quint_a = 3.4445
quint_b = -4.775
quint_c = 2.0315


def shards(iterate):
    iter_bf = iterate.astype(jnp.bfloat16)
    column_panel = lax.all_gather(iter_bf, "row", axis=0, tiled=True)
    gram_part = lax.psum_scatter(
        lax.dot_general(
            column_panel, iter_bf, (((1,), (1,)), ((), ())), preferred_element_type=jnp.float32
        ),
        "col",
        scatter_dimension=0,
        tiled=True,
    )
    gram_cols = lax.all_gather(gram_part.astype(jnp.bfloat16), "col", axis=0, tiled=True)
    first = lax.dot_general(
        gram_cols, column_panel, (((0,), (0,)), ((), ())), preferred_element_type=jnp.float32
    )
    first_bf = first.astype(jnp.bfloat16)
    second = lax.dot_general(
        gram_cols,
        lax.all_gather(first_bf, "row", axis=0, tiled=True),
        (((0,), (0,)), ((), ())),
        preferred_element_type=jnp.float32,
    )
    factor = 0.2 * math.sqrt(max(ORDER, COLS))
    return factor * (quint_a * iterate + quint_b * first + quint_c * second)


def solution(mesh):
    in_specs = (P(("mats", "row"), "col"),)
    out_specs = P(("mats", "row"), "col")
    return jax.shard_map(shards, mesh=mesh, in_specs=in_specs, out_specs=out_specs, check_vma=False)
```

profile of v0, /device:TPU:12, one launch (start us, length us, event | category | flops | bytes accessed | tf_op | source)
XLA Modules:
  0.0 738.8 jit_solution(2363879203535662324)
XLA Ops:
  6.5 0.0 all-gather.4.cloned.1.call-start
  6.5 5.5 convert_element_type.9
  12.0 0.0 all-gather.4.cloned.1.call-update
  12.1 0.0 reduce-scatter.2.cloned.1.call-start
  12.1 251.0 %all-gather.4.cloned.1.call-done = bf16[3584,2048]{1,0:T(8,128)(2,1)} async-done(((bf16[896,2048]{1,0:T(8,128)(2,1)}), bf16[3584,2048]{1,0:T(8,128)(2,1)}) %all-gather.4.cloned.1.call-update) | async-done | bytes 14680080 | tf_op jit(solution)/shard_map/all_gather | solution.py:19
  263.1 20.9 %fusion.1 = f32[3584,896]{1,0:T(8,128)} fusion(bf16[3584,2048]{1,0:T(8,128)(2,1)} %all-gather.4.cloned.1.call-done, bf16[896,2048]{1,0:T(8,128)(2,1)} %convert_element_type.9), kind=kOutput, calls=%fused_computation.2 | convolution fusion | flops 13153337344 | bytes 31195136 | tf_op jit(solution)/shard_map/dot_general | solution.py:21
  284.0 0.0 reduce-scatter.2.cloned.1.call-update
  284.0 0.0 all-gather.6.cloned.1.call-start
  284.0 101.8 %reduce-scatter.2.cloned.1.call-done = f32[896,896]{1,0:T(8,128)} async-done(((f32[3584,896]{1,0:T(8,128)}), f32[896,896]{1,0:T(8,128)}) %reduce-scatter.2.cloned.1.call-update) | async-done | bytes 3211280 | tf_op jit(solution)/shard_map/reduce_scatter | solution.py:20
  385.8 3.2 convert_element_type.10
  389.1 0.0 all-gather.6.cloned.1.call-update
  389.1 0.0 all-gather.8.cloned.1.call-start
  389.1 47.2 %all-gather.6.cloned.1.call-done = bf16[3584,896]{1,0:T(8,128)(2,1)} async-done(((bf16[896,896]{1,0:T(8,128)(2,1)}), bf16[3584,896]{1,0:T(8,128)(2,1)}) %all-gather.6.cloned.1.call-update) | async-done | bytes 6422544 | tf_op jit(solution)/shard_map/all_gather | solution.py:28
  436.4 21.1 %fusion = (bf16[896,2048]{1,0:T(8,128)(2,1)}, f32[896,2048]{1,0:T(8,128)}) fusion(bf16[3584,896]{1,0:T(8,128)(2,1)} %all-gather.6.cloned.1.call-done, bf16[3584,2048]{1,0:T(8,128)(2,1)} %all-gather.4.cloned.1.call-done), kind=kOutput, calls=%fused_computation.1 | convolution fusion | flops 13155172352 | bytes 32112640 | tf_op jit(solution)/shard_map/dot_general | solution.py:29
  457.5 0.0 all-gather.8.cloned.1.call-update
  457.5 249.9 %all-gather.8.cloned.1.call-done = bf16[3584,2048]{1,0:T(8,128)(2,1)} async-done(((bf16[896,2048]{1,0:T(8,128)(2,1)}), bf16[3584,2048]{1,0:T(8,128)(2,1)}) %all-gather.8.cloned.1.call-update) | async-done | bytes 14680080 | tf_op jit(solution)/shard_map/all_gather | solution.py:35
  707.4 24.9 %add_multiply_fusion = f32[896,2048]{1,0:T(8,128)} fusion(f32[896,2048]{1,0:T(8,128)} %get-tuple-element.6, f32[896,2048]{1,0:T(8,128)} %param.1, bf16[3584,896]{1,0:T(8,128)(2,1)} %all-gather.6.cloned.1.call-done, bf16[3584,2048]{1,0:T(8,128)(2,1)} %all-gather.8.cloned.1.call-done), kind=kOutput, calls=%fused_computation | convolution fusion | flops 13164347392 | bytes 43122688 | tf_op jit(solution)/shard_map/dot_general | solution.py:33
Async XLA Ops:
  6.5 256.5 %all-gather.4.cloned.1.call-start = ((), (), s32[]{:S(2)}) async-start(), calls=%async_computation.1 | async-start | bytes 18350080 | tf_op jit(solution)/shard_map/all_gather | solution.py:19
  12.1 373.8 %reduce-scatter.2.cloned.1.call-start = ((), (), s32[]{:S(2)}) async-start(), calls=%async_computation.2 | async-start | bytes 16056320 | tf_op jit(solution)/shard_map/reduce_scatter | solution.py:20
  284.0 152.4 %all-gather.6.cloned.1.call-start = ((), (), s32[]{:S(2)}) async-start(), calls=%async_computation.3 | async-start | bytes 8028160 | tf_op jit(solution)/shard_map/all_gather | solution.py:28
  389.1 318.4 %all-gather.8.cloned.1.call-start = ((), (), s32[]{:S(2)}) async-start(), calls=%async_computation.4 | async-start | bytes 18350080 | tf_op jit(solution)/shard_map/all_gather | solution.py:35
Sparse Core Ops, SparseCore 0:
  12.2 250.8 all-gather.3
  284.1 101.6 reduce-scatter.1
  389.2 47.1 all-gather.5
  457.6 249.7 all-gather.7
where the time goes:
time: 743 us; the launch traced here: 739 us
  waiting for transfers between devices  650 us (87%)
  matrix products  66.9 us (9%)
  between operations  13.1 us (2%)
  other arithmetic  8.72 us (1%)
    all_gather x1, waiting for transfers between devices, shards(): column_panel = lax.all_gather(iter_bf, 'row', axis=0, tiled=True)  251 us
    all_gather x1, waiting for transfers between devices, shards(): lax.all_gather(first_bf, 'row', axis=0, tiled=True)  250 us
    reduce_scatter x1, waiting for transfers between devices, shards(): lax.psum_scatter(lax.dot_general(column_panel, iter_bf, (((1,), (1,)), ((...  102 us
    all_gather x1, waiting for transfers between devices, shards(): lax.all_gather(gram_part.astype(jnp.bfloat16), 'col', axis=0, tiled=True)  47.2 us
    dot_general x1, matrix products, shards(): lax.dot_general(gram_cols, lax.all_gather(first_bf, 'row', axis=0, tiled=...  24.9 us
    dot_general x1, matrix products, shards(): lax.dot_general(gram_cols, column_panel, (((0,), (0,)), ((), ())), prefer...  21.1 us
    dot_general x1, matrix products, shards(): lax.dot_general(column_panel, iter_bf, (((1,), (1,)), ((), ())), preferre...  20.9 us
  transfers between devices with their start and end apart: 4, of which 4 were waited for; matrix products, arithmetic and copies ran while one was open for 0% of the time, Pallas kernels for 0%

commit v1 on v0

v1 whole, which is shorter than its diff:
```python
import functools
import math

import jax
import jax.numpy as jnp
from jax import lax
from jax.experimental import pallas as pl
from jax.experimental.pallas import tpu as pltpu
from jax.sharding import PartitionSpec as P

ORDER = 3584
COLS = 8192

BF16 = jnp.bfloat16
F32 = jnp.float32

quint_a = 3.4445
quint_b = -4.775
quint_c = 2.0315

FACTOR = 0.2 * math.sqrt(max(ORDER, COLS))

BLOCK = 512
BLOCKS = ORDER // BLOCK
DIAGS = 4
UNITS = 2 * BLOCKS
QUARTER = 64
SLAB = ORDER // 4
GROUP = COLS // 16
PIECES = (128, 256, 256, 256)
HALVES = 2
WIDE = GROUP // HALVES
THIRDS = ((0, 5), (5, 10), (10, 14))
VMEM = 60 << 20


def shards_rows(iterate):
    iter_bf = iterate.astype(BF16)
    column_panel = lax.all_gather(iter_bf, "row", axis=0, tiled=True)
    gram_part = lax.psum_scatter(
        lax.dot_general(
            column_panel, iter_bf, (((1,), (1,)), ((), ())), preferred_element_type=F32
        ),
        "col",
        scatter_dimension=0,
        tiled=True,
    )
    gram_cols = lax.all_gather(gram_part.astype(BF16), "col", axis=0, tiled=True)
    first = lax.dot_general(
        gram_cols, column_panel, (((0,), (0,)), ((), ())), preferred_element_type=F32
    )
    second = lax.dot_general(
        gram_cols,
        lax.all_gather(first.astype(BF16), "row", axis=0, tiled=True),
        (((0,), (0,)), ((), ())),
        preferred_element_type=F32,
    )
    return FACTOR * (quint_a * iterate + quint_b * first + quint_c * second)


def flip(bit, by):
    return 1 - bit if by else bit


def place():
    col = lax.axis_index("col")
    row = lax.axis_index("row")
    return lax.axis_index("mats"), col // 2, col % 2, row // 2, row % 2


def slab_of(high, low, step):
    return 2 * flip(high, step >> 1) + flip(low, step & 1)


def over_x(a):
    return lax.ppermute(a, "col", [(0, 2), (1, 3), (2, 0), (3, 1)])


def over_core(a):
    return lax.ppermute(a, "col", [(0, 1), (1, 0), (2, 3), (3, 2)])


def over_y(a):
    return lax.ppermute(a, "mats", [(0, 1), (1, 0)])


def over_z(a, step=1):
    return lax.ppermute(a, "row", [(z, z ^ step) for z in range(4)])


def home(a, step):
    pairs = []
    for y in range(2):
        for z in range(4):
            part, slab = z // 2, (2 * y + z % 2) ^ step
            pairs.append((4 * y + z, 4 * part + slab))
    return lax.ppermute(a, ("mats", "row"), pairs)


def dot(a, b, dims):
    return lax.dot_general(a, b, (dims, ((), ())), preferred_element_type=F32)


def gram_kernel(*refs):
    count = 16 * len(PIECES)
    pieces = refs[:count]
    keep_a, send_a, keep_b, send_b, panel, total, arrived = refs[count:]
    y, x, core, high, low = place()
    diag = 2 * x + core
    n = 0
    for source in range(4):
        for step in range(4):
            start = slab_of(high, low, step) * SLAB
            for rows in PIECES:
                spot = pl.ds(pl.multiple_of(start, 128), rows)
                pltpu.make_async_copy(
                    pieces[n], panel.at[source, spot, :], arrived.at[source]
                ).start()
                start += rows
                n += 1

    def rows_of(i):
        return pl.ds(pl.multiple_of(i * BLOCK, BLOCK), BLOCK)

    for source in range(4):
        pltpu.make_async_copy(panel.at[source], panel.at[source], arrived.at[source]).wait()

        def block(i, carry):
            j = lax.rem(i + diag, BLOCKS)
            part = dot(panel[source, rows_of(i), :], panel[source, rows_of(j), :], ((1,), (1,)))
            if source == 0:
                total[i] = part
            else:
                total[i] += part
            if source == 3:
                for b in range(2):
                    def quarter(half, qy, qz):
                        at = half * 256 + (2 * qy + qz) * QUARTER
                        return total[i, pl.ds(pl.multiple_of(at, QUARTER), QUARTER), :]

                    keep_a[i, b] = quarter(0, y, b)
                    send_a[i, b] = quarter(0, 1 - y, b).astype(BF16)
                    keep_b[i, b] = quarter(1, b, low)
                    send_b[i, b] = quarter(1, b, 1 - low).astype(BF16)
            return carry

        lax.fori_loop(0, BLOCKS, block, 0)


def gram_call(pieces):
    shape = (BLOCKS, 2, QUARTER, BLOCK)
    return pl.pallas_call(
        gram_kernel,
        out_shape=[
            jax.ShapeDtypeStruct(shape, F32),
            jax.ShapeDtypeStruct(shape, BF16),
            jax.ShapeDtypeStruct(shape, F32),
            jax.ShapeDtypeStruct(shape, BF16),
        ],
        in_specs=[pl.BlockSpec(memory_space=pl.ANY)] * len(pieces),
        out_specs=[pl.BlockSpec(memory_space=pltpu.VMEM)] * 4,
        scratch_shapes=[
            pltpu.VMEM((4, ORDER, GROUP), BF16),
            pltpu.VMEM((BLOCKS, BLOCK, BLOCK), F32),
            pltpu.SemaphoreType.DMA((4,)),
        ],
        compiler_params=pltpu.CompilerParams(vmem_limit_bytes=VMEM),
        cost_estimate=pl.CostEstimate(
            flops=2 * BLOCKS * BLOCK * BLOCK * 2048, bytes_accessed=20 << 20, transcendentals=0
        ),
        name="gram",
    )(*pieces)


def step_kernel(keys, half, *refs):
    gram_pieces = refs[: len(keys)]
    refs = refs[len(keys):]
    iter_pieces = refs[: 4 * len(PIECES)]
    refs = refs[4 * len(PIECES):]
    outs = refs[:4]
    gram, panel, first, total, result, here, there, gone = refs[4:]
    y, x, core, high, low = place()
    for (third, rx, ry, rz, rk), piece in zip(keys, gram_pieces):
        lo, hi = THIRDS[third]
        diag = 2 * flip(x, rx) + flip(core, rk)
        quarter = 2 * flip(y, ry) + flip(low, rz)
        pltpu.make_async_copy(piece, gram.at[diag, pl.ds(lo, hi - lo), quarter], here).start()
    n = 0
    for step in range(4):
        start = slab_of(high, low, step) * SLAB
        for rows in PIECES:
            spot = pl.ds(pl.multiple_of(start, 128), rows)
            pltpu.make_async_copy(
                iter_pieces[n].at[:, pl.ds(half * WIDE, WIDE)], panel.at[spot, :], there
            ).start()
            start += rows
            n += 1
    pltpu.make_async_copy(panel, panel, there).wait()
    pltpu.make_async_copy(gram, gram, here).wait()

    def rows_of(i):
        return pl.ds(pl.multiple_of(i * BLOCK, BLOCK), BLOCK)

    def block(d, i):
        return gram[d, pl.ds(2 * i, 2)].reshape(BLOCK, BLOCK)

    def apply(source, i):
        got = dot(block(0, i), source[rows_of(i), :], ((1,), (0,)))
        for d in range(1, DIAGS):
            j = lax.rem(i + d, BLOCKS)
            got += dot(block(d, i), source[rows_of(j), :], ((1,), (0,)))
            j = lax.rem(i + BLOCKS - d, BLOCKS)
            got += dot(block(d, j), source[rows_of(j), :], ((0,), (0,)))
        return got

    def one(i, carry):
        got = apply(panel, i)
        first[rows_of(i), :] = got.astype(BF16)
        total[rows_of(i), :] = quint_b * got
        return carry

    def two(i, carry):
        got = apply(first, i)
        result[rows_of(i), :] = (total[rows_of(i), :] + quint_c * got).astype(BF16)
        return carry

    lax.fori_loop(0, BLOCKS, one, 0)
    lax.fori_loop(0, BLOCKS, two, 0)
    copies = []
    for step in range(4):
        start = slab_of(y, low, step) * SLAB
        copies.append(
            pltpu.make_async_copy(
                result.at[pl.ds(pl.multiple_of(start, 128), SLAB), :], outs[step], gone.at[step]
            )
        )
        copies[-1].start()
    for copy in copies:
        copy.wait()


def step_call(keys, gram_pieces, iter_pieces, half):
    count = len(gram_pieces) + len(iter_pieces)
    return pl.pallas_call(
        functools.partial(step_kernel, keys, half),
        out_shape=[jax.ShapeDtypeStruct((SLAB, WIDE), BF16)] * 4,
        in_specs=[pl.BlockSpec(memory_space=pl.ANY)] * count,
        out_specs=[pl.BlockSpec(memory_space=pl.ANY)] * 4,
        scratch_shapes=[
            pltpu.VMEM((DIAGS, UNITS, 4, QUARTER, BLOCK), BF16),
            pltpu.VMEM((ORDER, WIDE), BF16),
            pltpu.VMEM((ORDER, WIDE), BF16),
            pltpu.VMEM((ORDER, WIDE), F32),
            pltpu.VMEM((ORDER, WIDE), BF16),
            pltpu.SemaphoreType.DMA,
            pltpu.SemaphoreType.DMA,
            pltpu.SemaphoreType.DMA((4,)),
        ],
        compiler_params=pltpu.CompilerParams(vmem_limit_bytes=VMEM),
        cost_estimate=pl.CostEstimate(
            flops=4 * ORDER * ORDER * WIDE, bytes_accessed=20 << 20, transcendentals=0
        ),
        name="step",
    )(*gram_pieces, *iter_pieces)


def pick(a, at, size, axis):
    return lax.dynamic_slice_in_dim(a, at, size, axis)


def shards_cube(iterate):
    y, x, core, high, low = place()
    aligned = y == high

    own = [[] for _ in range(4)]
    start = 0
    for rows in PIECES:
        band = iterate[start : start + rows]
        keep = pick(band, y * 2 * GROUP, 2 * GROUP, 1).astype(BF16)
        other = over_y(pick(band, (1 - y) * 2 * GROUP, 2 * GROUP, 1).astype(BF16))
        near = jnp.where(aligned, keep, other)
        far = jnp.where(aligned, other, keep)
        for step in (2, 3, 1, 0):
            source = far if step >> 1 else near
            chunk = pick(source, flip(low, step & 1) * GROUP, GROUP, 1)
            own[step].append(over_z(chunk, step) if step else chunk)
        start += rows
    own = [piece for step in own for piece in step]

    across = [over_x(piece) for piece in own]
    keep_a, send_a, keep_b, send_b = gram_call(
        own + across + [over_core(piece) for piece in own] + [over_core(piece) for piece in across]
    )

    sum_a = keep_a + over_y(send_a)
    sum_b = keep_b + over_z(send_b)
    got_a = over_z(pick(sum_a, 1 - low, 1, 1).astype(BF16))
    got_b = over_y(pick(sum_b, 1 - y, 1, 1).astype(BF16))
    done_a = (pick(sum_a, low, 1, 1) + got_a).astype(BF16)
    done_b = (pick(sum_b, y, 1, 1) + got_b).astype(BF16)
    mine = jnp.concatenate([done_a, done_b], axis=1).reshape(UNITS, QUARTER, BLOCK)

    moves = {0: over_x, 1: over_y, 2: over_z}
    keys, gram_pieces = [], []
    for third, (lo, hi) in enumerate(THIRDS):
        held = {(0, 0, 0): mine[lo:hi]}
        for turn in range(3):
            axis = (third + turn) % 3
            for key, piece in list(held.items()):
                new = tuple(1 if n == axis else bit for n, bit in enumerate(key))
                held[new] = moves[axis](piece)
        for key, piece in held.items():
            keys += [(third, *key, 0), (third, *key, 1)]
            gram_pieces += [piece, over_core(piece)]

    out = (FACTOR * quint_a) * iterate
    for half in range(HALVES):
        slabs = step_call(keys, gram_pieces, own, half)
        for step in (2, 3, 1, 0):
            got = home(slabs[step], step)
            at = slab_of(high, low, step) * GROUP + half * WIDE
            out = lax.dynamic_update_slice_in_dim(
                out, pick(out, at, WIDE, 1) + FACTOR * got.astype(F32), at, 1
            )
    return out


def solution(mesh):
    shards = shards_cube if dict(mesh.shape) == {"mats": 2, "col": 4, "row": 4} else shards_rows
    in_specs = (P(("mats", "row"), "col"),)
    out_specs = P(("mats", "row"), "col")
    return jax.shard_map(shards, mesh=mesh, in_specs=in_specs, out_specs=out_specs, check_vma=False)
```

time: 743 us -> 462 us (0.62)
  waiting for transfers between devices: 650 us -> 255 us
  starting transfers between devices: 0.13 us -> 88.1 us
  matrix products: 66.9 us -> 0 us
  Pallas kernels: 0 us -> 64 us
  other arithmetic: 8.72 us -> 32.8 us
  local copies, waits for them, and re-layouts: 0 us -> 16.6 us
  between operations: 13.1 us -> 1.14 us
    all_gather x3 -> x0, waiting for transfers between devices: 548 us -> none  [the longest x1 251 us: shards(): column_panel = lax.all_gather(iter_bf, 'row', axis=0, tiled=True)]
    ppermute x0 -> x121, waiting for transfers between devices: none -> 255 us  [the longest x21 79.5 us: over_z(): return lax.ppermute(a, 'row', [(z, z ^ step) for z in range(4)])]
    reduce_scatter x1 -> x0, waiting for transfers between devices: 102 us -> none  [shards(): lax.psum_scatter(lax.dot_general(column_panel, iter_bf, (((1,), (1,)), ((...]
    ppermute x0 -> x121, starting transfers between devices: none -> 88.1 us  [the longest x23 28 us: over_x(): return lax.ppermute(a, 'col', [(0, 2), (1, 3), (2, 0), (3, 1)])]
    dot_general x3 -> x0, matrix products: 66.9 us -> none  [the longest x1 24.9 us: shards(): lax.dot_general(gram_cols, lax.all_gather(first_bf, 'row', axis=0, tiled=...]
    pallas_call x0 -> x3, Pallas kernels: none -> 64 us  [the longest x2 45.5 us: step_call(): pl.pallas_call(functools.partial(step_kernel, keys, half), out_shape=[jax...]
    dynamic_update_slice x0 -> x8, other arithmetic: none -> 17.7 us  [shards_cube(): lax.dynamic_update_slice_in_dim(out, pick(out, at, WIDE, 1) + FACTOR * go...]
  transfers between devices with their start and end apart: 4 -> 121, of which waited for: 4 -> 52; matrix products, arithmetic and copies ran while one was open for 0% -> 8% of each run, Pallas kernels for 0% -> 5%
where the time goes in v1:
time: 462 us; the launch traced here: 458 us
  waiting for transfers between devices  255 us (55%)
  starting transfers between devices  88.1 us (19%)
  Pallas kernels  64 us (14%)
  other arithmetic  32.8 us (7%)
  local copies, waits for them, and re-layouts  16.6 us (4%)
    ppermute x21, waiting for transfers between devices, over_z(): return lax.ppermute(a, 'row', [(z, z ^ step) for z in range(4)])  79.5 us
    ppermute x13, waiting for transfers between devices, over_y(): return lax.ppermute(a, 'mats', [(0, 1), (1, 0)])  66.8 us
    ppermute x23, waiting for transfers between devices, over_x(): return lax.ppermute(a, 'col', [(0, 2), (1, 3), (2, 0), (3, 1)])  54.5 us
    ppermute x8, waiting for transfers between devices, home(): return lax.ppermute(a, ('mats', 'row'), pairs)  51.9 us
    pallas_call x2, Pallas kernels, step_call(): pl.pallas_call(functools.partial(step_kernel, keys, half), out_shape=[jax...  45.5 us
    ppermute x23, starting transfers between devices, over_x(): return lax.ppermute(a, 'col', [(0, 2), (1, 3), (2, 0), (3, 1)])  28 us
    ppermute x21, starting transfers between devices, over_z(): return lax.ppermute(a, 'row', [(z, z ^ step) for z in range(4)])  24.2 us
    pallas_call x1, Pallas kernels, gram_call(): pl.pallas_call(gram_kernel, out_shape=[jax.ShapeDtypeStruct(shape, F32),...  18.5 us
  transfers between devices with their start and end apart: 121, of which 52 were waited for; matrix products, arithmetic and copies ran while one was open for 8% of the time, Pallas kernels for 5%

profile of v1, /device:TPU:12, one launch (start us, length us, event | category | flops | bytes accessed | tf_op | source)
XLA Modules:
  0.0 457.6 jit_solution(14241947636403167973)
XLA Ops:
  2.7 3.3 fusion.1
  15.3 3.1 collective-permute-done.4.refs_4_.refs_52_
  18.4 4.5 collective-permute-done.2
  22.9 2.6 collective-permute-start.8
  25.5 8.6 %collective-permute-done.3 = bf16[256,1024]{1,0:T(8,128)(2,1)} collective-permute-done((bf16[256,1024]{1,0:T(8,128)(2,1)}, bf16[256,1024]{1,0:T(8,128)(2,1)}, u32[]{:S(2)}, u32[]{:S(2)}) %collective-permute-start.3) | collective-permute-done | bytes 524320 | tf_op jit(solution)/shard_map/ppermute | solution.py:84
  35.7 1.7 broadcast_select_fusion
  39.0 1.6 collective-permute-done.12.refs_12_.refs_60_
  42.4 1.9 collective-permute-done.1
  47.1 2.4 collective-permute-done.28.refs_28_
  54.2 3.0 collective-permute-start.10
  58.8 10.3 %collective-permute-done.6.refs_6_.refs_54_ = bf16[256,512]{1,0:T(8,128)(2,1)S(1)} collective-permute-done((bf16[256,512]{1,0:T(8,128)(2,1)S(1)}, bf16[256,512]{1,0:T(8,128)(2,1)S(1)}, u32[]{:S(2)}, u32[]{:S(2)}) %collective-permute-start.6) | collective-permute-done | bytes 262176 | tf_op jit(solution)/shard_map/ppermute | solution.py:88
  70.6 3.2 collective-permute-done.7.refs_7_.refs_55_
  75.4 10.9 %collective-permute-done.11.refs_11_.refs_59_ = bf16[256,512]{1,0:T(8,128)(2,1)S(1)} collective-permute-done((bf16[256,512]{1,0:T(8,128)(2,1)S(1)}, bf16[256,512]{1,0:T(8,128)(2,1)S(1)}, u32[]{:S(2)}, u32[]{:S(2)}) %collective-permute-start.11) | collective-permute-done | bytes 262176 | tf_op jit(solution)/shard_map/ppermute | solution.py:88
  86.4 4.3 collective-permute-done.14.refs_14_.refs_62_
  90.7 2.4 collective-permute-start.15
  94.5 8.3 %collective-permute-done.15.refs_15_.refs_63_ = bf16[256,512]{1,0:T(8,128)(2,1)S(1)} collective-permute-done((bf16[256,512]{1,0:T(8,128)(2,1)S(1)}, bf16[256,512]{1,0:T(8,128)(2,1)S(1)}, u32[]{:S(2)}, u32[]{:S(2)}) %collective-permute-start.15) | collective-permute-done | bytes 262176 | tf_op jit(solution)/shard_map/ppermute | solution.py:88
  102.8 3.7 collective-permute-start.9
  108.1 6.0 %collective-permute-done.5.refs_5_.refs_53_ = bf16[256,512]{1,0:T(8,128)(2,1)S(1)} collective-permute-done((bf16[256,512]{1,0:T(8,128)(2,1)S(1)}, bf16[256,512]{1,0:T(8,128)(2,1)S(1)}, u32[]{:S(2)}, u32[]{:S(2)}) %collective-permute-start.5) | collective-permute-done | bytes 262176 | tf_op jit(solution)/shard_map/ppermute | solution.py:88
  115.6 8.9 %collective-permute-done.9.refs_9_.refs_57_ = bf16[256,512]{1,0:T(8,128)(2,1)S(1)} collective-permute-done((bf16[256,512]{1,0:T(8,128)(2,1)S(1)}, bf16[256,512]{1,0:T(8,128)(2,1)S(1)}, u32[]{:S(2)}, u32[]{:S(2)}) %collective-permute-start.9) | collective-permute-done | bytes 262176 | tf_op jit(solution)/shard_map/ppermute | solution.py:88
  126.0 3.1 collective-permute-done.13.refs_13_.refs_61_
  133.2 5.2 %collective-permute-done.26.refs_26_ = bf16[256,512]{1,0:T(8,128)(2,1)S(1)} collective-permute-done((bf16[256,512]{1,0:T(8,128)(2,1)S(1)}, bf16[256,512]{1,0:T(8,128)(2,1)S(1)}, u32[]{:S(2)}, u32[]{:S(2)}) %collective-permute-start.26) | collective-permute-done | bytes 262176 | tf_op jit(solution)/shard_map/ppermute | solution.py:76
  138.3 5.6 %collective-permute-done.27.refs_27_ = bf16[256,512]{1,0:T(8,128)(2,1)S(1)} collective-permute-done((bf16[256,512]{1,0:T(8,128)(2,1)S(1)}, bf16[256,512]{1,0:T(8,128)(2,1)S(1)}, u32[]{:S(2)}, u32[]{:S(2)}) %collective-permute-start.27) | collective-permute-done | bytes 262176 | tf_op jit(solution)/shard_map/ppermute | solution.py:76
  144.0 5.6 %collective-permute-done.30.refs_30_ = bf16[256,512]{1,0:T(8,128)(2,1)S(1)} collective-permute-done((bf16[256,512]{1,0:T(8,128)(2,1)S(1)}, bf16[256,512]{1,0:T(8,128)(2,1)S(1)}, u32[]{:S(2)}, u32[]{:S(2)}) %collective-permute-start.30) | collective-permute-done | bytes 262176 | tf_op jit(solution)/shard_map/ppermute | solution.py:76
  149.6 3.8 collective-permute-done.31.refs_31_
  158.6 5.1 %collective-permute-done.21.refs_21_ = bf16[256,512]{1,0:T(8,128)(2,1)S(1)} collective-permute-done((bf16[256,512]{1,0:T(8,128)(2,1)S(1)}, bf16[256,512]{1,0:T(8,128)(2,1)S(1)}, u32[]{:S(2)}, u32[]{:S(2)}) %collective-permute-start.21) | collective-permute-done | bytes 262176 | tf_op jit(solution)/shard_map/ppermute | solution.py:76
  163.7 5.6 %collective-permute-done.25.refs_25_ = bf16[256,512]{1,0:T(8,128)(2,1)S(1)} collective-permute-done((bf16[256,512]{1,0:T(8,128)(2,1)S(1)}, bf16[256,512]{1,0:T(8,128)(2,1)S(1)}, u32[]{:S(2)}, u32[]{:S(2)}) %collective-permute-start.25) | collective-permute-done | bytes 262176 | tf_op jit(solution)/shard_map/ppermute | solution.py:76
  169.3 4.7 %collective-permute-done.29.refs_29_ = bf16[256,512]{1,0:T(8,128)(2,1)S(1)} collective-permute-done((bf16[256,512]{1,0:T(8,128)(2,1)S(1)}, bf16[256,512]{1,0:T(8,128)(2,1)S(1)}, u32[]{:S(2)}, u32[]{:S(2)}) %collective-permute-start.29) | collective-permute-done | bytes 262176 | tf_op jit(solution)/shard_map/ppermute | solution.py:76
  179.4 18.5 %gram.1 = (f32[7,2,64,512]{3,2,1,0:T(8,128)}, bf16[7,2,64,512]{3,2,1,0:T(8,128)(2,1)}, f32[7,2,64,512]{3,2,1,0:T(8,128)}, bf16[7,2,64,512]{3,2,1,0:T(8,128)(2,1)}) custom-call(bf16[128,512]{1,0:T(8,128)(2,1)} %copy-done.9, bf16[256,512]{1,0:T(8,128)(2,1)} %copy-done.7, bf16[256,512]{1,0:T(8,128)(2,1)} %copy-done.5, bf16[256,512]{1,0:T(8,128)(2,1)} %copy-done.6, ...), custom_call_target="tpu_custom_call" | custom-call | flops 7516192768 | bytes 20971520 | tf_op jit(solution)/shard_map/gram/pallas_call | solution.py:152
  198.6 22.0 %collective-permute-done.64 = bf16[7,2,64,512]{3,2,1,0:T(8,128)(2,1)S(1)} collective-permute-done((bf16[7,2,64,512]{3,2,1,0:T(8,128)(2,1)}, bf16[7,2,64,512]{3,2,1,0:T(8,128)(2,1)S(1)}, u32[]{:S(2)}, u32[]{:S(2)}) %collective-permute-start.64) | collective-permute-done | bytes 917536 | tf_op jit(solution)/shard_map/ppermute | solution.py:84
  220.6 1.8 convert_add_fusion.1
  224.5 2.3 convert_add_fusion
  229.5 7.1 %collective-permute-done.65 = bf16[7,1,64,512]{3,2,1,0:T(8,128)(2,1)} collective-permute-done((bf16[7,1,64,512]{3,2,1,0:T(8,128)(2,1)}, bf16[7,1,64,512]{3,2,1,0:T(8,128)(2,1)}, u32[]{:S(2)}, u32[]{:S(2)}) %collective-permute-start.65) | collective-permute-done | bytes 458784 | tf_op jit(solution)/shard_map/ppermute | solution.py:88
  238.1 2.9 collective-permute-done.67
  247.0 2.3 collective-permute-done.99.refs_34_
  249.9 3.4 collective-permute-done.101.refs_36_
  259.0 3.3 collective-permute-done.84.refs_18_
  262.3 4.4 collective-permute-done.71.refs_4_
  271.7 3.8 collective-permute-done.103.refs_38_
  275.5 2.0 collective-permute-done.107.refs_42_
  277.5 5.6 %collective-permute-done.109.refs_44_ = bf16[4,64,512]{2,1,0:T(8,128)(2,1)S(1)} collective-permute-done((bf16[4,64,512]{2,1,0:T(8,128)(2,1)S(1)}, bf16[4,64,512]{2,1,0:T(8,128)(2,1)S(1)}, u32[]{:S(2)}, u32[]{:S(2)}) %collective-permute-start.109) | collective-permute-done | bytes 262176 | tf_op jit(solution)/shard_map/ppermute | solution.py:84
  285.7 3.6 collective-permute-done.73.refs_6_
  290.0 3.7 collective-permute-done.77.refs_10_
  293.7 6.6 %collective-permute-done.79.refs_12_ = bf16[5,64,512]{2,1,0:T(8,128)(2,1)S(1)} collective-permute-done((bf16[5,64,512]{2,1,0:T(8,128)(2,1)S(1)}, bf16[5,64,512]{2,1,0:T(8,128)(2,1)S(1)}, u32[]{:S(2)}, u32[]{:S(2)}) %collective-permute-start.79) | collective-permute-done | bytes 327712 | tf_op jit(solution)/shard_map/ppermute | solution.py:88
  304.4 6.7 %collective-permute-done.111.refs_46_ = bf16[4,64,512]{2,1,0:T(8,128)(2,1)} collective-permute-done((bf16[4,64,512]{2,1,0:T(8,128)(2,1)S(1)}, bf16[4,64,512]{2,1,0:T(8,128)(2,1)}, u32[]{:S(2)}, u32[]{:S(2)}) %collective-permute-start.111) | collective-permute-done | bytes 262176 | tf_op jit(solution)/shard_map/ppermute | solution.py:84
  313.0 6.8 %collective-permute-done.96.refs_30_ = bf16[5,64,512]{2,1,0:T(8,128)(2,1)} collective-permute-done((bf16[5,64,512]{2,1,0:T(8,128)(2,1)S(1)}, bf16[5,64,512]{2,1,0:T(8,128)(2,1)}, u32[]{:S(2)}, u32[]{:S(2)}) %collective-permute-start.96) | collective-permute-done | bytes 327712 | tf_op jit(solution)/shard_map/ppermute | solution.py:76
  322.3 3.9 broadcast_multiply_fusion
  326.2 22.8 %step.2 = (bf16[896,256]{1,0:T(8,128)(2,1)}, bf16[896,256]{1,0:T(8,128)(2,1)}, bf16[896,256]{1,0:T(8,128)(2,1)}, bf16[896,256]{1,0:T(8,128)(2,1)}) custom-call(bf16[5,64,512]{2,1,0:T(8,128)(2,1)} %copy-done.4, bf16[5,64,512]{2,1,0:T(8,128)(2,1)} %copy-done.18, bf16[5,64,512]{2,1,0:T(8,128)(2,1)} %copy-done.12, bf16[5,64,512]{2,1,0:T(8,128)(2,1)} %copy-done.24, ...), custom_call_target="tpu_custom_call" | custom-call | flops 13153337344 | bytes 20971520 | tf_op jit(solution)/shard_map/step/pallas_call | solution.py:244
  349.8 3.8 collective-permute-start.114
  353.6 22.7 %step.3 = (bf16[896,256]{1,0:T(8,128)(2,1)}, bf16[896,256]{1,0:T(8,128)(2,1)}, bf16[896,256]{1,0:T(8,128)(2,1)}, bf16[896,256]{1,0:T(8,128)(2,1)}) custom-call(bf16[5,64,512]{2,1,0:T(8,128)(2,1)} %copy-done.4, bf16[5,64,512]{2,1,0:T(8,128)(2,1)} %copy-done.18, bf16[5,64,512]{2,1,0:T(8,128)(2,1)} %copy-done.12, bf16[5,64,512]{2,1,0:T(8,128)(2,1)} %copy-done.24, ...), custom_call_target="tpu_custom_call" | custom-call | flops 13153337344 | bytes 20971520 | tf_op jit(solution)/shard_map/step/pallas_call | solution.py:244
  376.9 6.5 %collective-permute-start.116 = (bf16[896,256]{1,0:T(8,128)(2,1)S(1)}, bf16[896,256]{1,0:T(8,128)(2,1)S(1)}, u32[]{:S(2)}, u32[]{:S(2)}) collective-permute-start(bf16[896,256]{1,0:T(8,128)(2,1)S(1)} %copy-done.10), channel_id=1, source_target_pairs={{0,0},{1,1},{2,16},{3,17},{16,2},{17,3},{18,18},{19,19},{4,4},{5,5... | collective-permute-start | bytes 1376264 | tf_op jit(solution)/shard_map/ppermute | solution.py:97
  383.5 2.2 add_dynamic-update-slice_fusion.7
  385.7 26.6 %collective-permute-done.114 = bf16[896,256]{1,0:T(8,128)(2,1)S(1)} collective-permute-done((bf16[896,256]{1,0:T(8,128)(2,1)}, bf16[896,256]{1,0:T(8,128)(2,1)S(1)}, u32[]{:S(2)}, u32[]{:S(2)}) %collective-permute-start.114) | collective-permute-done | bytes 458784 | tf_op jit(solution)/shard_map/ppermute | solution.py:97
  412.3 2.6 collective-permute-start.119
  414.9 2.2 add_dynamic-update-slice_fusion.6
  417.1 1.9 collective-permute-start.120
  419.0 2.2 add_dynamic-update-slice_fusion.5
  421.2 15.8 %collective-permute-done.116 = bf16[896,256]{1,0:T(8,128)(2,1)S(1)} collective-permute-done((bf16[896,256]{1,0:T(8,128)(2,1)S(1)}, bf16[896,256]{1,0:T(8,128)(2,1)S(1)}, u32[]{:S(2)}, u32[]{:S(2)}) %collective-permute-start.116) | collective-permute-done | bytes 458784 | tf_op jit(solution)/shard_map/ppermute | solution.py:97
  437.1 2.2 add_dynamic-update-slice_fusion.4
  439.3 2.2 add_dynamic-update-slice_fusion.3
  441.5 2.2 add_dynamic-update-slice_fusion.2
  443.7 6.6 %collective-permute-done.119 = bf16[896,256]{1,0:T(8,128)(2,1)S(1)} collective-permute-done((bf16[896,256]{1,0:T(8,128)(2,1)}, bf16[896,256]{1,0:T(8,128)(2,1)S(1)}, u32[]{:S(2)}, u32[]{:S(2)}) %collective-permute-start.119) | collective-permute-done | bytes 458784 | tf_op jit(solution)/shard_map/ppermute | solution.py:97
  450.3 2.2 add_dynamic-update-slice_fusion.1
  452.5 2.9 collective-permute-done.120
  455.4 2.2 add_dynamic-update-slice_fusion
  (421 shorter events, 86.5 us)
Async XLA Ops:
  2.2 10.0 %collective-permute-start = (bf16[128,1024]{1,0:T(8,128)(2,1)}, bf16[128,1024]{1,0:T(8,128)(2,1)S(1)}, u32[]{:S(2)}, u32[]{:S(2)}) collective-permute-start(bf16[128,1024]{1,0:T(8,128)(2,1)} %dynamic-slice_convert_fusion.8), channel_id=1, source_target_pairs={{0,16},{16,0},{1,17},{17,1},{2,18},{18,2},{3,19},{19,3},{4,20},{20... | collective-permute-start | bytes 786440 | tf_op jit(solution)/shard_map/ppermute | solution.py:84
  6.9 16.0 %collective-permute-start.2 = (bf16[256,1024]{1,0:T(8,128)(2,1)}, bf16[256,1024]{1,0:T(8,128)(2,1)}, u32[]{:S(2)}, u32[]{:S(2)}) collective-permute-start(bf16[256,1024]{1,0:T(8,128)(2,1)} %dynamic-slice_convert_fusion.2), channel_id=1, source_target_pairs={{0,16},{16,0},{1,17},{17,1},{2,18},{18,2},{3,19},{19,3},{4,20},{20... | collective-permute-start | bytes 1572872 | tf_op jit(solution)/shard_map/ppermute | solution.py:84
  9.3 24.9 %collective-permute-start.3 = (bf16[256,1024]{1,0:T(8,128)(2,1)}, bf16[256,1024]{1,0:T(8,128)(2,1)}, u32[]{:S(2)}, u32[]{:S(2)}) collective-permute-start(bf16[256,1024]{1,0:T(8,128)(2,1)} %dynamic-slice_convert_fusion), channel_id=1, source_target_pairs={{0,16},{16,0},{1,17},{17,1},{2,18},{18,2},{3,19},{19,3},{4,20},{20... | collective-permute-start | bytes 1572872 | tf_op jit(solution)/shard_map/ppermute | solution.py:84
  10.6 33.6 %collective-permute-start.1 = (bf16[256,1024]{1,0:T(8,128)(2,1)}, bf16[256,1024]{1,0:T(8,128)(2,1)}, u32[]{:S(2)}, u32[]{:S(2)}) collective-permute-start(bf16[256,1024]{1,0:T(8,128)(2,1)} %dynamic-slice_convert_fusion.4), channel_id=1, source_target_pairs={{0,16},{16,0},{1,17},{17,1},{2,18},{18,2},{3,19},{19,3},{4,20},{20... | collective-permute-start | bytes 1572872 | tf_op jit(solution)/shard_map/ppermute | solution.py:84
  13.8 26.9 %collective-permute-start.16 = (bf16[128,512]{1,0:T(8,128)(2,1)S(1)}, bf16[128,512]{1,0:T(8,128)(2,1)}, u32[]{:S(2)}, u32[]{:S(2)}) collective-permute-start(bf16[128,512]{1,0:T(8,128)(2,1)S(1)} %get-tuple-element.57.refs_0_.refs_48_), channel_id=1, source_target_pairs={{0,8},{4,12},{8,0},{12,4},{1,9},{5,13},{9,1},{13,5},{2,10},{6,14},... | collective-permute-start | bytes 393224 | tf_op jit(solution)/shard_map/ppermute | solution.py:76
  18.4 23.7 %collective-permute-start.32 = (bf16[128,512]{1,0:T(8,128)(2,1)S(1)}, bf16[128,512]{1,0:T(8,128)(2,1)}, u32[]{:S(2)}, u32[]{:S(2)}) collective-permute-start(bf16[128,512]{1,0:T(8,128)(2,1)S(1)} %get-tuple-element.57.refs_0_.refs_48_), channel_id=1, source_target_pairs={{0,4},{4,0},{8,12},{12,8},{1,5},{5,1},{9,13},{13,9},{2,6},{6,2},{1... | collective-permute-start | bytes 393224 | tf_op jit(solution)/shard_map/ppermute | solution.py:80
  22.9 14.6 %collective-permute-start.8 = (bf16[128,512]{1,0:T(8,128)(2,1)S(1)}, bf16[128,512]{1,0:T(8,128)(2,1)}, u32[]{:S(2)}, u32[]{:S(2)}) collective-permute-start(bf16[128,512]{1,0:T(8,128)(2,1)S(1)} %get-tuple-element.55), channel_id=1, source_target_pairs={{0,2},{1,3},{2,0},{3,1},{4,6},{5,7},{6,4},{7,5},{8,10},{9,11},{10,... | collective-permute-start | bytes 393224 | tf_op jit(solution)/shard_map/ppermute | solution.py:88
  51.5 17.6 %collective-permute-start.6 = (bf16[256,512]{1,0:T(8,128)(2,1)S(1)}, bf16[256,512]{1,0:T(8,128)(2,1)S(1)}, u32[]{:S(2)}, u32[]{:S(2)}) collective-permute-start(bf16[256,512]{1,0:T(8,128)(2,1)S(1)} %get-tuple-element.50), channel_id=1, source_target_pairs={{0,1},{1,0},{2,3},{3,2},{4,5},{5,4},{6,7},{7,6},{8,9},{9,8},{10,11... | collective-permute-start | bytes 786440 | tf_op jit(solution)/shard_map/ppermute | solution.py:88
  53.4 20.5 %collective-permute-start.7 = (bf16[256,512]{1,0:T(8,128)(2,1)S(1)}, bf16[256,512]{1,0:T(8,128)(2,1)S(1)}, u32[]{:S(2)}, u32[]{:S(2)}) collective-permute-start(bf16[256,512]{1,0:T(8,128)(2,1)S(1)} %get-tuple-element.48), channel_id=1, source_target_pairs={{0,1},{1,0},{2,3},{3,2},{4,5},{5,4},{6,7},{7,6},{8,9},{9,8},{10,11... | collective-permute-start | bytes 786440 | tf_op jit(solution)/shard_map/ppermute | solution.py:88
  54.2 19.7 %collective-permute-start.10 = (bf16[256,512]{1,0:T(8,128)(2,1)S(1)}, bf16[256,512]{1,0:T(8,128)(2,1)S(1)}, u32[]{:S(2)}, u32[]{:S(2)}) collective-permute-start(bf16[256,512]{1,0:T(8,128)(2,1)S(1)} %get-tuple-element.45), channel_id=1, source_target_pairs={{0,2},{1,3},{2,0},{3,1},{4,6},{5,7},{6,4},{7,5},{8,10},{9,11},{10,... | collective-permute-start | bytes 786440 | tf_op jit(solution)/shard_map/ppermute | solution.py:88
  57.1 29.2 %collective-permute-start.11 = (bf16[256,512]{1,0:T(8,128)(2,1)S(1)}, bf16[256,512]{1,0:T(8,128)(2,1)S(1)}, u32[]{:S(2)}, u32[]{:S(2)}) collective-permute-start(bf16[256,512]{1,0:T(8,128)(2,1)S(1)} %get-tuple-element.43), channel_id=1, source_target_pairs={{0,2},{1,3},{2,0},{3,1},{4,6},{5,7},{6,4},{7,5},{8,10},{9,11},{10,... | collective-permute-start | bytes 786440 | tf_op jit(solution)/shard_map/ppermute | solution.py:88
  57.2 33.5 %collective-permute-start.14 = (bf16[256,512]{1,0:T(8,128)(2,1)S(1)}, bf16[256,512]{1,0:T(8,128)(2,1)S(1)}, u32[]{:S(2)}, u32[]{:S(2)}) collective-permute-start(bf16[256,512]{1,0:T(8,128)(2,1)S(1)} %get-tuple-element.44), channel_id=1, source_target_pairs={{0,3},{1,2},{2,1},{3,0},{4,7},{5,6},{6,5},{7,4},{8,11},{9,10},{10,... | collective-permute-start | bytes 786440 | tf_op jit(solution)/shard_map/ppermute | solution.py:88
  69.1 33.7 %collective-permute-start.18 = (bf16[256,512]{1,0:T(8,128)(2,1)S(1)}, bf16[256,512]{1,0:T(8,128)(2,1)S(1)}, u32[]{:S(2)}, u32[]{:S(2)}) collective-permute-start(bf16[256,512]{1,0:T(8,128)(2,1)S(1)} %get-tuple-element.51.refs_2_.refs_50_), channel_id=1, source_target_pairs={{0,8},{4,12},{8,0},{12,4},{1,9},{5,13},{9,1},{13,5},{2,10},{6,14},... | collective-permute-start | bytes 786440 | tf_op jit(solution)/shard_map/ppermute | solution.py:76
  73.9 32.7 %collective-permute-start.34 = (bf16[256,512]{1,0:T(8,128)(2,1)S(1)}, bf16[256,512]{1,0:T(8,128)(2,1)S(1)}, u32[]{:S(2)}, u32[]{:S(2)}) collective-permute-start(bf16[256,512]{1,0:T(8,128)(2,1)S(1)} %get-tuple-element.51.refs_2_.refs_50_), channel_id=1, source_target_pairs={{0,4},{4,0},{8,12},{12,8},{1,5},{5,1},{9,13},{13,9},{2,6},{6,2},{1... | collective-permute-start | bytes 786440 | tf_op jit(solution)/shard_map/ppermute | solution.py:80
  73.9 32.7 %collective-permute-start.19 = (bf16[256,512]{1,0:T(8,128)(2,1)S(1)}, bf16[256,512]{1,0:T(8,128)(2,1)S(1)}, u32[]{:S(2)}, u32[]{:S(2)}) collective-permute-start(bf16[256,512]{1,0:T(8,128)(2,1)S(1)} %get-tuple-element.49.refs_3_.refs_51_), channel_id=1, source_target_pairs={{0,8},{4,12},{8,0},{12,4},{1,9},{5,13},{9,1},{13,5},{2,10},{6,14},... | collective-permute-start | bytes 786440 | tf_op jit(solution)/shard_map/ppermute | solution.py:76
  86.4 21.8 %collective-permute-start.35 = (bf16[256,512]{1,0:T(8,128)(2,1)S(1)}, bf16[256,512]{1,0:T(8,128)(2,1)S(1)}, u32[]{:S(2)}, u32[]{:S(2)}) collective-permute-start(bf16[256,512]{1,0:T(8,128)(2,1)S(1)} %get-tuple-element.49.refs_3_.refs_51_), channel_id=1, source_target_pairs={{0,4},{4,0},{8,12},{12,8},{1,5},{5,1},{9,13},{13,9},{2,6},{6,2},{1... | collective-permute-start | bytes 786440 | tf_op jit(solution)/shard_map/ppermute | solution.py:80
  90.7 12.1 %collective-permute-start.15 = (bf16[256,512]{1,0:T(8,128)(2,1)S(1)}, bf16[256,512]{1,0:T(8,128)(2,1)S(1)}, u32[]{:S(2)}, u32[]{:S(2)}) collective-permute-start(bf16[256,512]{1,0:T(8,128)(2,1)S(1)} %get-tuple-element.42), channel_id=1, source_target_pairs={{0,3},{1,2},{2,1},{3,0},{4,7},{5,6},{6,5},{7,4},{8,11},{9,10},{10,... | collective-permute-start | bytes 786440 | tf_op jit(solution)/shard_map/ppermute | solution.py:88
  102.8 11.3 %collective-permute-start.5 = (bf16[256,512]{1,0:T(8,128)(2,1)S(1)}, bf16[256,512]{1,0:T(8,128)(2,1)S(1)}, u32[]{:S(2)}, u32[]{:S(2)}) collective-permute-start(bf16[256,512]{1,0:T(8,128)(2,1)S(1)} %get-tuple-element.52), channel_id=1, source_target_pairs={{0,1},{1,0},{2,3},{3,2},{4,5},{5,4},{6,7},{7,6},{8,9},{9,8},{10,11... | collective-permute-start | bytes 786440 | tf_op jit(solution)/shard_map/ppermute | solution.py:88
  102.8 21.7 %collective-permute-start.9 = (bf16[256,512]{1,0:T(8,128)(2,1)S(1)}, bf16[256,512]{1,0:T(8,128)(2,1)S(1)}, u32[]{:S(2)}, u32[]{:S(2)}) collective-permute-start(bf16[256,512]{1,0:T(8,128)(2,1)S(1)} %get-tuple-element.47), channel_id=1, source_target_pairs={{0,2},{1,3},{2,0},{3,1},{4,6},{5,7},{6,4},{7,5},{8,10},{9,11},{10,... | collective-permute-start | bytes 786440 | tf_op jit(solution)/shard_map/ppermute | solution.py:88
  106.5 22.5 %collective-permute-start.13 = (bf16[256,512]{1,0:T(8,128)(2,1)S(1)}, bf16[256,512]{1,0:T(8,128)(2,1)S(1)}, u32[]{:S(2)}, u32[]{:S(2)}) collective-permute-start(bf16[256,512]{1,0:T(8,128)(2,1)S(1)} %get-tuple-element.46), channel_id=1, source_target_pairs={{0,3},{1,2},{2,1},{3,0},{4,7},{5,6},{6,5},{7,4},{8,11},{9,10},{10,... | collective-permute-start | bytes 786440 | tf_op jit(solution)/shard_map/ppermute | solution.py:88
  106.6 24.0 %collective-permute-start.17 = (bf16[256,512]{1,0:T(8,128)(2,1)S(1)}, bf16[256,512]{1,0:T(8,128)(2,1)S(1)}, u32[]{:S(2)}, u32[]{:S(2)}) collective-permute-start(bf16[256,512]{1,0:T(8,128)(2,1)S(1)} %get-tuple-element.53.refs_1_.refs_49_), channel_id=1, source_target_pairs={{0,8},{4,12},{8,0},{12,4},{1,9},{5,13},{9,1},{13,5},{2,10},{6,14},... | collective-permute-start | bytes 786440 | tf_op jit(solution)/shard_map/ppermute | solution.py:76
  108.1 23.0 %collective-permute-start.33 = (bf16[256,512]{1,0:T(8,128)(2,1)S(1)}, bf16[256,512]{1,0:T(8,128)(2,1)S(1)}, u32[]{:S(2)}, u32[]{:S(2)}) collective-permute-start(bf16[256,512]{1,0:T(8,128)(2,1)S(1)} %get-tuple-element.53.refs_1_.refs_49_), channel_id=1, source_target_pairs={{0,4},{4,0},{8,12},{12,8},{1,5},{5,1},{9,13},{13,9},{2,6},{6,2},{1... | collective-permute-start | bytes 786440 | tf_op jit(solution)/shard_map/ppermute | solution.py:80
  114.1 18.5 %collective-permute-start.22 = (bf16[256,512]{1,0:T(8,128)(2,1)S(1)}, bf16[256,512]{1,0:T(8,128)(2,1)S(1)}, u32[]{:S(2)}, u32[]{:S(2)}) collective-permute-start(bf16[256,512]{1,0:T(8,128)(2,1)S(1)} %collective-permute-done.6.refs_6_.refs_54_), channel_id=1, source_target_pairs={{0,8},{4,12},{8,0},{12,4},{1,9},{5,13},{9,1},{13,5},{2,10},{6,14},... | collective-permute-start | bytes 786440 | tf_op jit(solution)/shard_map/ppermute | solution.py:76
  129.1 9.3 %collective-permute-start.26 = (bf16[256,512]{1,0:T(8,128)(2,1)S(1)}, bf16[256,512]{1,0:T(8,128)(2,1)S(1)}, u32[]{:S(2)}, u32[]{:S(2)}) collective-permute-start(bf16[256,512]{1,0:T(8,128)(2,1)S(1)} %collective-permute-done.10.refs_10_.refs_58_), channel_id=1, source_target_pairs={{0,8},{4,12},{8,0},{12,4},{1,9},{5,13},{9,1},{13,5},{2,10},{6,14},... | collective-permute-start | bytes 786440 | tf_op jit(solution)/shard_map/ppermute | solution.py:76
  130.6 13.4 %collective-permute-start.27 = (bf16[256,512]{1,0:T(8,128)(2,1)S(1)}, bf16[256,512]{1,0:T(8,128)(2,1)S(1)}, u32[]{:S(2)}, u32[]{:S(2)}) collective-permute-start(bf16[256,512]{1,0:T(8,128)(2,1)S(1)} %collective-permute-done.11.refs_11_.refs_59_), channel_id=1, source_target_pairs={{0,8},{4,12},{8,0},{12,4},{1,9},{5,13},{9,1},{13,5},{2,10},{6,14},... | collective-permute-start | bytes 786440 | tf_op jit(solution)/shard_map/ppermute | solution.py:76
  131.1 18.4 %collective-permute-start.30 = (bf16[256,512]{1,0:T(8,128)(2,1)S(1)}, bf16[256,512]{1,0:T(8,128)(2,1)S(1)}, u32[]{:S(2)}, u32[]{:S(2)}) collective-permute-start(bf16[256,512]{1,0:T(8,128)(2,1)S(1)} %collective-permute-done.14.refs_14_.refs_62_), channel_id=1, source_target_pairs={{0,8},{4,12},{8,0},{12,4},{1,9},{5,13},{9,1},{13,5},{2,10},{6,14},... | collective-permute-start | bytes 786440 | tf_op jit(solution)/shard_map/ppermute | solution.py:76
  132.6 20.7 %collective-permute-start.31 = (bf16[256,512]{1,0:T(8,128)(2,1)S(1)}, bf16[256,512]{1,0:T(8,128)(2,1)S(1)}, u32[]{:S(2)}, u32[]{:S(2)}) collective-permute-start(bf16[256,512]{1,0:T(8,128)(2,1)S(1)} %collective-permute-done.15.refs_15_.refs_63_), channel_id=1, source_target_pairs={{0,8},{4,12},{8,0},{12,4},{1,9},{5,13},{9,1},{13,5},{2,10},{6,14},... | collective-permute-start | bytes 786440 | tf_op jit(solution)/shard_map/ppermute | solution.py:76
  133.2 20.2 %collective-permute-start.38 = (bf16[256,512]{1,0:T(8,128)(2,1)S(1)}, bf16[256,512]{1,0:T(8,128)(2,1)S(1)}, u32[]{:S(2)}, u32[]{:S(2)}) collective-permute-start(bf16[256,512]{1,0:T(8,128)(2,1)S(1)} %collective-permute-done.6.refs_6_.refs_54_), channel_id=1, source_target_pairs={{0,4},{4,0},{8,12},{12,8},{1,5},{5,1},{9,13},{13,9},{2,6},{6,2},{1... | collective-permute-start | bytes 786440 | tf_op jit(solution)/shard_map/ppermute | solution.py:80
  138.3 15.5 %collective-permute-start.39 = (bf16[256,512]{1,0:T(8,128)(2,1)S(1)}, bf16[256,512]{1,0:T(8,128)(2,1)S(1)}, u32[]{:S(2)}, u32[]{:S(2)}) collective-permute-start(bf16[256,512]{1,0:T(8,128)(2,1)S(1)} %collective-permute-done.7.refs_7_.refs_55_), channel_id=1, source_target_pairs={{0,4},{4,0},{8,12},{12,8},{1,5},{5,1},{9,13},{13,9},{2,6},{6,2},{1... | collective-permute-start | bytes 786440 | tf_op jit(solution)/shard_map/ppermute | solution.py:80
  144.0 10.0 %collective-permute-start.42 = (bf16[256,512]{1,0:T(8,128)(2,1)S(1)}, bf16[256,512]{1,0:T(8,128)(2,1)S(1)}, u32[]{:S(2)}, u32[]{:S(2)}) collective-permute-start(bf16[256,512]{1,0:T(8,128)(2,1)S(1)} %collective-permute-done.10.refs_10_.refs_58_), channel_id=1, source_target_pairs={{0,4},{4,0},{8,12},{12,8},{1,5},{5,1},{9,13},{13,9},{2,6},{6,2},{1... | collective-permute-start | bytes 786440 | tf_op jit(solution)/shard_map/ppermute | solution.py:80
  154.5 9.2 %collective-permute-start.21 = (bf16[256,512]{1,0:T(8,128)(2,1)S(1)}, bf16[256,512]{1,0:T(8,128)(2,1)S(1)}, u32[]{:S(2)}, u32[]{:S(2)}) collective-permute-start(bf16[256,512]{1,0:T(8,128)(2,1)S(1)} %collective-permute-done.5.refs_5_.refs_53_), channel_id=1, source_target_pairs={{0,8},{4,12},{8,0},{12,4},{1,9},{5,13},{9,1},{13,5},{2,10},{6,14},... | collective-permute-start | bytes 786440 | tf_op jit(solution)/shard_map/ppermute | solution.py:76
  156.0 13.3 %collective-permute-start.25 = (bf16[256,512]{1,0:T(8,128)(2,1)S(1)}, bf16[256,512]{1,0:T(8,128)(2,1)S(1)}, u32[]{:S(2)}, u32[]{:S(2)}) collective-permute-start(bf16[256,512]{1,0:T(8,128)(2,1)S(1)} %collective-permute-done.9.refs_9_.refs_57_), channel_id=1, source_target_pairs={{0,8},{4,12},{8,0},{12,4},{1,9},{5,13},{9,1},{13,5},{2,10},{6,14},... | collective-permute-start | bytes 786440 | tf_op jit(solution)/shard_map/ppermute | solution.py:76
  156.6 17.5 %collective-permute-start.29 = (bf16[256,512]{1,0:T(8,128)(2,1)S(1)}, bf16[256,512]{1,0:T(8,128)(2,1)S(1)}, u32[]{:S(2)}, u32[]{:S(2)}) collective-permute-start(bf16[256,512]{1,0:T(8,128)(2,1)S(1)} %collective-permute-done.13.refs_13_.refs_61_), channel_id=1, source_target_pairs={{0,8},{4,12},{8,0},{12,4},{1,9},{5,13},{9,1},{13,5},{2,10},{6,14},... | collective-permute-start | bytes 786440 | tf_op jit(solution)/shard_map/ppermute | solution.py:76
  158.1 16.0 %collective-permute-start.37 = (bf16[256,512]{1,0:T(8,128)(2,1)S(1)}, bf16[256,512]{1,0:T(8,128)(2,1)S(1)}, u32[]{:S(2)}, u32[]{:S(2)}) collective-permute-start(bf16[256,512]{1,0:T(8,128)(2,1)S(1)} %collective-permute-done.5.refs_5_.refs_53_), channel_id=1, source_target_pairs={{0,4},{4,0},{8,12},{12,8},{1,5},{5,1},{9,13},{13,9},{2,6},{6,2},{1... | collective-permute-start | bytes 786440 | tf_op jit(solution)/shard_map/ppermute | solution.py:80
  158.1 16.5 %collective-permute-start.41 = (bf16[256,512]{1,0:T(8,128)(2,1)S(1)}, bf16[256,512]{1,0:T(8,128)(2,1)S(1)}, u32[]{:S(2)}, u32[]{:S(2)}) collective-permute-start(bf16[256,512]{1,0:T(8,128)(2,1)S(1)} %collective-permute-done.9.refs_9_.refs_57_), channel_id=1, source_target_pairs={{0,4},{4,0},{8,12},{12,8},{1,5},{5,1},{9,13},{13,9},{2,6},{6,2},{1... | collective-permute-start | bytes 786440 | tf_op jit(solution)/shard_map/ppermute | solution.py:80
  163.7 11.0 %collective-permute-start.45 = (bf16[256,512]{1,0:T(8,128)(2,1)S(1)}, bf16[256,512]{1,0:T(8,128)(2,1)S(1)}, u32[]{:S(2)}, u32[]{:S(2)}) collective-permute-start(bf16[256,512]{1,0:T(8,128)(2,1)S(1)} %collective-permute-done.13.refs_13_.refs_61_), channel_id=1, source_target_pairs={{0,4},{4,0},{8,12},{12,8},{1,5},{5,1},{9,13},{13,9},{2,6},{6,2},{1... | collective-permute-start | bytes 786440 | tf_op jit(solution)/shard_map/ppermute | solution.py:80
  197.9 22.7 %collective-permute-start.64 = (bf16[7,2,64,512]{3,2,1,0:T(8,128)(2,1)}, bf16[7,2,64,512]{3,2,1,0:T(8,128)(2,1)S(1)}, u32[]{:S(2)}, u32[]{:S(2)}) collective-permute-start(bf16[7,2,64,512]{3,2,1,0:T(8,128)(2,1)} %get-tuple-element.18), channel_id=1, source_target_pairs={{0,16},{16,0},{1,17},{17,1},{2,18},{18,2},{3,19},{19,3},{4,20},{20... | collective-permute-start | bytes 2752520 | tf_op jit(solution)/shard_map/ppermute | solution.py:84
  198.6 25.9 %collective-permute-start.66 = (bf16[7,2,64,512]{3,2,1,0:T(8,128)(2,1)}, bf16[7,2,64,512]{3,2,1,0:T(8,128)(2,1)}, u32[]{:S(2)}, u32[]{:S(2)}) collective-permute-start(bf16[7,2,64,512]{3,2,1,0:T(8,128)(2,1)} %get-tuple-element.20), channel_id=1, source_target_pairs={{0,1},{1,0},{2,3},{3,2},{4,5},{5,4},{6,7},{7,6},{8,9},{9,8},{10,11... | collective-permute-start | bytes 2752520 | tf_op jit(solution)/shard_map/ppermute | solution.py:88
  224.5 12.2 %collective-permute-start.65 = (bf16[7,1,64,512]{3,2,1,0:T(8,128)(2,1)}, bf16[7,1,64,512]{3,2,1,0:T(8,128)(2,1)}, u32[]{:S(2)}, u32[]{:S(2)}) collective-permute-start(bf16[7,1,64,512]{3,2,1,0:T(8,128)(2,1)} %dynamic-slice_convert_fusion.7), channel_id=1, source_target_pairs={{0,1},{1,0},{2,3},{3,2},{4,5},{5,4},{6,7},{7,6},{8,9},{9,8},{10,11... | collective-permute-start | bytes 1376264 | tf_op jit(solution)/shard_map/ppermute | solution.py:88
  228.8 12.2 %collective-permute-start.67 = (bf16[7,1,64,512]{3,2,1,0:T(8,128)(2,1)}, bf16[7,1,64,512]{3,2,1,0:T(8,128)(2,1)}, u32[]{:S(2)}, u32[]{:S(2)}) collective-permute-start(bf16[7,1,64,512]{3,2,1,0:T(8,128)(2,1)} %dynamic-slice_convert_fusion.6), channel_id=1, source_target_pairs={{0,16},{16,0},{1,17},{17,1},{2,18},{18,2},{3,19},{19,3},{4,20},{20... | collective-permute-start | bytes 1376264 | tf_op jit(solution)/shard_map/ppermute | solution.py:84
  244.1 9.2 %collective-permute-start.101 = (bf16[4,64,512]{2,1,0:T(8,128)(2,1)S(1)}, bf16[4,64,512]{2,1,0:T(8,128)(2,1)S(1)}, u32[]{:S(2)}, u32[]{:S(2)}) collective-permute-start(bf16[4,64,512]{2,1,0:T(8,128)(2,1)S(1)} %bitcast.6), channel_id=1, source_target_pairs={{0,8},{4,12},{8,0},{12,4},{1,9},{5,13},{9,1},{13,5},{2,10},{6,14},... | collective-permute-start | bytes 786440 | tf_op jit(solution)/shard_map/ppermute | solution.py:76
  245.7 11.8 %collective-permute-start.69 = (bf16[5,64,512]{2,1,0:T(8,128)(2,1)S(1)}, bf16[5,64,512]{2,1,0:T(8,128)(2,1)S(1)}, u32[]{:S(2)}, u32[]{:S(2)}) collective-permute-start(bf16[5,64,512]{2,1,0:T(8,128)(2,1)S(1)} %get-tuple-element.39.refs_0_), channel_id=1, source_target_pairs={{0,8},{4,12},{8,0},{12,4},{1,9},{5,13},{9,1},{13,5},{2,10},{6,14},... | collective-permute-start | bytes 983048 | tf_op jit(solution)/shard_map/ppermute | solution.py:76
  249.3 13.0 %collective-permute-start.84 = (bf16[5,64,512]{2,1,0:T(8,128)(2,1)S(1)}, bf16[5,64,512]{2,1,0:T(8,128)(2,1)S(1)}, u32[]{:S(2)}, u32[]{:S(2)}) collective-permute-start(bf16[5,64,512]{2,1,0:T(8,128)(2,1)S(1)} %get-tuple-element.38.refs_16_), channel_id=1, source_target_pairs={{0,16},{16,0},{1,17},{17,1},{2,18},{18,2},{3,19},{19,3},{4,20},{20... | collective-permute-start | bytes 983048 | tf_op jit(solution)/shard_map/ppermute | solution.py:84
  253.3 13.4 %collective-permute-start.71 = (bf16[5,64,512]{2,1,0:T(8,128)(2,1)S(1)}, bf16[5,64,512]{2,1,0:T(8,128)(2,1)S(1)}, u32[]{:S(2)}, u32[]{:S(2)}) collective-permute-start(bf16[5,64,512]{2,1,0:T(8,128)(2,1)S(1)} %get-tuple-element.39.refs_0_), channel_id=1, source_target_pairs={{0,16},{16,0},{1,17},{17,1},{2,18},{18,2},{3,19},{19,3},{4,20},{20... | collective-permute-start | bytes 983048 | tf_op jit(solution)/shard_map/ppermute | solution.py:84
  255.3 11.4 %collective-permute-start.86 = (bf16[5,64,512]{2,1,0:T(8,128)(2,1)S(1)}, bf16[5,64,512]{2,1,0:T(8,128)(2,1)S(1)}, u32[]{:S(2)}, u32[]{:S(2)}) collective-permute-start(bf16[5,64,512]{2,1,0:T(8,128)(2,1)S(1)} %get-tuple-element.38.refs_16_), channel_id=1, source_target_pairs={{0,1},{1,0},{2,3},{3,2},{4,5},{5,4},{6,7},{7,6},{8,9},{9,8},{10,11... | collective-permute-start | bytes 983048 | tf_op jit(solution)/shard_map/ppermute | solution.py:88
  255.9 12.5 %collective-permute-start.75 = (bf16[5,64,512]{2,1,0:T(8,128)(2,1)S(1)}, bf16[5,64,512]{2,1,0:T(8,128)(2,1)S(1)}, u32[]{:S(2)}, u32[]{:S(2)}) collective-permute-start(bf16[5,64,512]{2,1,0:T(8,128)(2,1)S(1)} %get-tuple-element.39.refs_0_), channel_id=1, source_target_pairs={{0,1},{1,0},{2,3},{3,2},{4,5},{5,4},{6,7},{7,6},{8,9},{9,8},{10,11... | collective-permute-start | bytes 983048 | tf_op jit(solution)/shard_map/ppermute | solution.py:88
  257.5 11.4 %collective-permute-start.90 = (bf16[5,64,512]{2,1,0:T(8,128)(2,1)S(1)}, bf16[5,64,512]{2,1,0:T(8,128)(2,1)S(1)}, u32[]{:S(2)}, u32[]{:S(2)}) collective-permute-start(bf16[5,64,512]{2,1,0:T(8,128)(2,1)S(1)} %get-tuple-element.38.refs_16_), channel_id=1, source_target_pairs={{0,8},{4,12},{8,0},{12,4},{1,9},{5,13},{9,1},{13,5},{2,10},{6,14},... | collective-permute-start | bytes 983048 | tf_op jit(solution)/shard_map/ppermute | solution.py:76
  269.0 14.1 %collective-permute-start.109 = (bf16[4,64,512]{2,1,0:T(8,128)(2,1)S(1)}, bf16[4,64,512]{2,1,0:T(8,128)(2,1)S(1)}, u32[]{:S(2)}, u32[]{:S(2)}) collective-permute-start(bf16[4,64,512]{2,1,0:T(8,128)(2,1)S(1)} %collective-permute-done.101.refs_36_), channel_id=1, source_target_pairs={{0,16},{16,0},{1,17},{17,1},{2,18},{18,2},{3,19},{19,3},{4,20},{20... | collective-permute-start | bytes 786440 | tf_op jit(solution)/shard_map/ppermute | solution.py:84
  270.3 19.0 %collective-permute-start.73 = (bf16[5,64,512]{2,1,0:T(8,128)(2,1)S(1)}, bf16[5,64,512]{2,1,0:T(8,128)(2,1)S(1)}, u32[]{:S(2)}, u32[]{:S(2)}) collective-permute-start(bf16[5,64,512]{2,1,0:T(8,128)(2,1)S(1)} %collective-permute-done.69.refs_2_), channel_id=1, source_target_pairs={{0,16},{16,0},{1,17},{17,1},{2,18},{18,2},{3,19},{19,3},{4,20},{20... | collective-permute-start | bytes 983048 | tf_op jit(solution)/shard_map/ppermute | solution.py:84
  271.0 18.8 %collective-permute-start.88 = (bf16[5,64,512]{2,1,0:T(8,128)(2,1)S(1)}, bf16[5,64,512]{2,1,0:T(8,128)(2,1)S(1)}, u32[]{:S(2)}, u32[]{:S(2)}) collective-permute-start(bf16[5,64,512]{2,1,0:T(8,128)(2,1)S(1)} %collective-permute-done.84.refs_18_), channel_id=1, source_target_pairs={{0,1},{1,0},{2,3},{3,2},{4,5},{5,4},{6,7},{7,6},{8,9},{9,8},{10,11... | collective-permute-start | bytes 983048 | tf_op jit(solution)/shard_map/ppermute | solution.py:88
  283.1 10.6 %collective-permute-start.77 = (bf16[5,64,512]{2,1,0:T(8,128)(2,1)S(1)}, bf16[5,64,512]{2,1,0:T(8,128)(2,1)S(1)}, u32[]{:S(2)}, u32[]{:S(2)}) collective-permute-start(bf16[5,64,512]{2,1,0:T(8,128)(2,1)S(1)} %collective-permute-done.69.refs_2_), channel_id=1, source_target_pairs={{0,1},{1,0},{2,3},{3,2},{4,5},{5,4},{6,7},{7,6},{8,9},{9,8},{10,11... | collective-permute-start | bytes 983048 | tf_op jit(solution)/shard_map/ppermute | solution.py:88
  283.7 16.5 %collective-permute-start.79 = (bf16[5,64,512]{2,1,0:T(8,128)(2,1)S(1)}, bf16[5,64,512]{2,1,0:T(8,128)(2,1)S(1)}, u32[]{:S(2)}, u32[]{:S(2)}) collective-permute-start(bf16[5,64,512]{2,1,0:T(8,128)(2,1)S(1)} %collective-permute-done.71.refs_4_), channel_id=1, source_target_pairs={{0,1},{1,0},{2,3},{3,2},{4,5},{5,4},{6,7},{7,6},{8,9},{9,8},{10,11... | collective-permute-start | bytes 983048 | tf_op jit(solution)/shard_map/ppermute | solution.py:88
  285.2 15.1 %collective-permute-start.92 = (bf16[5,64,512]{2,1,0:T(8,128)(2,1)S(1)}, bf16[5,64,512]{2,1,0:T(8,128)(2,1)}, u32[]{:S(2)}, u32[]{:S(2)}) collective-permute-start(bf16[5,64,512]{2,1,0:T(8,128)(2,1)S(1)} %collective-permute-done.84.refs_18_), channel_id=1, source_target_pairs={{0,8},{4,12},{8,0},{12,4},{1,9},{5,13},{9,1},{13,5},{2,10},{6,14},... | collective-permute-start | bytes 983048 | tf_op jit(solution)/shard_map/ppermute | solution.py:76
  289.3 12.5 %collective-permute-start.94 = (bf16[5,64,512]{2,1,0:T(8,128)(2,1)S(1)}, bf16[5,64,512]{2,1,0:T(8,128)(2,1)}, u32[]{:S(2)}, u32[]{:S(2)}) collective-permute-start(bf16[5,64,512]{2,1,0:T(8,128)(2,1)S(1)} %collective-permute-done.86.refs_20_), channel_id=1, source_target_pairs={{0,8},{4,12},{8,0},{12,4},{1,9},{5,13},{9,1},{13,5},{2,10},{6,14},... | collective-permute-start | bytes 983048 | tf_op jit(solution)/shard_map/ppermute | solution.py:76
  289.9 11.9 %collective-permute-start.70 = (bf16[5,64,512]{2,1,0:T(8,128)(2,1)S(1)}, bf16[5,64,512]{2,1,0:T(8,128)(2,1)S(1)}, u32[]{:S(2)}, u32[]{:S(2)}) collective-permute-start(bf16[5,64,512]{2,1,0:T(8,128)(2,1)S(1)} %collective-permute-done.69.refs_2_), channel_id=1, source_target_pairs={{0,4},{4,0},{8,12},{12,8},{1,5},{5,1},{9,13},{13,9},{2,6},{6,2},{1... | collective-permute-start | bytes 983048 | tf_op jit(solution)/shard_map/ppermute | solution.py:80
  302.4 10.1 %collective-permute-start.81 = (bf16[5,64,512]{2,1,0:T(8,128)(2,1)S(1)}, bf16[5,64,512]{2,1,0:T(8,128)(2,1)}, u32[]{:S(2)}, u32[]{:S(2)}) collective-permute-start(bf16[5,64,512]{2,1,0:T(8,128)(2,1)S(1)} %collective-permute-done.73.refs_6_), channel_id=1, source_target_pairs={{0,1},{1,0},{2,3},{3,2},{4,5},{5,4},{6,7},{7,6},{8,9},{9,8},{10,11... | collective-permute-start | bytes 983048 | tf_op jit(solution)/shard_map/ppermute | solution.py:88
  349.0 34.4 %collective-permute-start.113 = (bf16[896,256]{1,0:T(8,128)(2,1)}, bf16[896,256]{1,0:T(8,128)(2,1)S(1)}, u32[]{:S(2)}, u32[]{:S(2)}) collective-permute-start(bf16[896,256]{1,0:T(8,128)(2,1)} %get-tuple-element.21), channel_id=1, source_target_pairs={{0,2},{1,3},{2,18},{3,19},{16,0},{17,1},{18,16},{19,17},{4,6},{5,7... | collective-permute-start | bytes 1376264 | tf_op jit(solution)/shard_map/ppermute | solution.py:97
  349.8 62.5 %collective-permute-start.114 = (bf16[896,256]{1,0:T(8,128)(2,1)}, bf16[896,256]{1,0:T(8,128)(2,1)S(1)}, u32[]{:S(2)}, u32[]{:S(2)}) collective-permute-start(bf16[896,256]{1,0:T(8,128)(2,1)} %get-tuple-element.22), channel_id=1, source_target_pairs={{0,3},{1,2},{2,19},{3,18},{16,1},{17,0},{18,17},{19,16},{4,7},{5,6... | collective-permute-start | bytes 1376264 | tf_op jit(solution)/shard_map/ppermute | solution.py:97
  376.3 63.0 %collective-permute-start.117 = (bf16[896,256]{1,0:T(8,128)(2,1)}, bf16[896,256]{1,0:T(8,128)(2,1)S(1)}, u32[]{:S(2)}, u32[]{:S(2)}) collective-permute-start(bf16[896,256]{1,0:T(8,128)(2,1)} %get-tuple-element.25), channel_id=1, source_target_pairs={{0,2},{1,3},{2,18},{3,19},{16,0},{17,1},{18,16},{19,17},{4,6},{5,7... | collective-permute-start | bytes 1376264 | tf_op jit(solution)/shard_map/ppermute | solution.py:97
  376.9 40.2 %collective-permute-start.115 = (bf16[896,256]{1,0:T(8,128)(2,1)S(1)}, bf16[896,256]{1,0:T(8,128)(2,1)S(1)}, u32[]{:S(2)}, u32[]{:S(2)}) collective-permute-start(bf16[896,256]{1,0:T(8,128)(2,1)S(1)} %copy-done.11), channel_id=1, source_target_pairs={{0,1},{1,0},{2,17},{3,16},{16,3},{17,2},{18,19},{19,18},{4,5},{5,4... | collective-permute-start | bytes 1376264 | tf_op jit(solution)/shard_map/ppermute | solution.py:97
  376.9 60.2 %collective-permute-start.116 = (bf16[896,256]{1,0:T(8,128)(2,1)S(1)}, bf16[896,256]{1,0:T(8,128)(2,1)S(1)}, u32[]{:S(2)}, u32[]{:S(2)}) collective-permute-start(bf16[896,256]{1,0:T(8,128)(2,1)S(1)} %copy-done.10), channel_id=1, source_target_pairs={{0,0},{1,1},{2,16},{3,17},{16,2},{17,3},{18,18},{19,19},{4,4},{5,5... | collective-permute-start | bytes 1376264 | tf_op jit(solution)/shard_map/ppermute | solution.py:97
  383.4 58.0 %collective-permute-start.118 = (bf16[896,256]{1,0:T(8,128)(2,1)}, bf16[896,256]{1,0:T(8,128)(2,1)S(1)}, u32[]{:S(2)}, u32[]{:S(2)}) collective-permute-start(bf16[896,256]{1,0:T(8,128)(2,1)} %get-tuple-element.26), channel_id=1, source_target_pairs={{0,3},{1,2},{2,19},{3,18},{16,1},{17,0},{18,17},{19,16},{4,7},{5,6... | collective-permute-start | bytes 1376264 | tf_op jit(solution)/shard_map/ppermute | solution.py:97
  412.3 38.0 %collective-permute-start.119 = (bf16[896,256]{1,0:T(8,128)(2,1)}, bf16[896,256]{1,0:T(8,128)(2,1)S(1)}, u32[]{:S(2)}, u32[]{:S(2)}) collective-permute-start(bf16[896,256]{1,0:T(8,128)(2,1)} %get-tuple-element.27), channel_id=1, source_target_pairs={{0,1},{1,0},{2,17},{3,16},{16,3},{17,2},{18,19},{19,18},{4,5},{5,4... | collective-permute-start | bytes 1376264 | tf_op jit(solution)/shard_map/ppermute | solution.py:97
  417.1 38.3 %collective-permute-start.120 = (bf16[896,256]{1,0:T(8,128)(2,1)}, bf16[896,256]{1,0:T(8,128)(2,1)S(1)}, u32[]{:S(2)}, u32[]{:S(2)}) collective-permute-start(bf16[896,256]{1,0:T(8,128)(2,1)} %get-tuple-element.28), channel_id=1, source_target_pairs={{0,0},{1,1},{2,16},{3,17},{16,2},{17,3},{18,18},{19,19},{4,4},{5,5... | collective-permute-start | bytes 1376264 | tf_op jit(solution)/shard_map/ppermute | solution.py:97
  (159 other events, 3710.5 us)

commit v2 on v0

v2 whole, which is shorter than its diff:
```python
import functools
import math

import jax
import jax.numpy as jnp
from jax import lax
from jax.experimental import pallas as pl
from jax.experimental.pallas import tpu as pltpu
from jax.sharding import PartitionSpec as P

ORDER = 3584
COLS = 8192

BF16 = jnp.bfloat16
F32 = jnp.float32

quint_a = 3.4445
quint_b = -4.775
quint_c = 2.0315

FACTOR = 0.2 * math.sqrt(max(ORDER, COLS))

BLOCK = 512
BLOCKS = ORDER // BLOCK
DIAGS = 4
MINE = DIAGS * BLOCKS // 2
THIRDS = ((0, 5), (5, 10), (10, 14))
PLACES = 8
UNIT = BLOCK // PLACES
TAIL = 16
SLAB = ORDER // 4
BAND = SLAB // BLOCKS
GROUP = COLS // 16
PIECES = (1, 2, 4)
HALVES = 2
WIDE = GROUP // HALVES
VMEM = 60 << 20


def shards_rows(iterate):
    iter_bf = iterate.astype(BF16)
    column_panel = lax.all_gather(iter_bf, "row", axis=0, tiled=True)
    gram_part = lax.psum_scatter(
        lax.dot_general(
            column_panel, iter_bf, (((1,), (1,)), ((), ())), preferred_element_type=F32
        ),
        "col",
        scatter_dimension=0,
        tiled=True,
    )
    gram_cols = lax.all_gather(gram_part.astype(BF16), "col", axis=0, tiled=True)
    first = lax.dot_general(
        gram_cols, column_panel, (((0,), (0,)), ((), ())), preferred_element_type=F32
    )
    second = lax.dot_general(
        gram_cols,
        lax.all_gather(first.astype(BF16), "row", axis=0, tiled=True),
        (((0,), (0,)), ((), ())),
        preferred_element_type=F32,
    )
    return FACTOR * (quint_a * iterate + quint_b * first + quint_c * second)


def flip(bit, by):
    return 1 - bit if by else bit


def place():
    col = lax.axis_index("col")
    row = lax.axis_index("row")
    return lax.axis_index("mats"), col // 2, col % 2, row // 2, row % 2


def slab_of(high, low, step):
    return 2 * flip(high, step >> 1) + flip(low, step & 1)


def place_of(x, y, low, by):
    return 4 * flip(x, by >> 2) + 2 * flip(y, by >> 1 & 1) + flip(low, by & 1)


def over_x(a):
    return lax.ppermute(a, "col", [(0, 2), (1, 3), (2, 0), (3, 1)])


def over_core(a):
    return lax.ppermute(a, "col", [(0, 1), (1, 0), (2, 3), (3, 2)])


def over_y(a):
    return lax.ppermute(a, "mats", [(0, 1), (1, 0)])


def over_z(a, step=1):
    return lax.ppermute(a, "row", [(z, z ^ step) for z in range(4)])


MOVES = {4: over_x, 2: over_y, 1: over_z}
ORDERS = ((4, 2, 1), (2, 1, 4), (1, 4, 2))


def home(a, step):
    pairs = []
    for y in range(2):
        for z in range(4):
            part, slab = z // 2, (2 * y + z % 2) ^ step
            pairs.append((4 * y + z, 4 * part + slab))
    return lax.ppermute(a, ("mats", "row"), pairs)


def dot(a, b, dims):
    return lax.dot_general(a, b, (dims, ((), ())), preferred_element_type=F32)


def place_of_block():
    return [(p, b) for p, blocks in enumerate(PIECES) for b in range(blocks)]


def on_diagonal(unit):
    shape = (UNIT, BLOCK)
    return lax.broadcasted_iota(jnp.int32, shape, 0) + unit * UNIT == lax.broadcasted_iota(
        jnp.int32, shape, 1
    )


def kept(third, stage):
    gone = sum(ORDERS[third][: stage + 1])
    return [by for by in range(PLACES) if not by & gone]


def sent(third, stage):
    return [by | ORDERS[third][stage] for by in kept(third, stage)]


def rows_sent(third, stage):
    lo, hi = THIRDS[third]
    return (hi - lo) * len(sent(third, stage)) * UNIT


def exchange_shapes(third, stage):
    lo, hi = THIRDS[third]
    return [
        jax.ShapeDtypeStruct((hi - lo, len(kept(third, stage)), UNIT, BLOCK), F32),
        jax.ShapeDtypeStruct((rows_sent(third, stage) + TAIL, BLOCK), BF16),
    ]


def write_sent(send, tail, e, parts, units, flag):
    left = jnp.zeros((1, BLOCK), F32)
    for n, (part, unit) in enumerate(zip(parts, units)):
        near = part.astype(BF16)
        row = (e * len(parts) + n) * UNIT
        send[pl.ds(row if isinstance(row, int) else pl.multiple_of(row, UNIT), UNIT), :] = near
        rest = jnp.where(on_diagonal(unit), part - near.astype(F32), 0.0)
        left += jnp.sum(rest, axis=0, keepdims=True)
    tail[pl.ds(e, 1), :] = left * flag


def gram_kernel(*refs):
    count = 2 * len(PIECES)
    inputs, refs = refs[:count], refs[count:]
    keeps, sends, refs = refs[0:6:2], refs[1:6:2], refs[6:]
    panel, turned, tails, arrived = refs[0], refs[1], refs[2:5], refs[5]
    y, x, core, high, low = place()
    for source in range(2):
        for i, (p, b) in enumerate(place_of_block()):
            for step in range(4):
                slab = slab_of(high, low, step)
                columns = pl.ds(source * GROUP, GROUP)
                pltpu.make_async_copy(
                    inputs[source * len(PIECES) + p].at[step, pl.ds(b * BAND, BAND), :],
                    panel.at[i, pl.ds(pl.multiple_of(slab * BAND, BAND), BAND), columns],
                    arrived.at[0],
                ).start()
                for n in range(2):
                    to_x, to_y = slab // 2, slab % 2
                    by = 4 * jnp.abs(to_x - x) + 2 * jnp.abs(to_y - y) + jnp.abs(n - low)
                    pltpu.make_async_copy(
                        inputs[source * len(PIECES) + p].at[step, pl.ds(b * BAND + n * UNIT, UNIT), :],
                        turned.at[i, pl.ds(pl.multiple_of(by * UNIT, UNIT), UNIT), columns],
                        arrived.at[1],
                    ).start()
    for tail in tails:
        tail[...] = jnp.zeros_like(tail)
    pltpu.make_async_copy(panel, panel, arrived.at[0]).wait()
    pltpu.make_async_copy(turned, turned, arrived.at[1]).wait()
    for third, (lo, hi) in enumerate(THIRDS):
        keep, send, tail = keeps[third], sends[third], tails[third]

        def block(e, carry):
            second = (e + lo >= BLOCKS).astype(jnp.int32)
            i = e + lo - BLOCKS * second
            j = lax.rem(i + 2 * core + second, BLOCKS)
            flag = jnp.logical_and(core == 0, second == 0).astype(F32)
            got = dot(turned[i], panel[j], ((1,), (1,)))
            for n, by in enumerate(kept(third, 0)):
                keep[e, n] = got[by * UNIT : (by + 1) * UNIT]
            parts = [got[by * UNIT : (by + 1) * UNIT] for by in sent(third, 0)]
            units = [place_of(x, y, low, by) for by in sent(third, 0)]
            write_sent(send, tail, e, parts, units, flag)
            return carry

        lax.fori_loop(0, hi - lo, block, 0)
        send[pl.ds(rows_sent(third, 0), TAIL), :] = tail[...].astype(BF16)


def add_kernel(stage, *refs):
    last = stage == 2
    keeps, gots = refs[0:6:2], refs[1:6:2]
    outs = refs[6:]
    y, x, core, high, low = place()
    for third, (lo, hi) in enumerate(THIRDS):
        keep, got = keeps[third], gots[third]
        held = kept(third, stage)
        left = got[pl.ds(rows_sent(third, stage), TAIL), :].astype(F32)
        if not last:
            nxt, send, tail = outs[2 * third], outs[2 * third + 1], outs[6 + third]
            tail[...] = jnp.zeros_like(tail)
        for e in range(hi - lo):
            diagonal = e + lo < BLOCKS
            sums = {}
            for n, by in enumerate(held):
                row = (e * len(held) + n) * UNIT
                here = keep[e, n] + got[row : row + UNIT, :].astype(F32)
                if diagonal:
                    unit = place_of(x, y, low, by)
                    here += jnp.where(on_diagonal(unit), left[e : e + 1, :], 0.0)
                sums[by] = here
            if last:
                outs[third][e] = sums[0].astype(BF16)
                continue
            for n, by in enumerate(kept(third, stage + 1)):
                nxt[e, n] = sums[by]
            going = sent(third, stage + 1)
            if diagonal:
                flag = (core == 0).astype(F32)
                units = [place_of(x, y, low, by) for by in going]
                write_sent(send, tail, e, [sums[by] for by in going], units, flag)
            else:
                for n, by in enumerate(going):
                    row = (e * len(going) + n) * UNIT
                    send[row : row + UNIT, :] = sums[by].astype(BF16)
        if not last:
            send[pl.ds(rows_sent(third, stage + 1), TAIL), :] = tail[...].astype(BF16)


def gram_call(inputs):
    return pl.pallas_call(
        gram_kernel,
        out_shape=[shape for third in range(3) for shape in exchange_shapes(third, 0)],
        in_specs=[pl.BlockSpec(memory_space=pl.ANY)] * len(inputs),
        out_specs=[pl.BlockSpec(memory_space=pltpu.VMEM)] * 6,
        scratch_shapes=[
            pltpu.VMEM((BLOCKS, BLOCK, 2 * GROUP), BF16),
            pltpu.VMEM((BLOCKS, BLOCK, 2 * GROUP), BF16),
        ]
        + [pltpu.VMEM((TAIL, BLOCK), F32)] * 3
        + [pltpu.SemaphoreType.DMA((2,))],
        compiler_params=pltpu.CompilerParams(vmem_limit_bytes=VMEM),
        cost_estimate=pl.CostEstimate(
            flops=2 * MINE * BLOCK * BLOCK * 2 * GROUP, bytes_accessed=24 << 20, transcendentals=0
        ),
        name="gram",
    )(*inputs)


def add_call(stage, inputs):
    if stage < 2:
        shapes = [shape for third in range(3) for shape in exchange_shapes(third, stage + 1)]
        scratch = [pltpu.VMEM((TAIL, BLOCK), F32)] * 3
    else:
        shapes = [jax.ShapeDtypeStruct((hi - lo, UNIT, BLOCK), BF16) for lo, hi in THIRDS]
        scratch = []
    return pl.pallas_call(
        functools.partial(add_kernel, stage),
        out_shape=shapes,
        in_specs=[pl.BlockSpec(memory_space=pltpu.VMEM)] * 6,
        out_specs=[pl.BlockSpec(memory_space=pltpu.VMEM)] * len(shapes),
        scratch_shapes=scratch,
        compiler_params=pltpu.CompilerParams(vmem_limit_bytes=40 << 20),
        cost_estimate=pl.CostEstimate(flops=1 << 22, bytes_accessed=16 << 20, transcendentals=0),
        name="add",
    )(*inputs)


def summed(parts):
    for stage in range(3):
        inputs = []
        for third in range(3):
            keep, send = parts[2 * third], parts[2 * third + 1]
            inputs += [keep, MOVES[ORDERS[third][stage]](send)]
        parts = add_call(stage, inputs)
    return parts


def gathered(mine):
    thirds = range(3)

    def move(stage, pieces):
        return [
            ([by ^ ORDERS[t][stage] for by in pieces[t][0]], MOVES[ORDERS[t][stage]](pieces[t][1]))
            for t in thirds
        ]

    def wave(*groups):
        return lax.optimization_barrier(groups)

    out = []

    def place_in(pieces, core):
        out.extend(((t, bys, core), piece) for t, (bys, piece) in enumerate(pieces))

    def across(pieces):
        place_in(pieces, 0)
        place_in([(bys, over_core(piece)) for bys, piece in pieces], 1)

    def merge(a, b):
        return [(p[0] + q[0], jnp.concatenate([p[1], q[1]])) for p, q in zip(a, b)]

    def unkeyed(pieces):
        return [piece for _, piece in pieces]

    def keyed(pieces, arrays):
        return [(bys, array) for (bys, _), array in zip(pieces, arrays)]

    own = [([0], piece) for piece in mine]
    pair = merge(own, move(0, own))
    pair = keyed(pair, wave(*unkeyed(pair)))
    second, third_a = move(1, pair), move(2, pair)
    across(pair)
    (got,) = wave((unkeyed(second), unkeyed(third_a), [piece for _, piece in out]))
    second, third_a = keyed(second, got[0]), keyed(third_a, got[1])
    out[:] = [(key, piece) for (key, _), piece in zip(out, got[2])]
    third_b = move(2, second)
    across(second)
    across(third_a)
    (got,) = wave((unkeyed(third_b), [piece for _, piece in out]))
    third_b = keyed(third_b, got[0])
    out[:] = [(key, piece) for (key, _), piece in zip(out, got[1])]
    across(third_b)
    return out


def step_kernel(keys, part, *refs):
    gram_pieces = refs[: len(keys)]
    refs = refs[len(keys) :]
    iter_pieces = refs[: len(PIECES)]
    outs = refs[len(PIECES) : len(PIECES) + 4]
    gram, panel, first, total, result, here, there, gone = refs[len(PIECES) + 4 :]
    y, x, core, high, low = place()
    for i, (p, b) in enumerate(place_of_block()):
        for step in range(4):
            pltpu.make_async_copy(
                iter_pieces[p].at[step, pl.ds(b * BAND, BAND), pl.ds(part * WIDE, WIDE)],
                panel.at[i, slab_of(high, low, step)],
                there,
            ).start()
    for (third, bys, other), piece in zip(keys, gram_pieces):
        lo, hi = THIRDS[third]
        for n, by in enumerate(bys):
            pltpu.make_async_copy(
                piece.at[n],
                gram.at[flip(core, other), pl.ds(lo, hi - lo), place_of(x, y, low, by)],
                here,
            ).start()
    pltpu.make_async_copy(panel, panel, there).wait()
    pltpu.make_async_copy(gram, gram, here).wait()

    def rows_of(i):
        return pl.ds(pl.multiple_of(i * BLOCK, BLOCK), BLOCK)

    def block(d, i):
        return gram[d // 2, BLOCKS * (d % 2) + i].reshape(BLOCK, BLOCK)

    def apply(source, i):
        got = dot(block(0, i), source(i), ((1,), (0,)))
        for d in range(1, DIAGS):
            j = lax.rem(i + d, BLOCKS)
            got += dot(block(d, i), source(j), ((1,), (0,)))
            j = lax.rem(i + BLOCKS - d, BLOCKS)
            got += dot(block(d, j), source(j), ((0,), (0,)))
        return got

    def iter_rows(i):
        return panel[i].reshape(BLOCK, WIDE)

    def one(i, carry):
        got = apply(iter_rows, i)
        first[rows_of(i), :] = got.astype(BF16)
        total[rows_of(i), :] = quint_a * iter_rows(i).astype(F32) + quint_b * got
        return carry

    def two(i, carry):
        got = apply(lambda j: first[rows_of(j), :], i)
        result[i] = (total[rows_of(i), :] + quint_c * got).astype(BF16).reshape(4, BAND, WIDE)
        return carry

    lax.fori_loop(0, BLOCKS, one, 0)
    lax.fori_loop(0, BLOCKS, two, 0)
    copies = []
    for step in range(4):
        copies.append(
            pltpu.make_async_copy(
                result.at[:, slab_of(y, low, step)], outs[step], gone.at[step]
            )
        )
        copies[-1].start()
    for copy in copies:
        copy.wait()


def step_call(keys, gram_pieces, iter_pieces, part):
    count = len(gram_pieces) + len(iter_pieces)
    return pl.pallas_call(
        functools.partial(step_kernel, keys, part),
        out_shape=[jax.ShapeDtypeStruct((BLOCKS, BAND, WIDE), BF16)] * 4,
        in_specs=[pl.BlockSpec(memory_space=pl.ANY)] * count,
        out_specs=[pl.BlockSpec(memory_space=pl.ANY)] * 4,
        scratch_shapes=[
            pltpu.VMEM((2, MINE, PLACES, UNIT, BLOCK), BF16),
            pltpu.VMEM((BLOCKS, 4, BAND, WIDE), BF16),
            pltpu.VMEM((ORDER, WIDE), BF16),
            pltpu.VMEM((ORDER, WIDE), F32),
            pltpu.VMEM((BLOCKS, 4, BAND, WIDE), BF16),
            pltpu.SemaphoreType.DMA,
            pltpu.SemaphoreType.DMA,
            pltpu.SemaphoreType.DMA((4,)),
        ],
        compiler_params=pltpu.CompilerParams(vmem_limit_bytes=VMEM),
        cost_estimate=pl.CostEstimate(
            flops=4 * ORDER * ORDER * WIDE, bytes_accessed=20 << 20, transcendentals=0
        ),
        name="step",
    )(*gram_pieces, *iter_pieces)


def pick(a, at, size, axis):
    return lax.dynamic_slice_in_dim(a, at, size, axis)


def panels(iterate):
    y, x, core, high, low = place()
    aligned = y == high
    starts = [sum(PIECES[:n]) * BAND for n in range(len(PIECES) + 1)]

    def cast(n, at):
        band = iterate[starts[n] : starts[n + 1]]
        return pick(band, at * 2 * GROUP, 2 * GROUP, 1).astype(BF16)

    def chunks(keep, other):
        near, far = jnp.where(aligned, keep, other), jnp.where(aligned, other, keep)
        return [
            pick(far if step >> 1 else near, flip(low, step & 1) * GROUP, GROUP, 1)
            for step in range(4)
        ]

    own, beside = [], []
    keep, other = cast(0, y), over_y(cast(0, 1 - y))
    for n in range(len(PIECES)):
        ready = chunks(keep, other)
        more = n + 1 < len(PIECES)
        ahead = [cast(n + 1, y), cast(n + 1, 1 - y)] if more else []
        ready, ahead, done = lax.optimization_barrier((ready, ahead, own[-1:]))
        got = [ready[0]] + [over_z(ready[step], step) for step in (1, 2, 3)]
        if more:
            keep, other = ahead[0], over_y(ahead[1])
        beside += [over_core(piece) for piece in done]
        own.append(jnp.stack(got))
    beside.append(over_core(own[-1]))
    return own, beside


def shards_cube(iterate):
    y, x, core, high, low = place()
    own, beside = panels(iterate)
    out = (FACTOR * quint_a) * (iterate - lax.reduce_precision(iterate, 8, 7))
    out, own[0] = lax.optimization_barrier((out, own[0]))
    mine = summed(gram_call(own + beside))
    entries = gathered([piece[None] for piece in mine])
    keys = [key for key, _ in entries]
    gram_pieces = [piece.reshape(-1, *piece.shape[-3:]) for _, piece in entries]

    before = None
    for part in range(HALVES):
        slabs = step_call(keys, gram_pieces, own, part)
        if before is not None:
            slabs, before = lax.optimization_barrier((slabs, before))
        got = [home(slabs[step], step) for step in range(4)]
        for step in range(4):
            at = slab_of(high, low, step) * GROUP + part * WIDE
            piece = FACTOR * got[step].reshape(SLAB, WIDE).astype(F32)
            out = lax.dynamic_update_slice_in_dim(out, pick(out, at, WIDE, 1) + piece, at, 1)
        before = got
    return out


def solution(mesh):
    shards = shards_cube if dict(mesh.shape) == {"mats": 2, "col": 4, "row": 4} else shards_rows
    in_specs = (P(("mats", "row"), "col"),)
    out_specs = P(("mats", "row"), "col")
    return jax.shard_map(shards, mesh=mesh, in_specs=in_specs, out_specs=out_specs, check_vma=False)
```

time: 743 us -> 394 us (0.53)
  waiting for transfers between devices: 650 us -> 237 us
  Pallas kernels: 0 us -> 70.7 us
  matrix products: 66.9 us -> 0 us
  starting transfers between devices: 0.13 us -> 47.2 us
  other arithmetic: 8.72 us -> 23.9 us
  local copies, waits for them, and re-layouts: 0 us -> 13.7 us
  between operations: 13.1 us -> 0.63 us
    all_gather x3 -> x0, waiting for transfers between devices: 548 us -> none  [the longest x1 251 us: shards(): column_panel = lax.all_gather(iter_bf, 'row', axis=0, tiled=True)]
    ppermute x0 -> x56, waiting for transfers between devices: none -> 237 us  [the longest x16 111 us: over_z(): return lax.ppermute(a, 'row', [(z, z ^ step) for z in range(4)])]
    reduce_scatter x1 -> x0, waiting for transfers between devices: 102 us -> none  [shards(): lax.psum_scatter(lax.dot_general(column_panel, iter_bf, (((1,), (1,)), ((...]
    pallas_call x0 -> x6, Pallas kernels: none -> 70.7 us  [the longest x2 45.6 us: step_call(): pl.pallas_call(functools.partial(step_kernel, keys, part), out_shape=[jax...]
    dot_general x3 -> x0, matrix products: 66.9 us -> none  [the longest x1 24.9 us: shards(): lax.dot_general(gram_cols, lax.all_gather(first_bf, 'row', axis=0, tiled=...]
    ppermute x0 -> x56, starting transfers between devices: none -> 47.2 us  [the longest x8 14.4 us: home(): return lax.ppermute(a, ('mats', 'row'), pairs)]
    dynamic_update_slice x0 -> x8, other arithmetic: none -> 17.5 us  [shards_cube(): lax.dynamic_update_slice_in_dim(out, pick(out, at, WIDE, 1) + piece, at, 1)]
    convert_element_type x2 -> x0, other arithmetic: 8.72 us -> none  [the longest x1 5.49 us: shards(): iter_bf = iterate.astype(jnp.bfloat16)]
  transfers between devices with their start and end apart: 4 -> 56, of which waited for: 4 -> 35; matrix products, arithmetic and copies ran while one was open for 0% -> 6% of each run, Pallas kernels for 0% -> 6%
where the time goes in v2:
time: 394 us; the launch traced here: 393 us
  waiting for transfers between devices  237 us (60%)
  Pallas kernels  70.7 us (18%)
  starting transfers between devices  47.2 us (12%)
  other arithmetic  23.9 us (6%)
  local copies, waits for them, and re-layouts  13.7 us (3%)
    ppermute x16, waiting for transfers between devices, over_z(): return lax.ppermute(a, 'row', [(z, z ^ step) for z in range(4)])  111 us
    pallas_call x2, Pallas kernels, step_call(): pl.pallas_call(functools.partial(step_kernel, keys, part), out_shape=[jax...  45.6 us
    ppermute x10, waiting for transfers between devices, over_y(): return lax.ppermute(a, 'mats', [(0, 1), (1, 0)])  42.2 us
    ppermute x8, waiting for transfers between devices, home(): return lax.ppermute(a, ('mats', 'row'), pairs)  42.2 us
    ppermute x7, waiting for transfers between devices, over_x(): return lax.ppermute(a, 'col', [(0, 2), (1, 3), (2, 0), (3, 1)])  37.7 us
    pallas_call x1, Pallas kernels, gram_call(): pl.pallas_call(gram_kernel, out_shape=[shape for third in range(3) for sh...  20.9 us
    dynamic_update_slice x8, other arithmetic, shards_cube(): lax.dynamic_update_slice_in_dim(out, pick(out, at, WIDE, 1) + piece, at, 1)  17.5 us
    ppermute x8, starting transfers between devices, home(): return lax.ppermute(a, ('mats', 'row'), pairs)  14.4 us
  transfers between devices with their start and end apart: 56, of which 35 were waited for; matrix products, arithmetic and copies ran while one was open for 6% of the time, Pallas kernels for 6%

profile of v2, /device:TPU:12, one launch (start us, length us, event | category | flops | bytes accessed | tf_op | source)
XLA Modules:
  0.0 393.4 jit_solution(13381346670480861631)
XLA Ops:
  0.0 1.3 slice.12
  1.9 1.7 slice.13
  3.8 5.7 %collective-permute-done = bf16[128,1024]{1,0:T(8,128)(2,1)S(1)} collective-permute-done((bf16[128,1024]{1,0:T(8,128)(2,1)S(1)}, bf16[128,1024]{1,0:T(8,128)(2,1)S(1)}, u32[]{:S(2)}, u32[]{:S(2)}) %collective-permute-start) | collective-permute-done | bytes 262176 | tf_op jit(solution)/shard_map/ppermute | solution.py:91
  10.2 2.5 slice.14
  13.0 2.8 collective-permute-start.2
  16.4 2.7 collective-permute-done.1
  19.1 5.1 %collective-permute-done.2 = bf16[128,512]{1,0:T(8,128)(2,1)S(1)} collective-permute-done((bf16[128,512]{1,0:T(8,128)(2,1)S(1)}, bf16[128,512]{1,0:T(8,128)(2,1)S(1)}, u32[]{:S(2)}, u32[]{:S(2)}) %collective-permute-start.2) | collective-permute-done | bytes 131104 | tf_op jit(solution)/shard_map/ppermute | solution.py:95
  24.2 2.3 collective-permute-done.3
  26.8 1.5 collective-permute-start.8
  28.4 3.0 collective-permute-start.6
  31.8 5.8 %collective-permute-done.5 = bf16[256,512]{1,0:T(8,128)(2,1)S(1)} collective-permute-done((bf16[256,512]{1,0:T(8,128)(2,1)S(1)}, bf16[256,512]{1,0:T(8,128)(2,1)S(1)}, u32[]{:S(2)}, u32[]{:S(2)}) %collective-permute-start.5) | collective-permute-done | bytes 262176 | tf_op jit(solution)/shard_map/ppermute | solution.py:95
  37.6 10.9 %collective-permute-done.6 = bf16[256,512]{1,0:T(8,128)(2,1)S(1)} collective-permute-done((bf16[256,512]{1,0:T(8,128)(2,1)S(1)}, bf16[256,512]{1,0:T(8,128)(2,1)S(1)}, u32[]{:S(2)}, u32[]{:S(2)}) %collective-permute-start.6) | collective-permute-done | bytes 262176 | tf_op jit(solution)/shard_map/ppermute | solution.py:95
  48.4 4.2 %collective-permute-done.7 = bf16[256,512]{1,0:T(8,128)(2,1)S(1)} collective-permute-done((bf16[256,512]{1,0:T(8,128)(2,1)S(1)}, bf16[256,512]{1,0:T(8,128)(2,1)S(1)}, u32[]{:S(2)}, u32[]{:S(2)}) %collective-permute-start.7) | collective-permute-done | bytes 262176 | tf_op jit(solution)/shard_map/ppermute | solution.py:95
  53.3 1.6 collective-permute-start.11
  54.8 2.8 collective-permute-start.9
  57.7 29.4 %collective-permute-done.10 = bf16[512,512]{1,0:T(8,128)(2,1)S(1)} collective-permute-done((bf16[512,512]{1,0:T(8,128)(2,1)S(1)}, bf16[512,512]{1,0:T(8,128)(2,1)S(1)}, u32[]{:S(2)}, u32[]{:S(2)}) %collective-permute-start.10) | collective-permute-done | bytes 524320 | tf_op jit(solution)/shard_map/ppermute | solution.py:95
  87.0 10.9 %collective-permute-done.11 = bf16[512,512]{1,0:T(8,128)(2,1)S(1)} collective-permute-done((bf16[512,512]{1,0:T(8,128)(2,1)S(1)}, bf16[512,512]{1,0:T(8,128)(2,1)S(1)}, u32[]{:S(2)}, u32[]{:S(2)}) %collective-permute-start.11) | collective-permute-done | bytes 524320 | tf_op jit(solution)/shard_map/ppermute | solution.py:95
  98.9 4.7 %fusion = f32[896,2048]{1,0:T(8,128)} fusion(f32[896,2048]{1,0:T(8,128)S(1)} %bitcast.38), kind=kLoop, calls=%fused_computation.1 | loop fusion | flops 5505024 | bytes 14680064 | tf_op jit(solution)/shard_map/mul | solution.py:476
  106.5 20.9 %gram.1 = (f32[5,4,64,512]{3,2,1,0:T(8,128)}, bf16[1296,512]{1,0:T(8,128)(2,1)}, f32[5,4,64,512]{3,2,1,0:T(8,128)}, bf16[1296,512]{1,0:T(8,128)(2,1)}, f32[4,4,6...) custom-call(bf16[4,128,512]{2,1,0:T(8,128)(2,1)} %copy-done.6, bf16[4,256,512]{2,1,0:T(8,128)(2,1)} %copy-done.3, ...), custom_call_target="tpu_custom_call" | custom-call | flops 7516192768 | bytes 25165824 | tf_op jit(solution)/shard_map/gram/pallas_call | solution.py:248
  127.4 1.5 collective-permute-start.15
  129.4 25.2 %collective-permute-done.17.refs_5_ = bf16[1040,512]{1,0:T(8,128)(2,1)S(1)} collective-permute-done((bf16[1040,512]{1,0:T(8,128)(2,1)}, bf16[1040,512]{1,0:T(8,128)(2,1)S(1)}, u32[]{:S(2)}, u32[]{:S(2)}) %collective-permute-start.17) | collective-permute-done | bytes 1064992 | tf_op jit(solution)/shard_map/ppermute | solution.py:95
  154.6 4.2 %collective-permute-done.15.refs_1_ = bf16[1296,512]{1,0:T(8,128)(2,1)S(1)} collective-permute-done((bf16[1296,512]{1,0:T(8,128)(2,1)}, bf16[1296,512]{1,0:T(8,128)(2,1)S(1)}, u32[]{:S(2)}, u32[]{:S(2)}) %collective-permute-start.15) | collective-permute-done | bytes 1327136 | tf_op jit(solution)/shard_map/ppermute | solution.py:83
  158.8 1.2 collective-permute-done.16.refs_3_
  160.0 1.7 copy-done
  161.8 1.6 copy-done.1
  163.4 3.2 add.164
  167.6 12.4 %collective-permute-done.20.refs_5_ = bf16[528,512]{1,0:T(8,128)(2,1)S(1)} collective-permute-done((bf16[528,512]{1,0:T(8,128)(2,1)S(1)}, bf16[528,512]{1,0:T(8,128)(2,1)S(1)}, u32[]{:S(2)}, u32[]{:S(2)}) %collective-permute-start.20) | collective-permute-done | bytes 540704 | tf_op jit(solution)/shard_map/ppermute | solution.py:83
  180.0 2.6 collective-permute-done.18.refs_1_
  184.5 1.5 collective-permute-start.23
  186.0 5.0 %collective-permute-done.23.refs_5_ = bf16[272,512]{1,0:T(8,128)(2,1)S(1)} collective-permute-done((bf16[272,512]{1,0:T(8,128)(2,1)S(1)}, bf16[272,512]{1,0:T(8,128)(2,1)S(1)}, u32[]{:S(2)}, u32[]{:S(2)}) %collective-permute-start.23) | collective-permute-done | bytes 278560 | tf_op jit(solution)/shard_map/ppermute | solution.py:91
  191.9 1.6 collective-permute-start.26
  193.5 1.5 collective-permute-start.25
  195.0 1.3 collective-permute-start.24
  196.3 2.0 collective-permute-done.26
  198.4 2.7 collective-permute-done.25
  201.2 2.5 collective-permute-done.24
  203.9 2.0 collective-permute-start.29
  205.8 1.9 collective-permute-start.32
  207.8 5.5 %collective-permute-done.29.refs_8_ = bf16[2,4,64,512]{3,2,1,0:T(8,128)(2,1)S(1)} collective-permute-done((bf16[2,4,64,512]{3,2,1,0:T(8,128)(2,1)S(1)}, bf16[2,4,64,512]{3,2,1,0:T(8,128)(2,1)S(1)}, u32[]{:S(2)}, u32[]{:S(2)}) %collective-permute-start.29) | collective-permute-done | bytes 524320 | tf_op jit(solution)/shard_map/ppermute | solution.py:83
  213.8 12.0 %collective-permute-done.32.refs_14_ = bf16[2,4,64,512]{3,2,1,0:T(8,128)(2,1)S(1)} collective-permute-done((bf16[2,4,64,512]{3,2,1,0:T(8,128)(2,1)S(1)}, bf16[2,4,64,512]{3,2,1,0:T(8,128)(2,1)S(1)}, u32[]{:S(2)}, u32[]{:S(2)}) %collective-permute-start.32) | collective-permute-done | bytes 524320 | tf_op jit(solution)/shard_map/ppermute | solution.py:91
  227.5 11.4 %collective-permute-done.28.refs_7_ = bf16[2,5,64,512]{3,2,1,0:T(8,128)(2,1)S(1)} collective-permute-done((bf16[2,5,64,512]{3,2,1,0:T(8,128)(2,1)S(1)}, bf16[2,5,64,512]{3,2,1,0:T(8,128)(2,1)S(1)}, u32[]{:S(2)}, u32[]{:S(2)}) %collective-permute-start.28) | collective-permute-done | bytes 655392 | tf_op jit(solution)/shard_map/ppermute | solution.py:95
  240.0 13.0 %collective-permute-done.38.refs_20_ = bf16[2,4,64,512]{3,2,1,0:T(8,128)(2,1)} collective-permute-done((bf16[2,4,64,512]{3,2,1,0:T(8,128)(2,1)S(1)}, bf16[2,4,64,512]{3,2,1,0:T(8,128)(2,1)}, u32[]{:S(2)}, u32[]{:S(2)}) %collective-permute-start.38) | collective-permute-done | bytes 524320 | tf_op jit(solution)/shard_map/ppermute | solution.py:91
  255.6 12.9 %collective-permute-done.37.refs_19_ = bf16[2,5,64,512]{3,2,1,0:T(8,128)(2,1)} collective-permute-done((bf16[2,5,64,512]{3,2,1,0:T(8,128)(2,1)S(1)}, bf16[2,5,64,512]{3,2,1,0:T(8,128)(2,1)}, u32[]{:S(2)}, u32[]{:S(2)}) %collective-permute-start.37) | collective-permute-done | bytes 655392 | tf_op jit(solution)/shard_map/ppermute | solution.py:83
  270.0 2.7 collective-permute-done.47.refs_23_
  272.8 22.8 %step.2 = (bf16[7,128,256]{2,1,0:T(8,128)(2,1)}, bf16[7,128,256]{2,1,0:T(8,128)(2,1)}, bf16[7,128,256]{2,1,0:T(8,128)(2,1)}, bf16[7,128,256]{2,1,0:T(8,128)(2,1)}) custom-call(bf16[2,5,64,512]{3,2,1,0:T(8,128)(2,1)} %copy-done.5, bf16[2,5,64,512]{3,2,1,0:T(8,128)(2,1)} %copy-done.4, bf16[2,4,64,512]{3,2,1,0:T(8,128)(2,1)} %copy-done.7, ...), custom_call_target="tpu_custom_call" | custom-call | flops 13153337344 | bytes 20971520 | tf_op jit(solution)/shard_map/step/pallas_call | solution.py:414
  295.6 3.6 collective-permute-start.48
  299.2 2.0 collective-permute-start.49
  301.3 2.4 collective-permute-start.51
  303.7 22.8 %step.3 = (bf16[7,128,256]{2,1,0:T(8,128)(2,1)}, bf16[7,128,256]{2,1,0:T(8,128)(2,1)}, bf16[7,128,256]{2,1,0:T(8,128)(2,1)}, bf16[7,128,256]{2,1,0:T(8,128)(2,1)}) custom-call(bf16[2,5,64,512]{3,2,1,0:T(8,128)(2,1)} %copy-done.5, bf16[2,5,64,512]{3,2,1,0:T(8,128)(2,1)} %copy-done.4, bf16[2,4,64,512]{3,2,1,0:T(8,128)(2,1)} %copy-done.7, ...), custom_call_target="tpu_custom_call" | custom-call | flops 13153337344 | bytes 20971520 | tf_op jit(solution)/shard_map/step/pallas_call | solution.py:414
  326.5 3.0 collective-permute-done.48
  329.5 11.9 %collective-permute-done.49 = bf16[7,128,256]{2,1,0:T(8,128)(2,1)S(1)} collective-permute-done((bf16[7,128,256]{2,1,0:T(8,128)(2,1)}, bf16[7,128,256]{2,1,0:T(8,128)(2,1)S(1)}, u32[]{:S(2)}, u32[]{:S(2)}) %collective-permute-start.49) | collective-permute-done | bytes 458784 | tf_op jit(solution)/shard_map/ppermute | solution.py:108
  341.4 2.6 collective-permute-done.51
  344.1 1.9 collective-permute-start.52
  347.0 3.4 collective-permute-start.55
  350.5 2.2 constant_dynamic-update-slice_fusion.7
  352.8 2.2 constant_dynamic-update-slice_fusion.6
  355.1 2.2 constant_dynamic-update-slice_fusion.5
  357.4 2.2 constant_dynamic-update-slice_fusion.4
  359.6 17.0 %collective-permute-done.52 = bf16[7,128,256]{2,1,0:T(8,128)(2,1)S(1)} collective-permute-done((bf16[7,128,256]{2,1,0:T(8,128)(2,1)}, bf16[7,128,256]{2,1,0:T(8,128)(2,1)S(1)}, u32[]{:S(2)}, u32[]{:S(2)}) %collective-permute-start.52) | collective-permute-done | bytes 458784 | tf_op jit(solution)/shard_map/ppermute | solution.py:108
  376.6 2.2 constant_dynamic-update-slice_fusion.3
  378.8 7.2 %collective-permute-done.53 = bf16[7,128,256]{2,1,0:T(8,128)(2,1)S(1)} collective-permute-done((bf16[7,128,256]{2,1,0:T(8,128)(2,1)}, bf16[7,128,256]{2,1,0:T(8,128)(2,1)S(1)}, u32[]{:S(2)}, u32[]{:S(2)}) %collective-permute-start.53) | collective-permute-done | bytes 458784 | tf_op jit(solution)/shard_map/ppermute | solution.py:108
  386.1 2.2 constant_dynamic-update-slice_fusion.2
  388.4 2.2 constant_dynamic-update-slice_fusion.1
  391.2 2.2 constant_dynamic-update-slice_fusion
  (144 shorter events, 21.4 us)
Async XLA Ops:
  1.3 8.1 %collective-permute-start = (bf16[128,1024]{1,0:T(8,128)(2,1)S(1)}, bf16[128,1024]{1,0:T(8,128)(2,1)S(1)}, u32[]{:S(2)}, u32[]{:S(2)}) collective-permute-start(bf16[128,1024]{1,0:T(8,128)(2,1)S(1)} %dynamic-slice_convert_fusion.4), channel_id=1, source_target_pairs={{0,16},{16,0},{1,17},{17,1},{2,18},{18,2},{3,19},{19,3},{4,20},{20... | collective-permute-start | bytes 786440 | tf_op jit(solution)/shard_map/ppermute | solution.py:91
  9.6 17.0 %collective-permute-start.4 = (bf16[256,1024]{1,0:T(8,128)(2,1)S(1)}, bf16[256,1024]{1,0:T(8,128)(2,1)S(1)}, u32[]{:S(2)}, u32[]{:S(2)}) collective-permute-start(bf16[256,1024]{1,0:T(8,128)(2,1)S(1)} %get-tuple-element.101), channel_id=1, source_target_pairs={{0,16},{16,0},{1,17},{17,1},{2,18},{18,2},{3,19},{19,3},{4,20},{20... | collective-permute-start | bytes 1572872 | tf_op jit(solution)/shard_map/ppermute | solution.py:91
  12.7 6.4 %collective-permute-start.1 = (bf16[128,512]{1,0:T(8,128)(2,1)S(1)}, bf16[128,512]{1,0:T(8,128)(2,1)S(1)}, u32[]{:S(2)}, u32[]{:S(2)}) collective-permute-start(bf16[128,512]{1,0:T(8,128)(2,1)S(1)} %get-tuple-element.95), channel_id=1, source_target_pairs={{0,1},{1,0},{2,3},{3,2},{4,5},{5,4},{6,7},{7,6},{8,9},{9,8},{10,11... | collective-permute-start | bytes 393224 | tf_op jit(solution)/shard_map/ppermute | solution.py:95
  13.0 11.2 %collective-permute-start.2 = (bf16[128,512]{1,0:T(8,128)(2,1)S(1)}, bf16[128,512]{1,0:T(8,128)(2,1)S(1)}, u32[]{:S(2)}, u32[]{:S(2)}) collective-permute-start(bf16[128,512]{1,0:T(8,128)(2,1)S(1)} %get-tuple-element.96), channel_id=1, source_target_pairs={{0,2},{1,3},{2,0},{3,1},{4,6},{5,7},{6,4},{7,5},{8,10},{9,11},{10,... | collective-permute-start | bytes 393224 | tf_op jit(solution)/shard_map/ppermute | solution.py:95
  15.8 10.7 %collective-permute-start.3 = (bf16[128,512]{1,0:T(8,128)(2,1)S(1)}, bf16[128,512]{1,0:T(8,128)(2,1)S(1)}, u32[]{:S(2)}, u32[]{:S(2)}) collective-permute-start(bf16[128,512]{1,0:T(8,128)(2,1)S(1)} %get-tuple-element.97), channel_id=1, source_target_pairs={{0,3},{1,2},{2,1},{3,0},{4,7},{5,6},{6,5},{7,4},{8,11},{9,10},{10,... | collective-permute-start | bytes 393224 | tf_op jit(solution)/shard_map/ppermute | solution.py:95
  26.6 72.2 %copy-start.6 = (bf16[4,128,512]{2,1,0:T(8,128)(2,1)}, bf16[4,128,512]{2,1,0:T(8,128)(2,1)S(1)}, u32[]{:S(2)}) copy-start(bf16[4,128,512]{2,1,0:T(8,128)(2,1)S(1)} %pad_maximum_fusion.4.refs_0_.refs_24_) | copy-start | bytes 1572868
  26.8 26.0 %collective-permute-start.8 = (bf16[512,1024]{1,0:T(8,128)(2,1)S(1)}, bf16[512,1024]{1,0:T(8,128)(2,1)S(1)}, u32[]{:S(2)}, u32[]{:S(2)}) collective-permute-start(bf16[512,1024]{1,0:T(8,128)(2,1)S(1)} %get-tuple-element.107), channel_id=1, source_target_pairs={{0,16},{16,0},{1,17},{17,1},{2,18},{18,2},{3,19},{19,3},{4,20},{20... | collective-permute-start | bytes 3145736 | tf_op jit(solution)/shard_map/ppermute | solution.py:91
  28.3 9.2 %collective-permute-start.5 = (bf16[256,512]{1,0:T(8,128)(2,1)S(1)}, bf16[256,512]{1,0:T(8,128)(2,1)S(1)}, u32[]{:S(2)}, u32[]{:S(2)}) collective-permute-start(bf16[256,512]{1,0:T(8,128)(2,1)S(1)} %get-tuple-element.103), channel_id=1, source_target_pairs={{0,1},{1,0},{2,3},{3,2},{4,5},{5,4},{6,7},{7,6},{8,9},{9,8},{10,11... | collective-permute-start | bytes 786440 | tf_op jit(solution)/shard_map/ppermute | solution.py:95
  28.4 20.0 %collective-permute-start.6 = (bf16[256,512]{1,0:T(8,128)(2,1)S(1)}, bf16[256,512]{1,0:T(8,128)(2,1)S(1)}, u32[]{:S(2)}, u32[]{:S(2)}) collective-permute-start(bf16[256,512]{1,0:T(8,128)(2,1)S(1)} %get-tuple-element.104), channel_id=1, source_target_pairs={{0,2},{1,3},{2,0},{3,1},{4,6},{5,7},{6,4},{7,5},{8,10},{9,11},{10,... | collective-permute-start | bytes 786440 | tf_op jit(solution)/shard_map/ppermute | solution.py:95
  31.4 21.2 %collective-permute-start.7 = (bf16[256,512]{1,0:T(8,128)(2,1)S(1)}, bf16[256,512]{1,0:T(8,128)(2,1)S(1)}, u32[]{:S(2)}, u32[]{:S(2)}) collective-permute-start(bf16[256,512]{1,0:T(8,128)(2,1)S(1)} %get-tuple-element.105), channel_id=1, source_target_pairs={{0,3},{1,2},{2,1},{3,0},{4,7},{5,6},{6,5},{7,4},{8,11},{9,10},{10,... | collective-permute-start | bytes 786440 | tf_op jit(solution)/shard_map/ppermute | solution.py:95
  52.6 46.3 %slice-start = ((s8[7340032]{0:T(1024)(128)(4,1)}), s8[4194304]{0:T(1024)(128)(4,1)S(1)}, s32[]{:S(2)}) async-start(s8[7340032]{0:T(1024)(128)(4,1)} %bitcast.37), calls=%async_computation | async-start | bytes 8388608
  52.8 50.8 %copy-start.3 = (bf16[4,256,512]{2,1,0:T(8,128)(2,1)}, bf16[4,256,512]{2,1,0:T(8,128)(2,1)S(1)}, u32[]{:S(2)}) copy-start(bf16[4,256,512]{2,1,0:T(8,128)(2,1)S(1)} %pad_maximum_fusion.1.refs_1_.refs_25_) | copy-start | bytes 3145732
  53.0 46.0 %slice-start.1 = ((s8[7340032]{0:T(1024)(128)(4,1)}), s8[3145728]{0:T(1024)(128)(4,1)S(1)}, s32[]{:S(2)}) async-start(s8[7340032]{0:T(1024)(128)(4,1)} %bitcast.37), calls=%async_computation.1 | async-start | bytes 6291456
  53.2 33.8 %collective-permute-start.10 = (bf16[512,512]{1,0:T(8,128)(2,1)S(1)}, bf16[512,512]{1,0:T(8,128)(2,1)S(1)}, u32[]{:S(2)}, u32[]{:S(2)}) collective-permute-start(bf16[512,512]{1,0:T(8,128)(2,1)S(1)} %get-tuple-element.110), channel_id=1, source_target_pairs={{0,2},{1,3},{2,0},{3,1},{4,6},{5,7},{6,4},{7,5},{8,10},{9,11},{10,... | collective-permute-start | bytes 1572872 | tf_op jit(solution)/shard_map/ppermute | solution.py:95
  53.3 44.7 %collective-permute-start.11 = (bf16[512,512]{1,0:T(8,128)(2,1)S(1)}, bf16[512,512]{1,0:T(8,128)(2,1)S(1)}, u32[]{:S(2)}, u32[]{:S(2)}) collective-permute-start(bf16[512,512]{1,0:T(8,128)(2,1)S(1)} %get-tuple-element.111), channel_id=1, source_target_pairs={{0,3},{1,2},{2,1},{3,0},{4,7},{5,6},{6,5},{7,4},{8,11},{9,10},{10,... | collective-permute-start | bytes 1572872 | tf_op jit(solution)/shard_map/ppermute | solution.py:95
  54.8 43.1 %collective-permute-start.9 = (bf16[512,512]{1,0:T(8,128)(2,1)S(1)}, bf16[512,512]{1,0:T(8,128)(2,1)S(1)}, u32[]{:S(2)}, u32[]{:S(2)}) collective-permute-start(bf16[512,512]{1,0:T(8,128)(2,1)S(1)} %get-tuple-element.109), channel_id=1, source_target_pairs={{0,1},{1,0},{2,3},{3,2},{4,5},{5,4},{6,7},{7,6},{8,9},{9,8},{10,11... | collective-permute-start | bytes 1572872 | tf_op jit(solution)/shard_map/ppermute | solution.py:95
  98.2 8.3 %collective-permute-start.14 = (bf16[4,512,512]{2,1,0:T(8,128)(2,1)S(1)}, bf16[4,512,512]{2,1,0:T(8,128)(2,1)}, u32[]{:S(2)}, u32[]{:S(2)}) collective-permute-start(bf16[4,512,512]{2,1,0:T(8,128)(2,1)S(1)} %pad_maximum_fusion.refs_2_.refs_26_), channel_id=1, source_target_pairs={{0,4},{4,0},{8,12},{12,8},{1,5},{5,1},{9,13},{13,9},{2,6},{6,2},{1... | collective-permute-start | bytes 6291464 | tf_op jit(solution)/shard_map/ppermute | solution.py:87
  98.3 6.4 %collective-permute-start.13 = (bf16[4,256,512]{2,1,0:T(8,128)(2,1)S(1)}, bf16[4,256,512]{2,1,0:T(8,128)(2,1)S(1)}, u32[]{:S(2)}, u32[]{:S(2)}) collective-permute-start(bf16[4,256,512]{2,1,0:T(8,128)(2,1)S(1)} %pad_maximum_fusion.1.refs_1_.refs_25_), channel_id=1, source_target_pairs={{0,4},{4,0},{8,12},{12,8},{1,5},{5,1},{9,13},{13,9},{2,6},{6,2},{1... | collective-permute-start | bytes 3145736 | tf_op jit(solution)/shard_map/ppermute | solution.py:87
  98.8 5.9 %collective-permute-start.12 = (bf16[4,128,512]{2,1,0:T(8,128)(2,1)S(1)}, bf16[4,128,512]{2,1,0:T(8,128)(2,1)S(1)}, u32[]{:S(2)}, u32[]{:S(2)}) collective-permute-start(bf16[4,128,512]{2,1,0:T(8,128)(2,1)S(1)} %pad_maximum_fusion.4.refs_0_.refs_24_), channel_id=1, source_target_pairs={{0,4},{4,0},{8,12},{12,8},{1,5},{5,1},{9,13},{13,9},{2,6},{6,2},{1... | collective-permute-start | bytes 1572872 | tf_op jit(solution)/shard_map/ppermute | solution.py:87
  127.4 31.4 %collective-permute-start.15 = (bf16[1296,512]{1,0:T(8,128)(2,1)}, bf16[1296,512]{1,0:T(8,128)(2,1)S(1)}, u32[]{:S(2)}, u32[]{:S(2)}) collective-permute-start(bf16[1296,512]{1,0:T(8,128)(2,1)} %get-tuple-element.115), channel_id=1, source_target_pairs={{0,8},{4,12},{8,0},{12,4},{1,9},{5,13},{9,1},{13,5},{2,10},{6,14},... | collective-permute-start | bytes 3981320 | tf_op jit(solution)/shard_map/ppermute | solution.py:83
  128.9 31.1 %collective-permute-start.16 = (bf16[1296,512]{1,0:T(8,128)(2,1)}, bf16[1296,512]{1,0:T(8,128)(2,1)S(1)}, u32[]{:S(2)}, u32[]{:S(2)}) collective-permute-start(bf16[1296,512]{1,0:T(8,128)(2,1)} %get-tuple-element.117), channel_id=1, source_target_pairs={{0,16},{16,0},{1,17},{17,1},{2,18},{18,2},{3,19},{19,3},{4,20},{20... | collective-permute-start | bytes 3981320 | tf_op jit(solution)/shard_map/ppermute | solution.py:91
  129.4 25.2 %collective-permute-start.17 = (bf16[1040,512]{1,0:T(8,128)(2,1)}, bf16[1040,512]{1,0:T(8,128)(2,1)S(1)}, u32[]{:S(2)}, u32[]{:S(2)}) collective-permute-start(bf16[1040,512]{1,0:T(8,128)(2,1)} %get-tuple-element.119), channel_id=1, source_target_pairs={{0,1},{1,0},{2,3},{3,2},{4,5},{5,4},{6,7},{7,6},{8,9},{9,8},{10,11... | collective-permute-start | bytes 3194888 | tf_op jit(solution)/shard_map/ppermute | solution.py:95
  166.6 16.0 %collective-permute-start.18 = (bf16[656,512]{1,0:T(8,128)(2,1)S(1)}, bf16[656,512]{1,0:T(8,128)(2,1)S(1)}, u32[]{:S(2)}, u32[]{:S(2)}) collective-permute-start(bf16[656,512]{1,0:T(8,128)(2,1)S(1)} %get-tuple-element.121), channel_id=1, source_target_pairs={{0,16},{16,0},{1,17},{17,1},{2,18},{18,2},{3,19},{19,3},{4,20},{20... | collective-permute-start | bytes 2015240 | tf_op jit(solution)/shard_map/ppermute | solution.py:91
  167.2 15.7 %collective-permute-start.19 = (bf16[656,512]{1,0:T(8,128)(2,1)S(1)}, bf16[656,512]{1,0:T(8,128)(2,1)S(1)}, u32[]{:S(2)}, u32[]{:S(2)}) collective-permute-start(bf16[656,512]{1,0:T(8,128)(2,1)S(1)} %get-tuple-element.123), channel_id=1, source_target_pairs={{0,1},{1,0},{2,3},{3,2},{4,5},{5,4},{6,7},{7,6},{8,9},{9,8},{10,11... | collective-permute-start | bytes 2015240 | tf_op jit(solution)/shard_map/ppermute | solution.py:95
  167.2 12.9 %collective-permute-start.20 = (bf16[528,512]{1,0:T(8,128)(2,1)S(1)}, bf16[528,512]{1,0:T(8,128)(2,1)S(1)}, u32[]{:S(2)}, u32[]{:S(2)}) collective-permute-start(bf16[528,512]{1,0:T(8,128)(2,1)S(1)} %get-tuple-element.125), channel_id=1, source_target_pairs={{0,8},{4,12},{8,0},{12,4},{1,9},{5,13},{9,1},{13,5},{2,10},{6,14},... | collective-permute-start | bytes 1622024 | tf_op jit(solution)/shard_map/ppermute | solution.py:83
  183.6 7.9 %collective-permute-start.21 = (bf16[336,512]{1,0:T(8,128)(2,1)S(1)}, bf16[336,512]{1,0:T(8,128)(2,1)S(1)}, u32[]{:S(2)}, u32[]{:S(2)}) collective-permute-start(bf16[336,512]{1,0:T(8,128)(2,1)S(1)} %get-tuple-element.127), channel_id=1, source_target_pairs={{0,1},{1,0},{2,3},{3,2},{4,5},{5,4},{6,7},{7,6},{8,9},{9,8},{10,11... | collective-permute-start | bytes 1032200 | tf_op jit(solution)/shard_map/ppermute | solution.py:95
  183.9 7.7 %collective-permute-start.22 = (bf16[336,512]{1,0:T(8,128)(2,1)S(1)}, bf16[336,512]{1,0:T(8,128)(2,1)S(1)}, u32[]{:S(2)}, u32[]{:S(2)}) collective-permute-start(bf16[336,512]{1,0:T(8,128)(2,1)S(1)} %get-tuple-element.129), channel_id=1, source_target_pairs={{0,8},{4,12},{8,0},{12,4},{1,9},{5,13},{9,1},{13,5},{2,10},{6,14},... | collective-permute-start | bytes 1032200 | tf_op jit(solution)/shard_map/ppermute | solution.py:83
  184.5 6.5 %collective-permute-start.23 = (bf16[272,512]{1,0:T(8,128)(2,1)S(1)}, bf16[272,512]{1,0:T(8,128)(2,1)S(1)}, u32[]{:S(2)}, u32[]{:S(2)}) collective-permute-start(bf16[272,512]{1,0:T(8,128)(2,1)S(1)} %get-tuple-element.131), channel_id=1, source_target_pairs={{0,16},{16,0},{1,17},{17,1},{2,18},{18,2},{3,19},{19,3},{4,20},{20... | collective-permute-start | bytes 835592 | tf_op jit(solution)/shard_map/ppermute | solution.py:91
  191.9 6.4 %collective-permute-start.26 = (bf16[1,4,64,512]{3,2,1,0:T(8,128)(2,1)S(1)}, bf16[1,4,64,512]{3,2,1,0:T(8,128)(2,1)S(1)}, u32[]{:S(2)}, u32[]{:S(2)}) collective-permute-start(bf16[1,4,64,512]{3,2,1,0:T(8,128)(2,1)S(1)} %bitcast.35), channel_id=1, source_target_pairs={{0,1},{1,0},{2,3},{3,2},{4,5},{5,4},{6,7},{7,6},{8,9},{9,8},{10,11... | collective-permute-start | bytes 786440 | tf_op jit(solution)/shard_map/ppermute | solution.py:95
  193.5 7.6 %collective-permute-start.25 = (bf16[1,5,64,512]{3,2,1,0:T(8,128)(2,1)S(1)}, bf16[1,5,64,512]{3,2,1,0:T(8,128)(2,1)S(1)}, u32[]{:S(2)}, u32[]{:S(2)}) collective-permute-start(bf16[1,5,64,512]{3,2,1,0:T(8,128)(2,1)S(1)} %bitcast.33), channel_id=1, source_target_pairs={{0,16},{16,0},{1,17},{17,1},{2,18},{18,2},{3,19},{19,3},{4,20},{20... | collective-permute-start | bytes 983048 | tf_op jit(solution)/shard_map/ppermute | solution.py:91
  195.0 8.7 %collective-permute-start.24 = (bf16[1,5,64,512]{3,2,1,0:T(8,128)(2,1)S(1)}, bf16[1,5,64,512]{3,2,1,0:T(8,128)(2,1)S(1)}, u32[]{:S(2)}, u32[]{:S(2)}) collective-permute-start(bf16[1,5,64,512]{3,2,1,0:T(8,128)(2,1)S(1)} %bitcast.31), channel_id=1, source_target_pairs={{0,8},{4,12},{8,0},{12,4},{1,9},{5,13},{9,1},{13,5},{2,10},{6,14},... | collective-permute-start | bytes 983048 | tf_op jit(solution)/shard_map/ppermute | solution.py:83
  198.4 74.4 %copy-start.7 = (bf16[2,4,64,512]{3,2,1,0:T(8,128)(2,1)}, bf16[2,4,64,512]{3,2,1,0:T(8,128)(2,1)S(1)}, u32[]{:S(2)}) copy-start(bf16[2,4,64,512]{3,2,1,0:T(8,128)(2,1)S(1)} %pad_maximum_fusion.5.refs_2_) | copy-start | bytes 1572868
  201.2 71.5 %copy-start.4 = (bf16[2,5,64,512]{3,2,1,0:T(8,128)(2,1)}, bf16[2,5,64,512]{3,2,1,0:T(8,128)(2,1)S(1)}, u32[]{:S(2)}) copy-start(bf16[2,5,64,512]{3,2,1,0:T(8,128)(2,1)S(1)} %pad_maximum_fusion.3.refs_1_) | copy-start | bytes 1966084
  203.8 69.0 %copy-start.5 = (bf16[2,5,64,512]{3,2,1,0:T(8,128)(2,1)}, bf16[2,5,64,512]{3,2,1,0:T(8,128)(2,1)S(1)}, u32[]{:S(2)}) copy-start(bf16[2,5,64,512]{3,2,1,0:T(8,128)(2,1)S(1)} %pad_maximum_fusion.2.refs_0_) | copy-start | bytes 1966084
  203.8 23.2 %collective-permute-start.27 = (bf16[2,5,64,512]{3,2,1,0:T(8,128)(2,1)S(1)}, bf16[2,5,64,512]{3,2,1,0:T(8,128)(2,1)S(1)}, u32[]{:S(2)}, u32[]{:S(2)}) collective-permute-start(bf16[2,5,64,512]{3,2,1,0:T(8,128)(2,1)S(1)} %pad_maximum_fusion.2.refs_0_), channel_id=1, source_target_pairs={{0,16},{16,0},{1,17},{17,1},{2,18},{18,2},{3,19},{19,3},{4,20},{20... | collective-permute-start | bytes 1966088 | tf_op jit(solution)/shard_map/ppermute | solution.py:91
  203.9 9.4 %collective-permute-start.29 = (bf16[2,4,64,512]{3,2,1,0:T(8,128)(2,1)S(1)}, bf16[2,4,64,512]{3,2,1,0:T(8,128)(2,1)S(1)}, u32[]{:S(2)}, u32[]{:S(2)}) collective-permute-start(bf16[2,4,64,512]{3,2,1,0:T(8,128)(2,1)S(1)} %pad_maximum_fusion.5.refs_2_), channel_id=1, source_target_pairs={{0,8},{4,12},{8,0},{12,4},{1,9},{5,13},{9,1},{13,5},{2,10},{6,14},... | collective-permute-start | bytes 1572872 | tf_op jit(solution)/shard_map/ppermute | solution.py:83
  205.8 20.0 %collective-permute-start.32 = (bf16[2,4,64,512]{3,2,1,0:T(8,128)(2,1)S(1)}, bf16[2,4,64,512]{3,2,1,0:T(8,128)(2,1)S(1)}, u32[]{:S(2)}, u32[]{:S(2)}) collective-permute-start(bf16[2,4,64,512]{3,2,1,0:T(8,128)(2,1)S(1)} %pad_maximum_fusion.5.refs_2_), channel_id=1, source_target_pairs={{0,16},{16,0},{1,17},{17,1},{2,18},{18,2},{3,19},{19,3},{4,20},{20... | collective-permute-start | bytes 1572872 | tf_op jit(solution)/shard_map/ppermute | solution.py:91
  207.8 19.2 %collective-permute-start.35 = (bf16[2,4,64,512]{3,2,1,0:T(8,128)(2,1)S(1)}, bf16[2,4,64,512]{3,2,1,0:T(8,128)(2,1)}, u32[]{:S(2)}, u32[]{:S(2)}) collective-permute-start(bf16[2,4,64,512]{3,2,1,0:T(8,128)(2,1)S(1)} %pad_maximum_fusion.5.refs_2_), channel_id=1, source_target_pairs={{0,4},{4,0},{8,12},{12,8},{1,5},{5,1},{9,13},{13,9},{2,6},{6,2},{1... | collective-permute-start | bytes 1572872 | tf_op jit(solution)/shard_map/ppermute | solution.py:87
  207.8 31.2 %collective-permute-start.30 = (bf16[2,5,64,512]{3,2,1,0:T(8,128)(2,1)S(1)}, bf16[2,5,64,512]{3,2,1,0:T(8,128)(2,1)S(1)}, u32[]{:S(2)}, u32[]{:S(2)}) collective-permute-start(bf16[2,5,64,512]{3,2,1,0:T(8,128)(2,1)S(1)} %pad_maximum_fusion.2.refs_0_), channel_id=1, source_target_pairs={{0,1},{1,0},{2,3},{3,2},{4,5},{5,4},{6,7},{7,6},{8,9},{9,8},{10,11... | collective-permute-start | bytes 1966088 | tf_op jit(solution)/shard_map/ppermute | solution.py:95
  213.3 25.7 %collective-permute-start.28 = (bf16[2,5,64,512]{3,2,1,0:T(8,128)(2,1)S(1)}, bf16[2,5,64,512]{3,2,1,0:T(8,128)(2,1)S(1)}, u32[]{:S(2)}, u32[]{:S(2)}) collective-permute-start(bf16[2,5,64,512]{3,2,1,0:T(8,128)(2,1)S(1)} %pad_maximum_fusion.3.refs_1_), channel_id=1, source_target_pairs={{0,1},{1,0},{2,3},{3,2},{4,5},{5,4},{6,7},{7,6},{8,9},{9,8},{10,11... | collective-permute-start | bytes 1966088 | tf_op jit(solution)/shard_map/ppermute | solution.py:95
  225.9 13.1 %collective-permute-start.31 = (bf16[2,5,64,512]{3,2,1,0:T(8,128)(2,1)S(1)}, bf16[2,5,64,512]{3,2,1,0:T(8,128)(2,1)S(1)}, u32[]{:S(2)}, u32[]{:S(2)}) collective-permute-start(bf16[2,5,64,512]{3,2,1,0:T(8,128)(2,1)S(1)} %pad_maximum_fusion.3.refs_1_), channel_id=1, source_target_pairs={{0,8},{4,12},{8,0},{12,4},{1,9},{5,13},{9,1},{13,5},{2,10},{6,14},... | collective-permute-start | bytes 1966088 | tf_op jit(solution)/shard_map/ppermute | solution.py:83
  227.0 12.0 %collective-permute-start.33 = (bf16[2,5,64,512]{3,2,1,0:T(8,128)(2,1)S(1)}, bf16[2,5,64,512]{3,2,1,0:T(8,128)(2,1)S(1)}, u32[]{:S(2)}, u32[]{:S(2)}) collective-permute-start(bf16[2,5,64,512]{3,2,1,0:T(8,128)(2,1)S(1)} %pad_maximum_fusion.2.refs_0_), channel_id=1, source_target_pairs={{0,4},{4,0},{8,12},{12,8},{1,5},{5,1},{9,13},{13,9},{2,6},{6,2},{1... | collective-permute-start | bytes 1966088 | tf_op jit(solution)/shard_map/ppermute | solution.py:87
  227.0 45.8 %copy-start.9 = (bf16[2,5,64,512]{3,2,1,0:T(8,128)(2,1)}, bf16[2,5,64,512]{3,2,1,0:T(8,128)(2,1)S(1)}, u32[]{:S(2)}) copy-start(bf16[2,5,64,512]{3,2,1,0:T(8,128)(2,1)S(1)} %collective-permute-done.27.refs_6_) | copy-start | bytes 1966084
  227.0 12.0 %collective-permute-start.34 = (bf16[2,5,64,512]{3,2,1,0:T(8,128)(2,1)S(1)}, bf16[2,5,64,512]{3,2,1,0:T(8,128)(2,1)S(1)}, u32[]{:S(2)}, u32[]{:S(2)}) collective-permute-start(bf16[2,5,64,512]{3,2,1,0:T(8,128)(2,1)S(1)} %pad_maximum_fusion.3.refs_1_), channel_id=1, source_target_pairs={{0,4},{4,0},{8,12},{12,8},{1,5},{5,1},{9,13},{13,9},{2,6},{6,2},{1... | collective-permute-start | bytes 1966088 | tf_op jit(solution)/shard_map/ppermute | solution.py:87
  239.0 16.5 %collective-permute-start.36 = (bf16[2,5,64,512]{3,2,1,0:T(8,128)(2,1)S(1)}, bf16[2,5,64,512]{3,2,1,0:T(8,128)(2,1)}, u32[]{:S(2)}, u32[]{:S(2)}) collective-permute-start(bf16[2,5,64,512]{3,2,1,0:T(8,128)(2,1)S(1)} %collective-permute-done.27.refs_6_), channel_id=1, source_target_pairs={{0,1},{1,0},{2,3},{3,2},{4,5},{5,4},{6,7},{7,6},{8,9},{9,8},{10,11... | collective-permute-start | bytes 1966088 | tf_op jit(solution)/shard_map/ppermute | solution.py:95
  239.4 13.6 %collective-permute-start.38 = (bf16[2,4,64,512]{3,2,1,0:T(8,128)(2,1)S(1)}, bf16[2,4,64,512]{3,2,1,0:T(8,128)(2,1)}, u32[]{:S(2)}, u32[]{:S(2)}) collective-permute-start(bf16[2,4,64,512]{3,2,1,0:T(8,128)(2,1)S(1)} %collective-permute-done.29.refs_8_), channel_id=1, source_target_pairs={{0,16},{16,0},{1,17},{17,1},{2,18},{18,2},{3,19},{19,3},{4,20},{20... | collective-permute-start | bytes 1572872 | tf_op jit(solution)/shard_map/ppermute | solution.py:91
  239.5 13.7 %collective-permute-start.41 = (bf16[2,4,64,512]{3,2,1,0:T(8,128)(2,1)S(1)}, bf16[2,4,64,512]{3,2,1,0:T(8,128)(2,1)S(1)}, u32[]{:S(2)}, u32[]{:S(2)}) collective-permute-start(bf16[2,4,64,512]{3,2,1,0:T(8,128)(2,1)S(1)} %collective-permute-done.29.refs_8_), channel_id=1, source_target_pairs={{0,4},{4,0},{8,12},{12,8},{1,5},{5,1},{9,13},{13,9},{2,6},{6,2},{1... | collective-permute-start | bytes 1572872 | tf_op jit(solution)/shard_map/ppermute | solution.py:87
  239.5 14.5 %collective-permute-start.44 = (bf16[2,4,64,512]{3,2,1,0:T(8,128)(2,1)S(1)}, bf16[2,4,64,512]{3,2,1,0:T(8,128)(2,1)S(1)}, u32[]{:S(2)}, u32[]{:S(2)}) collective-permute-start(bf16[2,4,64,512]{3,2,1,0:T(8,128)(2,1)S(1)} %collective-permute-done.32.refs_14_), channel_id=1, source_target_pairs={{0,4},{4,0},{8,12},{12,8},{1,5},{5,1},{9,13},{13,9},{2,6},{6,2},{1... | collective-permute-start | bytes 1572872 | tf_op jit(solution)/shard_map/ppermute | solution.py:87
  240.0 28.5 %collective-permute-start.39 = (bf16[2,5,64,512]{3,2,1,0:T(8,128)(2,1)S(1)}, bf16[2,5,64,512]{3,2,1,0:T(8,128)(2,1)S(1)}, u32[]{:S(2)}, u32[]{:S(2)}) collective-permute-start(bf16[2,5,64,512]{3,2,1,0:T(8,128)(2,1)S(1)} %collective-permute-done.27.refs_6_), channel_id=1, source_target_pairs={{0,4},{4,0},{8,12},{12,8},{1,5},{5,1},{9,13},{13,9},{2,6},{6,2},{1... | collective-permute-start | bytes 1966088 | tf_op jit(solution)/shard_map/ppermute | solution.py:87
  253.0 15.5 %collective-permute-start.37 = (bf16[2,5,64,512]{3,2,1,0:T(8,128)(2,1)S(1)}, bf16[2,5,64,512]{3,2,1,0:T(8,128)(2,1)}, u32[]{:S(2)}, u32[]{:S(2)}) collective-permute-start(bf16[2,5,64,512]{3,2,1,0:T(8,128)(2,1)S(1)} %collective-permute-done.28.refs_7_), channel_id=1, source_target_pairs={{0,8},{4,12},{8,0},{12,4},{1,9},{5,13},{9,1},{13,5},{2,10},{6,14},... | collective-permute-start | bytes 1966088 | tf_op jit(solution)/shard_map/ppermute | solution.py:83
  253.2 15.3 %collective-permute-start.40 = (bf16[2,5,64,512]{3,2,1,0:T(8,128)(2,1)S(1)}, bf16[2,5,64,512]{3,2,1,0:T(8,128)(2,1)S(1)}, u32[]{:S(2)}, u32[]{:S(2)}) collective-permute-start(bf16[2,5,64,512]{3,2,1,0:T(8,128)(2,1)S(1)} %collective-permute-done.28.refs_7_), channel_id=1, source_target_pairs={{0,4},{4,0},{8,12},{12,8},{1,5},{5,1},{9,13},{13,9},{2,6},{6,2},{1... | collective-permute-start | bytes 1966088 | tf_op jit(solution)/shard_map/ppermute | solution.py:87
  254.0 14.5 %collective-permute-start.42 = (bf16[2,5,64,512]{3,2,1,0:T(8,128)(2,1)S(1)}, bf16[2,5,64,512]{3,2,1,0:T(8,128)(2,1)S(1)}, u32[]{:S(2)}, u32[]{:S(2)}) collective-permute-start(bf16[2,5,64,512]{3,2,1,0:T(8,128)(2,1)S(1)} %collective-permute-done.30.refs_12_), channel_id=1, source_target_pairs={{0,4},{4,0},{8,12},{12,8},{1,5},{5,1},{9,13},{13,9},{2,6},{6,2},{1... | collective-permute-start | bytes 1966088 | tf_op jit(solution)/shard_map/ppermute | solution.py:87
  255.6 12.9 %collective-permute-start.43 = (bf16[2,5,64,512]{3,2,1,0:T(8,128)(2,1)S(1)}, bf16[2,5,64,512]{3,2,1,0:T(8,128)(2,1)S(1)}, u32[]{:S(2)}, u32[]{:S(2)}) collective-permute-start(bf16[2,5,64,512]{3,2,1,0:T(8,128)(2,1)S(1)} %collective-permute-done.31.refs_13_), channel_id=1, source_target_pairs={{0,4},{4,0},{8,12},{12,8},{1,5},{5,1},{9,13},{13,9},{2,6},{6,2},{1... | collective-permute-start | bytes 1966088 | tf_op jit(solution)/shard_map/ppermute | solution.py:87
  268.5 4.2 %collective-permute-start.45 = (bf16[2,5,64,512]{3,2,1,0:T(8,128)(2,1)}, bf16[2,5,64,512]{3,2,1,0:T(8,128)(2,1)}, u32[]{:S(2)}, u32[]{:S(2)}) collective-permute-start(bf16[2,5,64,512]{3,2,1,0:T(8,128)(2,1)} %collective-permute-done.36.refs_18_), channel_id=1, source_target_pairs={{0,4},{4,0},{8,12},{12,8},{1,5},{5,1},{9,13},{13,9},{2,6},{6,2},{1... | collective-permute-start | bytes 1966088 | tf_op jit(solution)/shard_map/ppermute | solution.py:87
  268.6 4.1 %collective-permute-start.46 = (bf16[2,5,64,512]{3,2,1,0:T(8,128)(2,1)}, bf16[2,5,64,512]{3,2,1,0:T(8,128)(2,1)}, u32[]{:S(2)}, u32[]{:S(2)}) collective-permute-start(bf16[2,5,64,512]{3,2,1,0:T(8,128)(2,1)} %collective-permute-done.37.refs_19_), channel_id=1, source_target_pairs={{0,4},{4,0},{8,12},{12,8},{1,5},{5,1},{9,13},{13,9},{2,6},{6,2},{1... | collective-permute-start | bytes 1966088 | tf_op jit(solution)/shard_map/ppermute | solution.py:87
  270.0 2.7 collective-permute-start.47
  295.6 33.9 %collective-permute-start.48 = (bf16[7,128,256]{2,1,0:T(8,128)(2,1)}, bf16[7,128,256]{2,1,0:T(8,128)(2,1)S(1)}, u32[]{:S(2)}, u32[]{:S(2)}) collective-permute-start(bf16[7,128,256]{2,1,0:T(8,128)(2,1)} %get-tuple-element.171), channel_id=1, source_target_pairs={{0,0},{1,1},{2,16},{3,17},{16,2},{17,3},{18,18},{19,19},{4,4},{5,5... | collective-permute-start | bytes 1376264 | tf_op jit(solution)/shard_map/ppermute | solution.py:108
  299.2 42.2 %collective-permute-start.49 = (bf16[7,128,256]{2,1,0:T(8,128)(2,1)}, bf16[7,128,256]{2,1,0:T(8,128)(2,1)S(1)}, u32[]{:S(2)}, u32[]{:S(2)}) collective-permute-start(bf16[7,128,256]{2,1,0:T(8,128)(2,1)} %get-tuple-element.172), channel_id=1, source_target_pairs={{0,1},{1,0},{2,17},{3,16},{16,3},{17,2},{18,19},{19,18},{4,5},{5,4... | collective-permute-start | bytes 1376264 | tf_op jit(solution)/shard_map/ppermute | solution.py:108
  301.3 40.1 %collective-permute-start.50 = (bf16[7,128,256]{2,1,0:T(8,128)(2,1)}, bf16[7,128,256]{2,1,0:T(8,128)(2,1)S(1)}, u32[]{:S(2)}, u32[]{:S(2)}) collective-permute-start(bf16[7,128,256]{2,1,0:T(8,128)(2,1)} %get-tuple-element.173), channel_id=1, source_target_pairs={{0,2},{1,3},{2,18},{3,19},{16,0},{17,1},{18,16},{19,17},{4,6},{5,7... | collective-permute-start | bytes 1376264 | tf_op jit(solution)/shard_map/ppermute | solution.py:108
  301.3 42.8 %collective-permute-start.51 = (bf16[7,128,256]{2,1,0:T(8,128)(2,1)}, bf16[7,128,256]{2,1,0:T(8,128)(2,1)S(1)}, u32[]{:S(2)}, u32[]{:S(2)}) collective-permute-start(bf16[7,128,256]{2,1,0:T(8,128)(2,1)} %get-tuple-element.174), channel_id=1, source_target_pairs={{0,3},{1,2},{2,19},{3,18},{16,1},{17,0},{18,17},{19,16},{4,7},{5,6... | collective-permute-start | bytes 1376264 | tf_op jit(solution)/shard_map/ppermute | solution.py:108
  344.1 32.5 %collective-permute-start.52 = (bf16[7,128,256]{2,1,0:T(8,128)(2,1)}, bf16[7,128,256]{2,1,0:T(8,128)(2,1)S(1)}, u32[]{:S(2)}, u32[]{:S(2)}) collective-permute-start(bf16[7,128,256]{2,1,0:T(8,128)(2,1)} %get-tuple-element.179), channel_id=1, source_target_pairs={{0,0},{1,1},{2,16},{3,17},{16,2},{17,3},{18,18},{19,19},{4,4},{5,5... | collective-permute-start | bytes 1376264 | tf_op jit(solution)/shard_map/ppermute | solution.py:108
  346.0 40.0 %collective-permute-start.53 = (bf16[7,128,256]{2,1,0:T(8,128)(2,1)}, bf16[7,128,256]{2,1,0:T(8,128)(2,1)S(1)}, u32[]{:S(2)}, u32[]{:S(2)}) collective-permute-start(bf16[7,128,256]{2,1,0:T(8,128)(2,1)} %get-tuple-element.180), channel_id=1, source_target_pairs={{0,1},{1,0},{2,17},{3,16},{16,3},{17,2},{18,19},{19,18},{4,5},{5,4... | collective-permute-start | bytes 1376264 | tf_op jit(solution)/shard_map/ppermute | solution.py:108
  347.0 41.3 %collective-permute-start.54 = (bf16[7,128,256]{2,1,0:T(8,128)(2,1)}, bf16[7,128,256]{2,1,0:T(8,128)(2,1)S(1)}, u32[]{:S(2)}, u32[]{:S(2)}) collective-permute-start(bf16[7,128,256]{2,1,0:T(8,128)(2,1)} %get-tuple-element.181), channel_id=1, source_target_pairs={{0,2},{1,3},{2,18},{3,19},{16,0},{17,1},{18,16},{19,17},{4,6},{5,7... | collective-permute-start | bytes 1376264 | tf_op jit(solution)/shard_map/ppermute | solution.py:108
  347.0 44.1 %collective-permute-start.55 = (bf16[7,128,256]{2,1,0:T(8,128)(2,1)}, bf16[7,128,256]{2,1,0:T(8,128)(2,1)S(1)}, u32[]{:S(2)}, u32[]{:S(2)}) collective-permute-start(bf16[7,128,256]{2,1,0:T(8,128)(2,1)} %get-tuple-element.182), channel_id=1, source_target_pairs={{0,3},{1,2},{2,19},{3,18},{16,1},{17,0},{18,17},{19,16},{4,7},{5,6... | collective-permute-start | bytes 1376264 | tf_op jit(solution)/shard_map/ppermute | solution.py:108
  (18 other events, 236.6 us)

commit v3 on v2

--- a/solution.py
+++ b/solution.py
@@ -34,7 +34,8 @@
 PIECES = (1, 2, 4)
 HALVES = 2
 WIDE = GROUP // HALVES
-VMEM = 60 << 20
+GRAM_VMEM = 28 << 20
+STEP_VMEM = 60 << 20
 
 
 def shards_rows(iterate):
@@ -158,50 +159,57 @@
 
 def gram_kernel(*refs):
     count = 2 * len(PIECES)
-    inputs, refs = refs[:count], refs[count:]
-    keeps, sends, refs = refs[0:6:2], refs[1:6:2], refs[6:]
-    panel, turned, tails, arrived = refs[0], refs[1], refs[2:5], refs[5]
+    inputs, outs, refs = refs[:count], refs[count : count + 6], refs[count + 6 :]
+    keeps, sends, tails = refs[0:6:2], refs[1:6:2], refs[6:9]
+    panel, arrived, gone = refs[9:]
     y, x, core, high, low = place()
     for source in range(2):
         for i, (p, b) in enumerate(place_of_block()):
             for step in range(4):
-                slab = slab_of(high, low, step)
-                columns = pl.ds(source * GROUP, GROUP)
+                spot = pl.multiple_of(slab_of(high, low, step) * BAND, BAND)
                 pltpu.make_async_copy(
                     inputs[source * len(PIECES) + p].at[step, pl.ds(b * BAND, BAND), :],
-                    panel.at[i, pl.ds(pl.multiple_of(slab * BAND, BAND), BAND), columns],
-                    arrived.at[0],
+                    panel.at[i, pl.ds(spot, BAND), pl.ds(source * GROUP, GROUP)],
+                    arrived,
                 ).start()
-                for n in range(2):
-                    to_x, to_y = slab // 2, slab % 2
-                    by = 4 * jnp.abs(to_x - x) + 2 * jnp.abs(to_y - y) + jnp.abs(n - low)
-                    pltpu.make_async_copy(
-                        inputs[source * len(PIECES) + p].at[step, pl.ds(b * BAND + n * UNIT, UNIT), :],
-                        turned.at[i, pl.ds(pl.multiple_of(by * UNIT, UNIT), UNIT), columns],
-                        arrived.at[1],
-                    ).start()
     for tail in tails:
         tail[...] = jnp.zeros_like(tail)
-    pltpu.make_async_copy(panel, panel, arrived.at[0]).wait()
-    pltpu.make_async_copy(turned, turned, arrived.at[1]).wait()
+    pltpu.make_async_copy(panel, panel, arrived).wait()
     for third, (lo, hi) in enumerate(THIRDS):
         keep, send, tail = keeps[third], sends[third], tails[third]
+        size = len(sent(third, 0)) * UNIT
 
         def block(e, carry):
             second = (e + lo >= BLOCKS).astype(jnp.int32)
             i = e + lo - BLOCKS * second
             j = lax.rem(i + 2 * core + second, BLOCKS)
             flag = jnp.logical_and(core == 0, second == 0).astype(F32)
-            got = dot(turned[i], panel[j], ((1,), (1,)))
+            rows = [
+                panel[i, pl.ds(pl.multiple_of(place_of(x, y, low, by) * UNIT, UNIT), UNIT), :]
+                for by in range(PLACES)
+            ]
+            got = dot(jnp.concatenate(rows), panel[j], ((1,), (1,)))
             for n, by in enumerate(kept(third, 0)):
                 keep[e, n] = got[by * UNIT : (by + 1) * UNIT]
             parts = [got[by * UNIT : (by + 1) * UNIT] for by in sent(third, 0)]
             units = [place_of(x, y, low, by) for by in sent(third, 0)]
             write_sent(send, tail, e, parts, units, flag)
+            pltpu.make_async_copy(keep.at[e], outs[2 * third].at[e], gone.at[2 * third]).start()
+            rows = pl.ds(pl.multiple_of(e * size, size), size)
+            pltpu.make_async_copy(
+                send.at[rows, :], outs[2 * third + 1].at[rows, :], gone.at[2 * third + 1]
+            ).start()
             return carry
 
         lax.fori_loop(0, hi - lo, block, 0)
-        send[pl.ds(rows_sent(third, 0), TAIL), :] = tail[...].astype(BF16)
+        rows = pl.ds(rows_sent(third, 0), TAIL)
+        send[rows, :] = tail[...].astype(BF16)
+        pltpu.make_async_copy(
+            send.at[rows, :], outs[2 * third + 1].at[rows, :], gone.at[2 * third + 1]
+        ).start()
+    for third in range(3):
+        for n, ref in ((2 * third, keeps[third]), (2 * third + 1, sends[third])):
+            pltpu.make_async_copy(ref, outs[n], gone.at[n]).wait()
 
 
 def add_kernel(stage, *refs):
@@ -245,18 +253,20 @@
 
 
 def gram_call(inputs):
+    shapes = [shape for third in range(3) for shape in exchange_shapes(third, 0)]
     return pl.pallas_call(
         gram_kernel,
-        out_shape=[shape for third in range(3) for shape in exchange_shapes(third, 0)],
+        out_shape=shapes,
         in_specs=[pl.BlockSpec(memory_space=pl.ANY)] * len(inputs),
-        out_specs=[pl.BlockSpec(memory_space=pltpu.VMEM)] * 6,
-        scratch_shapes=[
+        out_specs=[pl.BlockSpec(memory_space=pl.ANY)] * 6,
+        scratch_shapes=[pltpu.VMEM(shape.shape, shape.dtype) for shape in shapes]
+        + [pltpu.VMEM((TAIL, BLOCK), F32)] * 3
+        + [
             pltpu.VMEM((BLOCKS, BLOCK, 2 * GROUP), BF16),
-            pltpu.VMEM((BLOCKS, BLOCK, 2 * GROUP), BF16),
-        ]
-        + [pltpu.VMEM((TAIL, BLOCK), F32)] * 3
-        + [pltpu.SemaphoreType.DMA((2,))],
-        compiler_params=pltpu.CompilerParams(vmem_limit_bytes=VMEM),
+            pltpu.SemaphoreType.DMA,
+            pltpu.SemaphoreType.DMA((6,)),
+        ],
+        compiler_params=pltpu.CompilerParams(vmem_limit_bytes=GRAM_VMEM),
         cost_estimate=pl.CostEstimate(
             flops=2 * MINE * BLOCK * BLOCK * 2 * GROUP, bytes_accessed=24 << 20, transcendentals=0
         ),
@@ -323,20 +333,22 @@
     def keyed(pieces, arrays):
         return [(bys, array) for (bys, _), array in zip(pieces, arrays)]
 
+    def ordered(*groups):
+        done = wave([unkeyed(group) for group in groups], [piece for _, piece in out])
+        out[:] = [(key, piece) for (key, _), piece in zip(out, done[1])]
+        return [keyed(group, arrays) for group, arrays in zip(groups, done[0])]
+
     own = [([0], piece) for piece in mine]
-    pair = merge(own, move(0, own))
-    pair = keyed(pair, wave(*unkeyed(pair)))
-    second, third_a = move(1, pair), move(2, pair)
+    (pair,) = ordered(merge(own, move(0, own)))
+    second = move(1, pair)
     across(pair)
-    (got,) = wave((unkeyed(second), unkeyed(third_a), [piece for _, piece in out]))
-    second, third_a = keyed(second, got[0]), keyed(third_a, got[1])
-    out[:] = [(key, piece) for (key, _), piece in zip(out, got[2])]
+    pair, second = ordered(pair, second)
+    third_a = move(2, pair)
+    across(second)
+    second, third_a = ordered(second, third_a)
     third_b = move(2, second)
-    across(second)
     across(third_a)
-    (got,) = wave((unkeyed(third_b), [piece for _, piece in out]))
-    third_b = keyed(third_b, got[0])
-    out[:] = [(key, piece) for (key, _), piece in zip(out, got[1])]
+    (third_b,) = ordered(third_b)
     across(third_b)
     return out
 
@@ -426,7 +438,7 @@
             pltpu.SemaphoreType.DMA,
             pltpu.SemaphoreType.DMA((4,)),
         ],
-        compiler_params=pltpu.CompilerParams(vmem_limit_bytes=VMEM),
+        compiler_params=pltpu.CompilerParams(vmem_limit_bytes=STEP_VMEM),
         cost_estimate=pl.CostEstimate(
             flops=4 * ORDER * ORDER * WIDE, bytes_accessed=20 << 20, transcendentals=0
         ),

time: 394 us -> 366 us (0.929)
  waiting for transfers between devices: 237 us -> 219 us
  Pallas kernels: 70.7 us -> 63.1 us
  local copies, waits for them, and re-layouts: 13.7 us -> 8.12 us
    ppermute x16, waiting for transfers between devices: 111 us -> 102 us  [over_z(): return lax.ppermute(a, 'row', [(z, z ^ step) for z in range(4)])]
    ppermute x7, waiting for transfers between devices: 37.7 us -> 28.8 us  [over_x(): return lax.ppermute(a, 'col', [(0, 2), (1, 3), (2, 0), (3, 1)])]
    pallas_call x1, Pallas kernels: 20.9 us -> 13.3 us  [gram_call(): pl.pallas_call(gram_kernel, out_shape=shapes, in_specs=[pl.BlockSpec(memo...]
    ppermute x10, waiting for transfers between devices: 42.2 us -> 35.7 us  [over_y(): return lax.ppermute(a, 'mats', [(0, 1), (1, 0)])]
    ppermute x15, waiting for transfers between devices: 3.85 us -> 10 us  [over_core(): return lax.ppermute(a, 'col', [(0, 1), (1, 0), (2, 3), (3, 2)])]
    unnamed x52 -> x48, local copies, waits for them, and re-layouts: 7.55 us -> 1.96 us
  transfers between devices with their start and end apart: 56 -> 56, of which waited for: 35 -> 41; matrix products, arithmetic and copies ran while one was open for 6% -> 7% of each run, Pallas kernels for 6% -> 6%
where the time goes in v3:
time: 366 us; the launch traced here: 365 us
  waiting for transfers between devices  219 us (60%)
  Pallas kernels  63.1 us (17%)
  starting transfers between devices  50 us (14%)
  other arithmetic  23.9 us (7%)
  local copies, waits for them, and re-layouts  8.12 us (2%)
    ppermute x16, waiting for transfers between devices, over_z(): return lax.ppermute(a, 'row', [(z, z ^ step) for z in range(4)])  102 us
    pallas_call x2, Pallas kernels, step_call(): pl.pallas_call(functools.partial(step_kernel, keys, part), out_shape=[jax...  45.6 us
    ppermute x8, waiting for transfers between devices, home(): return lax.ppermute(a, ('mats', 'row'), pairs)  42.7 us
    ppermute x10, waiting for transfers between devices, over_y(): return lax.ppermute(a, 'mats', [(0, 1), (1, 0)])  35.7 us
    ppermute x7, waiting for transfers between devices, over_x(): return lax.ppermute(a, 'col', [(0, 2), (1, 3), (2, 0), (3, 1)])  28.8 us
    dynamic_update_slice x8, other arithmetic, shards_cube(): lax.dynamic_update_slice_in_dim(out, pick(out, at, WIDE, 1) + piece, at, 1)  17.5 us
    ppermute x16, starting transfers between devices, over_z(): return lax.ppermute(a, 'row', [(z, z ^ step) for z in range(4)])  15.1 us
    ppermute x8, starting transfers between devices, home(): return lax.ppermute(a, ('mats', 'row'), pairs)  13.9 us
  transfers between devices with their start and end apart: 56, of which 41 were waited for; matrix products, arithmetic and copies ran while one was open for 7% of the time, Pallas kernels for 6%

profile of v3, /device:TPU:12, one launch (start us, length us, event | category | flops | bytes accessed | tf_op | source)
XLA Modules:
  0.0 364.8 jit_solution(14396710747408071331)
XLA Ops:
  1.9 1.7 slice.13
  3.8 5.7 %collective-permute-done = bf16[128,1024]{1,0:T(8,128)(2,1)S(1)} collective-permute-done((bf16[128,1024]{1,0:T(8,128)(2,1)S(1)}, bf16[128,1024]{1,0:T(8,128)(2,1)S(1)}, u32[]{:S(2)}, u32[]{:S(2)}) %collective-permute-start) | collective-permute-done | bytes 262176 | tf_op jit(solution)/shard_map/ppermute | solution.py:92
  10.2 2.5 slice.14
  13.0 2.8 collective-permute-start.2
  16.4 2.7 collective-permute-done.1
  19.1 5.1 %collective-permute-done.2 = bf16[128,512]{1,0:T(8,128)(2,1)S(1)} collective-permute-done((bf16[128,512]{1,0:T(8,128)(2,1)S(1)}, bf16[128,512]{1,0:T(8,128)(2,1)S(1)}, u32[]{:S(2)}, u32[]{:S(2)}) %collective-permute-start.2) | collective-permute-done | bytes 131104 | tf_op jit(solution)/shard_map/ppermute | solution.py:96
  24.2 2.3 collective-permute-done.3
  26.8 1.5 collective-permute-start.8
  28.4 3.0 collective-permute-start.6
  31.8 5.8 %collective-permute-done.5 = bf16[256,512]{1,0:T(8,128)(2,1)S(1)} collective-permute-done((bf16[256,512]{1,0:T(8,128)(2,1)S(1)}, bf16[256,512]{1,0:T(8,128)(2,1)S(1)}, u32[]{:S(2)}, u32[]{:S(2)}) %collective-permute-start.5) | collective-permute-done | bytes 262176 | tf_op jit(solution)/shard_map/ppermute | solution.py:96
  37.6 10.9 %collective-permute-done.6 = bf16[256,512]{1,0:T(8,128)(2,1)S(1)} collective-permute-done((bf16[256,512]{1,0:T(8,128)(2,1)S(1)}, bf16[256,512]{1,0:T(8,128)(2,1)S(1)}, u32[]{:S(2)}, u32[]{:S(2)}) %collective-permute-start.6) | collective-permute-done | bytes 262176 | tf_op jit(solution)/shard_map/ppermute | solution.py:96
  48.4 4.2 %collective-permute-done.7 = bf16[256,512]{1,0:T(8,128)(2,1)S(1)} collective-permute-done((bf16[256,512]{1,0:T(8,128)(2,1)S(1)}, bf16[256,512]{1,0:T(8,128)(2,1)S(1)}, u32[]{:S(2)}, u32[]{:S(2)}) %collective-permute-start.7) | collective-permute-done | bytes 262176 | tf_op jit(solution)/shard_map/ppermute | solution.py:96
  53.3 1.6 collective-permute-start.11
  54.8 2.8 collective-permute-start.9
  57.7 29.4 %collective-permute-done.10 = bf16[512,512]{1,0:T(8,128)(2,1)S(1)} collective-permute-done((bf16[512,512]{1,0:T(8,128)(2,1)S(1)}, bf16[512,512]{1,0:T(8,128)(2,1)S(1)}, u32[]{:S(2)}, u32[]{:S(2)}) %collective-permute-start.10) | collective-permute-done | bytes 524320 | tf_op jit(solution)/shard_map/ppermute | solution.py:96
  87.0 10.9 %collective-permute-done.11 = bf16[512,512]{1,0:T(8,128)(2,1)S(1)} collective-permute-done((bf16[512,512]{1,0:T(8,128)(2,1)S(1)}, bf16[512,512]{1,0:T(8,128)(2,1)S(1)}, u32[]{:S(2)}, u32[]{:S(2)}) %collective-permute-start.11) | collective-permute-done | bytes 524320 | tf_op jit(solution)/shard_map/ppermute | solution.py:96
  98.9 4.7 %fusion = f32[896,2048]{1,0:T(8,128)} fusion(f32[896,2048]{1,0:T(8,128)S(1)} %bitcast.38), kind=kLoop, calls=%fused_computation.1 | loop fusion | flops 5505024 | bytes 14680064 | tf_op jit(solution)/shard_map/mul | solution.py:488
  104.7 13.3 %gram.1 = (f32[5,4,64,512]{3,2,1,0:T(8,128)S(1)}, bf16[1296,512]{1,0:T(8,128)(2,1)S(1)}, f32[5,4,64,512]{3,2,1,0:T(8,128)S(1)}, bf16[1296,512]{1,0:T(8,128)(2,1)...) custom-call(bf16[4,128,512]{2,1,0:T(8,128)(2,1)S(1)} %pad_maximum_fusion.4.refs_0_.refs_24_, ...), custom_call_target="tpu_custom_call" | custom-call | flops 7516192768 | bytes 25165824 | tf_op jit(solution)/shard_map/gram/pallas_call | solution.py:257
  119.5 1.5 collective-permute-start.15
  121.5 25.0 %collective-permute-done.17.refs_5_ = bf16[1040,512]{1,0:T(8,128)(2,1)S(1)} collective-permute-done((bf16[1040,512]{1,0:T(8,128)(2,1)S(1)}, bf16[1040,512]{1,0:T(8,128)(2,1)S(1)}, u32[]{:S(2)}, u32[]{:S(2)}) %collective-permute-start.17) | collective-permute-done | bytes 1064992 | tf_op jit(solution)/shard_map/ppermute | solution.py:96
  146.5 4.2 %collective-permute-done.15.refs_1_ = bf16[1296,512]{1,0:T(8,128)(2,1)S(1)} collective-permute-done((bf16[1296,512]{1,0:T(8,128)(2,1)S(1)}, bf16[1296,512]{1,0:T(8,128)(2,1)S(1)}, u32[]{:S(2)}, u32[]{:S(2)}) %collective-permute-start.15) | collective-permute-done | bytes 1327136 | tf_op jit(solution)/shard_map/ppermute | solution.py:84
  151.9 3.2 add.164
  156.2 12.4 %collective-permute-done.20.refs_5_ = bf16[528,512]{1,0:T(8,128)(2,1)S(1)} collective-permute-done((bf16[528,512]{1,0:T(8,128)(2,1)S(1)}, bf16[528,512]{1,0:T(8,128)(2,1)S(1)}, u32[]{:S(2)}, u32[]{:S(2)}) %collective-permute-start.20) | collective-permute-done | bytes 540704 | tf_op jit(solution)/shard_map/ppermute | solution.py:84
  168.6 2.6 collective-permute-done.18.refs_1_
  173.1 1.5 collective-permute-start.23
  174.6 5.0 %collective-permute-done.23.refs_5_ = bf16[272,512]{1,0:T(8,128)(2,1)S(1)} collective-permute-done((bf16[272,512]{1,0:T(8,128)(2,1)S(1)}, bf16[272,512]{1,0:T(8,128)(2,1)S(1)}, u32[]{:S(2)}, u32[]{:S(2)}) %collective-permute-start.23) | collective-permute-done | bytes 278560 | tf_op jit(solution)/shard_map/ppermute | solution.py:92
  180.5 1.6 collective-permute-start.26
  184.9 2.1 collective-permute-done.26
  187.0 2.2 collective-permute-done.25
  189.2 3.4 collective-permute-done.24
  192.7 1.8 collective-permute-start.29
  195.2 6.7 %collective-permute-done.29.refs_8_ = bf16[2,4,64,512]{3,2,1,0:T(8,128)(2,1)S(1)} collective-permute-done((bf16[2,4,64,512]{3,2,1,0:T(8,128)(2,1)S(1)}, bf16[2,4,64,512]{3,2,1,0:T(8,128)(2,1)S(1)}, u32[]{:S(2)}, u32[]{:S(2)}) %collective-permute-start.29) | collective-permute-done | bytes 524320 | tf_op jit(solution)/shard_map/ppermute | solution.py:84
  202.0 1.9 collective-permute-done.32.refs_5_
  205.3 1.9 collective-permute-start.35
  208.3 10.3 %collective-permute-done.35.refs_14_ = bf16[2,4,64,512]{3,2,1,0:T(8,128)(2,1)S(1)} collective-permute-done((bf16[2,4,64,512]{3,2,1,0:T(8,128)(2,1)S(1)}, bf16[2,4,64,512]{3,2,1,0:T(8,128)(2,1)S(1)}, u32[]{:S(2)}, u32[]{:S(2)}) %collective-permute-start.35) | collective-permute-done | bytes 524320 | tf_op jit(solution)/shard_map/ppermute | solution.py:92
  218.7 1.9 collective-permute-done.38.refs_11_
  222.0 1.5 collective-permute-start.41
  223.5 1.6 collective-permute-start.39
  225.1 1.7 collective-permute-start.40
  227.3 7.4 %collective-permute-done.41.refs_20_ = bf16[2,4,64,512]{3,2,1,0:T(8,128)(2,1)} collective-permute-done((bf16[2,4,64,512]{3,2,1,0:T(8,128)(2,1)S(1)}, bf16[2,4,64,512]{3,2,1,0:T(8,128)(2,1)}, u32[]{:S(2)}, u32[]{:S(2)}) %collective-permute-start.41) | collective-permute-done | bytes 524320 | tf_op jit(solution)/shard_map/ppermute | solution.py:92
  234.8 1.9 collective-permute-done.44.refs_17_
  236.7 1.6 collective-permute-done.39.refs_18_
  238.3 1.6 collective-permute-done.40.refs_19_
  241.0 3.2 collective-permute-done.47.refs_23_
  244.2 22.8 %step.2 = (bf16[7,128,256]{2,1,0:T(8,128)(2,1)}, bf16[7,128,256]{2,1,0:T(8,128)(2,1)}, bf16[7,128,256]{2,1,0:T(8,128)(2,1)}, bf16[7,128,256]{2,1,0:T(8,128)(2,1)}) custom-call(bf16[2,5,64,512]{3,2,1,0:T(8,128)(2,1)} %copy-done.5, bf16[2,5,64,512]{3,2,1,0:T(8,128)(2,1)} %copy-done.4, bf16[2,4,64,512]{3,2,1,0:T(8,128)(2,1)} %copy-done.6, ...), custom_call_target="tpu_custom_call" | custom-call | flops 13153337344 | bytes 20971520 | tf_op jit(solution)/shard_map/step/pallas_call | solution.py:426
  267.0 3.1 collective-permute-start.48
  270.1 1.9 collective-permute-start.49
  272.0 2.5 collective-permute-start.51
  274.6 22.8 %step.3 = (bf16[7,128,256]{2,1,0:T(8,128)(2,1)}, bf16[7,128,256]{2,1,0:T(8,128)(2,1)}, bf16[7,128,256]{2,1,0:T(8,128)(2,1)}, bf16[7,128,256]{2,1,0:T(8,128)(2,1)}) custom-call(bf16[2,5,64,512]{3,2,1,0:T(8,128)(2,1)} %copy-done.5, bf16[2,5,64,512]{3,2,1,0:T(8,128)(2,1)} %copy-done.4, bf16[2,4,64,512]{3,2,1,0:T(8,128)(2,1)} %copy-done.6, ...), custom_call_target="tpu_custom_call" | custom-call | flops 13153337344 | bytes 20971520 | tf_op jit(solution)/shard_map/step/pallas_call | solution.py:426
  297.4 3.5 collective-permute-done.48
  300.9 11.3 %collective-permute-done.49 = bf16[7,128,256]{2,1,0:T(8,128)(2,1)S(1)} collective-permute-done((bf16[7,128,256]{2,1,0:T(8,128)(2,1)}, bf16[7,128,256]{2,1,0:T(8,128)(2,1)S(1)}, u32[]{:S(2)}, u32[]{:S(2)}) %collective-permute-start.49) | collective-permute-done | bytes 458784 | tf_op jit(solution)/shard_map/ppermute | solution.py:109
  312.2 3.3 collective-permute-done.51
  315.5 1.9 collective-permute-start.52
  318.4 3.5 collective-permute-start.55
  322.0 2.2 constant_dynamic-update-slice_fusion.7
  324.2 2.2 constant_dynamic-update-slice_fusion.6
  326.5 2.2 constant_dynamic-update-slice_fusion.5
  328.8 2.2 constant_dynamic-update-slice_fusion.4
  331.0 16.9 %collective-permute-done.52 = bf16[7,128,256]{2,1,0:T(8,128)(2,1)S(1)} collective-permute-done((bf16[7,128,256]{2,1,0:T(8,128)(2,1)}, bf16[7,128,256]{2,1,0:T(8,128)(2,1)S(1)}, u32[]{:S(2)}, u32[]{:S(2)}) %collective-permute-start.52) | collective-permute-done | bytes 458784 | tf_op jit(solution)/shard_map/ppermute | solution.py:109
  348.0 2.2 constant_dynamic-update-slice_fusion.3
  350.2 7.2 %collective-permute-done.53 = bf16[7,128,256]{2,1,0:T(8,128)(2,1)S(1)} collective-permute-done((bf16[7,128,256]{2,1,0:T(8,128)(2,1)}, bf16[7,128,256]{2,1,0:T(8,128)(2,1)S(1)}, u32[]{:S(2)}, u32[]{:S(2)}) %collective-permute-start.53) | collective-permute-done | bytes 458784 | tf_op jit(solution)/shard_map/ppermute | solution.py:109
  357.5 2.2 constant_dynamic-update-slice_fusion.2
  359.8 2.2 constant_dynamic-update-slice_fusion.1
  362.6 2.2 constant_dynamic-update-slice_fusion
  (140 shorter events, 25.1 us)
Async XLA Ops:
  1.3 8.1 %collective-permute-start = (bf16[128,1024]{1,0:T(8,128)(2,1)S(1)}, bf16[128,1024]{1,0:T(8,128)(2,1)S(1)}, u32[]{:S(2)}, u32[]{:S(2)}) collective-permute-start(bf16[128,1024]{1,0:T(8,128)(2,1)S(1)} %dynamic-slice_convert_fusion.4), channel_id=1, source_target_pairs={{0,16},{16,0},{1,17},{17,1},{2,18},{18,2},{3,19},{19,3},{4,20},{20... | collective-permute-start | bytes 786440 | tf_op jit(solution)/shard_map/ppermute | solution.py:92
  9.6 17.0 %collective-permute-start.4 = (bf16[256,1024]{1,0:T(8,128)(2,1)S(1)}, bf16[256,1024]{1,0:T(8,128)(2,1)S(1)}, u32[]{:S(2)}, u32[]{:S(2)}) collective-permute-start(bf16[256,1024]{1,0:T(8,128)(2,1)S(1)} %get-tuple-element.119), channel_id=1, source_target_pairs={{0,16},{16,0},{1,17},{17,1},{2,18},{18,2},{3,19},{19,3},{4,20},{20... | collective-permute-start | bytes 1572872 | tf_op jit(solution)/shard_map/ppermute | solution.py:92
  12.7 6.4 %collective-permute-start.1 = (bf16[128,512]{1,0:T(8,128)(2,1)S(1)}, bf16[128,512]{1,0:T(8,128)(2,1)S(1)}, u32[]{:S(2)}, u32[]{:S(2)}) collective-permute-start(bf16[128,512]{1,0:T(8,128)(2,1)S(1)} %get-tuple-element.113), channel_id=1, source_target_pairs={{0,1},{1,0},{2,3},{3,2},{4,5},{5,4},{6,7},{7,6},{8,9},{9,8},{10,11... | collective-permute-start | bytes 393224 | tf_op jit(solution)/shard_map/ppermute | solution.py:96
  13.0 11.2 %collective-permute-start.2 = (bf16[128,512]{1,0:T(8,128)(2,1)S(1)}, bf16[128,512]{1,0:T(8,128)(2,1)S(1)}, u32[]{:S(2)}, u32[]{:S(2)}) collective-permute-start(bf16[128,512]{1,0:T(8,128)(2,1)S(1)} %get-tuple-element.114), channel_id=1, source_target_pairs={{0,2},{1,3},{2,0},{3,1},{4,6},{5,7},{6,4},{7,5},{8,10},{9,11},{10,... | collective-permute-start | bytes 393224 | tf_op jit(solution)/shard_map/ppermute | solution.py:96
  15.8 10.7 %collective-permute-start.3 = (bf16[128,512]{1,0:T(8,128)(2,1)S(1)}, bf16[128,512]{1,0:T(8,128)(2,1)S(1)}, u32[]{:S(2)}, u32[]{:S(2)}) collective-permute-start(bf16[128,512]{1,0:T(8,128)(2,1)S(1)} %get-tuple-element.115), channel_id=1, source_target_pairs={{0,3},{1,2},{2,1},{3,0},{4,7},{5,6},{6,5},{7,4},{8,11},{9,10},{10,... | collective-permute-start | bytes 393224 | tf_op jit(solution)/shard_map/ppermute | solution.py:96
  26.6 78.2 %copy-start.3 = (bf16[4,128,512]{2,1,0:T(8,128)(2,1)}, bf16[4,128,512]{2,1,0:T(8,128)(2,1)S(1)}, u32[]{:S(2)}) copy-start(bf16[4,128,512]{2,1,0:T(8,128)(2,1)S(1)} %pad_maximum_fusion.4.refs_0_.refs_24_) | copy-start | bytes 1572868
  26.8 26.0 %collective-permute-start.8 = (bf16[512,1024]{1,0:T(8,128)(2,1)S(1)}, bf16[512,1024]{1,0:T(8,128)(2,1)S(1)}, u32[]{:S(2)}, u32[]{:S(2)}) collective-permute-start(bf16[512,1024]{1,0:T(8,128)(2,1)S(1)} %get-tuple-element.125), channel_id=1, source_target_pairs={{0,16},{16,0},{1,17},{17,1},{2,18},{18,2},{3,19},{19,3},{4,20},{20... | collective-permute-start | bytes 3145736 | tf_op jit(solution)/shard_map/ppermute | solution.py:92
  28.3 9.2 %collective-permute-start.5 = (bf16[256,512]{1,0:T(8,128)(2,1)S(1)}, bf16[256,512]{1,0:T(8,128)(2,1)S(1)}, u32[]{:S(2)}, u32[]{:S(2)}) collective-permute-start(bf16[256,512]{1,0:T(8,128)(2,1)S(1)} %get-tuple-element.121), channel_id=1, source_target_pairs={{0,1},{1,0},{2,3},{3,2},{4,5},{5,4},{6,7},{7,6},{8,9},{9,8},{10,11... | collective-permute-start | bytes 786440 | tf_op jit(solution)/shard_map/ppermute | solution.py:96
  28.4 20.0 %collective-permute-start.6 = (bf16[256,512]{1,0:T(8,128)(2,1)S(1)}, bf16[256,512]{1,0:T(8,128)(2,1)S(1)}, u32[]{:S(2)}, u32[]{:S(2)}) collective-permute-start(bf16[256,512]{1,0:T(8,128)(2,1)S(1)} %get-tuple-element.122), channel_id=1, source_target_pairs={{0,2},{1,3},{2,0},{3,1},{4,6},{5,7},{6,4},{7,5},{8,10},{9,11},{10,... | collective-permute-start | bytes 786440 | tf_op jit(solution)/shard_map/ppermute | solution.py:96
  31.4 21.2 %collective-permute-start.7 = (bf16[256,512]{1,0:T(8,128)(2,1)S(1)}, bf16[256,512]{1,0:T(8,128)(2,1)S(1)}, u32[]{:S(2)}, u32[]{:S(2)}) collective-permute-start(bf16[256,512]{1,0:T(8,128)(2,1)S(1)} %get-tuple-element.123), channel_id=1, source_target_pairs={{0,3},{1,2},{2,1},{3,0},{4,7},{5,6},{6,5},{7,4},{8,11},{9,10},{10,... | collective-permute-start | bytes 786440 | tf_op jit(solution)/shard_map/ppermute | solution.py:96
  52.6 46.3 %slice-start = ((s8[7340032]{0:T(1024)(128)(4,1)}), s8[4194304]{0:T(1024)(128)(4,1)S(1)}, s32[]{:S(2)}) async-start(s8[7340032]{0:T(1024)(128)(4,1)} %bitcast.37), calls=%async_computation | async-start | bytes 8388608
  52.8 51.9 %copy-start.2 = (bf16[4,256,512]{2,1,0:T(8,128)(2,1)}, bf16[4,256,512]{2,1,0:T(8,128)(2,1)S(1)}, u32[]{:S(2)}) copy-start(bf16[4,256,512]{2,1,0:T(8,128)(2,1)S(1)} %pad_maximum_fusion.1.refs_1_.refs_25_) | copy-start | bytes 3145732
  53.0 45.9 %slice-start.1 = ((s8[7340032]{0:T(1024)(128)(4,1)}), s8[3145728]{0:T(1024)(128)(4,1)S(1)}, s32[]{:S(2)}) async-start(s8[7340032]{0:T(1024)(128)(4,1)} %bitcast.37), calls=%async_computation.1 | async-start | bytes 6291456
  53.2 33.8 %collective-permute-start.10 = (bf16[512,512]{1,0:T(8,128)(2,1)S(1)}, bf16[512,512]{1,0:T(8,128)(2,1)S(1)}, u32[]{:S(2)}, u32[]{:S(2)}) collective-permute-start(bf16[512,512]{1,0:T(8,128)(2,1)S(1)} %get-tuple-element.128), channel_id=1, source_target_pairs={{0,2},{1,3},{2,0},{3,1},{4,6},{5,7},{6,4},{7,5},{8,10},{9,11},{10,... | collective-permute-start | bytes 1572872 | tf_op jit(solution)/shard_map/ppermute | solution.py:96
  53.3 44.7 %collective-permute-start.11 = (bf16[512,512]{1,0:T(8,128)(2,1)S(1)}, bf16[512,512]{1,0:T(8,128)(2,1)S(1)}, u32[]{:S(2)}, u32[]{:S(2)}) collective-permute-start(bf16[512,512]{1,0:T(8,128)(2,1)S(1)} %get-tuple-element.129), channel_id=1, source_target_pairs={{0,3},{1,2},{2,1},{3,0},{4,7},{5,6},{6,5},{7,4},{8,11},{9,10},{10,... | collective-permute-start | bytes 1572872 | tf_op jit(solution)/shard_map/ppermute | solution.py:96
  54.8 43.1 %collective-permute-start.9 = (bf16[512,512]{1,0:T(8,128)(2,1)S(1)}, bf16[512,512]{1,0:T(8,128)(2,1)S(1)}, u32[]{:S(2)}, u32[]{:S(2)}) collective-permute-start(bf16[512,512]{1,0:T(8,128)(2,1)S(1)} %get-tuple-element.127), channel_id=1, source_target_pairs={{0,1},{1,0},{2,3},{3,2},{4,5},{5,4},{6,7},{7,6},{8,9},{9,8},{10,11... | collective-permute-start | bytes 1572872 | tf_op jit(solution)/shard_map/ppermute | solution.py:96
  98.2 6.5 %collective-permute-start.14 = (bf16[4,512,512]{2,1,0:T(8,128)(2,1)S(1)}, bf16[4,512,512]{2,1,0:T(8,128)(2,1)S(1)}, u32[]{:S(2)}, u32[]{:S(2)}) collective-permute-start(bf16[4,512,512]{2,1,0:T(8,128)(2,1)S(1)} %pad_maximum_fusion.refs_2_.refs_26_), channel_id=1, source_target_pairs={{0,4},{4,0},{8,12},{12,8},{1,5},{5,1},{9,13},{13,9},{2,6},{6,2},{1... | collective-permute-start | bytes 6291464 | tf_op jit(solution)/shard_map/ppermute | solution.py:88
  98.3 6.4 %collective-permute-start.13 = (bf16[4,256,512]{2,1,0:T(8,128)(2,1)S(1)}, bf16[4,256,512]{2,1,0:T(8,128)(2,1)S(1)}, u32[]{:S(2)}, u32[]{:S(2)}) collective-permute-start(bf16[4,256,512]{2,1,0:T(8,128)(2,1)S(1)} %pad_maximum_fusion.1.refs_1_.refs_25_), channel_id=1, source_target_pairs={{0,4},{4,0},{8,12},{12,8},{1,5},{5,1},{9,13},{13,9},{2,6},{6,2},{1... | collective-permute-start | bytes 3145736 | tf_op jit(solution)/shard_map/ppermute | solution.py:88
  98.8 5.9 %collective-permute-start.12 = (bf16[4,128,512]{2,1,0:T(8,128)(2,1)S(1)}, bf16[4,128,512]{2,1,0:T(8,128)(2,1)S(1)}, u32[]{:S(2)}, u32[]{:S(2)}) collective-permute-start(bf16[4,128,512]{2,1,0:T(8,128)(2,1)S(1)} %pad_maximum_fusion.4.refs_0_.refs_24_), channel_id=1, source_target_pairs={{0,4},{4,0},{8,12},{12,8},{1,5},{5,1},{9,13},{13,9},{2,6},{6,2},{1... | collective-permute-start | bytes 1572872 | tf_op jit(solution)/shard_map/ppermute | solution.py:88
  119.5 31.2 %collective-permute-start.15 = (bf16[1296,512]{1,0:T(8,128)(2,1)S(1)}, bf16[1296,512]{1,0:T(8,128)(2,1)S(1)}, u32[]{:S(2)}, u32[]{:S(2)}) collective-permute-start(bf16[1296,512]{1,0:T(8,128)(2,1)S(1)} %get-tuple-element.133), channel_id=1, source_target_pairs={{0,8},{4,12},{8,0},{12,4},{1,9},{5,13},{9,1},{13,5},{2,10},{6,14},... | collective-permute-start | bytes 3981320 | tf_op jit(solution)/shard_map/ppermute | solution.py:84
  121.0 30.9 %collective-permute-start.16 = (bf16[1296,512]{1,0:T(8,128)(2,1)S(1)}, bf16[1296,512]{1,0:T(8,128)(2,1)S(1)}, u32[]{:S(2)}, u32[]{:S(2)}) collective-permute-start(bf16[1296,512]{1,0:T(8,128)(2,1)S(1)} %get-tuple-element.135), channel_id=1, source_target_pairs={{0,16},{16,0},{1,17},{17,1},{2,18},{18,2},{3,19},{19,3},{4,20},{20... | collective-permute-start | bytes 3981320 | tf_op jit(solution)/shard_map/ppermute | solution.py:92
  121.5 25.0 %collective-permute-start.17 = (bf16[1040,512]{1,0:T(8,128)(2,1)S(1)}, bf16[1040,512]{1,0:T(8,128)(2,1)S(1)}, u32[]{:S(2)}, u32[]{:S(2)}) collective-permute-start(bf16[1040,512]{1,0:T(8,128)(2,1)S(1)} %get-tuple-element.137), channel_id=1, source_target_pairs={{0,1},{1,0},{2,3},{3,2},{4,5},{5,4},{6,7},{7,6},{8,9},{9,8},{10,11... | collective-permute-start | bytes 3194888 | tf_op jit(solution)/shard_map/ppermute | solution.py:96
  155.1 16.1 %collective-permute-start.18 = (bf16[656,512]{1,0:T(8,128)(2,1)S(1)}, bf16[656,512]{1,0:T(8,128)(2,1)S(1)}, u32[]{:S(2)}, u32[]{:S(2)}) collective-permute-start(bf16[656,512]{1,0:T(8,128)(2,1)S(1)} %get-tuple-element.139), channel_id=1, source_target_pairs={{0,16},{16,0},{1,17},{17,1},{2,18},{18,2},{3,19},{19,3},{4,20},{20... | collective-permute-start | bytes 2015240 | tf_op jit(solution)/shard_map/ppermute | solution.py:92
  155.7 15.7 %collective-permute-start.19 = (bf16[656,512]{1,0:T(8,128)(2,1)S(1)}, bf16[656,512]{1,0:T(8,128)(2,1)S(1)}, u32[]{:S(2)}, u32[]{:S(2)}) collective-permute-start(bf16[656,512]{1,0:T(8,128)(2,1)S(1)} %get-tuple-element.141), channel_id=1, source_target_pairs={{0,1},{1,0},{2,3},{3,2},{4,5},{5,4},{6,7},{7,6},{8,9},{9,8},{10,11... | collective-permute-start | bytes 2015240 | tf_op jit(solution)/shard_map/ppermute | solution.py:96
  155.7 12.9 %collective-permute-start.20 = (bf16[528,512]{1,0:T(8,128)(2,1)S(1)}, bf16[528,512]{1,0:T(8,128)(2,1)S(1)}, u32[]{:S(2)}, u32[]{:S(2)}) collective-permute-start(bf16[528,512]{1,0:T(8,128)(2,1)S(1)} %get-tuple-element.143), channel_id=1, source_target_pairs={{0,8},{4,12},{8,0},{12,4},{1,9},{5,13},{9,1},{13,5},{2,10},{6,14},... | collective-permute-start | bytes 1622024 | tf_op jit(solution)/shard_map/ppermute | solution.py:84
  172.1 7.9 %collective-permute-start.21 = (bf16[336,512]{1,0:T(8,128)(2,1)S(1)}, bf16[336,512]{1,0:T(8,128)(2,1)S(1)}, u32[]{:S(2)}, u32[]{:S(2)}) collective-permute-start(bf16[336,512]{1,0:T(8,128)(2,1)S(1)} %get-tuple-element.145), channel_id=1, source_target_pairs={{0,1},{1,0},{2,3},{3,2},{4,5},{5,4},{6,7},{7,6},{8,9},{9,8},{10,11... | collective-permute-start | bytes 1032200 | tf_op jit(solution)/shard_map/ppermute | solution.py:96
  172.5 7.8 %collective-permute-start.22 = (bf16[336,512]{1,0:T(8,128)(2,1)S(1)}, bf16[336,512]{1,0:T(8,128)(2,1)S(1)}, u32[]{:S(2)}, u32[]{:S(2)}) collective-permute-start(bf16[336,512]{1,0:T(8,128)(2,1)S(1)} %get-tuple-element.147), channel_id=1, source_target_pairs={{0,8},{4,12},{8,0},{12,4},{1,9},{5,13},{9,1},{13,5},{2,10},{6,14},... | collective-permute-start | bytes 1032200 | tf_op jit(solution)/shard_map/ppermute | solution.py:84
  173.1 6.5 %collective-permute-start.23 = (bf16[272,512]{1,0:T(8,128)(2,1)S(1)}, bf16[272,512]{1,0:T(8,128)(2,1)S(1)}, u32[]{:S(2)}, u32[]{:S(2)}) collective-permute-start(bf16[272,512]{1,0:T(8,128)(2,1)S(1)} %get-tuple-element.149), channel_id=1, source_target_pairs={{0,16},{16,0},{1,17},{17,1},{2,18},{18,2},{3,19},{19,3},{4,20},{20... | collective-permute-start | bytes 835592 | tf_op jit(solution)/shard_map/ppermute | solution.py:92
  180.5 6.4 %collective-permute-start.26 = (bf16[1,4,64,512]{3,2,1,0:T(8,128)(2,1)S(1)}, bf16[1,4,64,512]{3,2,1,0:T(8,128)(2,1)S(1)}, u32[]{:S(2)}, u32[]{:S(2)}) collective-permute-start(bf16[1,4,64,512]{3,2,1,0:T(8,128)(2,1)S(1)} %bitcast.35), channel_id=1, source_target_pairs={{0,1},{1,0},{2,3},{3,2},{4,5},{5,4},{6,7},{7,6},{8,9},{9,8},{10,11... | collective-permute-start | bytes 786440 | tf_op jit(solution)/shard_map/ppermute | solution.py:96
  182.1 7.1 %collective-permute-start.25 = (bf16[1,5,64,512]{3,2,1,0:T(8,128)(2,1)S(1)}, bf16[1,5,64,512]{3,2,1,0:T(8,128)(2,1)S(1)}, u32[]{:S(2)}, u32[]{:S(2)}) collective-permute-start(bf16[1,5,64,512]{3,2,1,0:T(8,128)(2,1)S(1)} %bitcast.33), channel_id=1, source_target_pairs={{0,16},{16,0},{1,17},{17,1},{2,18},{18,2},{3,19},{19,3},{4,20},{20... | collective-permute-start | bytes 983048 | tf_op jit(solution)/shard_map/ppermute | solution.py:92
  183.6 9.1 %collective-permute-start.24 = (bf16[1,5,64,512]{3,2,1,0:T(8,128)(2,1)S(1)}, bf16[1,5,64,512]{3,2,1,0:T(8,128)(2,1)S(1)}, u32[]{:S(2)}, u32[]{:S(2)}) collective-permute-start(bf16[1,5,64,512]{3,2,1,0:T(8,128)(2,1)S(1)} %bitcast.31), channel_id=1, source_target_pairs={{0,8},{4,12},{8,0},{12,4},{1,9},{5,13},{9,1},{13,5},{2,10},{6,14},... | collective-permute-start | bytes 983048 | tf_op jit(solution)/shard_map/ppermute | solution.py:84
  187.0 57.2 %copy-start.6 = (bf16[2,4,64,512]{3,2,1,0:T(8,128)(2,1)}, bf16[2,4,64,512]{3,2,1,0:T(8,128)(2,1)S(1)}, u32[]{:S(2)}) copy-start(bf16[2,4,64,512]{3,2,1,0:T(8,128)(2,1)S(1)} %pad_maximum_fusion.5.refs_2_) | copy-start | bytes 1572868
  189.2 55.0 %copy-start.4 = (bf16[2,5,64,512]{3,2,1,0:T(8,128)(2,1)}, bf16[2,5,64,512]{3,2,1,0:T(8,128)(2,1)S(1)}, u32[]{:S(2)}) copy-start(bf16[2,5,64,512]{3,2,1,0:T(8,128)(2,1)S(1)} %pad_maximum_fusion.3.refs_1_) | copy-start | bytes 1966084
  192.7 51.5 %copy-start.5 = (bf16[2,5,64,512]{3,2,1,0:T(8,128)(2,1)}, bf16[2,5,64,512]{3,2,1,0:T(8,128)(2,1)S(1)}, u32[]{:S(2)}) copy-start(bf16[2,5,64,512]{3,2,1,0:T(8,128)(2,1)S(1)} %pad_maximum_fusion.2.refs_0_) | copy-start | bytes 1966084
  192.7 9.2 %collective-permute-start.29 = (bf16[2,4,64,512]{3,2,1,0:T(8,128)(2,1)S(1)}, bf16[2,4,64,512]{3,2,1,0:T(8,128)(2,1)S(1)}, u32[]{:S(2)}, u32[]{:S(2)}) collective-permute-start(bf16[2,4,64,512]{3,2,1,0:T(8,128)(2,1)S(1)} %pad_maximum_fusion.5.refs_2_), channel_id=1, source_target_pairs={{0,8},{4,12},{8,0},{12,4},{1,9},{5,13},{9,1},{13,5},{2,10},{6,14},... | collective-permute-start | bytes 1572872 | tf_op jit(solution)/shard_map/ppermute | solution.py:84
  194.6 10.6 %collective-permute-start.27 = (bf16[2,5,64,512]{3,2,1,0:T(8,128)(2,1)S(1)}, bf16[2,5,64,512]{3,2,1,0:T(8,128)(2,1)S(1)}, u32[]{:S(2)}, u32[]{:S(2)}) collective-permute-start(bf16[2,5,64,512]{3,2,1,0:T(8,128)(2,1)S(1)} %pad_maximum_fusion.2.refs_0_), channel_id=1, source_target_pairs={{0,16},{16,0},{1,17},{17,1},{2,18},{18,2},{3,19},{19,3},{4,20},{20... | collective-permute-start | bytes 1966088 | tf_op jit(solution)/shard_map/ppermute | solution.py:92
  194.7 10.6 %collective-permute-start.28 = (bf16[2,5,64,512]{3,2,1,0:T(8,128)(2,1)S(1)}, bf16[2,5,64,512]{3,2,1,0:T(8,128)(2,1)S(1)}, u32[]{:S(2)}, u32[]{:S(2)}) collective-permute-start(bf16[2,5,64,512]{3,2,1,0:T(8,128)(2,1)S(1)} %pad_maximum_fusion.3.refs_1_), channel_id=1, source_target_pairs={{0,1},{1,0},{2,3},{3,2},{4,5},{5,4},{6,7},{7,6},{8,9},{9,8},{10,11... | collective-permute-start | bytes 1966088 | tf_op jit(solution)/shard_map/ppermute | solution.py:96
  194.7 10.6 %collective-permute-start.30 = (bf16[2,5,64,512]{3,2,1,0:T(8,128)(2,1)S(1)}, bf16[2,5,64,512]{3,2,1,0:T(8,128)(2,1)S(1)}, u32[]{:S(2)}, u32[]{:S(2)}) collective-permute-start(bf16[2,5,64,512]{3,2,1,0:T(8,128)(2,1)S(1)} %pad_maximum_fusion.2.refs_0_), channel_id=1, source_target_pairs={{0,4},{4,0},{8,12},{12,8},{1,5},{5,1},{9,13},{13,9},{2,6},{6,2},{1... | collective-permute-start | bytes 1966088 | tf_op jit(solution)/shard_map/ppermute | solution.py:88
  194.7 10.6 %collective-permute-start.31 = (bf16[2,5,64,512]{3,2,1,0:T(8,128)(2,1)S(1)}, bf16[2,5,64,512]{3,2,1,0:T(8,128)(2,1)S(1)}, u32[]{:S(2)}, u32[]{:S(2)}) collective-permute-start(bf16[2,5,64,512]{3,2,1,0:T(8,128)(2,1)S(1)} %pad_maximum_fusion.3.refs_1_), channel_id=1, source_target_pairs={{0,4},{4,0},{8,12},{12,8},{1,5},{5,1},{9,13},{13,9},{2,6},{6,2},{1... | collective-permute-start | bytes 1966088 | tf_op jit(solution)/shard_map/ppermute | solution.py:88
  202.0 1.9 collective-permute-start.32
  205.2 39.1 %copy-start.7 = (bf16[2,5,64,512]{3,2,1,0:T(8,128)(2,1)}, bf16[2,5,64,512]{3,2,1,0:T(8,128)(2,1)S(1)}, u32[]{:S(2)}) copy-start(bf16[2,5,64,512]{3,2,1,0:T(8,128)(2,1)S(1)} %collective-permute-done.27.refs_6_) | copy-start | bytes 1966084
  205.3 13.3 %collective-permute-start.35 = (bf16[2,4,64,512]{3,2,1,0:T(8,128)(2,1)S(1)}, bf16[2,4,64,512]{3,2,1,0:T(8,128)(2,1)S(1)}, u32[]{:S(2)}, u32[]{:S(2)}) collective-permute-start(bf16[2,4,64,512]{3,2,1,0:T(8,128)(2,1)S(1)} %pad_maximum_fusion.5.refs_2_), channel_id=1, source_target_pairs={{0,16},{16,0},{1,17},{17,1},{2,18},{18,2},{3,19},{19,3},{4,20},{20... | collective-permute-start | bytes 1572872 | tf_op jit(solution)/shard_map/ppermute | solution.py:92
  207.3 14.4 %collective-permute-start.33 = (bf16[2,5,64,512]{3,2,1,0:T(8,128)(2,1)S(1)}, bf16[2,5,64,512]{3,2,1,0:T(8,128)(2,1)S(1)}, u32[]{:S(2)}, u32[]{:S(2)}) collective-permute-start(bf16[2,5,64,512]{3,2,1,0:T(8,128)(2,1)S(1)} %pad_maximum_fusion.2.refs_0_), channel_id=1, source_target_pairs={{0,1},{1,0},{2,3},{3,2},{4,5},{5,4},{6,7},{7,6},{8,9},{9,8},{10,11... | collective-permute-start | bytes 1966088 | tf_op jit(solution)/shard_map/ppermute | solution.py:96
  207.3 14.7 %collective-permute-start.34 = (bf16[2,5,64,512]{3,2,1,0:T(8,128)(2,1)S(1)}, bf16[2,5,64,512]{3,2,1,0:T(8,128)(2,1)S(1)}, u32[]{:S(2)}, u32[]{:S(2)}) collective-permute-start(bf16[2,5,64,512]{3,2,1,0:T(8,128)(2,1)S(1)} %pad_maximum_fusion.3.refs_1_), channel_id=1, source_target_pairs={{0,8},{4,12},{8,0},{12,4},{1,9},{5,13},{9,1},{13,5},{2,10},{6,14},... | collective-permute-start | bytes 1966088 | tf_op jit(solution)/shard_map/ppermute | solution.py:84
  207.8 14.2 %collective-permute-start.36 = (bf16[2,5,64,512]{3,2,1,0:T(8,128)(2,1)S(1)}, bf16[2,5,64,512]{3,2,1,0:T(8,128)(2,1)S(1)}, u32[]{:S(2)}, u32[]{:S(2)}) collective-permute-start(bf16[2,5,64,512]{3,2,1,0:T(8,128)(2,1)S(1)} %collective-permute-done.27.refs_6_), channel_id=1, source_target_pairs={{0,4},{4,0},{8,12},{12,8},{1,5},{5,1},{9,13},{13,9},{2,6},{6,2},{1... | collective-permute-start | bytes 1966088 | tf_op jit(solution)/shard_map/ppermute | solution.py:88
  207.8 14.2 %collective-permute-start.37 = (bf16[2,5,64,512]{3,2,1,0:T(8,128)(2,1)S(1)}, bf16[2,5,64,512]{3,2,1,0:T(8,128)(2,1)S(1)}, u32[]{:S(2)}, u32[]{:S(2)}) collective-permute-start(bf16[2,5,64,512]{3,2,1,0:T(8,128)(2,1)S(1)} %collective-permute-done.28.refs_7_), channel_id=1, source_target_pairs={{0,4},{4,0},{8,12},{12,8},{1,5},{5,1},{9,13},{13,9},{2,6},{6,2},{1... | collective-permute-start | bytes 1966088 | tf_op jit(solution)/shard_map/ppermute | solution.py:88
  218.7 1.9 collective-permute-start.38
  222.0 12.8 %collective-permute-start.41 = (bf16[2,4,64,512]{3,2,1,0:T(8,128)(2,1)S(1)}, bf16[2,4,64,512]{3,2,1,0:T(8,128)(2,1)}, u32[]{:S(2)}, u32[]{:S(2)}) collective-permute-start(bf16[2,4,64,512]{3,2,1,0:T(8,128)(2,1)S(1)} %collective-permute-done.29.refs_8_), channel_id=1, source_target_pairs={{0,16},{16,0},{1,17},{17,1},{2,18},{18,2},{3,19},{19,3},{4,20},{20... | collective-permute-start | bytes 1572872 | tf_op jit(solution)/shard_map/ppermute | solution.py:92
  223.5 14.8 %collective-permute-start.39 = (bf16[2,5,64,512]{3,2,1,0:T(8,128)(2,1)S(1)}, bf16[2,5,64,512]{3,2,1,0:T(8,128)(2,1)}, u32[]{:S(2)}, u32[]{:S(2)}) collective-permute-start(bf16[2,5,64,512]{3,2,1,0:T(8,128)(2,1)S(1)} %collective-permute-done.27.refs_6_), channel_id=1, source_target_pairs={{0,1},{1,0},{2,3},{3,2},{4,5},{5,4},{6,7},{7,6},{8,9},{9,8},{10,11... | collective-permute-start | bytes 1966088 | tf_op jit(solution)/shard_map/ppermute | solution.py:96
  225.1 14.8 %collective-permute-start.40 = (bf16[2,5,64,512]{3,2,1,0:T(8,128)(2,1)S(1)}, bf16[2,5,64,512]{3,2,1,0:T(8,128)(2,1)}, u32[]{:S(2)}, u32[]{:S(2)}) collective-permute-start(bf16[2,5,64,512]{3,2,1,0:T(8,128)(2,1)S(1)} %collective-permute-done.28.refs_7_), channel_id=1, source_target_pairs={{0,8},{4,12},{8,0},{12,4},{1,9},{5,13},{9,1},{13,5},{2,10},{6,14},... | collective-permute-start | bytes 1966088 | tf_op jit(solution)/shard_map/ppermute | solution.py:84
  226.8 13.1 %collective-permute-start.42 = (bf16[2,5,64,512]{3,2,1,0:T(8,128)(2,1)S(1)}, bf16[2,5,64,512]{3,2,1,0:T(8,128)(2,1)S(1)}, u32[]{:S(2)}, u32[]{:S(2)}) collective-permute-start(bf16[2,5,64,512]{3,2,1,0:T(8,128)(2,1)S(1)} %collective-permute-done.33.refs_12_), channel_id=1, source_target_pairs={{0,4},{4,0},{8,12},{12,8},{1,5},{5,1},{9,13},{13,9},{2,6},{6,2},{1... | collective-permute-start | bytes 1966088 | tf_op jit(solution)/shard_map/ppermute | solution.py:88
  226.8 13.1 %collective-permute-start.43 = (bf16[2,5,64,512]{3,2,1,0:T(8,128)(2,1)S(1)}, bf16[2,5,64,512]{3,2,1,0:T(8,128)(2,1)S(1)}, u32[]{:S(2)}, u32[]{:S(2)}) collective-permute-start(bf16[2,5,64,512]{3,2,1,0:T(8,128)(2,1)S(1)} %collective-permute-done.34.refs_13_), channel_id=1, source_target_pairs={{0,4},{4,0},{8,12},{12,8},{1,5},{5,1},{9,13},{13,9},{2,6},{6,2},{1... | collective-permute-start | bytes 1966088 | tf_op jit(solution)/shard_map/ppermute | solution.py:88
  234.8 1.9 collective-permute-start.44
  240.0 4.2 %collective-permute-start.45 = (bf16[2,5,64,512]{3,2,1,0:T(8,128)(2,1)}, bf16[2,5,64,512]{3,2,1,0:T(8,128)(2,1)}, u32[]{:S(2)}, u32[]{:S(2)}) collective-permute-start(bf16[2,5,64,512]{3,2,1,0:T(8,128)(2,1)} %collective-permute-done.39.refs_18_), channel_id=1, source_target_pairs={{0,4},{4,0},{8,12},{12,8},{1,5},{5,1},{9,13},{13,9},{2,6},{6,2},{1... | collective-permute-start | bytes 1966088 | tf_op jit(solution)/shard_map/ppermute | solution.py:88
  240.1 4.1 %collective-permute-start.46 = (bf16[2,5,64,512]{3,2,1,0:T(8,128)(2,1)}, bf16[2,5,64,512]{3,2,1,0:T(8,128)(2,1)}, u32[]{:S(2)}, u32[]{:S(2)}) collective-permute-start(bf16[2,5,64,512]{3,2,1,0:T(8,128)(2,1)} %collective-permute-done.40.refs_19_), channel_id=1, source_target_pairs={{0,4},{4,0},{8,12},{12,8},{1,5},{5,1},{9,13},{13,9},{2,6},{6,2},{1... | collective-permute-start | bytes 1966088 | tf_op jit(solution)/shard_map/ppermute | solution.py:88
  241.0 3.2 collective-permute-start.47
  267.0 33.8 %collective-permute-start.48 = (bf16[7,128,256]{2,1,0:T(8,128)(2,1)}, bf16[7,128,256]{2,1,0:T(8,128)(2,1)S(1)}, u32[]{:S(2)}, u32[]{:S(2)}) collective-permute-start(bf16[7,128,256]{2,1,0:T(8,128)(2,1)} %get-tuple-element.207), channel_id=1, source_target_pairs={{0,0},{1,1},{2,16},{3,17},{16,2},{17,3},{18,18},{19,19},{4,4},{5,5... | collective-permute-start | bytes 1376264 | tf_op jit(solution)/shard_map/ppermute | solution.py:109
  270.1 42.0 %collective-permute-start.49 = (bf16[7,128,256]{2,1,0:T(8,128)(2,1)}, bf16[7,128,256]{2,1,0:T(8,128)(2,1)S(1)}, u32[]{:S(2)}, u32[]{:S(2)}) collective-permute-start(bf16[7,128,256]{2,1,0:T(8,128)(2,1)} %get-tuple-element.208), channel_id=1, source_target_pairs={{0,1},{1,0},{2,17},{3,16},{16,3},{17,2},{18,19},{19,18},{4,5},{5,4... | collective-permute-start | bytes 1376264 | tf_op jit(solution)/shard_map/ppermute | solution.py:109
  272.0 40.1 %collective-permute-start.50 = (bf16[7,128,256]{2,1,0:T(8,128)(2,1)}, bf16[7,128,256]{2,1,0:T(8,128)(2,1)S(1)}, u32[]{:S(2)}, u32[]{:S(2)}) collective-permute-start(bf16[7,128,256]{2,1,0:T(8,128)(2,1)} %get-tuple-element.209), channel_id=1, source_target_pairs={{0,2},{1,3},{2,18},{3,19},{16,0},{17,1},{18,16},{19,17},{4,6},{5,7... | collective-permute-start | bytes 1376264 | tf_op jit(solution)/shard_map/ppermute | solution.py:109
  272.0 43.5 %collective-permute-start.51 = (bf16[7,128,256]{2,1,0:T(8,128)(2,1)}, bf16[7,128,256]{2,1,0:T(8,128)(2,1)S(1)}, u32[]{:S(2)}, u32[]{:S(2)}) collective-permute-start(bf16[7,128,256]{2,1,0:T(8,128)(2,1)} %get-tuple-element.210), channel_id=1, source_target_pairs={{0,3},{1,2},{2,19},{3,18},{16,1},{17,0},{18,17},{19,16},{4,7},{5,6... | collective-permute-start | bytes 1376264 | tf_op jit(solution)/shard_map/ppermute | solution.py:109
  315.5 32.4 %collective-permute-start.52 = (bf16[7,128,256]{2,1,0:T(8,128)(2,1)}, bf16[7,128,256]{2,1,0:T(8,128)(2,1)S(1)}, u32[]{:S(2)}, u32[]{:S(2)}) collective-permute-start(bf16[7,128,256]{2,1,0:T(8,128)(2,1)} %get-tuple-element.215), channel_id=1, source_target_pairs={{0,0},{1,1},{2,16},{3,17},{16,2},{17,3},{18,18},{19,19},{4,4},{5,5... | collective-permute-start | bytes 1376264 | tf_op jit(solution)/shard_map/ppermute | solution.py:109
  317.4 40.0 %collective-permute-start.53 = (bf16[7,128,256]{2,1,0:T(8,128)(2,1)}, bf16[7,128,256]{2,1,0:T(8,128)(2,1)S(1)}, u32[]{:S(2)}, u32[]{:S(2)}) collective-permute-start(bf16[7,128,256]{2,1,0:T(8,128)(2,1)} %get-tuple-element.216), channel_id=1, source_target_pairs={{0,1},{1,0},{2,17},{3,16},{16,3},{17,2},{18,19},{19,18},{4,5},{5,4... | collective-permute-start | bytes 1376264 | tf_op jit(solution)/shard_map/ppermute | solution.py:109
  318.4 41.3 %collective-permute-start.54 = (bf16[7,128,256]{2,1,0:T(8,128)(2,1)}, bf16[7,128,256]{2,1,0:T(8,128)(2,1)S(1)}, u32[]{:S(2)}, u32[]{:S(2)}) collective-permute-start(bf16[7,128,256]{2,1,0:T(8,128)(2,1)} %get-tuple-element.217), channel_id=1, source_target_pairs={{0,2},{1,3},{2,18},{3,19},{16,0},{17,1},{18,16},{19,17},{4,6},{5,7... | collective-permute-start | bytes 1376264 | tf_op jit(solution)/shard_map/ppermute | solution.py:109
  318.4 44.1 %collective-permute-start.55 = (bf16[7,128,256]{2,1,0:T(8,128)(2,1)}, bf16[7,128,256]{2,1,0:T(8,128)(2,1)S(1)}, u32[]{:S(2)}, u32[]{:S(2)}) collective-permute-start(bf16[7,128,256]{2,1,0:T(8,128)(2,1)} %get-tuple-element.218), channel_id=1, source_target_pairs={{0,3},{1,2},{2,19},{3,18},{16,1},{17,0},{18,17},{19,16},{4,7},{5,6... | collective-permute-start | bytes 1376264 | tf_op jit(solution)/shard_map/ppermute | solution.py:109
  (16 other events, 261.8 us)

commit v4 on v3

--- a/solution.py
+++ b/solution.py
@@ -31,7 +31,9 @@
 SLAB = ORDER // 4
 BAND = SLAB // BLOCKS
 GROUP = COLS // 16
-PIECES = (1, 2, 4)
+HOPS = (1, 2, 4)
+LAST = (1, 2, 1)
+PIECES = (3, 4)
 HALVES = 2
 WIDE = GROUP // HALVES
 GRAM_VMEM = 28 << 20
@@ -99,6 +101,33 @@
 MOVES = {4: over_x, 2: over_y, 1: over_z}
 ORDERS = ((4, 2, 1), (2, 1, 4), (1, 4, 2))
 
+EARLY = (((0, 0), (1, 0), (2, 0)), ((0, 1), (1, 1), (0, 2)))
+LATE = [
+    (i, d) for d in range(DIAGS) for i in range(BLOCKS) if (i, d) not in EARLY[0] + EARLY[1]
+]
+LATE = (LATE[: MINE - 3], LATE[MINE - 3 :])
+EARLY_GROUPS = tuple(
+    ([core[lo:hi] for core in EARLY], order)
+    for (lo, hi), order in (((0, 3), (4, 2, 1)),)
+)
+LATE_GROUPS = tuple(
+    ([core[lo:hi] for core in LATE], order)
+    for (lo, hi), order in zip(((0, 4), (4, 8), (8, 11)), ORDERS)
+)
+SPOT = {
+    block: core * MINE + THIRDS[third][0] + n
+    for core in range(2)
+    for third in range(3)
+    for n, block in enumerate([EARLY[core][third]] + LATE_GROUPS[third][0][core])
+}
+
+
+def lookup(index, values):
+    got = values[0]
+    for n, value in enumerate(values[1:], 1):
+        got = jnp.where(index == n, value, got)
+    return got
+
 
 def home(a, step):
     pairs = []
@@ -124,25 +153,25 @@
     )
 
 
-def kept(third, stage):
-    gone = sum(ORDERS[third][: stage + 1])
+def kept(order, stage):
+    gone = sum(order[: stage + 1])
     return [by for by in range(PLACES) if not by & gone]
 
 
-def sent(third, stage):
-    return [by | ORDERS[third][stage] for by in kept(third, stage)]
-
-
-def rows_sent(third, stage):
-    lo, hi = THIRDS[third]
-    return (hi - lo) * len(sent(third, stage)) * UNIT
-
-
-def exchange_shapes(third, stage):
-    lo, hi = THIRDS[third]
+def sent(order, stage):
+    return [by | order[stage] for by in kept(order, stage)]
+
+
+def rows_sent(group, stage):
+    blocks, order = group
+    return len(blocks[0]) * len(sent(order, stage)) * UNIT
+
+
+def exchange_shapes(group, stage):
+    blocks, order = group
     return [
-        jax.ShapeDtypeStruct((hi - lo, len(kept(third, stage)), UNIT, BLOCK), F32),
-        jax.ShapeDtypeStruct((rows_sent(third, stage) + TAIL, BLOCK), BF16),
+        jax.ShapeDtypeStruct((len(blocks[0]), len(kept(order, stage)), UNIT, BLOCK), F32),
+        jax.ShapeDtypeStruct((rows_sent(group, stage) + TAIL, BLOCK), BF16),
     ]
 
 
@@ -152,80 +181,93 @@
         near = part.astype(BF16)
         row = (e * len(parts) + n) * UNIT
         send[pl.ds(row if isinstance(row, int) else pl.multiple_of(row, UNIT), UNIT), :] = near
-        rest = jnp.where(on_diagonal(unit), part - near.astype(F32), 0.0)
-        left += jnp.sum(rest, axis=0, keepdims=True)
-    tail[pl.ds(e, 1), :] = left * flag
-
-
-def gram_kernel(*refs):
-    count = 2 * len(PIECES)
-    inputs, outs, refs = refs[:count], refs[count : count + 6], refs[count + 6 :]
-    keeps, sends, tails = refs[0:6:2], refs[1:6:2], refs[6:9]
-    panel, arrived, gone = refs[9:]
+        if flag is not None:
+            rest = jnp.where(on_diagonal(unit), part - near.astype(F32), 0.0)
+            left += jnp.sum(rest, axis=0, keepdims=True)
+    if flag is not None:
+        tail[pl.ds(e, 1), :] = left * flag
+
+
+def gram_kernel(groups, pieces, *refs):
+    where = place_of_block()[: sum(PIECES[:pieces])]
+    inputs, refs = refs[: 2 * pieces], refs[2 * pieces :]
+    count = 2 * len(groups)
+    outs, refs = refs[:count], refs[count:]
+    keeps, sends, refs = refs[0:count:2], refs[1:count:2], refs[count:]
+    tails, (panel, arrived, gone) = refs[: len(groups)], refs[len(groups) :]
     y, x, core, high, low = place()
     for source in range(2):
-        for i, (p, b) in enumerate(place_of_block()):
+        for i, (p, b) in enumerate(where):
             for step in range(4):
                 spot = pl.multiple_of(slab_of(high, low, step) * BAND, BAND)
                 pltpu.make_async_copy(
-                    inputs[source * len(PIECES) + p].at[step, pl.ds(b * BAND, BAND), :],
+                    inputs[source * pieces + p].at[step, pl.ds(b * BAND, BAND), :],
                     panel.at[i, pl.ds(spot, BAND), pl.ds(source * GROUP, GROUP)],
                     arrived,
                 ).start()
     for tail in tails:
         tail[...] = jnp.zeros_like(tail)
     pltpu.make_async_copy(panel, panel, arrived).wait()
-    for third, (lo, hi) in enumerate(THIRDS):
-        keep, send, tail = keeps[third], sends[third], tails[third]
-        size = len(sent(third, 0)) * UNIT
+    for g, group in enumerate(groups):
+        blocks, order = group
+        keep, send, tail = keeps[g], sends[g], tails[g]
+        size = len(sent(order, 0)) * UNIT
+        diagonal = blocks[0][0][1] == 0
 
         def block(e, carry):
-            second = (e + lo >= BLOCKS).astype(jnp.int32)
-            i = e + lo - BLOCKS * second
-            j = lax.rem(i + 2 * core + second, BLOCKS)
-            flag = jnp.logical_and(core == 0, second == 0).astype(F32)
+            at = [
+                jnp.where(core == 0, lookup(e, [b[n] for b in blocks[0]]), lookup(e, [b[n] for b in blocks[1]]))
+                for n in range(2)
+            ]
+            i, j = at[0], lax.rem(at[0] + at[1], BLOCKS)
             rows = [
                 panel[i, pl.ds(pl.multiple_of(place_of(x, y, low, by) * UNIT, UNIT), UNIT), :]
                 for by in range(PLACES)
             ]
             got = dot(jnp.concatenate(rows), panel[j], ((1,), (1,)))
-            for n, by in enumerate(kept(third, 0)):
+            for n, by in enumerate(kept(order, 0)):
                 keep[e, n] = got[by * UNIT : (by + 1) * UNIT]
-            parts = [got[by * UNIT : (by + 1) * UNIT] for by in sent(third, 0)]
-            units = [place_of(x, y, low, by) for by in sent(third, 0)]
-            write_sent(send, tail, e, parts, units, flag)
-            pltpu.make_async_copy(keep.at[e], outs[2 * third].at[e], gone.at[2 * third]).start()
+            parts = [got[by * UNIT : (by + 1) * UNIT] for by in sent(order, 0)]
+            units = [place_of(x, y, low, by) for by in sent(order, 0)]
+            write_sent(send, tail, e, parts, units, (core == 0).astype(F32) if diagonal else None)
+            pltpu.make_async_copy(keep.at[e], outs[2 * g].at[e], gone.at[2 * g]).start()
             rows = pl.ds(pl.multiple_of(e * size, size), size)
             pltpu.make_async_copy(
-                send.at[rows, :], outs[2 * third + 1].at[rows, :], gone.at[2 * third + 1]
+                send.at[rows, :], outs[2 * g + 1].at[rows, :], gone.at[2 * g + 1]
             ).start()
             return carry
 
-        lax.fori_loop(0, hi - lo, block, 0)
-        rows = pl.ds(rows_sent(third, 0), TAIL)
+        lax.fori_loop(0, len(blocks[0]), block, 0)
+        rows = pl.ds(rows_sent(group, 0), TAIL)
         send[rows, :] = tail[...].astype(BF16)
         pltpu.make_async_copy(
-            send.at[rows, :], outs[2 * third + 1].at[rows, :], gone.at[2 * third + 1]
+            send.at[rows, :], outs[2 * g + 1].at[rows, :], gone.at[2 * g + 1]
         ).start()
-    for third in range(3):
-        for n, ref in ((2 * third, keeps[third]), (2 * third + 1, sends[third])):
+    for g in range(len(groups)):
+        for n, ref in ((2 * g, keeps[g]), (2 * g + 1, sends[g])):
             pltpu.make_async_copy(ref, outs[n], gone.at[n]).wait()
 
 
-def add_kernel(stage, *refs):
+def add_kernel(groups, stage, before, *refs):
     last = stage == 2
-    keeps, gots = refs[0:6:2], refs[1:6:2]
-    outs = refs[6:]
+    count = 2 * len(groups)
+    keeps, gots, refs = refs[0:count:2], refs[1:count:2], refs[count:]
+    early, outs = refs[:before], refs[before:]
     y, x, core, high, low = place()
-    for third, (lo, hi) in enumerate(THIRDS):
-        keep, got = keeps[third], gots[third]
-        held = kept(third, stage)
-        left = got[pl.ds(rows_sent(third, stage), TAIL), :].astype(F32)
+    for g, group in enumerate(groups):
+        blocks, order = group
+        keep, got = keeps[g], gots[g]
+        held = kept(order, stage)
+        diagonal = blocks[0][0][1] == 0
+        left = got[pl.ds(rows_sent(group, stage), TAIL), :].astype(F32)
+        skip = 0
+        if last and before:
+            skip = 1
+            outs[g][0] = early[0][g]
         if not last:
-            nxt, send, tail = outs[2 * third], outs[2 * third + 1], outs[6 + third]
+            nxt, send, tail = outs[2 * g], outs[2 * g + 1], outs[count + g]
             tail[...] = jnp.zeros_like(tail)
-        for e in range(hi - lo):
-            diagonal = e + lo < BLOCKS
+        for e in range(len(blocks[0])):
             sums = {}
             for n, by in enumerate(held):
                 row = (e * len(held) + n) * UNIT
@@ -235,72 +277,73 @@
                     here += jnp.where(on_diagonal(unit), left[e : e + 1, :], 0.0)
                 sums[by] = here
             if last:
-                outs[third][e] = sums[0].astype(BF16)
+                outs[g][skip + e] = sums[0].astype(BF16)
                 continue
-            for n, by in enumerate(kept(third, stage + 1)):
+            for n, by in enumerate(kept(order, stage + 1)):
                 nxt[e, n] = sums[by]
-            going = sent(third, stage + 1)
-            if diagonal:
-                flag = (core == 0).astype(F32)
-                units = [place_of(x, y, low, by) for by in going]
-                write_sent(send, tail, e, [sums[by] for by in going], units, flag)
-            else:
-                for n, by in enumerate(going):
-                    row = (e * len(going) + n) * UNIT
-                    send[row : row + UNIT, :] = sums[by].astype(BF16)
+            going = sent(order, stage + 1)
+            units = [place_of(x, y, low, by) for by in going]
+            flag = (core == 0).astype(F32) if diagonal else None
+            write_sent(send, tail, e, [sums[by] for by in going], units, flag)
         if not last:
-            send[pl.ds(rows_sent(third, stage + 1), TAIL), :] = tail[...].astype(BF16)
-
-
-def gram_call(inputs):
-    shapes = [shape for third in range(3) for shape in exchange_shapes(third, 0)]
+            send[pl.ds(rows_sent(group, stage + 1), TAIL), :] = tail[...].astype(BF16)
+
+
+def gram_call(groups, own, beside):
+    inputs = own + beside
+    rows = sum(PIECES[: len(own)])
+    shapes = [shape for group in groups for shape in exchange_shapes(group, 0)]
     return pl.pallas_call(
-        gram_kernel,
+        functools.partial(gram_kernel, groups, len(own)),
         out_shape=shapes,
         in_specs=[pl.BlockSpec(memory_space=pl.ANY)] * len(inputs),
-        out_specs=[pl.BlockSpec(memory_space=pl.ANY)] * 6,
+        out_specs=[pl.BlockSpec(memory_space=pl.ANY)] * len(shapes),
         scratch_shapes=[pltpu.VMEM(shape.shape, shape.dtype) for shape in shapes]
-        + [pltpu.VMEM((TAIL, BLOCK), F32)] * 3
+        + [pltpu.VMEM((TAIL, BLOCK), F32)] * len(groups)
         + [
-            pltpu.VMEM((BLOCKS, BLOCK, 2 * GROUP), BF16),
+            pltpu.VMEM((rows, BLOCK, 2 * GROUP), BF16),
             pltpu.SemaphoreType.DMA,
-            pltpu.SemaphoreType.DMA((6,)),
+            pltpu.SemaphoreType.DMA((len(shapes),)),
         ],
         compiler_params=pltpu.CompilerParams(vmem_limit_bytes=GRAM_VMEM),
         cost_estimate=pl.CostEstimate(
-            flops=2 * MINE * BLOCK * BLOCK * 2 * GROUP, bytes_accessed=24 << 20, transcendentals=0
+            flops=sum(len(group[0][0]) for group in groups) * BLOCK * BLOCK,
+            bytes_accessed=rows << 16,
+            transcendentals=0,
         ),
         name="gram",
     )(*inputs)
 
 
-def add_call(stage, inputs):
+def add_call(groups, stage, inputs, early):
     if stage < 2:
-        shapes = [shape for third in range(3) for shape in exchange_shapes(third, stage + 1)]
-        scratch = [pltpu.VMEM((TAIL, BLOCK), F32)] * 3
+        shapes = [shape for group in groups for shape in exchange_shapes(group, stage + 1)]
+        scratch = [pltpu.VMEM((TAIL, BLOCK), F32)] * len(groups)
+        early = []
     else:
-        shapes = [jax.ShapeDtypeStruct((hi - lo, UNIT, BLOCK), BF16) for lo, hi in THIRDS]
+        extra = 1 if early else 0
+        shapes = [
+            jax.ShapeDtypeStruct((len(blocks[0]) + extra, UNIT, BLOCK), BF16) for blocks, _ in groups
+        ]
         scratch = []
+    inputs = inputs + early
     return pl.pallas_call(
-        functools.partial(add_kernel, stage),
+        functools.partial(add_kernel, groups, stage, len(early)),
         out_shape=shapes,
-        in_specs=[pl.BlockSpec(memory_space=pltpu.VMEM)] * 6,
+        in_specs=[pl.BlockSpec(memory_space=pltpu.VMEM)] * len(inputs),
         out_specs=[pl.BlockSpec(memory_space=pltpu.VMEM)] * len(shapes),
         scratch_shapes=scratch,
         compiler_params=pltpu.CompilerParams(vmem_limit_bytes=40 << 20),
-        cost_estimate=pl.CostEstimate(flops=1 << 22, bytes_accessed=16 << 20, transcendentals=0),
+        cost_estimate=pl.CostEstimate(flops=1 << 16, bytes_accessed=1 << 16, transcendentals=0),
         name="add",
     )(*inputs)
 
 
-def summed(parts):
-    for stage in range(3):
-        inputs = []
-        for third in range(3):
-            keep, send = parts[2 * third], parts[2 * third + 1]
-            inputs += [keep, MOVES[ORDERS[third][stage]](send)]
-        parts = add_call(stage, inputs)
-    return parts
+def summed(groups, parts, stage, early=()):
+    inputs = []
+    for g, (_, order) in enumerate(groups):
+        inputs += [parts[2 * g], MOVES[order[stage]](parts[2 * g + 1])]
+    return add_call(groups, stage, inputs, list(early))
 
 
 def gathered(mine):
@@ -372,7 +415,9 @@
         for n, by in enumerate(bys):
             pltpu.make_async_copy(
                 piece.at[n],
-                gram.at[flip(core, other), pl.ds(lo, hi - lo), place_of(x, y, low, by)],
+                gram.at[
+                    pl.ds(flip(core, other) * MINE + lo, hi - lo), place_of(x, y, low, by)
+                ],
                 here,
             ).start()
     pltpu.make_async_copy(panel, panel, there).wait()
@@ -382,7 +427,7 @@
         return pl.ds(pl.multiple_of(i * BLOCK, BLOCK), BLOCK)
 
     def block(d, i):
-        return gram[d // 2, BLOCKS * (d % 2) + i].reshape(BLOCK, BLOCK)
+        return gram[lookup(i, [SPOT[n, d] for n in range(BLOCKS)])].reshape(BLOCK, BLOCK)
 
     def apply(source, i):
         got = dot(block(0, i), source(i), ((1,), (0,)))
@@ -429,7 +474,7 @@
         in_specs=[pl.BlockSpec(memory_space=pl.ANY)] * count,
         out_specs=[pl.BlockSpec(memory_space=pl.ANY)] * 4,
         scratch_shapes=[
-            pltpu.VMEM((2, MINE, PLACES, UNIT, BLOCK), BF16),
+            pltpu.VMEM((2 * MINE, PLACES, UNIT, BLOCK), BF16),
             pltpu.VMEM((BLOCKS, 4, BAND, WIDE), BF16),
             pltpu.VMEM((ORDER, WIDE), BF16),
             pltpu.VMEM((ORDER, WIDE), F32),
@@ -453,11 +498,11 @@
 def panels(iterate):
     y, x, core, high, low = place()
     aligned = y == high
-    starts = [sum(PIECES[:n]) * BAND for n in range(len(PIECES) + 1)]
+    starts = [sum(HOPS[:n]) * BAND for n in range(len(HOPS))]
 
     def cast(n, at):
-        band = iterate[starts[n] : starts[n + 1]]
-        return pick(band, at * 2 * GROUP, 2 * GROUP, 1).astype(BF16)
+        size = (HOPS[n] * BAND, 2 * GROUP)
+        return lax.dynamic_slice(iterate, (starts[n], at * 2 * GROUP), size).astype(BF16)
 
     def chunks(keep, other):
         near, far = jnp.where(aligned, keep, other), jnp.where(aligned, other, keep)
@@ -466,28 +511,47 @@
             for step in range(4)
         ]
 
-    own, beside = [], []
+    def travel(ready):
+        return [ready[0]] + [over_z(ready[step], step) for step in (1, 2, 3)]
+
+    def joined(pieces):
+        return jnp.stack([jnp.concatenate(slab) for slab in zip(*pieces)])
+
+    done = []
     keep, other = cast(0, y), over_y(cast(0, 1 - y))
-    for n in range(len(PIECES)):
-        ready = chunks(keep, other)
-        more = n + 1 < len(PIECES)
-        ahead = [cast(n + 1, y), cast(n + 1, 1 - y)] if more else []
-        ready, ahead, done = lax.optimization_barrier((ready, ahead, own[-1:]))
-        got = [ready[0]] + [over_z(ready[step], step) for step in (1, 2, 3)]
-        if more:
-            keep, other = ahead[0], over_y(ahead[1])
-        beside += [over_core(piece) for piece in done]
-        own.append(jnp.stack(got))
-    beside.append(over_core(own[-1]))
-    return own, beside
+    for n in range(len(HOPS) - 1):
+        ahead = [cast(n + 1, y), cast(n + 1, 1 - y)]
+        ready, ahead, done = lax.optimization_barrier((chunks(keep, other), ahead, done))
+        done.append(travel(ready))
+        keep, other = ahead[0], over_y(ahead[1])
+    ready = chunks(keep, other)
+    own = [joined(done)]
+    done, parts, start = [], None, 0
+    for n, blocks in enumerate(LAST):
+        stop = start + blocks * BAND
+        now, ready, done, own, parts = lax.optimization_barrier(
+            ([chunk[start:stop] for chunk in ready], ready, done, own, parts)
+        )
+        start = stop
+        done.append(travel(now))
+        if n == 0:
+            beside = [over_core(own[0])]
+            parts = gram_call(EARLY_GROUPS, own, beside)
+        else:
+            parts = summed(EARLY_GROUPS, parts, n - 1)
+    out = (FACTOR * quint_a) * (iterate - lax.reduce_precision(iterate, 8, 7))
+    out, parts, done = lax.optimization_barrier((out, parts, done))
+    own.append(joined(done))
+    beside.append(over_core(own[1]))
+    return own, beside, summed(EARLY_GROUPS, parts, 2), out
 
 
 def shards_cube(iterate):
     y, x, core, high, low = place()
-    own, beside = panels(iterate)
-    out = (FACTOR * quint_a) * (iterate - lax.reduce_precision(iterate, 8, 7))
-    out, own[0] = lax.optimization_barrier((out, own[0]))
-    mine = summed(gram_call(own + beside))
+    own, beside, early, out = panels(iterate)
+    mine = gram_call(LATE_GROUPS, own, beside)
+    for stage in range(3):
+        mine = summed(LATE_GROUPS, mine, stage, early)
     entries = gathered([piece[None] for piece in mine])
     keys = [key for key, _ in entries]
     gram_pieces = [piece.reshape(-1, *piece.shape[-3:]) for _, piece in entries]

time: 366 us -> 360 us (0.984)
  waiting for transfers between devices: 219 us -> 203 us
  starting transfers between devices: 50 us -> 62.6 us
    ppermute x16 -> x23, waiting for transfers between devices: 102 us -> 77.7 us  [over_z(): return lax.ppermute(a, 'row', [(z, z ^ step) for z in range(4)])]
    ppermute x16 -> x23, starting transfers between devices: 15.1 us -> 25.4 us  [over_z(): return lax.ppermute(a, 'row', [(z, z ^ step) for z in range(4)])]
    ppermute x7 -> x8, waiting for transfers between devices: 28.8 us -> 35.8 us  [over_x(): return lax.ppermute(a, 'col', [(0, 2), (1, 3), (2, 0), (3, 1)])]
    slice x3 -> x10, local copies, waits for them, and re-layouts: 5.51 us -> 0.17 us  [panels(): chunk[start:stop]]
    convert_element_type x3, local copies, waits for them, and re-layouts: 0.28 us -> 5.3 us  [cast(): lax.dynamic_slice(iterate, (starts[n], at * 2 * GROUP), size).astype(BF16)]
    ppermute x15 -> x14, waiting for transfers between devices: 10 us -> 13 us  [over_core(): return lax.ppermute(a, 'col', [(0, 1), (1, 0), (2, 3), (3, 2)])]
    ppermute x7 -> x8, starting transfers between devices: 7.95 us -> 10.1 us  [over_x(): return lax.ppermute(a, 'col', [(0, 2), (1, 3), (2, 0), (3, 1)])]
    pallas_call x4 -> x8, Pallas kernels: 17.5 us -> 16 us  [the longest x2 13.4 us: gram_call(): pl.pallas_call(functools.partial(gram_kernel, groups, len(own)), out_shap...]
  transfers between devices with their start and end apart: 56 -> 64, of which waited for: 41 -> 45; matrix products, arithmetic and copies ran while one was open for 7% -> 7% of each run, Pallas kernels for 6% -> 8%
where the time goes in v4:
time: 360 us; the launch traced here: 359 us
  waiting for transfers between devices  203 us (56%)
  starting transfers between devices  62.6 us (17%)
  Pallas kernels  61.8 us (17%)
  other arithmetic  25.2 us (7%)
  local copies, waits for them, and re-layouts  6.39 us (2%)
    ppermute x23, waiting for transfers between devices, over_z(): return lax.ppermute(a, 'row', [(z, z ^ step) for z in range(4)])  77.7 us
    pallas_call x2, Pallas kernels, step_call(): pl.pallas_call(functools.partial(step_kernel, keys, part), out_shape=[jax...  45.8 us
    ppermute x8, waiting for transfers between devices, home(): return lax.ppermute(a, ('mats', 'row'), pairs)  41.6 us
    ppermute x8, waiting for transfers between devices, over_x(): return lax.ppermute(a, 'col', [(0, 2), (1, 3), (2, 0), (3, 1)])  35.8 us
    ppermute x11, waiting for transfers between devices, over_y(): return lax.ppermute(a, 'mats', [(0, 1), (1, 0)])  34.7 us
    ppermute x23, starting transfers between devices, over_z(): return lax.ppermute(a, 'row', [(z, z ^ step) for z in range(4)])  25.4 us
    dynamic_update_slice x8, other arithmetic, shards_cube(): lax.dynamic_update_slice_in_dim(out, pick(out, at, WIDE, 1) + piece, at, 1)  17.5 us
    ppermute x8, starting transfers between devices, home(): return lax.ppermute(a, ('mats', 'row'), pairs)  14.9 us
  transfers between devices with their start and end apart: 64, of which 45 were waited for; matrix products, arithmetic and copies ran while one was open for 7% of the time, Pallas kernels for 8%

profile of v4, /device:TPU:12, one launch (start us, length us, event | category | flops | bytes accessed | tf_op | source)
XLA Modules:
  0.0 359.5 jit_solution(9987600458779689229)
XLA Ops:
  1.6 1.7 dynamic-slice_convert_fusion.2
  3.3 5.8 %collective-permute-done = bf16[128,1024]{1,0:T(8,128)(2,1)S(1)} collective-permute-done((bf16[128,1024]{1,0:T(8,128)(2,1)S(1)}, bf16[128,1024]{1,0:T(8,128)(2,1)S(1)}, u32[]{:S(2)}, u32[]{:S(2)}) %collective-permute-start) | collective-permute-done | bytes 262176 | tf_op jit(solution)/shard_map/ppermute | solution.py:94
  11.0 2.5 dynamic-slice_convert_fusion
  13.8 2.8 collective-permute-start.3
  17.1 6.2 %collective-permute-done.1 = bf16[256,1024]{1,0:T(8,128)(2,1)S(1)} collective-permute-done((bf16[256,1024]{1,0:T(8,128)(2,1)S(1)}, bf16[256,1024]{1,0:T(8,128)(2,1)S(1)}, u32[]{:S(2)}, u32[]{:S(2)}) %collective-permute-start.1) | collective-permute-done | bytes 524320 | tf_op jit(solution)/shard_map/ppermute | solution.py:94
  23.4 1.6 collective-permute-done.3
  25.0 2.3 collective-permute-done.4
  28.8 3.0 collective-permute-start.7
  32.3 5.7 %collective-permute-done.6 = bf16[256,512]{1,0:T(8,128)(2,1)S(1)} collective-permute-done((bf16[256,512]{1,0:T(8,128)(2,1)S(1)}, bf16[256,512]{1,0:T(8,128)(2,1)S(1)}, u32[]{:S(2)}, u32[]{:S(2)}) %collective-permute-start.6) | collective-permute-done | bytes 262176 | tf_op jit(solution)/shard_map/ppermute | solution.py:98
  38.1 10.8 %collective-permute-done.7 = bf16[256,512]{1,0:T(8,128)(2,1)S(1)} collective-permute-done((bf16[256,512]{1,0:T(8,128)(2,1)S(1)}, bf16[256,512]{1,0:T(8,128)(2,1)S(1)}, u32[]{:S(2)}, u32[]{:S(2)}) %collective-permute-start.7) | collective-permute-done | bytes 262176 | tf_op jit(solution)/shard_map/ppermute | solution.py:98
  48.9 4.2 %collective-permute-done.8 = bf16[256,512]{1,0:T(8,128)(2,1)S(1)} collective-permute-done((bf16[256,512]{1,0:T(8,128)(2,1)S(1)}, bf16[256,512]{1,0:T(8,128)(2,1)S(1)}, u32[]{:S(2)}, u32[]{:S(2)}) %collective-permute-start.8) | collective-permute-done | bytes 262176 | tf_op jit(solution)/shard_map/ppermute | solution.py:98
  55.4 3.0 collective-permute-start.9
  58.5 3.3 gram.2
  61.8 1.7 collective-permute-done.10
  63.4 4.5 %collective-permute-done.11 = bf16[128,512]{1,0:T(8,128)(2,1)S(1)} collective-permute-done((bf16[128,512]{1,0:T(8,128)(2,1)S(1)}, bf16[128,512]{1,0:T(8,128)(2,1)S(1)}, u32[]{:S(2)}, u32[]{:S(2)}) %collective-permute-start.11) | collective-permute-done | bytes 131104 | tf_op jit(solution)/shard_map/ppermute | solution.py:98
  67.9 1.5 collective-permute-start.16
  69.4 2.2 collective-permute-start.14
  72.9 14.6 %collective-permute-done.16.refs_1_ = bf16[784,512]{1,0:T(8,128)(2,1)S(1)} collective-permute-done((bf16[784,512]{1,0:T(8,128)(2,1)S(1)}, bf16[784,512]{1,0:T(8,128)(2,1)S(1)}, u32[]{:S(2)}, u32[]{:S(2)}) %collective-permute-start.16) | collective-permute-done | bytes 802848 | tf_op jit(solution)/shard_map/ppermute | solution.py:86
  89.6 5.7 %collective-permute-done.15 = bf16[256,512]{1,0:T(8,128)(2,1)S(1)} collective-permute-done((bf16[256,512]{1,0:T(8,128)(2,1)S(1)}, bf16[256,512]{1,0:T(8,128)(2,1)S(1)}, u32[]{:S(2)}, u32[]{:S(2)}) %collective-permute-start.15) | collective-permute-done | bytes 262176 | tf_op jit(solution)/shard_map/ppermute | solution.py:98
  95.7 2.2 collective-permute-start.19
  99.2 4.7 %fusion = f32[896,2048]{1,0:T(8,128)} fusion(f32[896,2048]{1,0:T(8,128)S(1)} %bitcast.42), kind=kLoop, calls=%fused_computation.1 | loop fusion | flops 5505024 | bytes 14680064 | tf_op jit(solution)/shard_map/mul | solution.py:542
  105.7 3.2 collective-permute-done.20
  109.4 4.1 %collective-permute-done.21.refs_3_ = bf16[4,512,512]{2,1,0:T(8,128)(2,1)S(1)} collective-permute-done((bf16[4,512,512]{2,1,0:T(8,128)(2,1)S(1)}, bf16[4,512,512]{2,1,0:T(8,128)(2,1)S(1)}, u32[]{:S(2)}, u32[]{:S(2)}) %collective-permute-start.21) | collective-permute-done | bytes 2097184 | tf_op jit(solution)/shard_map/ppermute | solution.py:90
  113.6 10.2 %gram.3 = (f32[4,4,64,512]{3,2,1,0:T(8,128)S(1)}, bf16[1040,512]{1,0:T(8,128)(2,1)S(1)}, f32[4,4,64,512]{3,2,1,0:T(8,128)S(1)}, bf16[1040,512]{1,0:T(8,128)(2,1)...) custom-call(bf16[4,384,512]{2,1,0:T(8,128)(2,1)S(1)} %pad_maximum_fusion.1.refs_0_.refs_24_, ...), custom_call_target="tpu_custom_call" | custom-call | flops 2883584 | bytes 458752 | tf_op jit(solution)/shard_map/gram/pallas_call | solution.py:296
  124.4 1.5 collective-permute-start.23
  125.9 19.4 %collective-permute-done.24.refs_5_ = bf16[784,512]{1,0:T(8,128)(2,1)S(1)} collective-permute-done((bf16[784,512]{1,0:T(8,128)(2,1)S(1)}, bf16[784,512]{1,0:T(8,128)(2,1)S(1)}, u32[]{:S(2)}, u32[]{:S(2)}) %collective-permute-start.24) | collective-permute-done | bytes 802848 | tf_op jit(solution)/shard_map/ppermute | solution.py:98
  145.3 4.1 %collective-permute-done.22.refs_1_ = bf16[1040,512]{1,0:T(8,128)(2,1)S(1)} collective-permute-done((bf16[1040,512]{1,0:T(8,128)(2,1)S(1)}, bf16[1040,512]{1,0:T(8,128)(2,1)S(1)}, u32[]{:S(2)}, u32[]{:S(2)}) %collective-permute-start.22) | collective-permute-done | bytes 1064992 | tf_op jit(solution)/shard_map/ppermute | solution.py:86
  150.6 1.6 collective-permute-start.25
  153.7 8.7 %collective-permute-done.27.refs_5_ = bf16[400,512]{1,0:T(8,128)(2,1)S(1)} collective-permute-done((bf16[400,512]{1,0:T(8,128)(2,1)S(1)}, bf16[400,512]{1,0:T(8,128)(2,1)S(1)}, u32[]{:S(2)}, u32[]{:S(2)}) %collective-permute-start.27) | collective-permute-done | bytes 409632 | tf_op jit(solution)/shard_map/ppermute | solution.py:86
  162.4 1.6 collective-permute-done.25.refs_1_
  167.4 1.7 collective-permute-start.31
  169.7 7.0 %collective-permute-done.31.refs_1_ = bf16[208,512]{1,0:T(8,128)(2,1)S(1)} collective-permute-done((bf16[208,512]{1,0:T(8,128)(2,1)S(1)}, bf16[208,512]{1,0:T(8,128)(2,1)S(1)}, u32[]{:S(2)}, u32[]{:S(2)}) %collective-permute-start.31) | collective-permute-done | bytes 213024 | tf_op jit(solution)/shard_map/ppermute | solution.py:98
  179.5 4.0 %collective-permute-done.34 = bf16[1,4,64,512]{3,2,1,0:T(8,128)(2,1)S(1)} collective-permute-done((bf16[1,4,64,512]{3,2,1,0:T(8,128)(2,1)S(1)}, bf16[1,4,64,512]{3,2,1,0:T(8,128)(2,1)S(1)}, u32[]{:S(2)}, u32[]{:S(2)}) %collective-permute-start.34) | collective-permute-done | bytes 262176 | tf_op jit(solution)/shard_map/ppermute | solution.py:98
  184.8 1.8 collective-permute-done.32
  188.2 1.5 collective-permute-start.35
  189.7 1.9 collective-permute-start.36
  192.1 4.3 %collective-permute-done.37.refs_8_ = bf16[2,4,64,512]{3,2,1,0:T(8,128)(2,1)S(1)} collective-permute-done((bf16[2,4,64,512]{3,2,1,0:T(8,128)(2,1)S(1)}, bf16[2,4,64,512]{3,2,1,0:T(8,128)(2,1)S(1)}, u32[]{:S(2)}, u32[]{:S(2)}) %collective-permute-start.37) | collective-permute-done | bytes 524320 | tf_op jit(solution)/shard_map/ppermute | solution.py:86
  196.5 1.9 collective-permute-done.40.refs_5_
  200.9 1.8 collective-permute-start.41
  204.1 9.0 %collective-permute-done.43.refs_14_ = bf16[2,4,64,512]{3,2,1,0:T(8,128)(2,1)S(1)} collective-permute-done((bf16[2,4,64,512]{3,2,1,0:T(8,128)(2,1)S(1)}, bf16[2,4,64,512]{3,2,1,0:T(8,128)(2,1)S(1)}, u32[]{:S(2)}, u32[]{:S(2)}) %collective-permute-start.43) | collective-permute-done | bytes 524320 | tf_op jit(solution)/shard_map/ppermute | solution.py:94
  213.2 1.9 collective-permute-done.46.refs_11_
  215.1 2.1 collective-permute-done.41.refs_12_
  221.4 9.2 %collective-permute-done.49.refs_20_ = bf16[2,4,64,512]{3,2,1,0:T(8,128)(2,1)} collective-permute-done((bf16[2,4,64,512]{3,2,1,0:T(8,128)(2,1)S(1)}, bf16[2,4,64,512]{3,2,1,0:T(8,128)(2,1)}, u32[]{:S(2)}, u32[]{:S(2)}) %collective-permute-start.49) | collective-permute-done | bytes 524320 | tf_op jit(solution)/shard_map/ppermute | solution.py:94
  230.6 1.9 collective-permute-done.52.refs_17_
  235.7 3.1 collective-permute-done.55.refs_23_
  238.8 22.9 %step.2 = (bf16[7,128,256]{2,1,0:T(8,128)(2,1)}, bf16[7,128,256]{2,1,0:T(8,128)(2,1)}, bf16[7,128,256]{2,1,0:T(8,128)(2,1)}, bf16[7,128,256]{2,1,0:T(8,128)(2,1)}) custom-call(bf16[2,5,64,512]{3,2,1,0:T(8,128)(2,1)} %copy-done.3, bf16[2,5,64,512]{3,2,1,0:T(8,128)(2,1)} %copy-done.2, bf16[2,4,64,512]{3,2,1,0:T(8,128)(2,1)} %copy-done.4, ...), custom_call_target="tpu_custom_call" | custom-call | flops 13153337344 | bytes 20971520 | tf_op jit(solution)/shard_map/step/pallas_call | solution.py:471
  261.8 4.1 %collective-permute-start.56 = (bf16[7,128,256]{2,1,0:T(8,128)(2,1)}, bf16[7,128,256]{2,1,0:T(8,128)(2,1)S(1)}, u32[]{:S(2)}, u32[]{:S(2)}) collective-permute-start(bf16[7,128,256]{2,1,0:T(8,128)(2,1)} %get-tuple-element.319), channel_id=1, source_target_pairs={{0,0},{1,1},{2,16},{3,17},{16,2},{17,3},{18,18},{19,19},{4,4},{5,5... | collective-permute-start | bytes 1376264 | tf_op jit(solution)/shard_map/ppermute | solution.py:138
  267.0 3.3 collective-permute-start.59
  270.3 22.9 %step.3 = (bf16[7,128,256]{2,1,0:T(8,128)(2,1)}, bf16[7,128,256]{2,1,0:T(8,128)(2,1)}, bf16[7,128,256]{2,1,0:T(8,128)(2,1)}, bf16[7,128,256]{2,1,0:T(8,128)(2,1)}) custom-call(bf16[2,5,64,512]{3,2,1,0:T(8,128)(2,1)} %copy-done.3, bf16[2,5,64,512]{3,2,1,0:T(8,128)(2,1)} %copy-done.2, bf16[2,4,64,512]{3,2,1,0:T(8,128)(2,1)} %copy-done.4, ...), custom_call_target="tpu_custom_call" | custom-call | flops 13153337344 | bytes 20971520 | tf_op jit(solution)/shard_map/step/pallas_call | solution.py:471
  293.2 2.8 collective-permute-done.56
  296.0 11.1 %collective-permute-done.57 = bf16[7,128,256]{2,1,0:T(8,128)(2,1)S(1)} collective-permute-done((bf16[7,128,256]{2,1,0:T(8,128)(2,1)}, bf16[7,128,256]{2,1,0:T(8,128)(2,1)S(1)}, u32[]{:S(2)}, u32[]{:S(2)}) %collective-permute-start.57) | collective-permute-done | bytes 458784 | tf_op jit(solution)/shard_map/ppermute | solution.py:138
  307.2 3.1 collective-permute-done.59
  310.2 1.9 collective-permute-start.60
  313.5 3.1 collective-permute-start.63
  316.7 2.2 constant_dynamic-update-slice_fusion.7
  319.0 2.2 constant_dynamic-update-slice_fusion.6
  321.3 2.2 constant_dynamic-update-slice_fusion.5
  323.5 2.2 constant_dynamic-update-slice_fusion.4
  325.7 17.3 %collective-permute-done.60 = bf16[7,128,256]{2,1,0:T(8,128)(2,1)S(1)} collective-permute-done((bf16[7,128,256]{2,1,0:T(8,128)(2,1)}, bf16[7,128,256]{2,1,0:T(8,128)(2,1)S(1)}, u32[]{:S(2)}, u32[]{:S(2)}) %collective-permute-start.60) | collective-permute-done | bytes 458784 | tf_op jit(solution)/shard_map/ppermute | solution.py:138
  343.2 2.2 constant_dynamic-update-slice_fusion.3
  345.3 7.2 %collective-permute-done.61 = bf16[7,128,256]{2,1,0:T(8,128)(2,1)S(1)} collective-permute-done((bf16[7,128,256]{2,1,0:T(8,128)(2,1)}, bf16[7,128,256]{2,1,0:T(8,128)(2,1)S(1)}, u32[]{:S(2)}, u32[]{:S(2)}) %collective-permute-start.61) | collective-permute-done | bytes 458784 | tf_op jit(solution)/shard_map/ppermute | solution.py:138
  352.7 2.2 constant_dynamic-update-slice_fusion.2
  354.9 2.2 constant_dynamic-update-slice_fusion.1
  357.3 2.2 constant_dynamic-update-slice_fusion
  (170 shorter events, 44.0 us)
Async XLA Ops:
  1.1 8.1 %collective-permute-start = (bf16[128,1024]{1,0:T(8,128)(2,1)S(1)}, bf16[128,1024]{1,0:T(8,128)(2,1)S(1)}, u32[]{:S(2)}, u32[]{:S(2)}) collective-permute-start(bf16[128,1024]{1,0:T(8,128)(2,1)S(1)} %dynamic-slice_convert_fusion.4), channel_id=1, source_target_pairs={{0,16},{16,0},{1,17},{17,1},{2,18},{18,2},{3,19},{19,3},{4,20},{20... | collective-permute-start | bytes 786440 | tf_op jit(solution)/shard_map/ppermute | solution.py:94
  10.4 12.9 %collective-permute-start.1 = (bf16[256,1024]{1,0:T(8,128)(2,1)S(1)}, bf16[256,1024]{1,0:T(8,128)(2,1)S(1)}, u32[]{:S(2)}, u32[]{:S(2)}) collective-permute-start(bf16[256,1024]{1,0:T(8,128)(2,1)S(1)} %get-tuple-element.169), channel_id=1, source_target_pairs={{0,16},{16,0},{1,17},{17,1},{2,18},{18,2},{3,19},{19,3},{4,20},{20... | collective-permute-start | bytes 1572872 | tf_op jit(solution)/shard_map/ppermute | solution.py:94
  13.5 9.9 %collective-permute-start.2 = (bf16[128,512]{1,0:T(8,128)(2,1)S(1)}, bf16[128,512]{1,0:T(8,128)(2,1)S(1)}, u32[]{:S(2)}, u32[]{:S(2)}) collective-permute-start(bf16[128,512]{1,0:T(8,128)(2,1)S(1)} %get-tuple-element.171), channel_id=1, source_target_pairs={{0,1},{1,0},{2,3},{3,2},{4,5},{5,4},{6,7},{7,6},{8,9},{9,8},{10,11... | collective-permute-start | bytes 393224 | tf_op jit(solution)/shard_map/ppermute | solution.py:98
  13.8 11.2 %collective-permute-start.3 = (bf16[128,512]{1,0:T(8,128)(2,1)S(1)}, bf16[128,512]{1,0:T(8,128)(2,1)S(1)}, u32[]{:S(2)}, u32[]{:S(2)}) collective-permute-start(bf16[128,512]{1,0:T(8,128)(2,1)S(1)} %get-tuple-element.172), channel_id=1, source_target_pairs={{0,2},{1,3},{2,0},{3,1},{4,6},{5,7},{6,4},{7,5},{8,10},{9,11},{10,... | collective-permute-start | bytes 393224 | tf_op jit(solution)/shard_map/ppermute | solution.py:98
  16.6 10.7 %collective-permute-start.4 = (bf16[128,512]{1,0:T(8,128)(2,1)S(1)}, bf16[128,512]{1,0:T(8,128)(2,1)S(1)}, u32[]{:S(2)}, u32[]{:S(2)}) collective-permute-start(bf16[128,512]{1,0:T(8,128)(2,1)S(1)} %get-tuple-element.173), channel_id=1, source_target_pairs={{0,3},{1,2},{2,1},{3,0},{4,7},{5,6},{6,5},{7,4},{8,11},{9,10},{10,... | collective-permute-start | bytes 393224 | tf_op jit(solution)/shard_map/ppermute | solution.py:98
  27.3 26.1 %collective-permute-start.5 = (bf16[512,1024]{1,0:T(8,128)(2,1)S(1)}, bf16[512,1024]{1,0:T(8,128)(2,1)S(1)}, u32[]{:S(2)}, u32[]{:S(2)}) collective-permute-start(bf16[512,1024]{1,0:T(8,128)(2,1)S(1)} %get-tuple-element.175), channel_id=1, source_target_pairs={{0,16},{16,0},{1,17},{17,1},{2,18},{18,2},{3,19},{19,3},{4,20},{20... | collective-permute-start | bytes 3145736 | tf_op jit(solution)/shard_map/ppermute | solution.py:94
  28.8 9.2 %collective-permute-start.6 = (bf16[256,512]{1,0:T(8,128)(2,1)S(1)}, bf16[256,512]{1,0:T(8,128)(2,1)S(1)}, u32[]{:S(2)}, u32[]{:S(2)}) collective-permute-start(bf16[256,512]{1,0:T(8,128)(2,1)S(1)} %get-tuple-element.179), channel_id=1, source_target_pairs={{0,1},{1,0},{2,3},{3,2},{4,5},{5,4},{6,7},{7,6},{8,9},{9,8},{10,11... | collective-permute-start | bytes 786440 | tf_op jit(solution)/shard_map/ppermute | solution.py:98
  28.8 20.1 %collective-permute-start.7 = (bf16[256,512]{1,0:T(8,128)(2,1)S(1)}, bf16[256,512]{1,0:T(8,128)(2,1)S(1)}, u32[]{:S(2)}, u32[]{:S(2)}) collective-permute-start(bf16[256,512]{1,0:T(8,128)(2,1)S(1)} %get-tuple-element.181), channel_id=1, source_target_pairs={{0,2},{1,3},{2,0},{3,1},{4,6},{5,7},{6,4},{7,5},{8,10},{9,11},{10,... | collective-permute-start | bytes 786440 | tf_op jit(solution)/shard_map/ppermute | solution.py:98
  31.9 21.2 %collective-permute-start.8 = (bf16[256,512]{1,0:T(8,128)(2,1)S(1)}, bf16[256,512]{1,0:T(8,128)(2,1)S(1)}, u32[]{:S(2)}, u32[]{:S(2)}) collective-permute-start(bf16[256,512]{1,0:T(8,128)(2,1)S(1)} %get-tuple-element.183), channel_id=1, source_target_pairs={{0,3},{1,2},{2,1},{3,0},{4,7},{5,6},{6,5},{7,4},{8,11},{9,10},{10,... | collective-permute-start | bytes 786440 | tf_op jit(solution)/shard_map/ppermute | solution.py:98
  53.9 4.6 %collective-permute-start.12 = (bf16[4,384,512]{2,1,0:T(8,128)(2,1)S(1)}, bf16[4,384,512]{2,1,0:T(8,128)(2,1)S(1)}, u32[]{:S(2)}, u32[]{:S(2)}) collective-permute-start(bf16[4,384,512]{2,1,0:T(8,128)(2,1)S(1)} %pad_maximum_fusion.1.refs_0_.refs_24_), channel_id=1, source_target_pairs={{0,4},{4,0},{8,12},{12,8},{1,5},{5,1},{9,13},{13,9},{2,6},{6,2},{1... | collective-permute-start | bytes 4718600 | tf_op jit(solution)/shard_map/ppermute | solution.py:90
  53.9 9.5 %collective-permute-start.10 = (bf16[128,512]{1,0:T(8,128)(2,1)S(1)}, bf16[128,512]{1,0:T(8,128)(2,1)S(1)}, u32[]{:S(2)}, u32[]{:S(2)}) collective-permute-start(bf16[128,512]{1,0:T(8,128)(2,1)S(1)} %get-tuple-element.190), channel_id=1, source_target_pairs={{0,2},{1,3},{2,0},{3,1},{4,6},{5,7},{6,4},{7,5},{8,10},{9,11},{10,... | collective-permute-start | bytes 393224 | tf_op jit(solution)/shard_map/ppermute | solution.py:98
  54.0 13.9 %collective-permute-start.11 = (bf16[128,512]{1,0:T(8,128)(2,1)S(1)}, bf16[128,512]{1,0:T(8,128)(2,1)S(1)}, u32[]{:S(2)}, u32[]{:S(2)}) collective-permute-start(bf16[128,512]{1,0:T(8,128)(2,1)S(1)} %get-tuple-element.191), channel_id=1, source_target_pairs={{0,3},{1,2},{2,1},{3,0},{4,7},{5,6},{6,5},{7,4},{8,11},{9,10},{10,... | collective-permute-start | bytes 393224 | tf_op jit(solution)/shard_map/ppermute | solution.py:98
  55.4 12.5 %collective-permute-start.9 = (bf16[128,512]{1,0:T(8,128)(2,1)S(1)}, bf16[128,512]{1,0:T(8,128)(2,1)S(1)}, u32[]{:S(2)}, u32[]{:S(2)}) collective-permute-start(bf16[128,512]{1,0:T(8,128)(2,1)S(1)} %get-tuple-element.189), channel_id=1, source_target_pairs={{0,1},{1,0},{2,3},{3,2},{4,5},{5,4},{6,7},{7,6},{8,9},{9,8},{10,11... | collective-permute-start | bytes 393224 | tf_op jit(solution)/shard_map/ppermute | solution.py:98
  67.9 19.7 %collective-permute-start.16 = (bf16[784,512]{1,0:T(8,128)(2,1)S(1)}, bf16[784,512]{1,0:T(8,128)(2,1)S(1)}, u32[]{:S(2)}, u32[]{:S(2)}) collective-permute-start(bf16[784,512]{1,0:T(8,128)(2,1)S(1)} %get-tuple-element.209), channel_id=1, source_target_pairs={{0,8},{4,12},{8,0},{12,4},{1,9},{5,13},{9,1},{13,5},{2,10},{6,14},... | collective-permute-start | bytes 2408456 | tf_op jit(solution)/shard_map/ppermute | solution.py:86
  69.4 18.7 %collective-permute-start.13 = (bf16[256,512]{1,0:T(8,128)(2,1)S(1)}, bf16[256,512]{1,0:T(8,128)(2,1)S(1)}, u32[]{:S(2)}, u32[]{:S(2)}) collective-permute-start(bf16[256,512]{1,0:T(8,128)(2,1)S(1)} %slice.41), channel_id=1, source_target_pairs={{0,1},{1,0},{2,3},{3,2},{4,5},{5,4},{6,7},{7,6},{8,9},{9,8},{10,11... | collective-permute-start | bytes 786440 | tf_op jit(solution)/shard_map/ppermute | solution.py:98
  69.4 20.2 %collective-permute-start.14 = (bf16[256,512]{1,0:T(8,128)(2,1)S(1)}, bf16[256,512]{1,0:T(8,128)(2,1)S(1)}, u32[]{:S(2)}, u32[]{:S(2)}) collective-permute-start(bf16[256,512]{1,0:T(8,128)(2,1)S(1)} %slice.42), channel_id=1, source_target_pairs={{0,2},{1,3},{2,0},{3,1},{4,6},{5,7},{6,4},{7,5},{8,10},{9,11},{10,... | collective-permute-start | bytes 786440 | tf_op jit(solution)/shard_map/ppermute | solution.py:98
  71.6 23.7 %collective-permute-start.15 = (bf16[256,512]{1,0:T(8,128)(2,1)S(1)}, bf16[256,512]{1,0:T(8,128)(2,1)S(1)}, u32[]{:S(2)}, u32[]{:S(2)}) collective-permute-start(bf16[256,512]{1,0:T(8,128)(2,1)S(1)} %slice.43), channel_id=1, source_target_pairs={{0,3},{1,2},{2,1},{3,0},{4,7},{5,6},{6,5},{7,4},{8,11},{9,10},{10,... | collective-permute-start | bytes 786440 | tf_op jit(solution)/shard_map/ppermute | solution.py:98
  95.2 9.8 %collective-permute-start.17 = (bf16[400,512]{1,0:T(8,128)(2,1)S(1)}, bf16[400,512]{1,0:T(8,128)(2,1)S(1)}, u32[]{:S(2)}, u32[]{:S(2)}) collective-permute-start(bf16[400,512]{1,0:T(8,128)(2,1)S(1)} %get-tuple-element.213), channel_id=1, source_target_pairs={{0,16},{16,0},{1,17},{17,1},{2,18},{18,2},{3,19},{19,3},{4,20},{20... | collective-permute-start | bytes 1228808 | tf_op jit(solution)/shard_map/ppermute | solution.py:94
  95.7 9.6 %collective-permute-start.18 = (bf16[128,512]{1,0:T(8,128)(2,1)S(1)}, bf16[128,512]{1,0:T(8,128)(2,1)S(1)}, u32[]{:S(2)}, u32[]{:S(2)}) collective-permute-start(bf16[128,512]{1,0:T(8,128)(2,1)S(1)} %slice.45), channel_id=1, source_target_pairs={{0,1},{1,0},{2,3},{3,2},{4,5},{5,4},{6,7},{7,6},{8,9},{9,8},{10,11... | collective-permute-start | bytes 393224 | tf_op jit(solution)/shard_map/ppermute | solution.py:98
  95.7 10.0 %collective-permute-start.19 = (bf16[128,512]{1,0:T(8,128)(2,1)S(1)}, bf16[128,512]{1,0:T(8,128)(2,1)S(1)}, u32[]{:S(2)}, u32[]{:S(2)}) collective-permute-start(bf16[128,512]{1,0:T(8,128)(2,1)S(1)} %slice.46), channel_id=1, source_target_pairs={{0,2},{1,3},{2,0},{3,1},{4,6},{5,7},{6,4},{7,5},{8,10},{9,11},{10,... | collective-permute-start | bytes 393224 | tf_op jit(solution)/shard_map/ppermute | solution.py:98
  97.9 11.0 %collective-permute-start.20 = (bf16[128,512]{1,0:T(8,128)(2,1)S(1)}, bf16[128,512]{1,0:T(8,128)(2,1)S(1)}, u32[]{:S(2)}, u32[]{:S(2)}) collective-permute-start(bf16[128,512]{1,0:T(8,128)(2,1)S(1)} %slice.47), channel_id=1, source_target_pairs={{0,3},{1,2},{2,1},{3,0},{4,7},{5,6},{6,5},{7,4},{8,11},{9,10},{10,... | collective-permute-start | bytes 393224 | tf_op jit(solution)/shard_map/ppermute | solution.py:98
  109.3 4.2 %collective-permute-start.21 = (bf16[4,512,512]{2,1,0:T(8,128)(2,1)S(1)}, bf16[4,512,512]{2,1,0:T(8,128)(2,1)S(1)}, u32[]{:S(2)}, u32[]{:S(2)}) collective-permute-start(bf16[4,512,512]{2,1,0:T(8,128)(2,1)S(1)} %pad_maximum_fusion.refs_1_.refs_25_), channel_id=1, source_target_pairs={{0,4},{4,0},{8,12},{12,8},{1,5},{5,1},{9,13},{13,9},{2,6},{6,2},{1... | collective-permute-start | bytes 6291464 | tf_op jit(solution)/shard_map/ppermute | solution.py:90
  123.8 25.6 %collective-permute-start.22 = (bf16[1040,512]{1,0:T(8,128)(2,1)S(1)}, bf16[1040,512]{1,0:T(8,128)(2,1)S(1)}, u32[]{:S(2)}, u32[]{:S(2)}) collective-permute-start(bf16[1040,512]{1,0:T(8,128)(2,1)S(1)} %get-tuple-element.243), channel_id=1, source_target_pairs={{0,8},{4,12},{8,0},{12,4},{1,9},{5,13},{9,1},{13,5},{2,10},{6,14},... | collective-permute-start | bytes 3194888 | tf_op jit(solution)/shard_map/ppermute | solution.py:86
  124.4 25.3 %collective-permute-start.23 = (bf16[1040,512]{1,0:T(8,128)(2,1)S(1)}, bf16[1040,512]{1,0:T(8,128)(2,1)S(1)}, u32[]{:S(2)}, u32[]{:S(2)}) collective-permute-start(bf16[1040,512]{1,0:T(8,128)(2,1)S(1)} %get-tuple-element.245), channel_id=1, source_target_pairs={{0,16},{16,0},{1,17},{17,1},{2,18},{18,2},{3,19},{19,3},{4,20},{20... | collective-permute-start | bytes 3194888 | tf_op jit(solution)/shard_map/ppermute | solution.py:94
  125.9 19.4 %collective-permute-start.24 = (bf16[784,512]{1,0:T(8,128)(2,1)S(1)}, bf16[784,512]{1,0:T(8,128)(2,1)S(1)}, u32[]{:S(2)}, u32[]{:S(2)}) collective-permute-start(bf16[784,512]{1,0:T(8,128)(2,1)S(1)} %get-tuple-element.247), channel_id=1, source_target_pairs={{0,1},{1,0},{2,3},{3,2},{4,5},{5,4},{6,7},{7,6},{8,9},{9,8},{10,11... | collective-permute-start | bytes 2408456 | tf_op jit(solution)/shard_map/ppermute | solution.py:98
  150.6 13.3 %collective-permute-start.25 = (bf16[528,512]{1,0:T(8,128)(2,1)S(1)}, bf16[528,512]{1,0:T(8,128)(2,1)S(1)}, u32[]{:S(2)}, u32[]{:S(2)}) collective-permute-start(bf16[528,512]{1,0:T(8,128)(2,1)S(1)} %get-tuple-element.249), channel_id=1, source_target_pairs={{0,16},{16,0},{1,17},{17,1},{2,18},{18,2},{3,19},{19,3},{4,20},{20... | collective-permute-start | bytes 1622024 | tf_op jit(solution)/shard_map/ppermute | solution.py:94
  152.2 13.0 %collective-permute-start.26 = (bf16[528,512]{1,0:T(8,128)(2,1)S(1)}, bf16[528,512]{1,0:T(8,128)(2,1)S(1)}, u32[]{:S(2)}, u32[]{:S(2)}) collective-permute-start(bf16[528,512]{1,0:T(8,128)(2,1)S(1)} %get-tuple-element.251), channel_id=1, source_target_pairs={{0,1},{1,0},{2,3},{3,2},{4,5},{5,4},{6,7},{7,6},{8,9},{9,8},{10,11... | collective-permute-start | bytes 1622024 | tf_op jit(solution)/shard_map/ppermute | solution.py:98
  152.2 10.1 %collective-permute-start.27 = (bf16[400,512]{1,0:T(8,128)(2,1)S(1)}, bf16[400,512]{1,0:T(8,128)(2,1)S(1)}, u32[]{:S(2)}, u32[]{:S(2)}) collective-permute-start(bf16[400,512]{1,0:T(8,128)(2,1)S(1)} %get-tuple-element.253), channel_id=1, source_target_pairs={{0,8},{4,12},{8,0},{12,4},{1,9},{5,13},{9,1},{13,5},{2,10},{6,14},... | collective-permute-start | bytes 1228808 | tf_op jit(solution)/shard_map/ppermute | solution.py:86
  165.7 11.2 %collective-permute-start.28 = (bf16[272,512]{1,0:T(8,128)(2,1)S(1)}, bf16[272,512]{1,0:T(8,128)(2,1)S(1)}, u32[]{:S(2)}, u32[]{:S(2)}) collective-permute-start(bf16[272,512]{1,0:T(8,128)(2,1)S(1)} %get-tuple-element.255), channel_id=1, source_target_pairs={{0,1},{1,0},{2,3},{3,2},{4,5},{5,4},{6,7},{7,6},{8,9},{9,8},{10,11... | collective-permute-start | bytes 835592 | tf_op jit(solution)/shard_map/ppermute | solution.py:98
  166.0 10.8 %collective-permute-start.29 = (bf16[272,512]{1,0:T(8,128)(2,1)S(1)}, bf16[272,512]{1,0:T(8,128)(2,1)S(1)}, u32[]{:S(2)}, u32[]{:S(2)}) collective-permute-start(bf16[272,512]{1,0:T(8,128)(2,1)S(1)} %get-tuple-element.257), channel_id=1, source_target_pairs={{0,8},{4,12},{8,0},{12,4},{1,9},{5,13},{9,1},{13,5},{2,10},{6,14},... | collective-permute-start | bytes 835592 | tf_op jit(solution)/shard_map/ppermute | solution.py:86
  167.4 9.3 %collective-permute-start.31 = (bf16[208,512]{1,0:T(8,128)(2,1)S(1)}, bf16[208,512]{1,0:T(8,128)(2,1)S(1)}, u32[]{:S(2)}, u32[]{:S(2)}) collective-permute-start(bf16[208,512]{1,0:T(8,128)(2,1)S(1)} %get-tuple-element.261), channel_id=1, source_target_pairs={{0,1},{1,0},{2,3},{3,2},{4,5},{5,4},{6,7},{7,6},{8,9},{9,8},{10,11... | collective-permute-start | bytes 638984 | tf_op jit(solution)/shard_map/ppermute | solution.py:98
  169.2 7.6 %collective-permute-start.30 = (bf16[208,512]{1,0:T(8,128)(2,1)S(1)}, bf16[208,512]{1,0:T(8,128)(2,1)S(1)}, u32[]{:S(2)}, u32[]{:S(2)}) collective-permute-start(bf16[208,512]{1,0:T(8,128)(2,1)S(1)} %get-tuple-element.259), channel_id=1, source_target_pairs={{0,16},{16,0},{1,17},{17,1},{2,18},{18,2},{3,19},{19,3},{4,20},{20... | collective-permute-start | bytes 638984 | tf_op jit(solution)/shard_map/ppermute | solution.py:94
  177.0 6.4 %collective-permute-start.34 = (bf16[1,4,64,512]{3,2,1,0:T(8,128)(2,1)S(1)}, bf16[1,4,64,512]{3,2,1,0:T(8,128)(2,1)S(1)}, u32[]{:S(2)}, u32[]{:S(2)}) collective-permute-start(bf16[1,4,64,512]{3,2,1,0:T(8,128)(2,1)S(1)} %bitcast.39), channel_id=1, source_target_pairs={{0,1},{1,0},{2,3},{3,2},{4,5},{5,4},{6,7},{7,6},{8,9},{9,8},{10,11... | collective-permute-start | bytes 786440 | tf_op jit(solution)/shard_map/ppermute | solution.py:98
  177.6 7.1 %collective-permute-start.33 = (bf16[1,5,64,512]{3,2,1,0:T(8,128)(2,1)S(1)}, bf16[1,5,64,512]{3,2,1,0:T(8,128)(2,1)S(1)}, u32[]{:S(2)}, u32[]{:S(2)}) collective-permute-start(bf16[1,5,64,512]{3,2,1,0:T(8,128)(2,1)S(1)} %bitcast.37), channel_id=1, source_target_pairs={{0,16},{16,0},{1,17},{17,1},{2,18},{18,2},{3,19},{19,3},{4,20},{20... | collective-permute-start | bytes 983048 | tf_op jit(solution)/shard_map/ppermute | solution.py:94
  178.1 8.5 %collective-permute-start.32 = (bf16[1,5,64,512]{3,2,1,0:T(8,128)(2,1)S(1)}, bf16[1,5,64,512]{3,2,1,0:T(8,128)(2,1)S(1)}, u32[]{:S(2)}, u32[]{:S(2)}) collective-permute-start(bf16[1,5,64,512]{3,2,1,0:T(8,128)(2,1)S(1)} %bitcast.35), channel_id=1, source_target_pairs={{0,8},{4,12},{8,0},{12,4},{1,9},{5,13},{9,1},{13,5},{2,10},{6,14},... | collective-permute-start | bytes 983048 | tf_op jit(solution)/shard_map/ppermute | solution.py:86
  186.7 9.8 %collective-permute-start.37 = (bf16[2,4,64,512]{3,2,1,0:T(8,128)(2,1)S(1)}, bf16[2,4,64,512]{3,2,1,0:T(8,128)(2,1)S(1)}, u32[]{:S(2)}, u32[]{:S(2)}) collective-permute-start(bf16[2,4,64,512]{3,2,1,0:T(8,128)(2,1)S(1)} %pad_maximum_fusion.4.refs_2_), channel_id=1, source_target_pairs={{0,8},{4,12},{8,0},{12,4},{1,9},{5,13},{9,1},{13,5},{2,10},{6,14},... | collective-permute-start | bytes 1572872 | tf_op jit(solution)/shard_map/ppermute | solution.py:86
  188.2 10.6 %collective-permute-start.35 = (bf16[2,5,64,512]{3,2,1,0:T(8,128)(2,1)S(1)}, bf16[2,5,64,512]{3,2,1,0:T(8,128)(2,1)S(1)}, u32[]{:S(2)}, u32[]{:S(2)}) collective-permute-start(bf16[2,5,64,512]{3,2,1,0:T(8,128)(2,1)S(1)} %pad_maximum_fusion.2.refs_0_), channel_id=1, source_target_pairs={{0,16},{16,0},{1,17},{17,1},{2,18},{18,2},{3,19},{19,3},{4,20},{20... | collective-permute-start | bytes 1966088 | tf_op jit(solution)/shard_map/ppermute | solution.py:94
  189.7 10.6 %collective-permute-start.36 = (bf16[2,5,64,512]{3,2,1,0:T(8,128)(2,1)S(1)}, bf16[2,5,64,512]{3,2,1,0:T(8,128)(2,1)S(1)}, u32[]{:S(2)}, u32[]{:S(2)}) collective-permute-start(bf16[2,5,64,512]{3,2,1,0:T(8,128)(2,1)S(1)} %pad_maximum_fusion.3.refs_1_), channel_id=1, source_target_pairs={{0,1},{1,0},{2,3},{3,2},{4,5},{5,4},{6,7},{7,6},{8,9},{9,8},{10,11... | collective-permute-start | bytes 1966088 | tf_op jit(solution)/shard_map/ppermute | solution.py:98
  191.6 8.7 %collective-permute-start.38 = (bf16[2,5,64,512]{3,2,1,0:T(8,128)(2,1)S(1)}, bf16[2,5,64,512]{3,2,1,0:T(8,128)(2,1)S(1)}, u32[]{:S(2)}, u32[]{:S(2)}) collective-permute-start(bf16[2,5,64,512]{3,2,1,0:T(8,128)(2,1)S(1)} %pad_maximum_fusion.2.refs_0_), channel_id=1, source_target_pairs={{0,4},{4,0},{8,12},{12,8},{1,5},{5,1},{9,13},{13,9},{2,6},{6,2},{1... | collective-permute-start | bytes 1966088 | tf_op jit(solution)/shard_map/ppermute | solution.py:90
  191.6 8.7 %collective-permute-start.39 = (bf16[2,5,64,512]{3,2,1,0:T(8,128)(2,1)S(1)}, bf16[2,5,64,512]{3,2,1,0:T(8,128)(2,1)S(1)}, u32[]{:S(2)}, u32[]{:S(2)}) collective-permute-start(bf16[2,5,64,512]{3,2,1,0:T(8,128)(2,1)S(1)} %pad_maximum_fusion.3.refs_1_), channel_id=1, source_target_pairs={{0,4},{4,0},{8,12},{12,8},{1,5},{5,1},{9,13},{13,9},{2,6},{6,2},{1... | collective-permute-start | bytes 1966088 | tf_op jit(solution)/shard_map/ppermute | solution.py:90
  196.5 1.9 collective-permute-start.40
  200.3 12.8 %collective-permute-start.43 = (bf16[2,4,64,512]{3,2,1,0:T(8,128)(2,1)S(1)}, bf16[2,4,64,512]{3,2,1,0:T(8,128)(2,1)S(1)}, u32[]{:S(2)}, u32[]{:S(2)}) collective-permute-start(bf16[2,4,64,512]{3,2,1,0:T(8,128)(2,1)S(1)} %pad_maximum_fusion.4.refs_2_), channel_id=1, source_target_pairs={{0,16},{16,0},{1,17},{17,1},{2,18},{18,2},{3,19},{19,3},{4,20},{20... | collective-permute-start | bytes 1572872 | tf_op jit(solution)/shard_map/ppermute | solution.py:94
  200.9 16.3 %collective-permute-start.41 = (bf16[2,5,64,512]{3,2,1,0:T(8,128)(2,1)S(1)}, bf16[2,5,64,512]{3,2,1,0:T(8,128)(2,1)S(1)}, u32[]{:S(2)}, u32[]{:S(2)}) collective-permute-start(bf16[2,5,64,512]{3,2,1,0:T(8,128)(2,1)S(1)} %pad_maximum_fusion.2.refs_0_), channel_id=1, source_target_pairs={{0,1},{1,0},{2,3},{3,2},{4,5},{5,4},{6,7},{7,6},{8,9},{9,8},{10,11... | collective-permute-start | bytes 1966088 | tf_op jit(solution)/shard_map/ppermute | solution.py:98
  202.7 15.7 %collective-permute-start.42 = (bf16[2,5,64,512]{3,2,1,0:T(8,128)(2,1)S(1)}, bf16[2,5,64,512]{3,2,1,0:T(8,128)(2,1)S(1)}, u32[]{:S(2)}, u32[]{:S(2)}) collective-permute-start(bf16[2,5,64,512]{3,2,1,0:T(8,128)(2,1)S(1)} %pad_maximum_fusion.3.refs_1_), channel_id=1, source_target_pairs={{0,8},{4,12},{8,0},{12,4},{1,9},{5,13},{9,1},{13,5},{2,10},{6,14},... | collective-permute-start | bytes 1966088 | tf_op jit(solution)/shard_map/ppermute | solution.py:86
  203.6 14.8 %collective-permute-start.44 = (bf16[2,5,64,512]{3,2,1,0:T(8,128)(2,1)S(1)}, bf16[2,5,64,512]{3,2,1,0:T(8,128)(2,1)S(1)}, u32[]{:S(2)}, u32[]{:S(2)}) collective-permute-start(bf16[2,5,64,512]{3,2,1,0:T(8,128)(2,1)S(1)} %collective-permute-done.35.refs_6_), channel_id=1, source_target_pairs={{0,4},{4,0},{8,12},{12,8},{1,5},{5,1},{9,13},{13,9},{2,6},{6,2},{1... | collective-permute-start | bytes 1966088 | tf_op jit(solution)/shard_map/ppermute | solution.py:90
  203.6 14.8 %collective-permute-start.45 = (bf16[2,5,64,512]{3,2,1,0:T(8,128)(2,1)S(1)}, bf16[2,5,64,512]{3,2,1,0:T(8,128)(2,1)S(1)}, u32[]{:S(2)}, u32[]{:S(2)}) collective-permute-start(bf16[2,5,64,512]{3,2,1,0:T(8,128)(2,1)S(1)} %collective-permute-done.36.refs_7_), channel_id=1, source_target_pairs={{0,4},{4,0},{8,12},{12,8},{1,5},{5,1},{9,13},{13,9},{2,6},{6,2},{1... | collective-permute-start | bytes 1966088 | tf_op jit(solution)/shard_map/ppermute | solution.py:90
  213.2 1.9 collective-permute-start.46
  218.4 12.1 %collective-permute-start.49 = (bf16[2,4,64,512]{3,2,1,0:T(8,128)(2,1)S(1)}, bf16[2,4,64,512]{3,2,1,0:T(8,128)(2,1)}, u32[]{:S(2)}, u32[]{:S(2)}) collective-permute-start(bf16[2,4,64,512]{3,2,1,0:T(8,128)(2,1)S(1)} %collective-permute-done.37.refs_8_), channel_id=1, source_target_pairs={{0,16},{16,0},{1,17},{17,1},{2,18},{18,2},{3,19},{19,3},{4,20},{20... | collective-permute-start | bytes 1572872 | tf_op jit(solution)/shard_map/ppermute | solution.py:94
  219.0 14.4 %collective-permute-start.47 = (bf16[2,5,64,512]{3,2,1,0:T(8,128)(2,1)S(1)}, bf16[2,5,64,512]{3,2,1,0:T(8,128)(2,1)}, u32[]{:S(2)}, u32[]{:S(2)}) collective-permute-start(bf16[2,5,64,512]{3,2,1,0:T(8,128)(2,1)S(1)} %collective-permute-done.35.refs_6_), channel_id=1, source_target_pairs={{0,1},{1,0},{2,3},{3,2},{4,5},{5,4},{6,7},{7,6},{8,9},{9,8},{10,11... | collective-permute-start | bytes 1966088 | tf_op jit(solution)/shard_map/ppermute | solution.py:98
  219.5 15.0 %collective-permute-start.48 = (bf16[2,5,64,512]{3,2,1,0:T(8,128)(2,1)S(1)}, bf16[2,5,64,512]{3,2,1,0:T(8,128)(2,1)}, u32[]{:S(2)}, u32[]{:S(2)}) collective-permute-start(bf16[2,5,64,512]{3,2,1,0:T(8,128)(2,1)S(1)} %collective-permute-done.36.refs_7_), channel_id=1, source_target_pairs={{0,8},{4,12},{8,0},{12,4},{1,9},{5,13},{9,1},{13,5},{2,10},{6,14},... | collective-permute-start | bytes 1966088 | tf_op jit(solution)/shard_map/ppermute | solution.py:86
  220.9 13.6 %collective-permute-start.50 = (bf16[2,5,64,512]{3,2,1,0:T(8,128)(2,1)S(1)}, bf16[2,5,64,512]{3,2,1,0:T(8,128)(2,1)S(1)}, u32[]{:S(2)}, u32[]{:S(2)}) collective-permute-start(bf16[2,5,64,512]{3,2,1,0:T(8,128)(2,1)S(1)} %collective-permute-done.41.refs_12_), channel_id=1, source_target_pairs={{0,4},{4,0},{8,12},{12,8},{1,5},{5,1},{9,13},{13,9},{2,6},{6,2},{1... | collective-permute-start | bytes 1966088 | tf_op jit(solution)/shard_map/ppermute | solution.py:90
  220.9 13.6 %collective-permute-start.51 = (bf16[2,5,64,512]{3,2,1,0:T(8,128)(2,1)S(1)}, bf16[2,5,64,512]{3,2,1,0:T(8,128)(2,1)S(1)}, u32[]{:S(2)}, u32[]{:S(2)}) collective-permute-start(bf16[2,5,64,512]{3,2,1,0:T(8,128)(2,1)S(1)} %collective-permute-done.42.refs_13_), channel_id=1, source_target_pairs={{0,4},{4,0},{8,12},{12,8},{1,5},{5,1},{9,13},{13,9},{2,6},{6,2},{1... | collective-permute-start | bytes 1966088 | tf_op jit(solution)/shard_map/ppermute | solution.py:90
  230.6 1.9 collective-permute-start.52
  234.6 4.2 %collective-permute-start.53 = (bf16[2,5,64,512]{3,2,1,0:T(8,128)(2,1)}, bf16[2,5,64,512]{3,2,1,0:T(8,128)(2,1)}, u32[]{:S(2)}, u32[]{:S(2)}) collective-permute-start(bf16[2,5,64,512]{3,2,1,0:T(8,128)(2,1)} %collective-permute-done.47.refs_18_), channel_id=1, source_target_pairs={{0,4},{4,0},{8,12},{12,8},{1,5},{5,1},{9,13},{13,9},{2,6},{6,2},{1... | collective-permute-start | bytes 1966088 | tf_op jit(solution)/shard_map/ppermute | solution.py:90
  234.7 4.1 %collective-permute-start.54 = (bf16[2,5,64,512]{3,2,1,0:T(8,128)(2,1)}, bf16[2,5,64,512]{3,2,1,0:T(8,128)(2,1)}, u32[]{:S(2)}, u32[]{:S(2)}) collective-permute-start(bf16[2,5,64,512]{3,2,1,0:T(8,128)(2,1)} %collective-permute-done.48.refs_19_), channel_id=1, source_target_pairs={{0,4},{4,0},{8,12},{12,8},{1,5},{5,1},{9,13},{13,9},{2,6},{6,2},{1... | collective-permute-start | bytes 1966088 | tf_op jit(solution)/shard_map/ppermute | solution.py:90
  235.7 3.1 collective-permute-start.55
  261.8 34.3 %collective-permute-start.56 = (bf16[7,128,256]{2,1,0:T(8,128)(2,1)}, bf16[7,128,256]{2,1,0:T(8,128)(2,1)S(1)}, u32[]{:S(2)}, u32[]{:S(2)}) collective-permute-start(bf16[7,128,256]{2,1,0:T(8,128)(2,1)} %get-tuple-element.319), channel_id=1, source_target_pairs={{0,0},{1,1},{2,16},{3,17},{16,2},{17,3},{18,18},{19,19},{4,4},{5,5... | collective-permute-start | bytes 1376264 | tf_op jit(solution)/shard_map/ppermute | solution.py:138
  265.8 41.3 %collective-permute-start.57 = (bf16[7,128,256]{2,1,0:T(8,128)(2,1)}, bf16[7,128,256]{2,1,0:T(8,128)(2,1)S(1)}, u32[]{:S(2)}, u32[]{:S(2)}) collective-permute-start(bf16[7,128,256]{2,1,0:T(8,128)(2,1)} %get-tuple-element.320), channel_id=1, source_target_pairs={{0,1},{1,0},{2,17},{3,16},{16,3},{17,2},{18,19},{19,18},{4,5},{5,4... | collective-permute-start | bytes 1376264 | tf_op jit(solution)/shard_map/ppermute | solution.py:138
  267.0 40.2 %collective-permute-start.58 = (bf16[7,128,256]{2,1,0:T(8,128)(2,1)}, bf16[7,128,256]{2,1,0:T(8,128)(2,1)S(1)}, u32[]{:S(2)}, u32[]{:S(2)}) collective-permute-start(bf16[7,128,256]{2,1,0:T(8,128)(2,1)} %get-tuple-element.321), channel_id=1, source_target_pairs={{0,2},{1,3},{2,18},{3,19},{16,0},{17,1},{18,16},{19,17},{4,6},{5,7... | collective-permute-start | bytes 1376264 | tf_op jit(solution)/shard_map/ppermute | solution.py:138
  267.0 43.2 %collective-permute-start.59 = (bf16[7,128,256]{2,1,0:T(8,128)(2,1)}, bf16[7,128,256]{2,1,0:T(8,128)(2,1)S(1)}, u32[]{:S(2)}, u32[]{:S(2)}) collective-permute-start(bf16[7,128,256]{2,1,0:T(8,128)(2,1)} %get-tuple-element.322), channel_id=1, source_target_pairs={{0,3},{1,2},{2,19},{3,18},{16,1},{17,0},{18,17},{19,16},{4,7},{5,6... | collective-permute-start | bytes 1376264 | tf_op jit(solution)/shard_map/ppermute | solution.py:138
  310.2 32.8 %collective-permute-start.60 = (bf16[7,128,256]{2,1,0:T(8,128)(2,1)}, bf16[7,128,256]{2,1,0:T(8,128)(2,1)S(1)}, u32[]{:S(2)}, u32[]{:S(2)}) collective-permute-start(bf16[7,128,256]{2,1,0:T(8,128)(2,1)} %get-tuple-element.327), channel_id=1, source_target_pairs={{0,0},{1,1},{2,16},{3,17},{16,2},{17,3},{18,18},{19,19},{4,4},{5,5... | collective-permute-start | bytes 1376264 | tf_op jit(solution)/shard_map/ppermute | solution.py:138
  312.1 40.4 %collective-permute-start.61 = (bf16[7,128,256]{2,1,0:T(8,128)(2,1)}, bf16[7,128,256]{2,1,0:T(8,128)(2,1)S(1)}, u32[]{:S(2)}, u32[]{:S(2)}) collective-permute-start(bf16[7,128,256]{2,1,0:T(8,128)(2,1)} %get-tuple-element.328), channel_id=1, source_target_pairs={{0,1},{1,0},{2,17},{3,16},{16,3},{17,2},{18,19},{19,18},{4,5},{5,4... | collective-permute-start | bytes 1376264 | tf_op jit(solution)/shard_map/ppermute | solution.py:138
  313.5 41.3 %collective-permute-start.62 = (bf16[7,128,256]{2,1,0:T(8,128)(2,1)}, bf16[7,128,256]{2,1,0:T(8,128)(2,1)S(1)}, u32[]{:S(2)}, u32[]{:S(2)}) collective-permute-start(bf16[7,128,256]{2,1,0:T(8,128)(2,1)} %get-tuple-element.329), channel_id=1, source_target_pairs={{0,2},{1,3},{2,18},{3,19},{16,0},{17,1},{18,16},{19,17},{4,6},{5,7... | collective-permute-start | bytes 1376264 | tf_op jit(solution)/shard_map/ppermute | solution.py:138
  313.5 43.7 %collective-permute-start.63 = (bf16[7,128,256]{2,1,0:T(8,128)(2,1)}, bf16[7,128,256]{2,1,0:T(8,128)(2,1)S(1)}, u32[]{:S(2)}, u32[]{:S(2)}) collective-permute-start(bf16[7,128,256]{2,1,0:T(8,128)(2,1)} %get-tuple-element.330), channel_id=1, source_target_pairs={{0,3},{1,2},{2,19},{3,18},{16,1},{17,0},{18,17},{19,16},{4,7},{5,6... | collective-permute-start | bytes 1376264 | tf_op jit(solution)/shard_map/ppermute | solution.py:138
  (22 other events, 613.2 us)

commit v5 on v4

--- a/solution.py
+++ b/solution.py
@@ -32,7 +32,7 @@
 BAND = SLAB // BLOCKS
 GROUP = COLS // 16
 HOPS = (1, 2, 4)
-LAST = (1, 2, 1)
+LAST = (2, 2)
 PIECES = (3, 4)
 HALVES = 2
 WIDE = GROUP // HALVES
@@ -307,7 +307,7 @@
         ],
         compiler_params=pltpu.CompilerParams(vmem_limit_bytes=GRAM_VMEM),
         cost_estimate=pl.CostEstimate(
-            flops=sum(len(group[0][0]) for group in groups) * BLOCK * BLOCK,
+            flops=len(own) // 2 * MINE * 2 * BLOCK * BLOCK * 2 * GROUP,
             bytes_accessed=rows << 16,
             transcendentals=0,
         ),
@@ -339,10 +339,13 @@
     )(*inputs)
 
 
-def summed(groups, parts, stage, early=()):
+def summed(groups, parts, stage, early=(), beside=None):
     inputs = []
     for g, (_, order) in enumerate(groups):
         inputs += [parts[2 * g], MOVES[order[stage]](parts[2 * g + 1])]
+    if beside is not None:
+        inputs, beside = lax.optimization_barrier((inputs, beside))
+        return add_call(groups, stage, inputs, list(early)), beside
     return add_call(groups, stage, inputs, list(early))
 
 
@@ -519,11 +522,11 @@
 
     done = []
     keep, other = cast(0, y), over_y(cast(0, 1 - y))
+    ahead = [(cast(n, y), cast(n, 1 - y)) for n in range(1, len(HOPS))]
     for n in range(len(HOPS) - 1):
-        ahead = [cast(n + 1, y), cast(n + 1, 1 - y)]
         ready, ahead, done = lax.optimization_barrier((chunks(keep, other), ahead, done))
         done.append(travel(ready))
-        keep, other = ahead[0], over_y(ahead[1])
+        keep, other = ahead[n][0], over_y(ahead[n][1])
     ready = chunks(keep, other)
     own = [joined(done)]
     done, parts, start = [], None, 0
@@ -543,14 +546,16 @@
     out, parts, done = lax.optimization_barrier((out, parts, done))
     own.append(joined(done))
     beside.append(over_core(own[1]))
-    return own, beside, summed(EARLY_GROUPS, parts, 2), out
+    return own, beside, parts, out
 
 
 def shards_cube(iterate):
     y, x, core, high, low = place()
     own, beside, early, out = panels(iterate)
-    mine = gram_call(LATE_GROUPS, own, beside)
-    for stage in range(3):
+    early, mine = summed(EARLY_GROUPS, early, 1, beside=gram_call(LATE_GROUPS, own, beside))
+    early = summed(EARLY_GROUPS, early, 2)
+    mine, early = lax.optimization_barrier((summed(LATE_GROUPS, mine, 0), early))
+    for stage in (1, 2):
         mine = summed(LATE_GROUPS, mine, stage, early)
     entries = gathered([piece[None] for piece in mine])
     keys = [key for key, _ in entries]

time: 360 us -> 354 us (0.983)
  starting transfers between devices: 62.6 us -> 56.4 us
    ppermute x11, waiting for transfers between devices: 34.7 us -> 43.2 us  [over_y(): return lax.ppermute(a, 'mats', [(0, 1), (1, 0)])]
    ppermute x8, waiting for transfers between devices: 35.8 us -> 29.5 us  [over_x(): return lax.ppermute(a, 'col', [(0, 2), (1, 3), (2, 0), (3, 1)])]
    ppermute x23 -> x20, starting transfers between devices: 25.4 us -> 21.8 us  [over_z(): return lax.ppermute(a, 'row', [(z, z ^ step) for z in range(4)])]
    ppermute x23 -> x20, waiting for transfers between devices: 77.7 us -> 75.6 us  [over_z(): return lax.ppermute(a, 'row', [(z, z ^ step) for z in range(4)])]
  transfers between devices with their start and end apart: 64 -> 61, of which waited for: 45 -> 38; matrix products, arithmetic and copies ran while one was open for 7% -> 7% of each run, Pallas kernels for 8% -> 11%
where the time goes in v5:
time: 354 us
  waiting for transfers between devices  203 us (57%)
  Pallas kernels  62 us (18%)
  starting transfers between devices  56.4 us (16%)
  other arithmetic  25.2 us (7%)
  local copies, waits for them, and re-layouts  6.4 us (2%)
    ppermute x20, waiting for transfers between devices, over_z(): return lax.ppermute(a, 'row', [(z, z ^ step) for z in range(4)])  75.6 us
    pallas_call x2, Pallas kernels, step_call(): pl.pallas_call(functools.partial(step_kernel, keys, part), out_shape=[jax...  46 us
    ppermute x11, waiting for transfers between devices, over_y(): return lax.ppermute(a, 'mats', [(0, 1), (1, 0)])  43.2 us
    ppermute x8, waiting for transfers between devices, home(): return lax.ppermute(a, ('mats', 'row'), pairs)  42.4 us
    ppermute x8, waiting for transfers between devices, over_x(): return lax.ppermute(a, 'col', [(0, 2), (1, 3), (2, 0), (3, 1)])  29.5 us
    ppermute x20, starting transfers between devices, over_z(): return lax.ppermute(a, 'row', [(z, z ^ step) for z in range(4)])  21.8 us
    dynamic_update_slice x8, other arithmetic, shards_cube(): lax.dynamic_update_slice_in_dim(out, pick(out, at, WIDE, 1) + piece, at, 1)  17.5 us
    ppermute x8, starting transfers between devices, home(): return lax.ppermute(a, ('mats', 'row'), pairs)  14.5 us
  transfers between devices with their start and end apart: 61, of which 38 were waited for; matrix products, arithmetic and copies ran while one was open for 7% of the time, Pallas kernels for 11%

profile of v5, /device:TPU:12, one launch (start us, length us, event | category | flops | bytes accessed | tf_op | source)
XLA Modules:
  0.0 353.6 jit_solution(5929692925553691380)
XLA Ops:
  1.6 1.7 dynamic-slice_convert_fusion.2
  3.3 2.5 dynamic-slice_convert_fusion
  5.9 3.3 collective-permute-done
  11.2 2.8 collective-permute-start.3
  14.4 8.8 %collective-permute-done.1 = bf16[256,1024]{1,0:T(8,128)(2,1)S(1)} collective-permute-done((bf16[256,1024]{1,0:T(8,128)(2,1)S(1)}, bf16[256,1024]{1,0:T(8,128)(2,1)S(1)}, u32[]{:S(2)}, u32[]{:S(2)}) %collective-permute-start.1) | collective-permute-done | bytes 524320 | tf_op jit(solution)/shard_map/ppermute | solution.py:94
  24.7 1.5 collective-permute-start.5
  26.2 3.0 collective-permute-start.7
  29.7 5.7 %collective-permute-done.6 = bf16[256,512]{1,0:T(8,128)(2,1)S(1)} collective-permute-done((bf16[256,512]{1,0:T(8,128)(2,1)S(1)}, bf16[256,512]{1,0:T(8,128)(2,1)S(1)}, u32[]{:S(2)}, u32[]{:S(2)}) %collective-permute-start.6) | collective-permute-done | bytes 262176 | tf_op jit(solution)/shard_map/ppermute | solution.py:98
  35.4 10.8 %collective-permute-done.7 = bf16[256,512]{1,0:T(8,128)(2,1)S(1)} collective-permute-done((bf16[256,512]{1,0:T(8,128)(2,1)S(1)}, bf16[256,512]{1,0:T(8,128)(2,1)S(1)}, u32[]{:S(2)}, u32[]{:S(2)}) %collective-permute-start.7) | collective-permute-done | bytes 262176 | tf_op jit(solution)/shard_map/ppermute | solution.py:98
  46.3 4.2 %collective-permute-done.8 = bf16[256,512]{1,0:T(8,128)(2,1)S(1)} collective-permute-done((bf16[256,512]{1,0:T(8,128)(2,1)S(1)}, bf16[256,512]{1,0:T(8,128)(2,1)S(1)}, u32[]{:S(2)}, u32[]{:S(2)}) %collective-permute-start.8) | collective-permute-done | bytes 262176 | tf_op jit(solution)/shard_map/ppermute | solution.py:98
  52.8 3.0 collective-permute-start.9
  55.9 3.3 gram.2
  59.2 10.2 %collective-permute-done.10 = bf16[256,512]{1,0:T(8,128)(2,1)S(1)} collective-permute-done((bf16[256,512]{1,0:T(8,128)(2,1)S(1)}, bf16[256,512]{1,0:T(8,128)(2,1)S(1)}, u32[]{:S(2)}, u32[]{:S(2)}) %collective-permute-start.10) | collective-permute-done | bytes 262176 | tf_op jit(solution)/shard_map/ppermute | solution.py:98
  69.4 7.1 %collective-permute-done.11 = bf16[256,512]{1,0:T(8,128)(2,1)S(1)} collective-permute-done((bf16[256,512]{1,0:T(8,128)(2,1)S(1)}, bf16[256,512]{1,0:T(8,128)(2,1)S(1)}, u32[]{:S(2)}, u32[]{:S(2)}) %collective-permute-start.11) | collective-permute-done | bytes 262176 | tf_op jit(solution)/shard_map/ppermute | solution.py:98
  76.5 1.5 collective-permute-start.13
  78.0 2.2 collective-permute-start.15
  81.5 4.7 %fusion = f32[896,2048]{1,0:T(8,128)} fusion(f32[896,2048]{1,0:T(8,128)S(1)} %bitcast.42), kind=kLoop, calls=%fused_computation.1 | loop fusion | flops 5505024 | bytes 14680064 | tf_op jit(solution)/shard_map/mul | solution.py:545
  86.2 9.9 %collective-permute-done.13.refs_1_ = bf16[784,512]{1,0:T(8,128)(2,1)S(1)} collective-permute-done((bf16[784,512]{1,0:T(8,128)(2,1)S(1)}, bf16[784,512]{1,0:T(8,128)(2,1)S(1)}, u32[]{:S(2)}, u32[]{:S(2)}) %collective-permute-start.13) | collective-permute-done | bytes 802848 | tf_op jit(solution)/shard_map/ppermute | solution.py:86
  96.7 1.5 collective-permute-done.15
  98.2 5.7 %collective-permute-done.16 = bf16[256,512]{1,0:T(8,128)(2,1)S(1)} collective-permute-done((bf16[256,512]{1,0:T(8,128)(2,1)S(1)}, bf16[256,512]{1,0:T(8,128)(2,1)S(1)}, u32[]{:S(2)}, u32[]{:S(2)}) %collective-permute-start.16) | collective-permute-done | bytes 262176 | tf_op jit(solution)/shard_map/ppermute | solution.py:98
  105.3 3.3 collective-permute-done.18.refs_3_
  108.6 10.2 %gram.3 = (f32[4,4,64,512]{3,2,1,0:T(8,128)S(1)}, bf16[1040,512]{1,0:T(8,128)(2,1)S(1)}, f32[4,4,64,512]{3,2,1,0:T(8,128)S(1)}, bf16[1040,512]{1,0:T(8,128)(2,1)...) custom-call(bf16[4,384,512]{2,1,0:T(8,128)(2,1)S(1)} %pad_maximum_fusion.1.refs_0_.refs_24_, ...), custom_call_target="tpu_custom_call" | custom-call | flops 7516192768 | bytes 458752 | tf_op jit(solution)/shard_map/gram/pallas_call | solution.py:296
  120.4 2.1 collective-permute-start.22
  122.5 21.6 %collective-permute-done.22.refs_1_ = bf16[208,512]{1,0:T(8,128)(2,1)S(1)} collective-permute-done((bf16[208,512]{1,0:T(8,128)(2,1)S(1)}, bf16[208,512]{1,0:T(8,128)(2,1)S(1)}, u32[]{:S(2)}, u32[]{:S(2)}) %collective-permute-start.22) | collective-permute-done | bytes 213024 | tf_op jit(solution)/shard_map/ppermute | solution.py:98
  146.8 1.5 collective-permute-start.25
  148.3 8.3 %collective-permute-done.25.refs_5_ = bf16[400,512]{1,0:T(8,128)(2,1)S(1)} collective-permute-done((bf16[400,512]{1,0:T(8,128)(2,1)S(1)}, bf16[400,512]{1,0:T(8,128)(2,1)S(1)}, u32[]{:S(2)}, u32[]{:S(2)}) %collective-permute-start.25) | collective-permute-done | bytes 409632 | tf_op jit(solution)/shard_map/ppermute | solution.py:86
  156.6 2.3 collective-permute-done.23.refs_1_
  160.3 1.5 collective-permute-start.27
  162.9 4.6 %collective-permute-done.28.refs_5_ = bf16[208,512]{1,0:T(8,128)(2,1)S(1)} collective-permute-done((bf16[208,512]{1,0:T(8,128)(2,1)S(1)}, bf16[208,512]{1,0:T(8,128)(2,1)S(1)}, u32[]{:S(2)}, u32[]{:S(2)}) %collective-permute-start.28) | collective-permute-done | bytes 213024 | tf_op jit(solution)/shard_map/ppermute | solution.py:94
  167.8 2.4 collective-permute-start.31
  171.5 3.1 collective-permute-done.31
  174.6 3.6 %collective-permute-done.30 = bf16[1,5,64,512]{3,2,1,0:T(8,128)(2,1)S(1)} collective-permute-done((bf16[1,5,64,512]{3,2,1,0:T(8,128)(2,1)S(1)}, bf16[1,5,64,512]{3,2,1,0:T(8,128)(2,1)S(1)}, u32[]{:S(2)}, u32[]{:S(2)}) %collective-permute-start.30) | collective-permute-done | bytes 327712 | tf_op jit(solution)/shard_map/ppermute | solution.py:94
  178.3 2.7 collective-permute-done.29
  181.2 1.4 collective-permute-start.32
  183.1 7.3 %collective-permute-done.34.refs_8_ = bf16[2,4,64,512]{3,2,1,0:T(8,128)(2,1)S(1)} collective-permute-done((bf16[2,4,64,512]{3,2,1,0:T(8,128)(2,1)S(1)}, bf16[2,4,64,512]{3,2,1,0:T(8,128)(2,1)S(1)}, u32[]{:S(2)}, u32[]{:S(2)}) %collective-permute-start.34) | collective-permute-done | bytes 524320 | tf_op jit(solution)/shard_map/ppermute | solution.py:86
  190.4 1.9 collective-permute-done.37.refs_5_
  194.4 1.5 collective-permute-start.39
  196.4 10.6 %collective-permute-done.40.refs_14_ = bf16[2,4,64,512]{3,2,1,0:T(8,128)(2,1)S(1)} collective-permute-done((bf16[2,4,64,512]{3,2,1,0:T(8,128)(2,1)S(1)}, bf16[2,4,64,512]{3,2,1,0:T(8,128)(2,1)S(1)}, u32[]{:S(2)}, u32[]{:S(2)}) %collective-permute-start.40) | collective-permute-done | bytes 524320 | tf_op jit(solution)/shard_map/ppermute | solution.py:94
  207.1 1.9 collective-permute-done.43.refs_11_
  209.0 2.0 collective-permute-done.38.refs_12_
  211.7 1.7 collective-permute-start.44
  214.2 9.7 %collective-permute-done.46.refs_20_ = bf16[2,4,64,512]{3,2,1,0:T(8,128)(2,1)} collective-permute-done((bf16[2,4,64,512]{3,2,1,0:T(8,128)(2,1)S(1)}, bf16[2,4,64,512]{3,2,1,0:T(8,128)(2,1)}, u32[]{:S(2)}, u32[]{:S(2)}) %collective-permute-start.46) | collective-permute-done | bytes 524320 | tf_op jit(solution)/shard_map/ppermute | solution.py:94
  224.0 1.9 collective-permute-done.49.refs_17_
  229.2 3.1 collective-permute-done.52.refs_23_
  232.4 23.1 %step.2 = (bf16[7,128,256]{2,1,0:T(8,128)(2,1)}, bf16[7,128,256]{2,1,0:T(8,128)(2,1)}, bf16[7,128,256]{2,1,0:T(8,128)(2,1)}, bf16[7,128,256]{2,1,0:T(8,128)(2,1)}) custom-call(bf16[2,5,64,512]{3,2,1,0:T(8,128)(2,1)} %copy-done.3, bf16[2,5,64,512]{3,2,1,0:T(8,128)(2,1)} %copy-done.2, bf16[2,4,64,512]{3,2,1,0:T(8,128)(2,1)} %copy-done.4, ...), custom_call_target="tpu_custom_call" | custom-call | flops 13153337344 | bytes 20971520 | tf_op jit(solution)/shard_map/step/pallas_call | solution.py:474
  255.5 3.7 %collective-permute-start.53 = (bf16[7,128,256]{2,1,0:T(8,128)(2,1)}, bf16[7,128,256]{2,1,0:T(8,128)(2,1)S(1)}, u32[]{:S(2)}, u32[]{:S(2)}) collective-permute-start(bf16[7,128,256]{2,1,0:T(8,128)(2,1)} %get-tuple-element.307), channel_id=1, source_target_pairs={{0,0},{1,1},{2,16},{3,17},{16,2},{17,3},{18,18},{19,19},{4,4},{5,5... | collective-permute-start | bytes 1376264 | tf_op jit(solution)/shard_map/ppermute | solution.py:138
  260.6 3.1 collective-permute-start.56
  263.6 22.9 %step.3 = (bf16[7,128,256]{2,1,0:T(8,128)(2,1)}, bf16[7,128,256]{2,1,0:T(8,128)(2,1)}, bf16[7,128,256]{2,1,0:T(8,128)(2,1)}, bf16[7,128,256]{2,1,0:T(8,128)(2,1)}) custom-call(bf16[2,5,64,512]{3,2,1,0:T(8,128)(2,1)} %copy-done.3, bf16[2,5,64,512]{3,2,1,0:T(8,128)(2,1)} %copy-done.2, bf16[2,4,64,512]{3,2,1,0:T(8,128)(2,1)} %copy-done.4, ...), custom_call_target="tpu_custom_call" | custom-call | flops 13153337344 | bytes 20971520 | tf_op jit(solution)/shard_map/step/pallas_call | solution.py:474
  286.5 3.5 collective-permute-done.53
  290.0 10.7 %collective-permute-done.54 = bf16[7,128,256]{2,1,0:T(8,128)(2,1)S(1)} collective-permute-done((bf16[7,128,256]{2,1,0:T(8,128)(2,1)}, bf16[7,128,256]{2,1,0:T(8,128)(2,1)S(1)}, u32[]{:S(2)}, u32[]{:S(2)}) %collective-permute-start.54) | collective-permute-done | bytes 458784 | tf_op jit(solution)/shard_map/ppermute | solution.py:138
  300.7 3.3 collective-permute-done.56
  304.0 1.9 collective-permute-start.57
  305.9 1.7 collective-permute-start.58
  307.6 2.7 collective-permute-start.60
  310.4 2.2 constant_dynamic-update-slice_fusion.7
  312.7 2.2 constant_dynamic-update-slice_fusion.6
  315.0 2.2 constant_dynamic-update-slice_fusion.5
  317.3 2.2 constant_dynamic-update-slice_fusion.4
  319.5 17.3 %collective-permute-done.57 = bf16[7,128,256]{2,1,0:T(8,128)(2,1)S(1)} collective-permute-done((bf16[7,128,256]{2,1,0:T(8,128)(2,1)}, bf16[7,128,256]{2,1,0:T(8,128)(2,1)S(1)}, u32[]{:S(2)}, u32[]{:S(2)}) %collective-permute-start.57) | collective-permute-done | bytes 458784 | tf_op jit(solution)/shard_map/ppermute | solution.py:138
  336.9 2.2 constant_dynamic-update-slice_fusion.3
  339.1 7.6 %collective-permute-done.58 = bf16[7,128,256]{2,1,0:T(8,128)(2,1)S(1)} collective-permute-done((bf16[7,128,256]{2,1,0:T(8,128)(2,1)}, bf16[7,128,256]{2,1,0:T(8,128)(2,1)S(1)}, u32[]{:S(2)}, u32[]{:S(2)}) %collective-permute-start.58) | collective-permute-done | bytes 458784 | tf_op jit(solution)/shard_map/ppermute | solution.py:138
  346.8 2.2 constant_dynamic-update-slice_fusion.2
  349.1 2.2 constant_dynamic-update-slice_fusion.1
  351.4 2.2 constant_dynamic-update-slice_fusion
  (160 shorter events, 30.2 us)
Async XLA Ops:
  1.1 8.1 %collective-permute-start = (bf16[128,1024]{1,0:T(8,128)(2,1)S(1)}, bf16[128,1024]{1,0:T(8,128)(2,1)S(1)}, u32[]{:S(2)}, u32[]{:S(2)}) collective-permute-start(bf16[128,1024]{1,0:T(8,128)(2,1)S(1)} %dynamic-slice_convert_fusion.4), channel_id=1, source_target_pairs={{0,16},{16,0},{1,17},{17,1},{2,18},{18,2},{3,19},{19,3},{4,20},{20... | collective-permute-start | bytes 786440 | tf_op jit(solution)/shard_map/ppermute | solution.py:94
  10.4 12.9 %collective-permute-start.1 = (bf16[256,1024]{1,0:T(8,128)(2,1)S(1)}, bf16[256,1024]{1,0:T(8,128)(2,1)S(1)}, u32[]{:S(2)}, u32[]{:S(2)}) collective-permute-start(bf16[256,1024]{1,0:T(8,128)(2,1)S(1)} %get-tuple-element.163), channel_id=1, source_target_pairs={{0,16},{16,0},{1,17},{17,1},{2,18},{18,2},{3,19},{19,3},{4,20},{20... | collective-permute-start | bytes 1572872 | tf_op jit(solution)/shard_map/ppermute | solution.py:94
  10.9 12.5 %collective-permute-start.2 = (bf16[128,512]{1,0:T(8,128)(2,1)S(1)}, bf16[128,512]{1,0:T(8,128)(2,1)S(1)}, u32[]{:S(2)}, u32[]{:S(2)}) collective-permute-start(bf16[128,512]{1,0:T(8,128)(2,1)S(1)} %get-tuple-element.167), channel_id=1, source_target_pairs={{0,1},{1,0},{2,3},{3,2},{4,5},{5,4},{6,7},{7,6},{8,9},{9,8},{10,11... | collective-permute-start | bytes 393224 | tf_op jit(solution)/shard_map/ppermute | solution.py:98
  11.2 12.3 %collective-permute-start.3 = (bf16[128,512]{1,0:T(8,128)(2,1)S(1)}, bf16[128,512]{1,0:T(8,128)(2,1)S(1)}, u32[]{:S(2)}, u32[]{:S(2)}) collective-permute-start(bf16[128,512]{1,0:T(8,128)(2,1)S(1)} %get-tuple-element.168), channel_id=1, source_target_pairs={{0,2},{1,3},{2,0},{3,1},{4,6},{5,7},{6,4},{7,5},{8,10},{9,11},{10,... | collective-permute-start | bytes 393224 | tf_op jit(solution)/shard_map/ppermute | solution.py:98
  14.0 10.7 %collective-permute-start.4 = (bf16[128,512]{1,0:T(8,128)(2,1)S(1)}, bf16[128,512]{1,0:T(8,128)(2,1)S(1)}, u32[]{:S(2)}, u32[]{:S(2)}) collective-permute-start(bf16[128,512]{1,0:T(8,128)(2,1)S(1)} %get-tuple-element.169), channel_id=1, source_target_pairs={{0,3},{1,2},{2,1},{3,0},{4,7},{5,6},{6,5},{7,4},{8,11},{9,10},{10,... | collective-permute-start | bytes 393224 | tf_op jit(solution)/shard_map/ppermute | solution.py:98
  24.7 26.1 %collective-permute-start.5 = (bf16[512,1024]{1,0:T(8,128)(2,1)S(1)}, bf16[512,1024]{1,0:T(8,128)(2,1)S(1)}, u32[]{:S(2)}, u32[]{:S(2)}) collective-permute-start(bf16[512,1024]{1,0:T(8,128)(2,1)S(1)} %get-tuple-element.171), channel_id=1, source_target_pairs={{0,16},{16,0},{1,17},{17,1},{2,18},{18,2},{3,19},{19,3},{4,20},{20... | collective-permute-start | bytes 3145736 | tf_op jit(solution)/shard_map/ppermute | solution.py:94
  26.2 9.2 %collective-permute-start.6 = (bf16[256,512]{1,0:T(8,128)(2,1)S(1)}, bf16[256,512]{1,0:T(8,128)(2,1)S(1)}, u32[]{:S(2)}, u32[]{:S(2)}) collective-permute-start(bf16[256,512]{1,0:T(8,128)(2,1)S(1)} %get-tuple-element.175), channel_id=1, source_target_pairs={{0,1},{1,0},{2,3},{3,2},{4,5},{5,4},{6,7},{7,6},{8,9},{9,8},{10,11... | collective-permute-start | bytes 786440 | tf_op jit(solution)/shard_map/ppermute | solution.py:98
  26.2 20.1 %collective-permute-start.7 = (bf16[256,512]{1,0:T(8,128)(2,1)S(1)}, bf16[256,512]{1,0:T(8,128)(2,1)S(1)}, u32[]{:S(2)}, u32[]{:S(2)}) collective-permute-start(bf16[256,512]{1,0:T(8,128)(2,1)S(1)} %get-tuple-element.177), channel_id=1, source_target_pairs={{0,2},{1,3},{2,0},{3,1},{4,6},{5,7},{6,4},{7,5},{8,10},{9,11},{10,... | collective-permute-start | bytes 786440 | tf_op jit(solution)/shard_map/ppermute | solution.py:98
  29.2 21.2 %collective-permute-start.8 = (bf16[256,512]{1,0:T(8,128)(2,1)S(1)}, bf16[256,512]{1,0:T(8,128)(2,1)S(1)}, u32[]{:S(2)}, u32[]{:S(2)}) collective-permute-start(bf16[256,512]{1,0:T(8,128)(2,1)S(1)} %get-tuple-element.179), channel_id=1, source_target_pairs={{0,3},{1,2},{2,1},{3,0},{4,7},{5,6},{6,5},{7,4},{8,11},{9,10},{10,... | collective-permute-start | bytes 786440 | tf_op jit(solution)/shard_map/ppermute | solution.py:98
  50.7 57.8 %copy-start = (bf16[4,384,512]{2,1,0:T(8,128)(2,1)}, bf16[4,384,512]{2,1,0:T(8,128)(2,1)S(1)}, u32[]{:S(2)}) copy-start(bf16[4,384,512]{2,1,0:T(8,128)(2,1)S(1)} %pad_maximum_fusion.1.refs_0_.refs_24_) | copy-start | bytes 4718596
  51.3 4.6 %collective-permute-start.12 = (bf16[4,384,512]{2,1,0:T(8,128)(2,1)S(1)}, bf16[4,384,512]{2,1,0:T(8,128)(2,1)S(1)}, u32[]{:S(2)}, u32[]{:S(2)}) collective-permute-start(bf16[4,384,512]{2,1,0:T(8,128)(2,1)S(1)} %pad_maximum_fusion.1.refs_0_.refs_24_), channel_id=1, source_target_pairs={{0,4},{4,0},{8,12},{12,8},{1,5},{5,1},{9,13},{13,9},{2,6},{6,2},{1... | collective-permute-start | bytes 4718600 | tf_op jit(solution)/shard_map/ppermute | solution.py:90
  51.3 18.0 %collective-permute-start.10 = (bf16[256,512]{1,0:T(8,128)(2,1)S(1)}, bf16[256,512]{1,0:T(8,128)(2,1)S(1)}, u32[]{:S(2)}, u32[]{:S(2)}) collective-permute-start(bf16[256,512]{1,0:T(8,128)(2,1)S(1)} %get-tuple-element.186), channel_id=1, source_target_pairs={{0,2},{1,3},{2,0},{3,1},{4,6},{5,7},{6,4},{7,5},{8,10},{9,11},{10,... | collective-permute-start | bytes 786440 | tf_op jit(solution)/shard_map/ppermute | solution.py:98
  51.4 25.1 %collective-permute-start.11 = (bf16[256,512]{1,0:T(8,128)(2,1)S(1)}, bf16[256,512]{1,0:T(8,128)(2,1)S(1)}, u32[]{:S(2)}, u32[]{:S(2)}) collective-permute-start(bf16[256,512]{1,0:T(8,128)(2,1)S(1)} %get-tuple-element.187), channel_id=1, source_target_pairs={{0,3},{1,2},{2,1},{3,0},{4,7},{5,6},{6,5},{7,4},{8,11},{9,10},{10,... | collective-permute-start | bytes 786440 | tf_op jit(solution)/shard_map/ppermute | solution.py:98
  52.8 23.7 %collective-permute-start.9 = (bf16[256,512]{1,0:T(8,128)(2,1)S(1)}, bf16[256,512]{1,0:T(8,128)(2,1)S(1)}, u32[]{:S(2)}, u32[]{:S(2)}) collective-permute-start(bf16[256,512]{1,0:T(8,128)(2,1)S(1)} %get-tuple-element.185), channel_id=1, source_target_pairs={{0,1},{1,0},{2,3},{3,2},{4,5},{5,4},{6,7},{7,6},{8,9},{9,8},{10,11... | collective-permute-start | bytes 786440 | tf_op jit(solution)/shard_map/ppermute | solution.py:98
  76.5 19.6 %collective-permute-start.13 = (bf16[784,512]{1,0:T(8,128)(2,1)S(1)}, bf16[784,512]{1,0:T(8,128)(2,1)S(1)}, u32[]{:S(2)}, u32[]{:S(2)}) collective-permute-start(bf16[784,512]{1,0:T(8,128)(2,1)S(1)} %get-tuple-element.192), channel_id=1, source_target_pairs={{0,8},{4,12},{8,0},{12,4},{1,9},{5,13},{9,1},{13,5},{2,10},{6,14},... | collective-permute-start | bytes 2408456 | tf_op jit(solution)/shard_map/ppermute | solution.py:86
  78.0 18.7 %collective-permute-start.14 = (bf16[256,512]{1,0:T(8,128)(2,1)S(1)}, bf16[256,512]{1,0:T(8,128)(2,1)S(1)}, u32[]{:S(2)}, u32[]{:S(2)}) collective-permute-start(bf16[256,512]{1,0:T(8,128)(2,1)S(1)} %slice.29), channel_id=1, source_target_pairs={{0,1},{1,0},{2,3},{3,2},{4,5},{5,4},{6,7},{7,6},{8,9},{9,8},{10,11... | collective-permute-start | bytes 786440 | tf_op jit(solution)/shard_map/ppermute | solution.py:98
  78.0 20.2 %collective-permute-start.15 = (bf16[256,512]{1,0:T(8,128)(2,1)S(1)}, bf16[256,512]{1,0:T(8,128)(2,1)S(1)}, u32[]{:S(2)}, u32[]{:S(2)}) collective-permute-start(bf16[256,512]{1,0:T(8,128)(2,1)S(1)} %slice.30), channel_id=1, source_target_pairs={{0,2},{1,3},{2,0},{3,1},{4,6},{5,7},{6,4},{7,5},{8,10},{9,11},{10,... | collective-permute-start | bytes 786440 | tf_op jit(solution)/shard_map/ppermute | solution.py:98
  80.2 23.7 %collective-permute-start.16 = (bf16[256,512]{1,0:T(8,128)(2,1)S(1)}, bf16[256,512]{1,0:T(8,128)(2,1)S(1)}, u32[]{:S(2)}, u32[]{:S(2)}) collective-permute-start(bf16[256,512]{1,0:T(8,128)(2,1)S(1)} %slice.31), channel_id=1, source_target_pairs={{0,3},{1,2},{2,1},{3,0},{4,7},{5,6},{6,5},{7,4},{8,11},{9,10},{10,... | collective-permute-start | bytes 786440 | tf_op jit(solution)/shard_map/ppermute | solution.py:98
  104.3 4.2 %collective-permute-start.18 = (bf16[4,512,512]{2,1,0:T(8,128)(2,1)S(1)}, bf16[4,512,512]{2,1,0:T(8,128)(2,1)S(1)}, u32[]{:S(2)}, u32[]{:S(2)}) collective-permute-start(bf16[4,512,512]{2,1,0:T(8,128)(2,1)S(1)} %pad_maximum_fusion.refs_1_.refs_25_), channel_id=1, source_target_pairs={{0,4},{4,0},{8,12},{12,8},{1,5},{5,1},{9,13},{13,9},{2,6},{6,2},{1... | collective-permute-start | bytes 6291464 | tf_op jit(solution)/shard_map/ppermute | solution.py:90
  104.4 14.3 %collective-permute-start.17 = (bf16[400,512]{1,0:T(8,128)(2,1)S(1)}, bf16[400,512]{1,0:T(8,128)(2,1)S(1)}, u32[]{:S(2)}, u32[]{:S(2)}) collective-permute-start(bf16[400,512]{1,0:T(8,128)(2,1)S(1)} %get-tuple-element.205), channel_id=1, source_target_pairs={{0,16},{16,0},{1,17},{17,1},{2,18},{18,2},{3,19},{19,3},{4,20},{20... | collective-permute-start | bytes 1228808 | tf_op jit(solution)/shard_map/ppermute | solution.py:94
  118.8 25.6 %collective-permute-start.19 = (bf16[1040,512]{1,0:T(8,128)(2,1)S(1)}, bf16[1040,512]{1,0:T(8,128)(2,1)S(1)}, u32[]{:S(2)}, u32[]{:S(2)}) collective-permute-start(bf16[1040,512]{1,0:T(8,128)(2,1)S(1)} %get-tuple-element.222), channel_id=1, source_target_pairs={{0,8},{4,12},{8,0},{12,4},{1,9},{5,13},{9,1},{13,5},{2,10},{6,14},... | collective-permute-start | bytes 3194888 | tf_op jit(solution)/shard_map/ppermute | solution.py:86
  119.4 25.3 %collective-permute-start.20 = (bf16[1040,512]{1,0:T(8,128)(2,1)S(1)}, bf16[1040,512]{1,0:T(8,128)(2,1)S(1)}, u32[]{:S(2)}, u32[]{:S(2)}) collective-permute-start(bf16[1040,512]{1,0:T(8,128)(2,1)S(1)} %get-tuple-element.224), channel_id=1, source_target_pairs={{0,16},{16,0},{1,17},{17,1},{2,18},{18,2},{3,19},{19,3},{4,20},{20... | collective-permute-start | bytes 3194888 | tf_op jit(solution)/shard_map/ppermute | solution.py:94
  120.2 24.0 %collective-permute-start.21 = (bf16[784,512]{1,0:T(8,128)(2,1)S(1)}, bf16[784,512]{1,0:T(8,128)(2,1)S(1)}, u32[]{:S(2)}, u32[]{:S(2)}) collective-permute-start(bf16[784,512]{1,0:T(8,128)(2,1)S(1)} %get-tuple-element.226), channel_id=1, source_target_pairs={{0,1},{1,0},{2,3},{3,2},{4,5},{5,4},{6,7},{7,6},{8,9},{9,8},{10,11... | collective-permute-start | bytes 2408456 | tf_op jit(solution)/shard_map/ppermute | solution.py:98
  120.4 23.7 %collective-permute-start.22 = (bf16[208,512]{1,0:T(8,128)(2,1)S(1)}, bf16[208,512]{1,0:T(8,128)(2,1)S(1)}, u32[]{:S(2)}, u32[]{:S(2)}) collective-permute-start(bf16[208,512]{1,0:T(8,128)(2,1)S(1)} %get-tuple-element.236), channel_id=1, source_target_pairs={{0,1},{1,0},{2,3},{3,2},{4,5},{5,4},{6,7},{7,6},{8,9},{9,8},{10,11... | collective-permute-start | bytes 638984 | tf_op jit(solution)/shard_map/ppermute | solution.py:98
  145.6 13.3 %collective-permute-start.23 = (bf16[528,512]{1,0:T(8,128)(2,1)S(1)}, bf16[528,512]{1,0:T(8,128)(2,1)S(1)}, u32[]{:S(2)}, u32[]{:S(2)}) collective-permute-start(bf16[528,512]{1,0:T(8,128)(2,1)S(1)} %get-tuple-element.238), channel_id=1, source_target_pairs={{0,16},{16,0},{1,17},{17,1},{2,18},{18,2},{3,19},{19,3},{4,20},{20... | collective-permute-start | bytes 1622024 | tf_op jit(solution)/shard_map/ppermute | solution.py:94
  146.5 12.9 %collective-permute-start.24 = (bf16[528,512]{1,0:T(8,128)(2,1)S(1)}, bf16[528,512]{1,0:T(8,128)(2,1)S(1)}, u32[]{:S(2)}, u32[]{:S(2)}) collective-permute-start(bf16[528,512]{1,0:T(8,128)(2,1)S(1)} %get-tuple-element.240), channel_id=1, source_target_pairs={{0,1},{1,0},{2,3},{3,2},{4,5},{5,4},{6,7},{7,6},{8,9},{9,8},{10,11... | collective-permute-start | bytes 1622024 | tf_op jit(solution)/shard_map/ppermute | solution.py:98
  146.8 9.8 %collective-permute-start.25 = (bf16[400,512]{1,0:T(8,128)(2,1)S(1)}, bf16[400,512]{1,0:T(8,128)(2,1)S(1)}, u32[]{:S(2)}, u32[]{:S(2)}) collective-permute-start(bf16[400,512]{1,0:T(8,128)(2,1)S(1)} %get-tuple-element.242), channel_id=1, source_target_pairs={{0,8},{4,12},{8,0},{12,4},{1,9},{5,13},{9,1},{13,5},{2,10},{6,14},... | collective-permute-start | bytes 1228808 | tf_op jit(solution)/shard_map/ppermute | solution.py:86
  159.9 7.7 %collective-permute-start.26 = (bf16[272,512]{1,0:T(8,128)(2,1)S(1)}, bf16[272,512]{1,0:T(8,128)(2,1)S(1)}, u32[]{:S(2)}, u32[]{:S(2)}) collective-permute-start(bf16[272,512]{1,0:T(8,128)(2,1)S(1)} %get-tuple-element.244), channel_id=1, source_target_pairs={{0,1},{1,0},{2,3},{3,2},{4,5},{5,4},{6,7},{7,6},{8,9},{9,8},{10,11... | collective-permute-start | bytes 835592 | tf_op jit(solution)/shard_map/ppermute | solution.py:98
  160.3 7.3 %collective-permute-start.27 = (bf16[272,512]{1,0:T(8,128)(2,1)S(1)}, bf16[272,512]{1,0:T(8,128)(2,1)S(1)}, u32[]{:S(2)}, u32[]{:S(2)}) collective-permute-start(bf16[272,512]{1,0:T(8,128)(2,1)S(1)} %get-tuple-element.246), channel_id=1, source_target_pairs={{0,8},{4,12},{8,0},{12,4},{1,9},{5,13},{9,1},{13,5},{2,10},{6,14},... | collective-permute-start | bytes 835592 | tf_op jit(solution)/shard_map/ppermute | solution.py:86
  161.7 5.8 %collective-permute-start.28 = (bf16[208,512]{1,0:T(8,128)(2,1)S(1)}, bf16[208,512]{1,0:T(8,128)(2,1)S(1)}, u32[]{:S(2)}, u32[]{:S(2)}) collective-permute-start(bf16[208,512]{1,0:T(8,128)(2,1)S(1)} %get-tuple-element.248), channel_id=1, source_target_pairs={{0,16},{16,0},{1,17},{17,1},{2,18},{18,2},{3,19},{19,3},{4,20},{20... | collective-permute-start | bytes 638984 | tf_op jit(solution)/shard_map/ppermute | solution.py:94
  167.8 6.8 %collective-permute-start.31 = (bf16[1,4,64,512]{3,2,1,0:T(8,128)(2,1)S(1)}, bf16[1,4,64,512]{3,2,1,0:T(8,128)(2,1)S(1)}, u32[]{:S(2)}, u32[]{:S(2)}) collective-permute-start(bf16[1,4,64,512]{3,2,1,0:T(8,128)(2,1)S(1)} %bitcast.39), channel_id=1, source_target_pairs={{0,1},{1,0},{2,3},{3,2},{4,5},{5,4},{6,7},{7,6},{8,9},{9,8},{10,11... | collective-permute-start | bytes 786440 | tf_op jit(solution)/shard_map/ppermute | solution.py:98
  170.2 8.0 %collective-permute-start.30 = (bf16[1,5,64,512]{3,2,1,0:T(8,128)(2,1)S(1)}, bf16[1,5,64,512]{3,2,1,0:T(8,128)(2,1)S(1)}, u32[]{:S(2)}, u32[]{:S(2)}) collective-permute-start(bf16[1,5,64,512]{3,2,1,0:T(8,128)(2,1)S(1)} %bitcast.37), channel_id=1, source_target_pairs={{0,16},{16,0},{1,17},{17,1},{2,18},{18,2},{3,19},{19,3},{4,20},{20... | collective-permute-start | bytes 983048 | tf_op jit(solution)/shard_map/ppermute | solution.py:94
  171.2 9.8 %collective-permute-start.29 = (bf16[1,5,64,512]{3,2,1,0:T(8,128)(2,1)S(1)}, bf16[1,5,64,512]{3,2,1,0:T(8,128)(2,1)S(1)}, u32[]{:S(2)}, u32[]{:S(2)}) collective-permute-start(bf16[1,5,64,512]{3,2,1,0:T(8,128)(2,1)S(1)} %bitcast.35), channel_id=1, source_target_pairs={{0,8},{4,12},{8,0},{12,4},{1,9},{5,13},{9,1},{13,5},{2,10},{6,14},... | collective-permute-start | bytes 983048 | tf_op jit(solution)/shard_map/ppermute | solution.py:86
  174.6 57.7 %copy-start.4 = (bf16[2,4,64,512]{3,2,1,0:T(8,128)(2,1)}, bf16[2,4,64,512]{3,2,1,0:T(8,128)(2,1)S(1)}, u32[]{:S(2)}) copy-start(bf16[2,4,64,512]{3,2,1,0:T(8,128)(2,1)S(1)} %pad_maximum_fusion.4.refs_2_) | copy-start | bytes 1572868
  178.3 54.1 %copy-start.2 = (bf16[2,5,64,512]{3,2,1,0:T(8,128)(2,1)}, bf16[2,5,64,512]{3,2,1,0:T(8,128)(2,1)S(1)}, u32[]{:S(2)}) copy-start(bf16[2,5,64,512]{3,2,1,0:T(8,128)(2,1)S(1)} %pad_maximum_fusion.3.refs_1_) | copy-start | bytes 1966084
  181.1 9.2 %collective-permute-start.34 = (bf16[2,4,64,512]{3,2,1,0:T(8,128)(2,1)S(1)}, bf16[2,4,64,512]{3,2,1,0:T(8,128)(2,1)S(1)}, u32[]{:S(2)}, u32[]{:S(2)}) collective-permute-start(bf16[2,4,64,512]{3,2,1,0:T(8,128)(2,1)S(1)} %pad_maximum_fusion.4.refs_2_), channel_id=1, source_target_pairs={{0,8},{4,12},{8,0},{12,4},{1,9},{5,13},{9,1},{13,5},{2,10},{6,14},... | collective-permute-start | bytes 1572872 | tf_op jit(solution)/shard_map/ppermute | solution.py:86
  181.2 11.1 %collective-permute-start.32 = (bf16[2,5,64,512]{3,2,1,0:T(8,128)(2,1)S(1)}, bf16[2,5,64,512]{3,2,1,0:T(8,128)(2,1)S(1)}, u32[]{:S(2)}, u32[]{:S(2)}) collective-permute-start(bf16[2,5,64,512]{3,2,1,0:T(8,128)(2,1)S(1)} %pad_maximum_fusion.2.refs_0_), channel_id=1, source_target_pairs={{0,16},{16,0},{1,17},{17,1},{2,18},{18,2},{3,19},{19,3},{4,20},{20... | collective-permute-start | bytes 1966088 | tf_op jit(solution)/shard_map/ppermute | solution.py:94
  182.6 10.6 %collective-permute-start.33 = (bf16[2,5,64,512]{3,2,1,0:T(8,128)(2,1)S(1)}, bf16[2,5,64,512]{3,2,1,0:T(8,128)(2,1)S(1)}, u32[]{:S(2)}, u32[]{:S(2)}) collective-permute-start(bf16[2,5,64,512]{3,2,1,0:T(8,128)(2,1)S(1)} %pad_maximum_fusion.3.refs_1_), channel_id=1, source_target_pairs={{0,1},{1,0},{2,3},{3,2},{4,5},{5,4},{6,7},{7,6},{8,9},{9,8},{10,11... | collective-permute-start | bytes 1966088 | tf_op jit(solution)/shard_map/ppermute | solution.py:98
  182.6 10.6 %collective-permute-start.35 = (bf16[2,5,64,512]{3,2,1,0:T(8,128)(2,1)S(1)}, bf16[2,5,64,512]{3,2,1,0:T(8,128)(2,1)S(1)}, u32[]{:S(2)}, u32[]{:S(2)}) collective-permute-start(bf16[2,5,64,512]{3,2,1,0:T(8,128)(2,1)S(1)} %pad_maximum_fusion.2.refs_0_), channel_id=1, source_target_pairs={{0,4},{4,0},{8,12},{12,8},{1,5},{5,1},{9,13},{13,9},{2,6},{6,2},{1... | collective-permute-start | bytes 1966088 | tf_op jit(solution)/shard_map/ppermute | solution.py:90
  182.6 10.6 %collective-permute-start.36 = (bf16[2,5,64,512]{3,2,1,0:T(8,128)(2,1)S(1)}, bf16[2,5,64,512]{3,2,1,0:T(8,128)(2,1)S(1)}, u32[]{:S(2)}, u32[]{:S(2)}) collective-permute-start(bf16[2,5,64,512]{3,2,1,0:T(8,128)(2,1)S(1)} %pad_maximum_fusion.3.refs_1_), channel_id=1, source_target_pairs={{0,4},{4,0},{8,12},{12,8},{1,5},{5,1},{9,13},{13,9},{2,6},{6,2},{1... | collective-permute-start | bytes 1966088 | tf_op jit(solution)/shard_map/ppermute | solution.py:90
  190.4 1.9 collective-permute-start.37
  193.2 13.8 %collective-permute-start.40 = (bf16[2,4,64,512]{3,2,1,0:T(8,128)(2,1)S(1)}, bf16[2,4,64,512]{3,2,1,0:T(8,128)(2,1)S(1)}, u32[]{:S(2)}, u32[]{:S(2)}) collective-permute-start(bf16[2,4,64,512]{3,2,1,0:T(8,128)(2,1)S(1)} %pad_maximum_fusion.4.refs_2_), channel_id=1, source_target_pairs={{0,16},{16,0},{1,17},{17,1},{2,18},{18,2},{3,19},{19,3},{4,20},{20... | collective-permute-start | bytes 1572872 | tf_op jit(solution)/shard_map/ppermute | solution.py:94
  194.4 16.5 %collective-permute-start.38 = (bf16[2,5,64,512]{3,2,1,0:T(8,128)(2,1)S(1)}, bf16[2,5,64,512]{3,2,1,0:T(8,128)(2,1)S(1)}, u32[]{:S(2)}, u32[]{:S(2)}) collective-permute-start(bf16[2,5,64,512]{3,2,1,0:T(8,128)(2,1)S(1)} %pad_maximum_fusion.2.refs_0_), channel_id=1, source_target_pairs={{0,1},{1,0},{2,3},{3,2},{4,5},{5,4},{6,7},{7,6},{8,9},{9,8},{10,11... | collective-permute-start | bytes 1966088 | tf_op jit(solution)/shard_map/ppermute | solution.py:98
  194.4 16.5 %collective-permute-start.39 = (bf16[2,5,64,512]{3,2,1,0:T(8,128)(2,1)S(1)}, bf16[2,5,64,512]{3,2,1,0:T(8,128)(2,1)S(1)}, u32[]{:S(2)}, u32[]{:S(2)}) collective-permute-start(bf16[2,5,64,512]{3,2,1,0:T(8,128)(2,1)S(1)} %pad_maximum_fusion.3.refs_1_), channel_id=1, source_target_pairs={{0,8},{4,12},{8,0},{12,4},{1,9},{5,13},{9,1},{13,5},{2,10},{6,14},... | collective-permute-start | bytes 1966088 | tf_op jit(solution)/shard_map/ppermute | solution.py:86
  195.9 15.0 %collective-permute-start.41 = (bf16[2,5,64,512]{3,2,1,0:T(8,128)(2,1)S(1)}, bf16[2,5,64,512]{3,2,1,0:T(8,128)(2,1)S(1)}, u32[]{:S(2)}, u32[]{:S(2)}) collective-permute-start(bf16[2,5,64,512]{3,2,1,0:T(8,128)(2,1)S(1)} %collective-permute-done.32.refs_6_), channel_id=1, source_target_pairs={{0,4},{4,0},{8,12},{12,8},{1,5},{5,1},{9,13},{13,9},{2,6},{6,2},{1... | collective-permute-start | bytes 1966088 | tf_op jit(solution)/shard_map/ppermute | solution.py:90
  195.9 15.0 %collective-permute-start.42 = (bf16[2,5,64,512]{3,2,1,0:T(8,128)(2,1)S(1)}, bf16[2,5,64,512]{3,2,1,0:T(8,128)(2,1)S(1)}, u32[]{:S(2)}, u32[]{:S(2)}) collective-permute-start(bf16[2,5,64,512]{3,2,1,0:T(8,128)(2,1)S(1)} %collective-permute-done.33.refs_7_), channel_id=1, source_target_pairs={{0,4},{4,0},{8,12},{12,8},{1,5},{5,1},{9,13},{13,9},{2,6},{6,2},{1... | collective-permute-start | bytes 1966088 | tf_op jit(solution)/shard_map/ppermute | solution.py:90
  207.1 1.9 collective-permute-start.43
  211.0 13.0 %collective-permute-start.46 = (bf16[2,4,64,512]{3,2,1,0:T(8,128)(2,1)S(1)}, bf16[2,4,64,512]{3,2,1,0:T(8,128)(2,1)}, u32[]{:S(2)}, u32[]{:S(2)}) collective-permute-start(bf16[2,4,64,512]{3,2,1,0:T(8,128)(2,1)S(1)} %collective-permute-done.34.refs_8_), channel_id=1, source_target_pairs={{0,16},{16,0},{1,17},{17,1},{2,18},{18,2},{3,19},{19,3},{4,20},{20... | collective-permute-start | bytes 1572872 | tf_op jit(solution)/shard_map/ppermute | solution.py:94
  211.7 15.3 %collective-permute-start.44 = (bf16[2,5,64,512]{3,2,1,0:T(8,128)(2,1)S(1)}, bf16[2,5,64,512]{3,2,1,0:T(8,128)(2,1)}, u32[]{:S(2)}, u32[]{:S(2)}) collective-permute-start(bf16[2,5,64,512]{3,2,1,0:T(8,128)(2,1)S(1)} %collective-permute-done.32.refs_6_), channel_id=1, source_target_pairs={{0,1},{1,0},{2,3},{3,2},{4,5},{5,4},{6,7},{7,6},{8,9},{9,8},{10,11... | collective-permute-start | bytes 1966088 | tf_op jit(solution)/shard_map/ppermute | solution.py:98
  213.5 14.6 %collective-permute-start.45 = (bf16[2,5,64,512]{3,2,1,0:T(8,128)(2,1)S(1)}, bf16[2,5,64,512]{3,2,1,0:T(8,128)(2,1)}, u32[]{:S(2)}, u32[]{:S(2)}) collective-permute-start(bf16[2,5,64,512]{3,2,1,0:T(8,128)(2,1)S(1)} %collective-permute-done.33.refs_7_), channel_id=1, source_target_pairs={{0,8},{4,12},{8,0},{12,4},{1,9},{5,13},{9,1},{13,5},{2,10},{6,14},... | collective-permute-start | bytes 1966088 | tf_op jit(solution)/shard_map/ppermute | solution.py:86
  213.7 14.4 %collective-permute-start.47 = (bf16[2,5,64,512]{3,2,1,0:T(8,128)(2,1)S(1)}, bf16[2,5,64,512]{3,2,1,0:T(8,128)(2,1)S(1)}, u32[]{:S(2)}, u32[]{:S(2)}) collective-permute-start(bf16[2,5,64,512]{3,2,1,0:T(8,128)(2,1)S(1)} %collective-permute-done.38.refs_12_), channel_id=1, source_target_pairs={{0,4},{4,0},{8,12},{12,8},{1,5},{5,1},{9,13},{13,9},{2,6},{6,2},{1... | collective-permute-start | bytes 1966088 | tf_op jit(solution)/shard_map/ppermute | solution.py:90
  213.7 14.4 %collective-permute-start.48 = (bf16[2,5,64,512]{3,2,1,0:T(8,128)(2,1)S(1)}, bf16[2,5,64,512]{3,2,1,0:T(8,128)(2,1)S(1)}, u32[]{:S(2)}, u32[]{:S(2)}) collective-permute-start(bf16[2,5,64,512]{3,2,1,0:T(8,128)(2,1)S(1)} %collective-permute-done.39.refs_13_), channel_id=1, source_target_pairs={{0,4},{4,0},{8,12},{12,8},{1,5},{5,1},{9,13},{13,9},{2,6},{6,2},{1... | collective-permute-start | bytes 1966088 | tf_op jit(solution)/shard_map/ppermute | solution.py:90
  224.0 1.9 collective-permute-start.49
  228.1 4.2 %collective-permute-start.50 = (bf16[2,5,64,512]{3,2,1,0:T(8,128)(2,1)}, bf16[2,5,64,512]{3,2,1,0:T(8,128)(2,1)}, u32[]{:S(2)}, u32[]{:S(2)}) collective-permute-start(bf16[2,5,64,512]{3,2,1,0:T(8,128)(2,1)} %collective-permute-done.44.refs_18_), channel_id=1, source_target_pairs={{0,4},{4,0},{8,12},{12,8},{1,5},{5,1},{9,13},{13,9},{2,6},{6,2},{1... | collective-permute-start | bytes 1966088 | tf_op jit(solution)/shard_map/ppermute | solution.py:90
  228.2 4.1 %collective-permute-start.51 = (bf16[2,5,64,512]{3,2,1,0:T(8,128)(2,1)}, bf16[2,5,64,512]{3,2,1,0:T(8,128)(2,1)}, u32[]{:S(2)}, u32[]{:S(2)}) collective-permute-start(bf16[2,5,64,512]{3,2,1,0:T(8,128)(2,1)} %collective-permute-done.45.refs_19_), channel_id=1, source_target_pairs={{0,4},{4,0},{8,12},{12,8},{1,5},{5,1},{9,13},{13,9},{2,6},{6,2},{1... | collective-permute-start | bytes 1966088 | tf_op jit(solution)/shard_map/ppermute | solution.py:90
  229.2 3.1 collective-permute-start.52
  255.5 34.5 %collective-permute-start.53 = (bf16[7,128,256]{2,1,0:T(8,128)(2,1)}, bf16[7,128,256]{2,1,0:T(8,128)(2,1)S(1)}, u32[]{:S(2)}, u32[]{:S(2)}) collective-permute-start(bf16[7,128,256]{2,1,0:T(8,128)(2,1)} %get-tuple-element.307), channel_id=1, source_target_pairs={{0,0},{1,1},{2,16},{3,17},{16,2},{17,3},{18,18},{19,19},{4,4},{5,5... | collective-permute-start | bytes 1376264 | tf_op jit(solution)/shard_map/ppermute | solution.py:138
  259.2 41.5 %collective-permute-start.54 = (bf16[7,128,256]{2,1,0:T(8,128)(2,1)}, bf16[7,128,256]{2,1,0:T(8,128)(2,1)S(1)}, u32[]{:S(2)}, u32[]{:S(2)}) collective-permute-start(bf16[7,128,256]{2,1,0:T(8,128)(2,1)} %get-tuple-element.308), channel_id=1, source_target_pairs={{0,1},{1,0},{2,17},{3,16},{16,3},{17,2},{18,19},{19,18},{4,5},{5,4... | collective-permute-start | bytes 1376264 | tf_op jit(solution)/shard_map/ppermute | solution.py:138
  260.6 40.1 %collective-permute-start.55 = (bf16[7,128,256]{2,1,0:T(8,128)(2,1)}, bf16[7,128,256]{2,1,0:T(8,128)(2,1)S(1)}, u32[]{:S(2)}, u32[]{:S(2)}) collective-permute-start(bf16[7,128,256]{2,1,0:T(8,128)(2,1)} %get-tuple-element.309), channel_id=1, source_target_pairs={{0,2},{1,3},{2,18},{3,19},{16,0},{17,1},{18,16},{19,17},{4,6},{5,7... | collective-permute-start | bytes 1376264 | tf_op jit(solution)/shard_map/ppermute | solution.py:138
  260.6 43.4 %collective-permute-start.56 = (bf16[7,128,256]{2,1,0:T(8,128)(2,1)}, bf16[7,128,256]{2,1,0:T(8,128)(2,1)S(1)}, u32[]{:S(2)}, u32[]{:S(2)}) collective-permute-start(bf16[7,128,256]{2,1,0:T(8,128)(2,1)} %get-tuple-element.310), channel_id=1, source_target_pairs={{0,3},{1,2},{2,19},{3,18},{16,1},{17,0},{18,17},{19,16},{4,7},{5,6... | collective-permute-start | bytes 1376264 | tf_op jit(solution)/shard_map/ppermute | solution.py:138
  304.0 32.8 %collective-permute-start.57 = (bf16[7,128,256]{2,1,0:T(8,128)(2,1)}, bf16[7,128,256]{2,1,0:T(8,128)(2,1)S(1)}, u32[]{:S(2)}, u32[]{:S(2)}) collective-permute-start(bf16[7,128,256]{2,1,0:T(8,128)(2,1)} %get-tuple-element.315), channel_id=1, source_target_pairs={{0,0},{1,1},{2,16},{3,17},{16,2},{17,3},{18,18},{19,19},{4,4},{5,5... | collective-permute-start | bytes 1376264 | tf_op jit(solution)/shard_map/ppermute | solution.py:138
  305.9 40.8 %collective-permute-start.58 = (bf16[7,128,256]{2,1,0:T(8,128)(2,1)}, bf16[7,128,256]{2,1,0:T(8,128)(2,1)S(1)}, u32[]{:S(2)}, u32[]{:S(2)}) collective-permute-start(bf16[7,128,256]{2,1,0:T(8,128)(2,1)} %get-tuple-element.316), channel_id=1, source_target_pairs={{0,1},{1,0},{2,17},{3,16},{16,3},{17,2},{18,19},{19,18},{4,5},{5,4... | collective-permute-start | bytes 1376264 | tf_op jit(solution)/shard_map/ppermute | solution.py:138
  307.6 41.3 %collective-permute-start.59 = (bf16[7,128,256]{2,1,0:T(8,128)(2,1)}, bf16[7,128,256]{2,1,0:T(8,128)(2,1)S(1)}, u32[]{:S(2)}, u32[]{:S(2)}) collective-permute-start(bf16[7,128,256]{2,1,0:T(8,128)(2,1)} %get-tuple-element.317), channel_id=1, source_target_pairs={{0,2},{1,3},{2,18},{3,19},{16,0},{17,1},{18,16},{19,17},{4,6},{5,7... | collective-permute-start | bytes 1376264 | tf_op jit(solution)/shard_map/ppermute | solution.py:138
  307.6 43.6 %collective-permute-start.60 = (bf16[7,128,256]{2,1,0:T(8,128)(2,1)}, bf16[7,128,256]{2,1,0:T(8,128)(2,1)S(1)}, u32[]{:S(2)}, u32[]{:S(2)}) collective-permute-start(bf16[7,128,256]{2,1,0:T(8,128)(2,1)} %get-tuple-element.318), channel_id=1, source_target_pairs={{0,3},{1,2},{2,19},{3,18},{16,1},{17,0},{18,17},{19,16},{4,7},{5,6... | collective-permute-start | bytes 1376264 | tf_op jit(solution)/shard_map/ppermute | solution.py:138
  (19 other events, 416.3 us)

commit v6 on v5

--- a/solution.py
+++ b/solution.py
@@ -142,8 +142,8 @@
     return lax.dot_general(a, b, (dims, ((), ())), preferred_element_type=F32)
 
 
-def place_of_block():
-    return [(p, b) for p, blocks in enumerate(PIECES) for b in range(blocks)]
+def block_rows(p):
+    return pl.ds(sum(PIECES[:p]), PIECES[p])
 
 
 def on_diagonal(unit):
@@ -189,7 +189,6 @@
 
 
 def gram_kernel(groups, pieces, *refs):
-    where = place_of_block()[: sum(PIECES[:pieces])]
     inputs, refs = refs[: 2 * pieces], refs[2 * pieces :]
     count = 2 * len(groups)
     outs, refs = refs[:count], refs[count:]
@@ -197,12 +196,13 @@
     tails, (panel, arrived, gone) = refs[: len(groups)], refs[len(groups) :]
     y, x, core, high, low = place()
     for source in range(2):
-        for i, (p, b) in enumerate(where):
+        for p in range(pieces):
             for step in range(4):
                 spot = pl.multiple_of(slab_of(high, low, step) * BAND, BAND)
+                columns = pl.ds(source * GROUP, GROUP)
                 pltpu.make_async_copy(
-                    inputs[source * pieces + p].at[step, pl.ds(b * BAND, BAND), :],
-                    panel.at[i, pl.ds(spot, BAND), pl.ds(source * GROUP, GROUP)],
+                    inputs[source * pieces + p].at[step],
+                    panel.at[block_rows(p), pl.ds(spot, BAND), columns],
                     arrived,
                 ).start()
     for tail in tails:
@@ -380,8 +380,8 @@
         return [(bys, array) for (bys, _), array in zip(pieces, arrays)]
 
     def ordered(*groups):
-        done = wave([unkeyed(group) for group in groups], [piece for _, piece in out])
-        out[:] = [(key, piece) for (key, _), piece in zip(out, done[1])]
+        done = wave([unkeyed(group) for group in groups], [piece for _, piece in out[:-6]])
+        out[:-6] = [(key, piece) for (key, _), piece in zip(out, done[1])]
         return [keyed(group, arrays) for group, arrays in zip(groups, done[0])]
 
     own = [([0], piece) for piece in mine]
@@ -394,7 +394,6 @@
     second, third_a = ordered(second, third_a)
     third_b = move(2, second)
     across(third_a)
-    (third_b,) = ordered(third_b)
     across(third_b)
     return out
 
@@ -406,11 +405,11 @@
     outs = refs[len(PIECES) : len(PIECES) + 4]
     gram, panel, first, total, result, here, there, gone = refs[len(PIECES) + 4 :]
     y, x, core, high, low = place()
-    for i, (p, b) in enumerate(place_of_block()):
+    for p in range(len(PIECES)):
         for step in range(4):
             pltpu.make_async_copy(
-                iter_pieces[p].at[step, pl.ds(b * BAND, BAND), pl.ds(part * WIDE, WIDE)],
-                panel.at[i, slab_of(high, low, step)],
+                iter_pieces[p].at[step, :, :, pl.ds(part * WIDE, WIDE)],
+                panel.at[block_rows(p), slab_of(high, low, step)],
                 there,
             ).start()
     for (third, bys, other), piece in zip(keys, gram_pieces):
@@ -453,20 +452,16 @@
     def two(i, carry):
         got = apply(lambda j: first[rows_of(j), :], i)
         result[i] = (total[rows_of(i), :] + quint_c * got).astype(BF16).reshape(4, BAND, WIDE)
+        for step in range(4):
+            pltpu.make_async_copy(
+                result.at[i, slab_of(y, low, step)], outs[step].at[i], gone.at[step]
+            ).start()
         return carry
 
     lax.fori_loop(0, BLOCKS, one, 0)
     lax.fori_loop(0, BLOCKS, two, 0)
-    copies = []
     for step in range(4):
-        copies.append(
-            pltpu.make_async_copy(
-                result.at[:, slab_of(y, low, step)], outs[step], gone.at[step]
-            )
-        )
-        copies[-1].start()
-    for copy in copies:
-        copy.wait()
+        pltpu.make_async_copy(result.at[:, 0], outs[step], gone.at[step]).wait()
 
 
 def step_call(keys, gram_pieces, iter_pieces, part):
@@ -518,7 +513,7 @@
         return [ready[0]] + [over_z(ready[step], step) for step in (1, 2, 3)]
 
     def joined(pieces):
-        return jnp.stack([jnp.concatenate(slab) for slab in zip(*pieces)])
+        return jnp.stack([jnp.concatenate(slab) for slab in zip(*pieces)]).reshape(4, -1, BAND, GROUP)
 
     done = []
     keep, other = cast(0, y), over_y(cast(0, 1 - y))

time: 354 us -> 350 us (0.989)
  waiting for transfers between devices: 203 us -> 198 us
    ppermute x14, waiting for transfers between devices: 12.1 us -> 5.18 us  [over_core(): return lax.ppermute(a, 'col', [(0, 1), (1, 0), (2, 3), (3, 2)])]
where the time goes in v6:
time: 350 us; the launch traced here: 349 us
  waiting for transfers between devices  198 us (57%)
  Pallas kernels  60.9 us (17%)
  starting transfers between devices  56.3 us (16%)
  other arithmetic  25.3 us (7%)
  local copies, waits for them, and re-layouts  7.29 us (2%)
    ppermute x20, waiting for transfers between devices, over_z(): return lax.ppermute(a, 'row', [(z, z ^ step) for z in range(4)])  76.1 us
    pallas_call x2, Pallas kernels, step_call(): pl.pallas_call(functools.partial(step_kernel, keys, part), out_shape=[jax...  45 us
    ppermute x8, waiting for transfers between devices, home(): return lax.ppermute(a, ('mats', 'row'), pairs)  43.8 us
    ppermute x11, waiting for transfers between devices, over_y(): return lax.ppermute(a, 'mats', [(0, 1), (1, 0)])  43.4 us
    ppermute x8, waiting for transfers between devices, over_x(): return lax.ppermute(a, 'col', [(0, 2), (1, 3), (2, 0), (3, 1)])  30.1 us
    ppermute x20, starting transfers between devices, over_z(): return lax.ppermute(a, 'row', [(z, z ^ step) for z in range(4)])  21.7 us
    dynamic_update_slice x8, other arithmetic, shards_cube(): lax.dynamic_update_slice_in_dim(out, pick(out, at, WIDE, 1) + piece, at, 1)  17.5 us
    ppermute x8, starting transfers between devices, home(): return lax.ppermute(a, ('mats', 'row'), pairs)  13.7 us
  transfers between devices with their start and end apart: 61, of which 38 were waited for; matrix products, arithmetic and copies ran while one was open for 7% of the time, Pallas kernels for 11%

profile of v6, /device:TPU:12, one launch (start us, length us, event | category | flops | bytes accessed | tf_op | source)
XLA Modules:
  0.0 349.0 jit_solution(5431435180977257984)
XLA Ops:
  1.6 1.7 dynamic-slice_convert_fusion.2
  3.3 2.5 dynamic-slice_convert_fusion
  5.9 3.3 collective-permute-done
  11.2 2.8 collective-permute-start.3
  14.4 8.8 %collective-permute-done.1 = bf16[256,1024]{1,0:T(8,128)(2,1)S(1)} collective-permute-done((bf16[256,1024]{1,0:T(8,128)(2,1)S(1)}, bf16[256,1024]{1,0:T(8,128)(2,1)S(1)}, u32[]{:S(2)}, u32[]{:S(2)}) %collective-permute-start.1) | collective-permute-done | bytes 524320 | tf_op jit(solution)/shard_map/ppermute | solution.py:94
  24.7 1.5 collective-permute-start.5
  26.2 3.0 collective-permute-start.7
  29.7 5.7 %collective-permute-done.6 = bf16[256,512]{1,0:T(8,128)(2,1)S(1)} collective-permute-done((bf16[256,512]{1,0:T(8,128)(2,1)S(1)}, bf16[256,512]{1,0:T(8,128)(2,1)S(1)}, u32[]{:S(2)}, u32[]{:S(2)}) %collective-permute-start.6) | collective-permute-done | bytes 262176 | tf_op jit(solution)/shard_map/ppermute | solution.py:98
  35.4 10.8 %collective-permute-done.7 = bf16[256,512]{1,0:T(8,128)(2,1)S(1)} collective-permute-done((bf16[256,512]{1,0:T(8,128)(2,1)S(1)}, bf16[256,512]{1,0:T(8,128)(2,1)S(1)}, u32[]{:S(2)}, u32[]{:S(2)}) %collective-permute-start.7) | collective-permute-done | bytes 262176 | tf_op jit(solution)/shard_map/ppermute | solution.py:98
  46.3 4.2 %collective-permute-done.8 = bf16[256,512]{1,0:T(8,128)(2,1)S(1)} collective-permute-done((bf16[256,512]{1,0:T(8,128)(2,1)S(1)}, bf16[256,512]{1,0:T(8,128)(2,1)S(1)}, u32[]{:S(2)}, u32[]{:S(2)}) %collective-permute-start.8) | collective-permute-done | bytes 262176 | tf_op jit(solution)/shard_map/ppermute | solution.py:98
  51.5 1.4 collective-permute-start.11
  52.9 3.0 collective-permute-start.9
  56.0 3.1 gram.2
  59.2 10.3 %collective-permute-done.10 = bf16[256,512]{1,0:T(8,128)(2,1)S(1)} collective-permute-done((bf16[256,512]{1,0:T(8,128)(2,1)S(1)}, bf16[256,512]{1,0:T(8,128)(2,1)S(1)}, u32[]{:S(2)}, u32[]{:S(2)}) %collective-permute-start.10) | collective-permute-done | bytes 262176 | tf_op jit(solution)/shard_map/ppermute | solution.py:98
  69.5 7.1 %collective-permute-done.11 = bf16[256,512]{1,0:T(8,128)(2,1)S(1)} collective-permute-done((bf16[256,512]{1,0:T(8,128)(2,1)S(1)}, bf16[256,512]{1,0:T(8,128)(2,1)S(1)}, u32[]{:S(2)}, u32[]{:S(2)}) %collective-permute-start.11) | collective-permute-done | bytes 262176 | tf_op jit(solution)/shard_map/ppermute | solution.py:98
  76.6 1.5 collective-permute-start.13
  78.1 2.2 collective-permute-start.15
  81.6 4.7 %fusion = f32[896,2048]{1,0:T(8,128)} fusion(f32[896,2048]{1,0:T(8,128)S(1)} %bitcast.34), kind=kLoop, calls=%fused_computation.1 | loop fusion | flops 5505024 | bytes 14680064 | tf_op jit(solution)/shard_map/mul | solution.py:540
  86.3 9.9 %collective-permute-done.13.refs_1_ = bf16[784,512]{1,0:T(8,128)(2,1)S(1)} collective-permute-done((bf16[784,512]{1,0:T(8,128)(2,1)S(1)}, bf16[784,512]{1,0:T(8,128)(2,1)S(1)}, u32[]{:S(2)}, u32[]{:S(2)}) %collective-permute-start.13) | collective-permute-done | bytes 802848 | tf_op jit(solution)/shard_map/ppermute | solution.py:86
  96.8 1.5 collective-permute-done.15
  98.3 5.7 %collective-permute-done.16 = bf16[256,512]{1,0:T(8,128)(2,1)S(1)} collective-permute-done((bf16[256,512]{1,0:T(8,128)(2,1)S(1)}, bf16[256,512]{1,0:T(8,128)(2,1)S(1)}, u32[]{:S(2)}, u32[]{:S(2)}) %collective-permute-start.16) | collective-permute-done | bytes 262176 | tf_op jit(solution)/shard_map/ppermute | solution.py:98
  105.4 3.3 collective-permute-done.18.refs_3_
  108.7 10.2 %gram.3 = (f32[4,4,64,512]{3,2,1,0:T(8,128)S(1)}, bf16[1040,512]{1,0:T(8,128)(2,1)S(1)}, f32[4,4,64,512]{3,2,1,0:T(8,128)S(1)}, bf16[1040,512]{1,0:T(8,128)(2,1)...) custom-call(bf16[4,3,128,512]{3,2,1,0:T(8,128)(2,1)S(1)} %pad_maximum_fusion.1.refs_0_.refs_24_, ...), custom_call_target="tpu_custom_call" | custom-call | flops 7516192768 | bytes 458752 | tf_op jit(solution)/shard_map/gram/pallas_call | solution.py:296
  120.6 2.1 collective-permute-start.22
  122.7 21.6 %collective-permute-done.22.refs_1_ = bf16[208,512]{1,0:T(8,128)(2,1)S(1)} collective-permute-done((bf16[208,512]{1,0:T(8,128)(2,1)S(1)}, bf16[208,512]{1,0:T(8,128)(2,1)S(1)}, u32[]{:S(2)}, u32[]{:S(2)}) %collective-permute-start.22) | collective-permute-done | bytes 213024 | tf_op jit(solution)/shard_map/ppermute | solution.py:98
  147.0 1.5 collective-permute-start.25
  148.5 8.4 %collective-permute-done.25.refs_5_ = bf16[400,512]{1,0:T(8,128)(2,1)S(1)} collective-permute-done((bf16[400,512]{1,0:T(8,128)(2,1)S(1)}, bf16[400,512]{1,0:T(8,128)(2,1)S(1)}, u32[]{:S(2)}, u32[]{:S(2)}) %collective-permute-start.25) | collective-permute-done | bytes 409632 | tf_op jit(solution)/shard_map/ppermute | solution.py:86
  156.8 2.3 collective-permute-done.23.refs_1_
  160.5 1.4 collective-permute-start.27
  163.1 4.6 %collective-permute-done.28.refs_5_ = bf16[208,512]{1,0:T(8,128)(2,1)S(1)} collective-permute-done((bf16[208,512]{1,0:T(8,128)(2,1)S(1)}, bf16[208,512]{1,0:T(8,128)(2,1)S(1)}, u32[]{:S(2)}, u32[]{:S(2)}) %collective-permute-start.28) | collective-permute-done | bytes 213024 | tf_op jit(solution)/shard_map/ppermute | solution.py:94
  167.9 2.4 collective-permute-start.31
  171.6 3.1 collective-permute-done.31
  174.8 3.6 %collective-permute-done.30 = bf16[1,5,64,512]{3,2,1,0:T(8,128)(2,1)S(1)} collective-permute-done((bf16[1,5,64,512]{3,2,1,0:T(8,128)(2,1)S(1)}, bf16[1,5,64,512]{3,2,1,0:T(8,128)(2,1)S(1)}, u32[]{:S(2)}, u32[]{:S(2)}) %collective-permute-start.30) | collective-permute-done | bytes 327712 | tf_op jit(solution)/shard_map/ppermute | solution.py:94
  178.5 2.7 collective-permute-done.29
  181.4 1.4 collective-permute-start.32
  183.2 7.3 %collective-permute-done.34.refs_8_ = bf16[2,4,64,512]{3,2,1,0:T(8,128)(2,1)S(1)} collective-permute-done((bf16[2,4,64,512]{3,2,1,0:T(8,128)(2,1)S(1)}, bf16[2,4,64,512]{3,2,1,0:T(8,128)(2,1)S(1)}, u32[]{:S(2)}, u32[]{:S(2)}) %collective-permute-start.34) | collective-permute-done | bytes 524320 | tf_op jit(solution)/shard_map/ppermute | solution.py:86
  190.5 1.5 collective-permute-done.32.refs_6_
  193.3 3.4 collective-permute-start.36
  197.5 8.4 %collective-permute-done.37.refs_14_ = bf16[2,4,64,512]{3,2,1,0:T(8,128)(2,1)S(1)} collective-permute-done((bf16[2,4,64,512]{3,2,1,0:T(8,128)(2,1)S(1)}, bf16[2,4,64,512]{3,2,1,0:T(8,128)(2,1)S(1)}, u32[]{:S(2)}, u32[]{:S(2)}) %collective-permute-start.37) | collective-permute-done | bytes 524320 | tf_op jit(solution)/shard_map/ppermute | solution.py:94
  205.9 2.0 collective-permute-done.35.refs_12_
  208.0 1.7 collective-permute-start.47
  211.7 10.6 %collective-permute-done.49.refs_20_ = bf16[2,4,64,512]{3,2,1,0:T(8,128)(2,1)} collective-permute-done((bf16[2,4,64,512]{3,2,1,0:T(8,128)(2,1)S(1)}, bf16[2,4,64,512]{3,2,1,0:T(8,128)(2,1)}, u32[]{:S(2)}, u32[]{:S(2)}) %collective-permute-start.49) | collective-permute-done | bytes 524320 | tf_op jit(solution)/shard_map/ppermute | solution.py:94
  223.4 1.5 collective-permute-done.48.refs_19_
  226.3 1.9 collective-permute-done.52.refs_23_
  228.2 22.5 %step.2 = (bf16[7,128,256]{2,1,0:T(8,128)(2,1)}, bf16[7,128,256]{2,1,0:T(8,128)(2,1)}, bf16[7,128,256]{2,1,0:T(8,128)(2,1)}, bf16[7,128,256]{2,1,0:T(8,128)(2,1)}) custom-call(bf16[2,5,64,512]{3,2,1,0:T(8,128)(2,1)} %copy-done.3, bf16[2,5,64,512]{3,2,1,0:T(8,128)(2,1)} %copy-done.2, bf16[2,4,64,512]{3,2,1,0:T(8,128)(2,1)} %copy-done.4, ...), custom_call_target="tpu_custom_call" | custom-call | flops 13153337344 | bytes 20971520 | tf_op jit(solution)/shard_map/step/pallas_call | solution.py:469
  250.7 2.9 collective-permute-start.53
  253.6 2.6 collective-permute-start.54
  256.2 1.8 collective-permute-start.56
  258.1 22.4 %step.3 = (bf16[7,128,256]{2,1,0:T(8,128)(2,1)}, bf16[7,128,256]{2,1,0:T(8,128)(2,1)}, bf16[7,128,256]{2,1,0:T(8,128)(2,1)}, bf16[7,128,256]{2,1,0:T(8,128)(2,1)}) custom-call(bf16[2,5,64,512]{3,2,1,0:T(8,128)(2,1)} %copy-done.3, bf16[2,5,64,512]{3,2,1,0:T(8,128)(2,1)} %copy-done.2, bf16[2,4,64,512]{3,2,1,0:T(8,128)(2,1)} %copy-done.4, ...), custom_call_target="tpu_custom_call" | custom-call | flops 13153337344 | bytes 20971520 | tf_op jit(solution)/shard_map/step/pallas_call | solution.py:469
  280.5 3.8 %collective-permute-done.53 = bf16[7,128,256]{2,1,0:T(8,128)(2,1)S(1)} collective-permute-done((bf16[7,128,256]{2,1,0:T(8,128)(2,1)}, bf16[7,128,256]{2,1,0:T(8,128)(2,1)S(1)}, u32[]{:S(2)}, u32[]{:S(2)}) %collective-permute-start.53) | collective-permute-done | bytes 458784 | tf_op jit(solution)/shard_map/ppermute | solution.py:138
  284.4 12.0 %collective-permute-done.54 = bf16[7,128,256]{2,1,0:T(8,128)(2,1)S(1)} collective-permute-done((bf16[7,128,256]{2,1,0:T(8,128)(2,1)}, bf16[7,128,256]{2,1,0:T(8,128)(2,1)S(1)}, u32[]{:S(2)}, u32[]{:S(2)}) %collective-permute-start.54) | collective-permute-done | bytes 458784 | tf_op jit(solution)/shard_map/ppermute | solution.py:138
  296.4 3.0 collective-permute-done.56
  299.4 1.9 collective-permute-start.57
  301.9 3.9 %collective-permute-start.60 = (bf16[7,128,256]{2,1,0:T(8,128)(2,1)}, bf16[7,128,256]{2,1,0:T(8,128)(2,1)S(1)}, u32[]{:S(2)}, u32[]{:S(2)}) collective-permute-start(bf16[7,128,256]{2,1,0:T(8,128)(2,1)} %get-tuple-element.252), channel_id=1, source_target_pairs={{0,3},{1,2},{2,19},{3,18},{16,1},{17,0},{18,17},{19,16},{4,7},{5,6... | collective-permute-start | bytes 1376264 | tf_op jit(solution)/shard_map/ppermute | solution.py:138
  305.9 2.2 constant_dynamic-update-slice_fusion.7
  308.2 2.2 constant_dynamic-update-slice_fusion.6
  310.4 2.2 constant_dynamic-update-slice_fusion.5
  312.7 2.2 constant_dynamic-update-slice_fusion.4
  314.9 16.5 %collective-permute-done.57 = bf16[7,128,256]{2,1,0:T(8,128)(2,1)S(1)} collective-permute-done((bf16[7,128,256]{2,1,0:T(8,128)(2,1)}, bf16[7,128,256]{2,1,0:T(8,128)(2,1)S(1)}, u32[]{:S(2)}, u32[]{:S(2)}) %collective-permute-start.57) | collective-permute-done | bytes 458784 | tf_op jit(solution)/shard_map/ppermute | solution.py:138
  331.5 2.2 constant_dynamic-update-slice_fusion.3
  333.7 7.2 %collective-permute-done.58 = bf16[7,128,256]{2,1,0:T(8,128)(2,1)S(1)} collective-permute-done((bf16[7,128,256]{2,1,0:T(8,128)(2,1)}, bf16[7,128,256]{2,1,0:T(8,128)(2,1)S(1)}, u32[]{:S(2)}, u32[]{:S(2)}) %collective-permute-start.58) | collective-permute-done | bytes 458784 | tf_op jit(solution)/shard_map/ppermute | solution.py:138
  341.0 2.2 constant_dynamic-update-slice_fusion.2
  343.3 2.2 constant_dynamic-update-slice_fusion.1
  346.8 2.2 constant_dynamic-update-slice_fusion
  (152 shorter events, 28.5 us)
Async XLA Ops:
  1.1 8.1 %collective-permute-start = (bf16[128,1024]{1,0:T(8,128)(2,1)S(1)}, bf16[128,1024]{1,0:T(8,128)(2,1)S(1)}, u32[]{:S(2)}, u32[]{:S(2)}) collective-permute-start(bf16[128,1024]{1,0:T(8,128)(2,1)S(1)} %dynamic-slice_convert_fusion.4), channel_id=1, source_target_pairs={{0,16},{16,0},{1,17},{17,1},{2,18},{18,2},{3,19},{19,3},{4,20},{20... | collective-permute-start | bytes 786440 | tf_op jit(solution)/shard_map/ppermute | solution.py:94
  10.4 12.9 %collective-permute-start.1 = (bf16[256,1024]{1,0:T(8,128)(2,1)S(1)}, bf16[256,1024]{1,0:T(8,128)(2,1)S(1)}, u32[]{:S(2)}, u32[]{:S(2)}) collective-permute-start(bf16[256,1024]{1,0:T(8,128)(2,1)S(1)} %get-tuple-element.130), channel_id=1, source_target_pairs={{0,16},{16,0},{1,17},{17,1},{2,18},{18,2},{3,19},{19,3},{4,20},{20... | collective-permute-start | bytes 1572872 | tf_op jit(solution)/shard_map/ppermute | solution.py:94
  10.9 12.5 %collective-permute-start.2 = (bf16[128,512]{1,0:T(8,128)(2,1)S(1)}, bf16[128,512]{1,0:T(8,128)(2,1)S(1)}, u32[]{:S(2)}, u32[]{:S(2)}) collective-permute-start(bf16[128,512]{1,0:T(8,128)(2,1)S(1)} %get-tuple-element.134), channel_id=1, source_target_pairs={{0,1},{1,0},{2,3},{3,2},{4,5},{5,4},{6,7},{7,6},{8,9},{9,8},{10,11... | collective-permute-start | bytes 393224 | tf_op jit(solution)/shard_map/ppermute | solution.py:98
  11.2 12.3 %collective-permute-start.3 = (bf16[128,512]{1,0:T(8,128)(2,1)S(1)}, bf16[128,512]{1,0:T(8,128)(2,1)S(1)}, u32[]{:S(2)}, u32[]{:S(2)}) collective-permute-start(bf16[128,512]{1,0:T(8,128)(2,1)S(1)} %get-tuple-element.135), channel_id=1, source_target_pairs={{0,2},{1,3},{2,0},{3,1},{4,6},{5,7},{6,4},{7,5},{8,10},{9,11},{10,... | collective-permute-start | bytes 393224 | tf_op jit(solution)/shard_map/ppermute | solution.py:98
  14.0 10.7 %collective-permute-start.4 = (bf16[128,512]{1,0:T(8,128)(2,1)S(1)}, bf16[128,512]{1,0:T(8,128)(2,1)S(1)}, u32[]{:S(2)}, u32[]{:S(2)}) collective-permute-start(bf16[128,512]{1,0:T(8,128)(2,1)S(1)} %get-tuple-element.136), channel_id=1, source_target_pairs={{0,3},{1,2},{2,1},{3,0},{4,7},{5,6},{6,5},{7,4},{8,11},{9,10},{10,... | collective-permute-start | bytes 393224 | tf_op jit(solution)/shard_map/ppermute | solution.py:98
  24.7 26.1 %collective-permute-start.5 = (bf16[512,1024]{1,0:T(8,128)(2,1)S(1)}, bf16[512,1024]{1,0:T(8,128)(2,1)S(1)}, u32[]{:S(2)}, u32[]{:S(2)}) collective-permute-start(bf16[512,1024]{1,0:T(8,128)(2,1)S(1)} %get-tuple-element.138), channel_id=1, source_target_pairs={{0,16},{16,0},{1,17},{17,1},{2,18},{18,2},{3,19},{19,3},{4,20},{20... | collective-permute-start | bytes 3145736 | tf_op jit(solution)/shard_map/ppermute | solution.py:94
  26.2 9.2 %collective-permute-start.6 = (bf16[256,512]{1,0:T(8,128)(2,1)S(1)}, bf16[256,512]{1,0:T(8,128)(2,1)S(1)}, u32[]{:S(2)}, u32[]{:S(2)}) collective-permute-start(bf16[256,512]{1,0:T(8,128)(2,1)S(1)} %get-tuple-element.142), channel_id=1, source_target_pairs={{0,1},{1,0},{2,3},{3,2},{4,5},{5,4},{6,7},{7,6},{8,9},{9,8},{10,11... | collective-permute-start | bytes 786440 | tf_op jit(solution)/shard_map/ppermute | solution.py:98
  26.2 20.1 %collective-permute-start.7 = (bf16[256,512]{1,0:T(8,128)(2,1)S(1)}, bf16[256,512]{1,0:T(8,128)(2,1)S(1)}, u32[]{:S(2)}, u32[]{:S(2)}) collective-permute-start(bf16[256,512]{1,0:T(8,128)(2,1)S(1)} %get-tuple-element.144), channel_id=1, source_target_pairs={{0,2},{1,3},{2,0},{3,1},{4,6},{5,7},{6,4},{7,5},{8,10},{9,11},{10,... | collective-permute-start | bytes 786440 | tf_op jit(solution)/shard_map/ppermute | solution.py:98
  29.2 21.2 %collective-permute-start.8 = (bf16[256,512]{1,0:T(8,128)(2,1)S(1)}, bf16[256,512]{1,0:T(8,128)(2,1)S(1)}, u32[]{:S(2)}, u32[]{:S(2)}) collective-permute-start(bf16[256,512]{1,0:T(8,128)(2,1)S(1)} %get-tuple-element.146), channel_id=1, source_target_pairs={{0,3},{1,2},{2,1},{3,0},{4,7},{5,6},{6,5},{7,4},{8,11},{9,10},{10,... | collective-permute-start | bytes 786440 | tf_op jit(solution)/shard_map/ppermute | solution.py:98
  50.7 58.0 %copy-start = (bf16[4,3,128,512]{3,2,1,0:T(8,128)(2,1)}, bf16[4,3,128,512]{3,2,1,0:T(8,128)(2,1)S(1)}, u32[]{:S(2)}) copy-start(bf16[4,3,128,512]{3,2,1,0:T(8,128)(2,1)S(1)} %pad_maximum_fusion.1.refs_0_.refs_24_) | copy-start | bytes 4718596
  51.4 4.6 %collective-permute-start.12 = (bf16[4,3,128,512]{3,2,1,0:T(8,128)(2,1)S(1)}, bf16[4,3,128,512]{3,2,1,0:T(8,128)(2,1)S(1)}, u32[]{:S(2)}, u32[]{:S(2)}) collective-permute-start(bf16[4,3,128,512]{3,2,1,0:T(8,128)(2,1)S(1)} %pad_maximum_fusion.1.refs_0_.refs_24_), channel_id=1, source_target_pairs={{0,4},{4,0},{8,12},{12,8},{1,5},{5,1},{9,13},{13,9},{2,6},{6,2},{1... | collective-permute-start | bytes 4718600 | tf_op jit(solution)/shard_map/ppermute | solution.py:90
  51.5 18.0 %collective-permute-start.10 = (bf16[256,512]{1,0:T(8,128)(2,1)S(1)}, bf16[256,512]{1,0:T(8,128)(2,1)S(1)}, u32[]{:S(2)}, u32[]{:S(2)}) collective-permute-start(bf16[256,512]{1,0:T(8,128)(2,1)S(1)} %get-tuple-element.153), channel_id=1, source_target_pairs={{0,2},{1,3},{2,0},{3,1},{4,6},{5,7},{6,4},{7,5},{8,10},{9,11},{10,... | collective-permute-start | bytes 786440 | tf_op jit(solution)/shard_map/ppermute | solution.py:98
  51.5 25.1 %collective-permute-start.11 = (bf16[256,512]{1,0:T(8,128)(2,1)S(1)}, bf16[256,512]{1,0:T(8,128)(2,1)S(1)}, u32[]{:S(2)}, u32[]{:S(2)}) collective-permute-start(bf16[256,512]{1,0:T(8,128)(2,1)S(1)} %get-tuple-element.154), channel_id=1, source_target_pairs={{0,3},{1,2},{2,1},{3,0},{4,7},{5,6},{6,5},{7,4},{8,11},{9,10},{10,... | collective-permute-start | bytes 786440 | tf_op jit(solution)/shard_map/ppermute | solution.py:98
  52.9 23.7 %collective-permute-start.9 = (bf16[256,512]{1,0:T(8,128)(2,1)S(1)}, bf16[256,512]{1,0:T(8,128)(2,1)S(1)}, u32[]{:S(2)}, u32[]{:S(2)}) collective-permute-start(bf16[256,512]{1,0:T(8,128)(2,1)S(1)} %get-tuple-element.152), channel_id=1, source_target_pairs={{0,1},{1,0},{2,3},{3,2},{4,5},{5,4},{6,7},{7,6},{8,9},{9,8},{10,11... | collective-permute-start | bytes 786440 | tf_op jit(solution)/shard_map/ppermute | solution.py:98
  76.6 19.6 %collective-permute-start.13 = (bf16[784,512]{1,0:T(8,128)(2,1)S(1)}, bf16[784,512]{1,0:T(8,128)(2,1)S(1)}, u32[]{:S(2)}, u32[]{:S(2)}) collective-permute-start(bf16[784,512]{1,0:T(8,128)(2,1)S(1)} %get-tuple-element.159), channel_id=1, source_target_pairs={{0,8},{4,12},{8,0},{12,4},{1,9},{5,13},{9,1},{13,5},{2,10},{6,14},... | collective-permute-start | bytes 2408456 | tf_op jit(solution)/shard_map/ppermute | solution.py:86
  78.1 18.7 %collective-permute-start.14 = (bf16[256,512]{1,0:T(8,128)(2,1)S(1)}, bf16[256,512]{1,0:T(8,128)(2,1)S(1)}, u32[]{:S(2)}, u32[]{:S(2)}) collective-permute-start(bf16[256,512]{1,0:T(8,128)(2,1)S(1)} %slice.29), channel_id=1, source_target_pairs={{0,1},{1,0},{2,3},{3,2},{4,5},{5,4},{6,7},{7,6},{8,9},{9,8},{10,11... | collective-permute-start | bytes 786440 | tf_op jit(solution)/shard_map/ppermute | solution.py:98
  78.1 20.2 %collective-permute-start.15 = (bf16[256,512]{1,0:T(8,128)(2,1)S(1)}, bf16[256,512]{1,0:T(8,128)(2,1)S(1)}, u32[]{:S(2)}, u32[]{:S(2)}) collective-permute-start(bf16[256,512]{1,0:T(8,128)(2,1)S(1)} %slice.30), channel_id=1, source_target_pairs={{0,2},{1,3},{2,0},{3,1},{4,6},{5,7},{6,4},{7,5},{8,10},{9,11},{10,... | collective-permute-start | bytes 786440 | tf_op jit(solution)/shard_map/ppermute | solution.py:98
  80.3 23.7 %collective-permute-start.16 = (bf16[256,512]{1,0:T(8,128)(2,1)S(1)}, bf16[256,512]{1,0:T(8,128)(2,1)S(1)}, u32[]{:S(2)}, u32[]{:S(2)}) collective-permute-start(bf16[256,512]{1,0:T(8,128)(2,1)S(1)} %slice.31), channel_id=1, source_target_pairs={{0,3},{1,2},{2,1},{3,0},{4,7},{5,6},{6,5},{7,4},{8,11},{9,10},{10,... | collective-permute-start | bytes 786440 | tf_op jit(solution)/shard_map/ppermute | solution.py:98
  104.5 4.2 %collective-permute-start.18 = (bf16[4,4,128,512]{3,2,1,0:T(8,128)(2,1)S(1)}, bf16[4,4,128,512]{3,2,1,0:T(8,128)(2,1)S(1)}, u32[]{:S(2)}, u32[]{:S(2)}) collective-permute-start(bf16[4,4,128,512]{3,2,1,0:T(8,128)(2,1)S(1)} %pad_maximum_fusion.refs_1_.refs_25_), channel_id=1, source_target_pairs={{0,4},{4,0},{8,12},{12,8},{1,5},{5,1},{9,13},{13,9},{2,6},{6,2},{1... | collective-permute-start | bytes 6291464 | tf_op jit(solution)/shard_map/ppermute | solution.py:90
  104.5 14.4 %collective-permute-start.17 = (bf16[400,512]{1,0:T(8,128)(2,1)S(1)}, bf16[400,512]{1,0:T(8,128)(2,1)S(1)}, u32[]{:S(2)}, u32[]{:S(2)}) collective-permute-start(bf16[400,512]{1,0:T(8,128)(2,1)S(1)} %get-tuple-element.172), channel_id=1, source_target_pairs={{0,16},{16,0},{1,17},{17,1},{2,18},{18,2},{3,19},{19,3},{4,20},{20... | collective-permute-start | bytes 1228808 | tf_op jit(solution)/shard_map/ppermute | solution.py:94
  118.9 25.6 %collective-permute-start.19 = (bf16[1040,512]{1,0:T(8,128)(2,1)S(1)}, bf16[1040,512]{1,0:T(8,128)(2,1)S(1)}, u32[]{:S(2)}, u32[]{:S(2)}) collective-permute-start(bf16[1040,512]{1,0:T(8,128)(2,1)S(1)} %get-tuple-element.189), channel_id=1, source_target_pairs={{0,8},{4,12},{8,0},{12,4},{1,9},{5,13},{9,1},{13,5},{2,10},{6,14},... | collective-permute-start | bytes 3194888 | tf_op jit(solution)/shard_map/ppermute | solution.py:86
  119.5 25.3 %collective-permute-start.20 = (bf16[1040,512]{1,0:T(8,128)(2,1)S(1)}, bf16[1040,512]{1,0:T(8,128)(2,1)S(1)}, u32[]{:S(2)}, u32[]{:S(2)}) collective-permute-start(bf16[1040,512]{1,0:T(8,128)(2,1)S(1)} %get-tuple-element.191), channel_id=1, source_target_pairs={{0,16},{16,0},{1,17},{17,1},{2,18},{18,2},{3,19},{19,3},{4,20},{20... | collective-permute-start | bytes 3194888 | tf_op jit(solution)/shard_map/ppermute | solution.py:94
  120.3 24.0 %collective-permute-start.21 = (bf16[784,512]{1,0:T(8,128)(2,1)S(1)}, bf16[784,512]{1,0:T(8,128)(2,1)S(1)}, u32[]{:S(2)}, u32[]{:S(2)}) collective-permute-start(bf16[784,512]{1,0:T(8,128)(2,1)S(1)} %get-tuple-element.193), channel_id=1, source_target_pairs={{0,1},{1,0},{2,3},{3,2},{4,5},{5,4},{6,7},{7,6},{8,9},{9,8},{10,11... | collective-permute-start | bytes 2408456 | tf_op jit(solution)/shard_map/ppermute | solution.py:98
  120.6 23.7 %collective-permute-start.22 = (bf16[208,512]{1,0:T(8,128)(2,1)S(1)}, bf16[208,512]{1,0:T(8,128)(2,1)S(1)}, u32[]{:S(2)}, u32[]{:S(2)}) collective-permute-start(bf16[208,512]{1,0:T(8,128)(2,1)S(1)} %get-tuple-element.203), channel_id=1, source_target_pairs={{0,1},{1,0},{2,3},{3,2},{4,5},{5,4},{6,7},{7,6},{8,9},{9,8},{10,11... | collective-permute-start | bytes 638984 | tf_op jit(solution)/shard_map/ppermute | solution.py:98
  145.8 13.3 %collective-permute-start.23 = (bf16[528,512]{1,0:T(8,128)(2,1)S(1)}, bf16[528,512]{1,0:T(8,128)(2,1)S(1)}, u32[]{:S(2)}, u32[]{:S(2)}) collective-permute-start(bf16[528,512]{1,0:T(8,128)(2,1)S(1)} %get-tuple-element.205), channel_id=1, source_target_pairs={{0,16},{16,0},{1,17},{17,1},{2,18},{18,2},{3,19},{19,3},{4,20},{20... | collective-permute-start | bytes 1622024 | tf_op jit(solution)/shard_map/ppermute | solution.py:94
  146.7 12.9 %collective-permute-start.24 = (bf16[528,512]{1,0:T(8,128)(2,1)S(1)}, bf16[528,512]{1,0:T(8,128)(2,1)S(1)}, u32[]{:S(2)}, u32[]{:S(2)}) collective-permute-start(bf16[528,512]{1,0:T(8,128)(2,1)S(1)} %get-tuple-element.207), channel_id=1, source_target_pairs={{0,1},{1,0},{2,3},{3,2},{4,5},{5,4},{6,7},{7,6},{8,9},{9,8},{10,11... | collective-permute-start | bytes 1622024 | tf_op jit(solution)/shard_map/ppermute | solution.py:98
  147.0 9.9 %collective-permute-start.25 = (bf16[400,512]{1,0:T(8,128)(2,1)S(1)}, bf16[400,512]{1,0:T(8,128)(2,1)S(1)}, u32[]{:S(2)}, u32[]{:S(2)}) collective-permute-start(bf16[400,512]{1,0:T(8,128)(2,1)S(1)} %get-tuple-element.209), channel_id=1, source_target_pairs={{0,8},{4,12},{8,0},{12,4},{1,9},{5,13},{9,1},{13,5},{2,10},{6,14},... | collective-permute-start | bytes 1228808 | tf_op jit(solution)/shard_map/ppermute | solution.py:86
  160.1 7.6 %collective-permute-start.26 = (bf16[272,512]{1,0:T(8,128)(2,1)S(1)}, bf16[272,512]{1,0:T(8,128)(2,1)S(1)}, u32[]{:S(2)}, u32[]{:S(2)}) collective-permute-start(bf16[272,512]{1,0:T(8,128)(2,1)S(1)} %get-tuple-element.211), channel_id=1, source_target_pairs={{0,1},{1,0},{2,3},{3,2},{4,5},{5,4},{6,7},{7,6},{8,9},{9,8},{10,11... | collective-permute-start | bytes 835592 | tf_op jit(solution)/shard_map/ppermute | solution.py:98
  160.5 7.3 %collective-permute-start.27 = (bf16[272,512]{1,0:T(8,128)(2,1)S(1)}, bf16[272,512]{1,0:T(8,128)(2,1)S(1)}, u32[]{:S(2)}, u32[]{:S(2)}) collective-permute-start(bf16[272,512]{1,0:T(8,128)(2,1)S(1)} %get-tuple-element.213), channel_id=1, source_target_pairs={{0,8},{4,12},{8,0},{12,4},{1,9},{5,13},{9,1},{13,5},{2,10},{6,14},... | collective-permute-start | bytes 835592 | tf_op jit(solution)/shard_map/ppermute | solution.py:86
  161.9 5.8 %collective-permute-start.28 = (bf16[208,512]{1,0:T(8,128)(2,1)S(1)}, bf16[208,512]{1,0:T(8,128)(2,1)S(1)}, u32[]{:S(2)}, u32[]{:S(2)}) collective-permute-start(bf16[208,512]{1,0:T(8,128)(2,1)S(1)} %get-tuple-element.215), channel_id=1, source_target_pairs={{0,16},{16,0},{1,17},{17,1},{2,18},{18,2},{3,19},{19,3},{4,20},{20... | collective-permute-start | bytes 638984 | tf_op jit(solution)/shard_map/ppermute | solution.py:94
  167.9 6.8 %collective-permute-start.31 = (bf16[1,4,64,512]{3,2,1,0:T(8,128)(2,1)S(1)}, bf16[1,4,64,512]{3,2,1,0:T(8,128)(2,1)S(1)}, u32[]{:S(2)}, u32[]{:S(2)}) collective-permute-start(bf16[1,4,64,512]{3,2,1,0:T(8,128)(2,1)S(1)} %bitcast.31), channel_id=1, source_target_pairs={{0,1},{1,0},{2,3},{3,2},{4,5},{5,4},{6,7},{7,6},{8,9},{9,8},{10,11... | collective-permute-start | bytes 786440 | tf_op jit(solution)/shard_map/ppermute | solution.py:98
  170.4 8.0 %collective-permute-start.30 = (bf16[1,5,64,512]{3,2,1,0:T(8,128)(2,1)S(1)}, bf16[1,5,64,512]{3,2,1,0:T(8,128)(2,1)S(1)}, u32[]{:S(2)}, u32[]{:S(2)}) collective-permute-start(bf16[1,5,64,512]{3,2,1,0:T(8,128)(2,1)S(1)} %bitcast.29), channel_id=1, source_target_pairs={{0,16},{16,0},{1,17},{17,1},{2,18},{18,2},{3,19},{19,3},{4,20},{20... | collective-permute-start | bytes 983048 | tf_op jit(solution)/shard_map/ppermute | solution.py:94
  171.4 9.8 %collective-permute-start.29 = (bf16[1,5,64,512]{3,2,1,0:T(8,128)(2,1)S(1)}, bf16[1,5,64,512]{3,2,1,0:T(8,128)(2,1)S(1)}, u32[]{:S(2)}, u32[]{:S(2)}) collective-permute-start(bf16[1,5,64,512]{3,2,1,0:T(8,128)(2,1)S(1)} %bitcast.27), channel_id=1, source_target_pairs={{0,8},{4,12},{8,0},{12,4},{1,9},{5,13},{9,1},{13,5},{2,10},{6,14},... | collective-permute-start | bytes 983048 | tf_op jit(solution)/shard_map/ppermute | solution.py:86
  174.8 53.4 %copy-start.4 = (bf16[2,4,64,512]{3,2,1,0:T(8,128)(2,1)}, bf16[2,4,64,512]{3,2,1,0:T(8,128)(2,1)S(1)}, u32[]{:S(2)}) copy-start(bf16[2,4,64,512]{3,2,1,0:T(8,128)(2,1)S(1)} %pad_maximum_fusion.8.refs_2_) | copy-start | bytes 1572868
  178.5 49.7 %copy-start.2 = (bf16[2,5,64,512]{3,2,1,0:T(8,128)(2,1)}, bf16[2,5,64,512]{3,2,1,0:T(8,128)(2,1)S(1)}, u32[]{:S(2)}) copy-start(bf16[2,5,64,512]{3,2,1,0:T(8,128)(2,1)S(1)} %pad_maximum_fusion.3.refs_1_) | copy-start | bytes 1966084
  181.3 9.2 %collective-permute-start.34 = (bf16[2,4,64,512]{3,2,1,0:T(8,128)(2,1)S(1)}, bf16[2,4,64,512]{3,2,1,0:T(8,128)(2,1)S(1)}, u32[]{:S(2)}, u32[]{:S(2)}) collective-permute-start(bf16[2,4,64,512]{3,2,1,0:T(8,128)(2,1)S(1)} %pad_maximum_fusion.8.refs_2_), channel_id=1, source_target_pairs={{0,8},{4,12},{8,0},{12,4},{1,9},{5,13},{9,1},{13,5},{2,10},{6,14},... | collective-permute-start | bytes 1572872 | tf_op jit(solution)/shard_map/ppermute | solution.py:86
  181.4 10.7 %collective-permute-start.32 = (bf16[2,5,64,512]{3,2,1,0:T(8,128)(2,1)S(1)}, bf16[2,5,64,512]{3,2,1,0:T(8,128)(2,1)S(1)}, u32[]{:S(2)}, u32[]{:S(2)}) collective-permute-start(bf16[2,5,64,512]{3,2,1,0:T(8,128)(2,1)S(1)} %pad_maximum_fusion.2.refs_0_), channel_id=1, source_target_pairs={{0,16},{16,0},{1,17},{17,1},{2,18},{18,2},{3,19},{19,3},{4,20},{20... | collective-permute-start | bytes 1966088 | tf_op jit(solution)/shard_map/ppermute | solution.py:94
  182.7 10.6 %collective-permute-start.33 = (bf16[2,5,64,512]{3,2,1,0:T(8,128)(2,1)S(1)}, bf16[2,5,64,512]{3,2,1,0:T(8,128)(2,1)S(1)}, u32[]{:S(2)}, u32[]{:S(2)}) collective-permute-start(bf16[2,5,64,512]{3,2,1,0:T(8,128)(2,1)S(1)} %pad_maximum_fusion.3.refs_1_), channel_id=1, source_target_pairs={{0,1},{1,0},{2,3},{3,2},{4,5},{5,4},{6,7},{7,6},{8,9},{9,8},{10,11... | collective-permute-start | bytes 1966088 | tf_op jit(solution)/shard_map/ppermute | solution.py:98
  182.7 14.0 %collective-permute-start.40 = (bf16[2,4,64,512]{3,2,1,0:T(8,128)(2,1)S(1)}, bf16[2,4,64,512]{3,2,1,0:T(8,128)(2,1)S(1)}, u32[]{:S(2)}, u32[]{:S(2)}) collective-permute-start(bf16[2,4,64,512]{3,2,1,0:T(8,128)(2,1)S(1)} %pad_maximum_fusion.8.refs_2_), channel_id=1, source_target_pairs={{0,4},{4,0},{8,12},{12,8},{1,5},{5,1},{9,13},{13,9},{2,6},{6,2},{1... | collective-permute-start | bytes 1572872 | tf_op jit(solution)/shard_map/ppermute | solution.py:90
  182.7 14.2 %collective-permute-start.38 = (bf16[2,5,64,512]{3,2,1,0:T(8,128)(2,1)S(1)}, bf16[2,5,64,512]{3,2,1,0:T(8,128)(2,1)S(1)}, u32[]{:S(2)}, u32[]{:S(2)}) collective-permute-start(bf16[2,5,64,512]{3,2,1,0:T(8,128)(2,1)S(1)} %pad_maximum_fusion.2.refs_0_), channel_id=1, source_target_pairs={{0,4},{4,0},{8,12},{12,8},{1,5},{5,1},{9,13},{13,9},{2,6},{6,2},{1... | collective-permute-start | bytes 1966088 | tf_op jit(solution)/shard_map/ppermute | solution.py:90
  190.5 7.0 %collective-permute-start.39 = (bf16[2,5,64,512]{3,2,1,0:T(8,128)(2,1)S(1)}, bf16[2,5,64,512]{3,2,1,0:T(8,128)(2,1)S(1)}, u32[]{:S(2)}, u32[]{:S(2)}) collective-permute-start(bf16[2,5,64,512]{3,2,1,0:T(8,128)(2,1)S(1)} %pad_maximum_fusion.3.refs_1_), channel_id=1, source_target_pairs={{0,4},{4,0},{8,12},{12,8},{1,5},{5,1},{9,13},{13,9},{2,6},{6,2},{1... | collective-permute-start | bytes 1966088 | tf_op jit(solution)/shard_map/ppermute | solution.py:90
  193.3 14.6 %collective-permute-start.35 = (bf16[2,5,64,512]{3,2,1,0:T(8,128)(2,1)S(1)}, bf16[2,5,64,512]{3,2,1,0:T(8,128)(2,1)}, u32[]{:S(2)}, u32[]{:S(2)}) collective-permute-start(bf16[2,5,64,512]{3,2,1,0:T(8,128)(2,1)S(1)} %pad_maximum_fusion.2.refs_0_), channel_id=1, source_target_pairs={{0,1},{1,0},{2,3},{3,2},{4,5},{5,4},{6,7},{7,6},{8,9},{9,8},{10,11... | collective-permute-start | bytes 1966088 | tf_op jit(solution)/shard_map/ppermute | solution.py:98
  193.3 14.6 %collective-permute-start.36 = (bf16[2,5,64,512]{3,2,1,0:T(8,128)(2,1)S(1)}, bf16[2,5,64,512]{3,2,1,0:T(8,128)(2,1)}, u32[]{:S(2)}, u32[]{:S(2)}) collective-permute-start(bf16[2,5,64,512]{3,2,1,0:T(8,128)(2,1)S(1)} %pad_maximum_fusion.3.refs_1_), channel_id=1, source_target_pairs={{0,8},{4,12},{8,0},{12,4},{1,9},{5,13},{9,1},{13,5},{2,10},{6,14},... | collective-permute-start | bytes 1966088 | tf_op jit(solution)/shard_map/ppermute | solution.py:86
  196.7 9.2 %collective-permute-start.37 = (bf16[2,4,64,512]{3,2,1,0:T(8,128)(2,1)S(1)}, bf16[2,4,64,512]{3,2,1,0:T(8,128)(2,1)S(1)}, u32[]{:S(2)}, u32[]{:S(2)}) collective-permute-start(bf16[2,4,64,512]{3,2,1,0:T(8,128)(2,1)S(1)} %pad_maximum_fusion.8.refs_2_), channel_id=1, source_target_pairs={{0,16},{16,0},{1,17},{17,1},{2,18},{18,2},{3,19},{19,3},{4,20},{20... | collective-permute-start | bytes 1572872 | tf_op jit(solution)/shard_map/ppermute | solution.py:94
  196.9 13.0 %collective-permute-start.43 = (bf16[2,4,64,512]{3,2,1,0:T(8,128)(2,1)S(1)}, bf16[2,4,64,512]{3,2,1,0:T(8,128)(2,1)S(1)}, u32[]{:S(2)}, u32[]{:S(2)}) collective-permute-start(bf16[2,4,64,512]{3,2,1,0:T(8,128)(2,1)S(1)} %collective-permute-done.34.refs_8_), channel_id=1, source_target_pairs={{0,4},{4,0},{8,12},{12,8},{1,5},{5,1},{9,13},{13,9},{2,6},{6,2},{1... | collective-permute-start | bytes 1572872 | tf_op jit(solution)/shard_map/ppermute | solution.py:90
  197.5 13.7 %collective-permute-start.41 = (bf16[2,5,64,512]{3,2,1,0:T(8,128)(2,1)S(1)}, bf16[2,5,64,512]{3,2,1,0:T(8,128)(2,1)S(1)}, u32[]{:S(2)}, u32[]{:S(2)}) collective-permute-start(bf16[2,5,64,512]{3,2,1,0:T(8,128)(2,1)S(1)} %collective-permute-done.32.refs_6_), channel_id=1, source_target_pairs={{0,4},{4,0},{8,12},{12,8},{1,5},{5,1},{9,13},{13,9},{2,6},{6,2},{1... | collective-permute-start | bytes 1966088 | tf_op jit(solution)/shard_map/ppermute | solution.py:90
  205.9 5.3 %collective-permute-start.42 = (bf16[2,5,64,512]{3,2,1,0:T(8,128)(2,1)S(1)}, bf16[2,5,64,512]{3,2,1,0:T(8,128)(2,1)S(1)}, u32[]{:S(2)}, u32[]{:S(2)}) collective-permute-start(bf16[2,5,64,512]{3,2,1,0:T(8,128)(2,1)S(1)} %collective-permute-done.33.refs_7_), channel_id=1, source_target_pairs={{0,4},{4,0},{8,12},{12,8},{1,5},{5,1},{9,13},{13,9},{2,6},{6,2},{1... | collective-permute-start | bytes 1966088 | tf_op jit(solution)/shard_map/ppermute | solution.py:90
  208.0 15.5 %collective-permute-start.47 = (bf16[2,5,64,512]{3,2,1,0:T(8,128)(2,1)S(1)}, bf16[2,5,64,512]{3,2,1,0:T(8,128)(2,1)}, u32[]{:S(2)}, u32[]{:S(2)}) collective-permute-start(bf16[2,5,64,512]{3,2,1,0:T(8,128)(2,1)S(1)} %collective-permute-done.32.refs_6_), channel_id=1, source_target_pairs={{0,1},{1,0},{2,3},{3,2},{4,5},{5,4},{6,7},{7,6},{8,9},{9,8},{10,11... | collective-permute-start | bytes 1966088 | tf_op jit(solution)/shard_map/ppermute | solution.py:98
  209.6 15.3 %collective-permute-start.48 = (bf16[2,5,64,512]{3,2,1,0:T(8,128)(2,1)S(1)}, bf16[2,5,64,512]{3,2,1,0:T(8,128)(2,1)}, u32[]{:S(2)}, u32[]{:S(2)}) collective-permute-start(bf16[2,5,64,512]{3,2,1,0:T(8,128)(2,1)S(1)} %collective-permute-done.33.refs_7_), channel_id=1, source_target_pairs={{0,8},{4,12},{8,0},{12,4},{1,9},{5,13},{9,1},{13,5},{2,10},{6,14},... | collective-permute-start | bytes 1966088 | tf_op jit(solution)/shard_map/ppermute | solution.py:86
  209.9 12.5 %collective-permute-start.49 = (bf16[2,4,64,512]{3,2,1,0:T(8,128)(2,1)S(1)}, bf16[2,4,64,512]{3,2,1,0:T(8,128)(2,1)}, u32[]{:S(2)}, u32[]{:S(2)}) collective-permute-start(bf16[2,4,64,512]{3,2,1,0:T(8,128)(2,1)S(1)} %collective-permute-done.34.refs_8_), channel_id=1, source_target_pairs={{0,16},{16,0},{1,17},{17,1},{2,18},{18,2},{3,19},{19,3},{4,20},{20... | collective-permute-start | bytes 1572872 | tf_op jit(solution)/shard_map/ppermute | solution.py:94
  211.2 13.7 %collective-permute-start.46 = (bf16[2,4,64,512]{3,2,1,0:T(8,128)(2,1)S(1)}, bf16[2,4,64,512]{3,2,1,0:T(8,128)(2,1)S(1)}, u32[]{:S(2)}, u32[]{:S(2)}) collective-permute-start(bf16[2,4,64,512]{3,2,1,0:T(8,128)(2,1)S(1)} %collective-permute-done.37.refs_14_), channel_id=1, source_target_pairs={{0,4},{4,0},{8,12},{12,8},{1,5},{5,1},{9,13},{13,9},{2,6},{6,2},{1... | collective-permute-start | bytes 1572872 | tf_op jit(solution)/shard_map/ppermute | solution.py:90
  211.2 15.0 %collective-permute-start.44 = (bf16[2,5,64,512]{3,2,1,0:T(8,128)(2,1)}, bf16[2,5,64,512]{3,2,1,0:T(8,128)(2,1)}, u32[]{:S(2)}, u32[]{:S(2)}) collective-permute-start(bf16[2,5,64,512]{3,2,1,0:T(8,128)(2,1)} %collective-permute-done.35.refs_12_), channel_id=1, source_target_pairs={{0,4},{4,0},{8,12},{12,8},{1,5},{5,1},{9,13},{13,9},{2,6},{6,2},{1... | collective-permute-start | bytes 1966088 | tf_op jit(solution)/shard_map/ppermute | solution.py:90
  222.4 3.9 %collective-permute-start.45 = (bf16[2,5,64,512]{3,2,1,0:T(8,128)(2,1)}, bf16[2,5,64,512]{3,2,1,0:T(8,128)(2,1)}, u32[]{:S(2)}, u32[]{:S(2)}) collective-permute-start(bf16[2,5,64,512]{3,2,1,0:T(8,128)(2,1)} %collective-permute-done.36.refs_13_), channel_id=1, source_target_pairs={{0,4},{4,0},{8,12},{12,8},{1,5},{5,1},{9,13},{13,9},{2,6},{6,2},{1... | collective-permute-start | bytes 1966088 | tf_op jit(solution)/shard_map/ppermute | solution.py:90
  223.4 4.7 %collective-permute-start.50 = (bf16[2,5,64,512]{3,2,1,0:T(8,128)(2,1)}, bf16[2,5,64,512]{3,2,1,0:T(8,128)(2,1)}, u32[]{:S(2)}, u32[]{:S(2)}) collective-permute-start(bf16[2,5,64,512]{3,2,1,0:T(8,128)(2,1)} %collective-permute-done.47.refs_18_), channel_id=1, source_target_pairs={{0,4},{4,0},{8,12},{12,8},{1,5},{5,1},{9,13},{13,9},{2,6},{6,2},{1... | collective-permute-start | bytes 1966088 | tf_op jit(solution)/shard_map/ppermute | solution.py:90
  224.9 3.2 collective-permute-start.51
  225.8 2.4 collective-permute-start.52
  250.7 33.6 %collective-permute-start.53 = (bf16[7,128,256]{2,1,0:T(8,128)(2,1)}, bf16[7,128,256]{2,1,0:T(8,128)(2,1)S(1)}, u32[]{:S(2)}, u32[]{:S(2)}) collective-permute-start(bf16[7,128,256]{2,1,0:T(8,128)(2,1)} %get-tuple-element.241), channel_id=1, source_target_pairs={{0,0},{1,1},{2,16},{3,17},{16,2},{17,3},{18,18},{19,19},{4,4},{5,5... | collective-permute-start | bytes 1376264 | tf_op jit(solution)/shard_map/ppermute | solution.py:138
  253.6 42.8 %collective-permute-start.54 = (bf16[7,128,256]{2,1,0:T(8,128)(2,1)}, bf16[7,128,256]{2,1,0:T(8,128)(2,1)S(1)}, u32[]{:S(2)}, u32[]{:S(2)}) collective-permute-start(bf16[7,128,256]{2,1,0:T(8,128)(2,1)} %get-tuple-element.242), channel_id=1, source_target_pairs={{0,1},{1,0},{2,17},{3,16},{16,3},{17,2},{18,19},{19,18},{4,5},{5,4... | collective-permute-start | bytes 1376264 | tf_op jit(solution)/shard_map/ppermute | solution.py:138
  256.2 40.1 %collective-permute-start.55 = (bf16[7,128,256]{2,1,0:T(8,128)(2,1)}, bf16[7,128,256]{2,1,0:T(8,128)(2,1)S(1)}, u32[]{:S(2)}, u32[]{:S(2)}) collective-permute-start(bf16[7,128,256]{2,1,0:T(8,128)(2,1)} %get-tuple-element.243), channel_id=1, source_target_pairs={{0,2},{1,3},{2,18},{3,19},{16,0},{17,1},{18,16},{19,17},{4,6},{5,7... | collective-permute-start | bytes 1376264 | tf_op jit(solution)/shard_map/ppermute | solution.py:138
  256.2 43.2 %collective-permute-start.56 = (bf16[7,128,256]{2,1,0:T(8,128)(2,1)}, bf16[7,128,256]{2,1,0:T(8,128)(2,1)S(1)}, u32[]{:S(2)}, u32[]{:S(2)}) collective-permute-start(bf16[7,128,256]{2,1,0:T(8,128)(2,1)} %get-tuple-element.244), channel_id=1, source_target_pairs={{0,3},{1,2},{2,19},{3,18},{16,1},{17,0},{18,17},{19,16},{4,7},{5,6... | collective-permute-start | bytes 1376264 | tf_op jit(solution)/shard_map/ppermute | solution.py:138
  299.4 32.0 %collective-permute-start.57 = (bf16[7,128,256]{2,1,0:T(8,128)(2,1)}, bf16[7,128,256]{2,1,0:T(8,128)(2,1)S(1)}, u32[]{:S(2)}, u32[]{:S(2)}) collective-permute-start(bf16[7,128,256]{2,1,0:T(8,128)(2,1)} %get-tuple-element.249), channel_id=1, source_target_pairs={{0,0},{1,1},{2,16},{3,17},{16,2},{17,3},{18,18},{19,19},{4,4},{5,5... | collective-permute-start | bytes 1376264 | tf_op jit(solution)/shard_map/ppermute | solution.py:138
  301.3 39.5 %collective-permute-start.58 = (bf16[7,128,256]{2,1,0:T(8,128)(2,1)}, bf16[7,128,256]{2,1,0:T(8,128)(2,1)S(1)}, u32[]{:S(2)}, u32[]{:S(2)}) collective-permute-start(bf16[7,128,256]{2,1,0:T(8,128)(2,1)} %get-tuple-element.250), channel_id=1, source_target_pairs={{0,1},{1,0},{2,17},{3,16},{16,3},{17,2},{18,19},{19,18},{4,5},{5,4... | collective-permute-start | bytes 1376264 | tf_op jit(solution)/shard_map/ppermute | solution.py:138
  301.9 41.3 %collective-permute-start.59 = (bf16[7,128,256]{2,1,0:T(8,128)(2,1)}, bf16[7,128,256]{2,1,0:T(8,128)(2,1)S(1)}, u32[]{:S(2)}, u32[]{:S(2)}) collective-permute-start(bf16[7,128,256]{2,1,0:T(8,128)(2,1)} %get-tuple-element.251), channel_id=1, source_target_pairs={{0,2},{1,3},{2,18},{3,19},{16,0},{17,1},{18,16},{19,17},{4,6},{5,7... | collective-permute-start | bytes 1376264 | tf_op jit(solution)/shard_map/ppermute | solution.py:138
  301.9 44.8 %collective-permute-start.60 = (bf16[7,128,256]{2,1,0:T(8,128)(2,1)}, bf16[7,128,256]{2,1,0:T(8,128)(2,1)S(1)}, u32[]{:S(2)}, u32[]{:S(2)}) collective-permute-start(bf16[7,128,256]{2,1,0:T(8,128)(2,1)} %get-tuple-element.252), channel_id=1, source_target_pairs={{0,3},{1,2},{2,19},{3,18},{16,1},{17,0},{18,17},{19,16},{4,7},{5,6... | collective-permute-start | bytes 1376264 | tf_op jit(solution)/shard_map/ppermute | solution.py:138
  (15 other events, 346.7 us)

commit v7 on v6

--- a/solution.py
+++ b/solution.py
@@ -33,7 +33,7 @@
 GROUP = COLS // 16
 HOPS = (1, 2, 4)
 LAST = (2, 2)
-PIECES = (3, 4)
+PIECES = (3, 2, 2)
 HALVES = 2
 WIDE = GROUP // HALVES
 GRAM_VMEM = 28 << 20
@@ -385,7 +385,7 @@
         return [keyed(group, arrays) for group, arrays in zip(groups, done[0])]
 
     own = [([0], piece) for piece in mine]
-    (pair,) = ordered(merge(own, move(0, own)))
+    pair = merge(own, move(0, own))
     second = move(1, pair)
     across(pair)
     pair, second = ordered(pair, second)
@@ -537,10 +537,12 @@
             parts = gram_call(EARLY_GROUPS, own, beside)
         else:
             parts = summed(EARLY_GROUPS, parts, n - 1)
+            own.append(joined(done[:1]))
+            beside.append(over_core(own[1]))
     out = (FACTOR * quint_a) * (iterate - lax.reduce_precision(iterate, 8, 7))
     out, parts, done = lax.optimization_barrier((out, parts, done))
-    own.append(joined(done))
-    beside.append(over_core(own[1]))
+    own.append(joined(done[1:]))
+    beside.append(over_core(own[2]))
     return own, beside, parts, out
 
 

time: 350 us -> 344 us (0.983)
    ppermute x8, waiting for transfers between devices: 30.1 us -> 26.2 us  [over_x(): return lax.ppermute(a, 'col', [(0, 2), (1, 3), (2, 0), (3, 1)])]
  transfers between devices with their start and end apart: 61 -> 62, of which waited for: 38 -> 38; matrix products, arithmetic and copies ran while one was open for 7% -> 8% of each run, Pallas kernels for 11% -> 11%
where the time goes in v7:
time: 344 us
  waiting for transfers between devices  196 us (57%)
  Pallas kernels  60.6 us (18%)
  starting transfers between devices  54.1 us (16%)
  other arithmetic  25.2 us (7%)
  local copies, waits for them, and re-layouts  6.7 us (2%)
    ppermute x20, waiting for transfers between devices, over_z(): return lax.ppermute(a, 'row', [(z, z ^ step) for z in range(4)])  76.7 us
    ppermute x11, waiting for transfers between devices, over_y(): return lax.ppermute(a, 'mats', [(0, 1), (1, 0)])  46.3 us
    pallas_call x2, Pallas kernels, step_call(): pl.pallas_call(functools.partial(step_kernel, keys, part), out_shape=[jax...  45 us
    ppermute x8, waiting for transfers between devices, home(): return lax.ppermute(a, ('mats', 'row'), pairs)  42.9 us
    ppermute x8, waiting for transfers between devices, over_x(): return lax.ppermute(a, 'col', [(0, 2), (1, 3), (2, 0), (3, 1)])  26.2 us
    ppermute x20, starting transfers between devices, over_z(): return lax.ppermute(a, 'row', [(z, z ^ step) for z in range(4)])  21 us
    dynamic_update_slice x8, other arithmetic, shards_cube(): lax.dynamic_update_slice_in_dim(out, pick(out, at, WIDE, 1) + piece, at, 1)  17.5 us
    ppermute x8, starting transfers between devices, home(): return lax.ppermute(a, ('mats', 'row'), pairs)  14.1 us
  transfers between devices with their start and end apart: 62, of which 38 were waited for; matrix products, arithmetic and copies ran while one was open for 8% of the time, Pallas kernels for 11%

profile of v7, /device:TPU:12, one launch (start us, length us, event | category | flops | bytes accessed | tf_op | source)
XLA Modules:
  0.0 343.6 jit_solution(16396594991298115303)
XLA Ops:
  1.6 1.7 dynamic-slice_convert_fusion.2
  3.3 2.5 dynamic-slice_convert_fusion
  5.9 3.3 collective-permute-done
  11.2 2.8 collective-permute-start.3
  14.4 8.8 %collective-permute-done.1 = bf16[256,1024]{1,0:T(8,128)(2,1)S(1)} collective-permute-done((bf16[256,1024]{1,0:T(8,128)(2,1)S(1)}, bf16[256,1024]{1,0:T(8,128)(2,1)S(1)}, u32[]{:S(2)}, u32[]{:S(2)}) %collective-permute-start.1) | collective-permute-done | bytes 524320 | tf_op jit(solution)/shard_map/ppermute | solution.py:94
  23.5 1.2 collective-permute-done.4
  24.7 1.5 collective-permute-start.5
  26.2 3.0 collective-permute-start.7
  29.7 5.7 %collective-permute-done.6 = bf16[256,512]{1,0:T(8,128)(2,1)S(1)} collective-permute-done((bf16[256,512]{1,0:T(8,128)(2,1)S(1)}, bf16[256,512]{1,0:T(8,128)(2,1)S(1)}, u32[]{:S(2)}, u32[]{:S(2)}) %collective-permute-start.6) | collective-permute-done | bytes 262176 | tf_op jit(solution)/shard_map/ppermute | solution.py:98
  35.4 10.8 %collective-permute-done.7 = bf16[256,512]{1,0:T(8,128)(2,1)S(1)} collective-permute-done((bf16[256,512]{1,0:T(8,128)(2,1)S(1)}, bf16[256,512]{1,0:T(8,128)(2,1)S(1)}, u32[]{:S(2)}, u32[]{:S(2)}) %collective-permute-start.7) | collective-permute-done | bytes 262176 | tf_op jit(solution)/shard_map/ppermute | solution.py:98
  46.3 4.2 %collective-permute-done.8 = bf16[256,512]{1,0:T(8,128)(2,1)S(1)} collective-permute-done((bf16[256,512]{1,0:T(8,128)(2,1)S(1)}, bf16[256,512]{1,0:T(8,128)(2,1)S(1)}, u32[]{:S(2)}, u32[]{:S(2)}) %collective-permute-start.8) | collective-permute-done | bytes 262176 | tf_op jit(solution)/shard_map/ppermute | solution.py:98
  51.5 1.4 collective-permute-start.11
  52.9 3.0 collective-permute-start.9
  56.0 3.1 gram.2
  59.2 10.3 %collective-permute-done.10 = bf16[256,512]{1,0:T(8,128)(2,1)S(1)} collective-permute-done((bf16[256,512]{1,0:T(8,128)(2,1)S(1)}, bf16[256,512]{1,0:T(8,128)(2,1)S(1)}, u32[]{:S(2)}, u32[]{:S(2)}) %collective-permute-start.10) | collective-permute-done | bytes 262176 | tf_op jit(solution)/shard_map/ppermute | solution.py:98
  69.5 7.1 %collective-permute-done.11 = bf16[256,512]{1,0:T(8,128)(2,1)S(1)} collective-permute-done((bf16[256,512]{1,0:T(8,128)(2,1)S(1)}, bf16[256,512]{1,0:T(8,128)(2,1)S(1)}, u32[]{:S(2)}, u32[]{:S(2)}) %collective-permute-start.11) | collective-permute-done | bytes 262176 | tf_op jit(solution)/shard_map/ppermute | solution.py:98
  76.6 1.5 collective-permute-start.13
  78.1 2.2 collective-permute-start.15
  80.3 1.3 collective-permute-start.16
  81.6 4.7 %fusion = f32[896,2048]{1,0:T(8,128)} fusion(f32[896,2048]{1,0:T(8,128)S(1)} %bitcast.38), kind=kLoop, calls=%fused_computation.1 | loop fusion | flops 5505024 | bytes 14680064 | tf_op jit(solution)/shard_map/mul | solution.py:542
  86.6 9.7 %collective-permute-done.13.refs_1_ = bf16[784,512]{1,0:T(8,128)(2,1)S(1)} collective-permute-done((bf16[784,512]{1,0:T(8,128)(2,1)S(1)}, bf16[784,512]{1,0:T(8,128)(2,1)S(1)}, u32[]{:S(2)}, u32[]{:S(2)}) %collective-permute-start.13) | collective-permute-done | bytes 802848 | tf_op jit(solution)/shard_map/ppermute | solution.py:86
  96.8 1.5 collective-permute-done.15
  98.3 5.7 %collective-permute-done.16 = bf16[256,512]{1,0:T(8,128)(2,1)S(1)} collective-permute-done((bf16[256,512]{1,0:T(8,128)(2,1)S(1)}, bf16[256,512]{1,0:T(8,128)(2,1)S(1)}, u32[]{:S(2)}, u32[]{:S(2)}) %collective-permute-start.16) | collective-permute-done | bytes 262176 | tf_op jit(solution)/shard_map/ppermute | solution.py:98
  105.1 1.8 collective-permute-done.19.refs_5_
  106.9 9.9 %gram.3 = (f32[4,4,64,512]{3,2,1,0:T(8,128)S(1)}, bf16[1040,512]{1,0:T(8,128)(2,1)S(1)}, f32[4,4,64,512]{3,2,1,0:T(8,128)S(1)}, bf16[1040,512]{1,0:T(8,128)(2,1)...) custom-call(bf16[4,3,128,512]{3,2,1,0:T(8,128)(2,1)S(1)} %pad_maximum_fusion.refs_0_.refs_24_, ...), custom_call_target="tpu_custom_call" | custom-call | flops 7516192768 | bytes 458752 | tf_op jit(solution)/shard_map/gram/pallas_call | solution.py:296
  118.5 2.1 collective-permute-start.23
  120.6 21.6 %collective-permute-done.23.refs_1_ = bf16[208,512]{1,0:T(8,128)(2,1)S(1)} collective-permute-done((bf16[208,512]{1,0:T(8,128)(2,1)S(1)}, bf16[208,512]{1,0:T(8,128)(2,1)S(1)}, u32[]{:S(2)}, u32[]{:S(2)}) %collective-permute-start.23) | collective-permute-done | bytes 213024 | tf_op jit(solution)/shard_map/ppermute | solution.py:98
  144.9 1.5 collective-permute-start.26
  146.4 8.4 %collective-permute-done.26.refs_5_ = bf16[400,512]{1,0:T(8,128)(2,1)S(1)} collective-permute-done((bf16[400,512]{1,0:T(8,128)(2,1)S(1)}, bf16[400,512]{1,0:T(8,128)(2,1)S(1)}, u32[]{:S(2)}, u32[]{:S(2)}) %collective-permute-start.26) | collective-permute-done | bytes 409632 | tf_op jit(solution)/shard_map/ppermute | solution.py:86
  154.8 2.3 collective-permute-done.24.refs_1_
  158.4 1.4 collective-permute-start.28
  159.8 1.2 collective-permute-start.29
  161.0 4.6 %collective-permute-done.29.refs_5_ = bf16[208,512]{1,0:T(8,128)(2,1)S(1)} collective-permute-done((bf16[208,512]{1,0:T(8,128)(2,1)S(1)}, bf16[208,512]{1,0:T(8,128)(2,1)S(1)}, u32[]{:S(2)}, u32[]{:S(2)}) %collective-permute-start.29) | collective-permute-done | bytes 213024 | tf_op jit(solution)/shard_map/ppermute | solution.py:94
  165.9 2.4 collective-permute-start.32
  169.6 3.7 %collective-permute-done.32 = bf16[1,4,64,512]{3,2,1,0:T(8,128)(2,1)S(1)} collective-permute-done((bf16[1,4,64,512]{3,2,1,0:T(8,128)(2,1)S(1)}, bf16[1,4,64,512]{3,2,1,0:T(8,128)(2,1)S(1)}, u32[]{:S(2)}, u32[]{:S(2)}) %collective-permute-start.32) | collective-permute-done | bytes 262176 | tf_op jit(solution)/shard_map/ppermute | solution.py:98
  173.5 3.6 %collective-permute-done.31 = bf16[1,5,64,512]{3,2,1,0:T(8,128)(2,1)S(1)} collective-permute-done((bf16[1,5,64,512]{3,2,1,0:T(8,128)(2,1)S(1)}, bf16[1,5,64,512]{3,2,1,0:T(8,128)(2,1)S(1)}, u32[]{:S(2)}, u32[]{:S(2)}) %collective-permute-start.31) | collective-permute-done | bytes 327712 | tf_op jit(solution)/shard_map/ppermute | solution.py:94
  177.2 2.8 collective-permute-done.30
  181.5 4.0 %collective-permute-done.35.refs_8_ = bf16[2,4,64,512]{3,2,1,0:T(8,128)(2,1)S(1)} collective-permute-done((bf16[2,4,64,512]{3,2,1,0:T(8,128)(2,1)S(1)}, bf16[2,4,64,512]{3,2,1,0:T(8,128)(2,1)S(1)}, u32[]{:S(2)}, u32[]{:S(2)}) %collective-permute-start.35) | collective-permute-done | bytes 524320 | tf_op jit(solution)/shard_map/ppermute | solution.py:86
  185.6 2.2 collective-permute-done.34.refs_7_
  187.8 3.2 collective-permute-done.33.refs_6_
  192.5 9.4 %collective-permute-done.38.refs_14_ = bf16[2,4,64,512]{3,2,1,0:T(8,128)(2,1)S(1)} collective-permute-done((bf16[2,4,64,512]{3,2,1,0:T(8,128)(2,1)S(1)}, bf16[2,4,64,512]{3,2,1,0:T(8,128)(2,1)S(1)}, u32[]{:S(2)}, u32[]{:S(2)}) %collective-permute-start.38) | collective-permute-done | bytes 524320 | tf_op jit(solution)/shard_map/ppermute | solution.py:94
  207.1 11.0 %collective-permute-done.50.refs_20_ = bf16[2,4,64,512]{3,2,1,0:T(8,128)(2,1)} collective-permute-done((bf16[2,4,64,512]{3,2,1,0:T(8,128)(2,1)S(1)}, bf16[2,4,64,512]{3,2,1,0:T(8,128)(2,1)}, u32[]{:S(2)}, u32[]{:S(2)}) %collective-permute-start.50) | collective-permute-done | bytes 524320 | tf_op jit(solution)/shard_map/ppermute | solution.py:94
  220.8 2.5 collective-permute-done.53.refs_23_
  223.3 22.5 %step.2 = (bf16[7,128,256]{2,1,0:T(8,128)(2,1)}, bf16[7,128,256]{2,1,0:T(8,128)(2,1)}, bf16[7,128,256]{2,1,0:T(8,128)(2,1)}, bf16[7,128,256]{2,1,0:T(8,128)(2,1)}) custom-call(bf16[2,5,64,512]{3,2,1,0:T(8,128)(2,1)} %copy-done.4, bf16[2,5,64,512]{3,2,1,0:T(8,128)(2,1)} %copy-done.3, bf16[2,4,64,512]{3,2,1,0:T(8,128)(2,1)} %copy-done.5, ...), custom_call_target="tpu_custom_call" | custom-call | flops 13153337344 | bytes 20971520 | tf_op jit(solution)/shard_map/step/pallas_call | solution.py:469
  245.9 3.3 collective-permute-start.54
  249.2 1.9 collective-permute-start.55
  251.1 2.5 collective-permute-start.57
  253.6 22.4 %step.3 = (bf16[7,128,256]{2,1,0:T(8,128)(2,1)}, bf16[7,128,256]{2,1,0:T(8,128)(2,1)}, bf16[7,128,256]{2,1,0:T(8,128)(2,1)}, bf16[7,128,256]{2,1,0:T(8,128)(2,1)}) custom-call(bf16[2,5,64,512]{3,2,1,0:T(8,128)(2,1)} %copy-done.4, bf16[2,5,64,512]{3,2,1,0:T(8,128)(2,1)} %copy-done.3, bf16[2,4,64,512]{3,2,1,0:T(8,128)(2,1)} %copy-done.5, ...), custom_call_target="tpu_custom_call" | custom-call | flops 13153337344 | bytes 20971520 | tf_op jit(solution)/shard_map/step/pallas_call | solution.py:469
  276.1 3.8 %collective-permute-done.54 = bf16[7,128,256]{2,1,0:T(8,128)(2,1)S(1)} collective-permute-done((bf16[7,128,256]{2,1,0:T(8,128)(2,1)}, bf16[7,128,256]{2,1,0:T(8,128)(2,1)S(1)}, u32[]{:S(2)}, u32[]{:S(2)}) %collective-permute-start.54) | collective-permute-done | bytes 458784 | tf_op jit(solution)/shard_map/ppermute | solution.py:138
  279.8 11.6 %collective-permute-done.55 = bf16[7,128,256]{2,1,0:T(8,128)(2,1)S(1)} collective-permute-done((bf16[7,128,256]{2,1,0:T(8,128)(2,1)}, bf16[7,128,256]{2,1,0:T(8,128)(2,1)S(1)}, u32[]{:S(2)}, u32[]{:S(2)}) %collective-permute-start.55) | collective-permute-done | bytes 458784 | tf_op jit(solution)/shard_map/ppermute | solution.py:138
  291.5 2.8 collective-permute-done.57
  294.3 1.9 collective-permute-start.58
  296.2 1.2 collective-permute-start.59
  297.4 3.3 collective-permute-start.61
  300.8 2.2 constant_dynamic-update-slice_fusion.7
  303.1 2.2 constant_dynamic-update-slice_fusion.6
  305.3 2.2 constant_dynamic-update-slice_fusion.5
  307.6 2.2 constant_dynamic-update-slice_fusion.4
  309.8 17.1 %collective-permute-done.58 = bf16[7,128,256]{2,1,0:T(8,128)(2,1)S(1)} collective-permute-done((bf16[7,128,256]{2,1,0:T(8,128)(2,1)}, bf16[7,128,256]{2,1,0:T(8,128)(2,1)S(1)}, u32[]{:S(2)}, u32[]{:S(2)}) %collective-permute-start.58) | collective-permute-done | bytes 458784 | tf_op jit(solution)/shard_map/ppermute | solution.py:138
  327.0 2.2 constant_dynamic-update-slice_fusion.3
  329.2 7.2 %collective-permute-done.59 = bf16[7,128,256]{2,1,0:T(8,128)(2,1)S(1)} collective-permute-done((bf16[7,128,256]{2,1,0:T(8,128)(2,1)}, bf16[7,128,256]{2,1,0:T(8,128)(2,1)S(1)}, u32[]{:S(2)}, u32[]{:S(2)}) %collective-permute-start.59) | collective-permute-done | bytes 458784 | tf_op jit(solution)/shard_map/ppermute | solution.py:138
  336.5 2.2 constant_dynamic-update-slice_fusion.2
  338.8 2.2 constant_dynamic-update-slice_fusion.1
  341.4 2.2 constant_dynamic-update-slice_fusion
  (153 shorter events, 27.2 us)
Async XLA Ops:
  1.1 8.1 %collective-permute-start = (bf16[128,1024]{1,0:T(8,128)(2,1)S(1)}, bf16[128,1024]{1,0:T(8,128)(2,1)S(1)}, u32[]{:S(2)}, u32[]{:S(2)}) collective-permute-start(bf16[128,1024]{1,0:T(8,128)(2,1)S(1)} %dynamic-slice_convert_fusion.4), channel_id=1, source_target_pairs={{0,16},{16,0},{1,17},{17,1},{2,18},{18,2},{3,19},{19,3},{4,20},{20... | collective-permute-start | bytes 786440 | tf_op jit(solution)/shard_map/ppermute | solution.py:94
  10.4 12.9 %collective-permute-start.1 = (bf16[256,1024]{1,0:T(8,128)(2,1)S(1)}, bf16[256,1024]{1,0:T(8,128)(2,1)S(1)}, u32[]{:S(2)}, u32[]{:S(2)}) collective-permute-start(bf16[256,1024]{1,0:T(8,128)(2,1)S(1)} %get-tuple-element.123), channel_id=1, source_target_pairs={{0,16},{16,0},{1,17},{17,1},{2,18},{18,2},{3,19},{19,3},{4,20},{20... | collective-permute-start | bytes 1572872 | tf_op jit(solution)/shard_map/ppermute | solution.py:94
  10.9 12.5 %collective-permute-start.2 = (bf16[128,512]{1,0:T(8,128)(2,1)S(1)}, bf16[128,512]{1,0:T(8,128)(2,1)S(1)}, u32[]{:S(2)}, u32[]{:S(2)}) collective-permute-start(bf16[128,512]{1,0:T(8,128)(2,1)S(1)} %get-tuple-element.127), channel_id=1, source_target_pairs={{0,1},{1,0},{2,3},{3,2},{4,5},{5,4},{6,7},{7,6},{8,9},{9,8},{10,11... | collective-permute-start | bytes 393224 | tf_op jit(solution)/shard_map/ppermute | solution.py:98
  11.2 12.3 %collective-permute-start.3 = (bf16[128,512]{1,0:T(8,128)(2,1)S(1)}, bf16[128,512]{1,0:T(8,128)(2,1)S(1)}, u32[]{:S(2)}, u32[]{:S(2)}) collective-permute-start(bf16[128,512]{1,0:T(8,128)(2,1)S(1)} %get-tuple-element.128), channel_id=1, source_target_pairs={{0,2},{1,3},{2,0},{3,1},{4,6},{5,7},{6,4},{7,5},{8,10},{9,11},{10,... | collective-permute-start | bytes 393224 | tf_op jit(solution)/shard_map/ppermute | solution.py:98
  14.0 10.7 %collective-permute-start.4 = (bf16[128,512]{1,0:T(8,128)(2,1)S(1)}, bf16[128,512]{1,0:T(8,128)(2,1)S(1)}, u32[]{:S(2)}, u32[]{:S(2)}) collective-permute-start(bf16[128,512]{1,0:T(8,128)(2,1)S(1)} %get-tuple-element.129), channel_id=1, source_target_pairs={{0,3},{1,2},{2,1},{3,0},{4,7},{5,6},{6,5},{7,4},{8,11},{9,10},{10,... | collective-permute-start | bytes 393224 | tf_op jit(solution)/shard_map/ppermute | solution.py:98
  24.7 26.1 %collective-permute-start.5 = (bf16[512,1024]{1,0:T(8,128)(2,1)S(1)}, bf16[512,1024]{1,0:T(8,128)(2,1)S(1)}, u32[]{:S(2)}, u32[]{:S(2)}) collective-permute-start(bf16[512,1024]{1,0:T(8,128)(2,1)S(1)} %get-tuple-element.131), channel_id=1, source_target_pairs={{0,16},{16,0},{1,17},{17,1},{2,18},{18,2},{3,19},{19,3},{4,20},{20... | collective-permute-start | bytes 3145736 | tf_op jit(solution)/shard_map/ppermute | solution.py:94
  26.2 9.2 %collective-permute-start.6 = (bf16[256,512]{1,0:T(8,128)(2,1)S(1)}, bf16[256,512]{1,0:T(8,128)(2,1)S(1)}, u32[]{:S(2)}, u32[]{:S(2)}) collective-permute-start(bf16[256,512]{1,0:T(8,128)(2,1)S(1)} %get-tuple-element.135), channel_id=1, source_target_pairs={{0,1},{1,0},{2,3},{3,2},{4,5},{5,4},{6,7},{7,6},{8,9},{9,8},{10,11... | collective-permute-start | bytes 786440 | tf_op jit(solution)/shard_map/ppermute | solution.py:98
  26.2 20.1 %collective-permute-start.7 = (bf16[256,512]{1,0:T(8,128)(2,1)S(1)}, bf16[256,512]{1,0:T(8,128)(2,1)S(1)}, u32[]{:S(2)}, u32[]{:S(2)}) collective-permute-start(bf16[256,512]{1,0:T(8,128)(2,1)S(1)} %get-tuple-element.137), channel_id=1, source_target_pairs={{0,2},{1,3},{2,0},{3,1},{4,6},{5,7},{6,4},{7,5},{8,10},{9,11},{10,... | collective-permute-start | bytes 786440 | tf_op jit(solution)/shard_map/ppermute | solution.py:98
  29.2 21.2 %collective-permute-start.8 = (bf16[256,512]{1,0:T(8,128)(2,1)S(1)}, bf16[256,512]{1,0:T(8,128)(2,1)S(1)}, u32[]{:S(2)}, u32[]{:S(2)}) collective-permute-start(bf16[256,512]{1,0:T(8,128)(2,1)S(1)} %get-tuple-element.139), channel_id=1, source_target_pairs={{0,3},{1,2},{2,1},{3,0},{4,7},{5,6},{6,5},{7,4},{8,11},{9,10},{10,... | collective-permute-start | bytes 786440 | tf_op jit(solution)/shard_map/ppermute | solution.py:98
  50.7 56.1 %copy-start = (bf16[4,3,128,512]{3,2,1,0:T(8,128)(2,1)}, bf16[4,3,128,512]{3,2,1,0:T(8,128)(2,1)S(1)}, u32[]{:S(2)}) copy-start(bf16[4,3,128,512]{3,2,1,0:T(8,128)(2,1)S(1)} %pad_maximum_fusion.refs_0_.refs_24_) | copy-start | bytes 4718596
  51.4 4.6 %collective-permute-start.12 = (bf16[4,3,128,512]{3,2,1,0:T(8,128)(2,1)S(1)}, bf16[4,3,128,512]{3,2,1,0:T(8,128)(2,1)S(1)}, u32[]{:S(2)}, u32[]{:S(2)}) collective-permute-start(bf16[4,3,128,512]{3,2,1,0:T(8,128)(2,1)S(1)} %pad_maximum_fusion.refs_0_.refs_24_), channel_id=1, source_target_pairs={{0,4},{4,0},{8,12},{12,8},{1,5},{5,1},{9,13},{13,9},{2,6},{6,2},{1... | collective-permute-start | bytes 4718600 | tf_op jit(solution)/shard_map/ppermute | solution.py:90
  51.5 18.0 %collective-permute-start.10 = (bf16[256,512]{1,0:T(8,128)(2,1)S(1)}, bf16[256,512]{1,0:T(8,128)(2,1)S(1)}, u32[]{:S(2)}, u32[]{:S(2)}) collective-permute-start(bf16[256,512]{1,0:T(8,128)(2,1)S(1)} %get-tuple-element.146), channel_id=1, source_target_pairs={{0,2},{1,3},{2,0},{3,1},{4,6},{5,7},{6,4},{7,5},{8,10},{9,11},{10,... | collective-permute-start | bytes 786440 | tf_op jit(solution)/shard_map/ppermute | solution.py:98
  51.5 25.1 %collective-permute-start.11 = (bf16[256,512]{1,0:T(8,128)(2,1)S(1)}, bf16[256,512]{1,0:T(8,128)(2,1)S(1)}, u32[]{:S(2)}, u32[]{:S(2)}) collective-permute-start(bf16[256,512]{1,0:T(8,128)(2,1)S(1)} %get-tuple-element.147), channel_id=1, source_target_pairs={{0,3},{1,2},{2,1},{3,0},{4,7},{5,6},{6,5},{7,4},{8,11},{9,10},{10,... | collective-permute-start | bytes 786440 | tf_op jit(solution)/shard_map/ppermute | solution.py:98
  52.9 23.7 %collective-permute-start.9 = (bf16[256,512]{1,0:T(8,128)(2,1)S(1)}, bf16[256,512]{1,0:T(8,128)(2,1)S(1)}, u32[]{:S(2)}, u32[]{:S(2)}) collective-permute-start(bf16[256,512]{1,0:T(8,128)(2,1)S(1)} %get-tuple-element.145), channel_id=1, source_target_pairs={{0,1},{1,0},{2,3},{3,2},{4,5},{5,4},{6,7},{7,6},{8,9},{9,8},{10,11... | collective-permute-start | bytes 786440 | tf_op jit(solution)/shard_map/ppermute | solution.py:98
  76.6 19.6 %collective-permute-start.13 = (bf16[784,512]{1,0:T(8,128)(2,1)S(1)}, bf16[784,512]{1,0:T(8,128)(2,1)S(1)}, u32[]{:S(2)}, u32[]{:S(2)}) collective-permute-start(bf16[784,512]{1,0:T(8,128)(2,1)S(1)} %get-tuple-element.152), channel_id=1, source_target_pairs={{0,8},{4,12},{8,0},{12,4},{1,9},{5,13},{9,1},{13,5},{2,10},{6,14},... | collective-permute-start | bytes 2408456 | tf_op jit(solution)/shard_map/ppermute | solution.py:86
  78.1 18.7 %collective-permute-start.14 = (bf16[256,512]{1,0:T(8,128)(2,1)S(1)}, bf16[256,512]{1,0:T(8,128)(2,1)S(1)}, u32[]{:S(2)}, u32[]{:S(2)}) collective-permute-start(bf16[256,512]{1,0:T(8,128)(2,1)S(1)} %slice.29), channel_id=1, source_target_pairs={{0,1},{1,0},{2,3},{3,2},{4,5},{5,4},{6,7},{7,6},{8,9},{9,8},{10,11... | collective-permute-start | bytes 786440 | tf_op jit(solution)/shard_map/ppermute | solution.py:98
  78.1 20.2 %collective-permute-start.15 = (bf16[256,512]{1,0:T(8,128)(2,1)S(1)}, bf16[256,512]{1,0:T(8,128)(2,1)S(1)}, u32[]{:S(2)}, u32[]{:S(2)}) collective-permute-start(bf16[256,512]{1,0:T(8,128)(2,1)S(1)} %slice.30), channel_id=1, source_target_pairs={{0,2},{1,3},{2,0},{3,1},{4,6},{5,7},{6,4},{7,5},{8,10},{9,11},{10,... | collective-permute-start | bytes 786440 | tf_op jit(solution)/shard_map/ppermute | solution.py:98
  80.3 23.7 %collective-permute-start.16 = (bf16[256,512]{1,0:T(8,128)(2,1)S(1)}, bf16[256,512]{1,0:T(8,128)(2,1)S(1)}, u32[]{:S(2)}, u32[]{:S(2)}) collective-permute-start(bf16[256,512]{1,0:T(8,128)(2,1)S(1)} %slice.31), channel_id=1, source_target_pairs={{0,3},{1,2},{2,1},{3,0},{4,7},{5,6},{6,5},{7,4},{8,11},{9,10},{10,... | collective-permute-start | bytes 786440 | tf_op jit(solution)/shard_map/ppermute | solution.py:98
  86.5 18.6 %collective-permute-start.18 = (bf16[4,2,128,512]{3,2,1,0:T(8,128)(2,1)S(1)}, bf16[4,2,128,512]{3,2,1,0:T(8,128)(2,1)S(1)}, u32[]{:S(2)}, u32[]{:S(2)}) collective-permute-start(bf16[4,2,128,512]{3,2,1,0:T(8,128)(2,1)S(1)} %pad_maximum_fusion.1.refs_1_.refs_25_), channel_id=1, source_target_pairs={{0,4},{4,0},{8,12},{12,8},{1,5},{5,1},{9,13},{13,9},{2,6},{6,2},{1... | collective-permute-start | bytes 3145736 | tf_op jit(solution)/shard_map/ppermute | solution.py:90
  104.1 2.7 collective-permute-start.19
  104.2 12.6 %collective-permute-start.17 = (bf16[400,512]{1,0:T(8,128)(2,1)S(1)}, bf16[400,512]{1,0:T(8,128)(2,1)S(1)}, u32[]{:S(2)}, u32[]{:S(2)}) collective-permute-start(bf16[400,512]{1,0:T(8,128)(2,1)S(1)} %get-tuple-element.165), channel_id=1, source_target_pairs={{0,16},{16,0},{1,17},{17,1},{2,18},{18,2},{3,19},{19,3},{4,20},{20... | collective-permute-start | bytes 1228808 | tf_op jit(solution)/shard_map/ppermute | solution.py:94
  116.9 25.6 %collective-permute-start.20 = (bf16[1040,512]{1,0:T(8,128)(2,1)S(1)}, bf16[1040,512]{1,0:T(8,128)(2,1)S(1)}, u32[]{:S(2)}, u32[]{:S(2)}) collective-permute-start(bf16[1040,512]{1,0:T(8,128)(2,1)S(1)} %get-tuple-element.178), channel_id=1, source_target_pairs={{0,8},{4,12},{8,0},{12,4},{1,9},{5,13},{9,1},{13,5},{2,10},{6,14},... | collective-permute-start | bytes 3194888 | tf_op jit(solution)/shard_map/ppermute | solution.py:86
  117.5 25.3 %collective-permute-start.21 = (bf16[1040,512]{1,0:T(8,128)(2,1)S(1)}, bf16[1040,512]{1,0:T(8,128)(2,1)S(1)}, u32[]{:S(2)}, u32[]{:S(2)}) collective-permute-start(bf16[1040,512]{1,0:T(8,128)(2,1)S(1)} %get-tuple-element.180), channel_id=1, source_target_pairs={{0,16},{16,0},{1,17},{17,1},{2,18},{18,2},{3,19},{19,3},{4,20},{20... | collective-permute-start | bytes 3194888 | tf_op jit(solution)/shard_map/ppermute | solution.py:94
  118.3 24.0 %collective-permute-start.22 = (bf16[784,512]{1,0:T(8,128)(2,1)S(1)}, bf16[784,512]{1,0:T(8,128)(2,1)S(1)}, u32[]{:S(2)}, u32[]{:S(2)}) collective-permute-start(bf16[784,512]{1,0:T(8,128)(2,1)S(1)} %get-tuple-element.182), channel_id=1, source_target_pairs={{0,1},{1,0},{2,3},{3,2},{4,5},{5,4},{6,7},{7,6},{8,9},{9,8},{10,11... | collective-permute-start | bytes 2408456 | tf_op jit(solution)/shard_map/ppermute | solution.py:98
  118.5 23.7 %collective-permute-start.23 = (bf16[208,512]{1,0:T(8,128)(2,1)S(1)}, bf16[208,512]{1,0:T(8,128)(2,1)S(1)}, u32[]{:S(2)}, u32[]{:S(2)}) collective-permute-start(bf16[208,512]{1,0:T(8,128)(2,1)S(1)} %get-tuple-element.192), channel_id=1, source_target_pairs={{0,1},{1,0},{2,3},{3,2},{4,5},{5,4},{6,7},{7,6},{8,9},{9,8},{10,11... | collective-permute-start | bytes 638984 | tf_op jit(solution)/shard_map/ppermute | solution.py:98
  143.7 13.3 %collective-permute-start.24 = (bf16[528,512]{1,0:T(8,128)(2,1)S(1)}, bf16[528,512]{1,0:T(8,128)(2,1)S(1)}, u32[]{:S(2)}, u32[]{:S(2)}) collective-permute-start(bf16[528,512]{1,0:T(8,128)(2,1)S(1)} %get-tuple-element.194), channel_id=1, source_target_pairs={{0,16},{16,0},{1,17},{17,1},{2,18},{18,2},{3,19},{19,3},{4,20},{20... | collective-permute-start | bytes 1622024 | tf_op jit(solution)/shard_map/ppermute | solution.py:94
  144.6 12.9 %collective-permute-start.25 = (bf16[528,512]{1,0:T(8,128)(2,1)S(1)}, bf16[528,512]{1,0:T(8,128)(2,1)S(1)}, u32[]{:S(2)}, u32[]{:S(2)}) collective-permute-start(bf16[528,512]{1,0:T(8,128)(2,1)S(1)} %get-tuple-element.196), channel_id=1, source_target_pairs={{0,1},{1,0},{2,3},{3,2},{4,5},{5,4},{6,7},{7,6},{8,9},{9,8},{10,11... | collective-permute-start | bytes 1622024 | tf_op jit(solution)/shard_map/ppermute | solution.py:98
  144.9 9.9 %collective-permute-start.26 = (bf16[400,512]{1,0:T(8,128)(2,1)S(1)}, bf16[400,512]{1,0:T(8,128)(2,1)S(1)}, u32[]{:S(2)}, u32[]{:S(2)}) collective-permute-start(bf16[400,512]{1,0:T(8,128)(2,1)S(1)} %get-tuple-element.198), channel_id=1, source_target_pairs={{0,8},{4,12},{8,0},{12,4},{1,9},{5,13},{9,1},{13,5},{2,10},{6,14},... | collective-permute-start | bytes 1228808 | tf_op jit(solution)/shard_map/ppermute | solution.py:86
  158.0 7.6 %collective-permute-start.27 = (bf16[272,512]{1,0:T(8,128)(2,1)S(1)}, bf16[272,512]{1,0:T(8,128)(2,1)S(1)}, u32[]{:S(2)}, u32[]{:S(2)}) collective-permute-start(bf16[272,512]{1,0:T(8,128)(2,1)S(1)} %get-tuple-element.200), channel_id=1, source_target_pairs={{0,1},{1,0},{2,3},{3,2},{4,5},{5,4},{6,7},{7,6},{8,9},{9,8},{10,11... | collective-permute-start | bytes 835592 | tf_op jit(solution)/shard_map/ppermute | solution.py:98
  158.4 7.3 %collective-permute-start.28 = (bf16[272,512]{1,0:T(8,128)(2,1)S(1)}, bf16[272,512]{1,0:T(8,128)(2,1)S(1)}, u32[]{:S(2)}, u32[]{:S(2)}) collective-permute-start(bf16[272,512]{1,0:T(8,128)(2,1)S(1)} %get-tuple-element.202), channel_id=1, source_target_pairs={{0,8},{4,12},{8,0},{12,4},{1,9},{5,13},{9,1},{13,5},{2,10},{6,14},... | collective-permute-start | bytes 835592 | tf_op jit(solution)/shard_map/ppermute | solution.py:86
  159.8 5.8 %collective-permute-start.29 = (bf16[208,512]{1,0:T(8,128)(2,1)S(1)}, bf16[208,512]{1,0:T(8,128)(2,1)S(1)}, u32[]{:S(2)}, u32[]{:S(2)}) collective-permute-start(bf16[208,512]{1,0:T(8,128)(2,1)S(1)} %get-tuple-element.204), channel_id=1, source_target_pairs={{0,16},{16,0},{1,17},{17,1},{2,18},{18,2},{3,19},{19,3},{4,20},{20... | collective-permute-start | bytes 638984 | tf_op jit(solution)/shard_map/ppermute | solution.py:94
  165.9 7.5 %collective-permute-start.32 = (bf16[1,4,64,512]{3,2,1,0:T(8,128)(2,1)S(1)}, bf16[1,4,64,512]{3,2,1,0:T(8,128)(2,1)S(1)}, u32[]{:S(2)}, u32[]{:S(2)}) collective-permute-start(bf16[1,4,64,512]{3,2,1,0:T(8,128)(2,1)S(1)} %bitcast.35), channel_id=1, source_target_pairs={{0,1},{1,0},{2,3},{3,2},{4,5},{5,4},{6,7},{7,6},{8,9},{9,8},{10,11... | collective-permute-start | bytes 786440 | tf_op jit(solution)/shard_map/ppermute | solution.py:98
  168.3 8.7 %collective-permute-start.31 = (bf16[1,5,64,512]{3,2,1,0:T(8,128)(2,1)S(1)}, bf16[1,5,64,512]{3,2,1,0:T(8,128)(2,1)S(1)}, u32[]{:S(2)}, u32[]{:S(2)}) collective-permute-start(bf16[1,5,64,512]{3,2,1,0:T(8,128)(2,1)S(1)} %bitcast.33), channel_id=1, source_target_pairs={{0,16},{16,0},{1,17},{17,1},{2,18},{18,2},{3,19},{19,3},{4,20},{20... | collective-permute-start | bytes 983048 | tf_op jit(solution)/shard_map/ppermute | solution.py:94
  169.3 10.6 %collective-permute-start.30 = (bf16[1,5,64,512]{3,2,1,0:T(8,128)(2,1)S(1)}, bf16[1,5,64,512]{3,2,1,0:T(8,128)(2,1)S(1)}, u32[]{:S(2)}, u32[]{:S(2)}) collective-permute-start(bf16[1,5,64,512]{3,2,1,0:T(8,128)(2,1)S(1)} %bitcast.31), channel_id=1, source_target_pairs={{0,8},{4,12},{8,0},{12,4},{1,9},{5,13},{9,1},{13,5},{2,10},{6,14},... | collective-permute-start | bytes 983048 | tf_op jit(solution)/shard_map/ppermute | solution.py:86
  173.4 49.9 %copy-start.5 = (bf16[2,4,64,512]{3,2,1,0:T(8,128)(2,1)}, bf16[2,4,64,512]{3,2,1,0:T(8,128)(2,1)S(1)}, u32[]{:S(2)}) copy-start(bf16[2,4,64,512]{3,2,1,0:T(8,128)(2,1)S(1)} %pad_maximum_fusion.5.refs_2_) | copy-start | bytes 1572868
  173.4 12.2 %collective-permute-start.35 = (bf16[2,4,64,512]{3,2,1,0:T(8,128)(2,1)S(1)}, bf16[2,4,64,512]{3,2,1,0:T(8,128)(2,1)S(1)}, u32[]{:S(2)}, u32[]{:S(2)}) collective-permute-start(bf16[2,4,64,512]{3,2,1,0:T(8,128)(2,1)S(1)} %pad_maximum_fusion.5.refs_2_), channel_id=1, source_target_pairs={{0,8},{4,12},{8,0},{12,4},{1,9},{5,13},{9,1},{13,5},{2,10},{6,14},... | collective-permute-start | bytes 1572872 | tf_op jit(solution)/shard_map/ppermute | solution.py:86
  177.1 10.7 %collective-permute-start.34 = (bf16[2,5,64,512]{3,2,1,0:T(8,128)(2,1)S(1)}, bf16[2,5,64,512]{3,2,1,0:T(8,128)(2,1)S(1)}, u32[]{:S(2)}, u32[]{:S(2)}) collective-permute-start(bf16[2,5,64,512]{3,2,1,0:T(8,128)(2,1)S(1)} %pad_maximum_fusion.4.refs_1_), channel_id=1, source_target_pairs={{0,1},{1,0},{2,3},{3,2},{4,5},{5,4},{6,7},{7,6},{8,9},{9,8},{10,11... | collective-permute-start | bytes 1966088 | tf_op jit(solution)/shard_map/ppermute | solution.py:98
  180.0 10.9 %collective-permute-start.33 = (bf16[2,5,64,512]{3,2,1,0:T(8,128)(2,1)S(1)}, bf16[2,5,64,512]{3,2,1,0:T(8,128)(2,1)S(1)}, u32[]{:S(2)}, u32[]{:S(2)}) collective-permute-start(bf16[2,5,64,512]{3,2,1,0:T(8,128)(2,1)S(1)} %pad_maximum_fusion.3.refs_0_), channel_id=1, source_target_pairs={{0,16},{16,0},{1,17},{17,1},{2,18},{18,2},{3,19},{19,3},{4,20},{20... | collective-permute-start | bytes 1966088 | tf_op jit(solution)/shard_map/ppermute | solution.py:94
  181.0 10.1 %collective-permute-start.41 = (bf16[2,4,64,512]{3,2,1,0:T(8,128)(2,1)S(1)}, bf16[2,4,64,512]{3,2,1,0:T(8,128)(2,1)S(1)}, u32[]{:S(2)}, u32[]{:S(2)}) collective-permute-start(bf16[2,4,64,512]{3,2,1,0:T(8,128)(2,1)S(1)} %pad_maximum_fusion.5.refs_2_), channel_id=1, source_target_pairs={{0,4},{4,0},{8,12},{12,8},{1,5},{5,1},{9,13},{13,9},{2,6},{6,2},{1... | collective-permute-start | bytes 1572872 | tf_op jit(solution)/shard_map/ppermute | solution.py:90
  181.0 11.0 %collective-permute-start.40 = (bf16[2,5,64,512]{3,2,1,0:T(8,128)(2,1)S(1)}, bf16[2,5,64,512]{3,2,1,0:T(8,128)(2,1)S(1)}, u32[]{:S(2)}, u32[]{:S(2)}) collective-permute-start(bf16[2,5,64,512]{3,2,1,0:T(8,128)(2,1)S(1)} %pad_maximum_fusion.4.refs_1_), channel_id=1, source_target_pairs={{0,4},{4,0},{8,12},{12,8},{1,5},{5,1},{9,13},{13,9},{2,6},{6,2},{1... | collective-permute-start | bytes 1966088 | tf_op jit(solution)/shard_map/ppermute | solution.py:90
  185.6 6.5 %collective-permute-start.39 = (bf16[2,5,64,512]{3,2,1,0:T(8,128)(2,1)S(1)}, bf16[2,5,64,512]{3,2,1,0:T(8,128)(2,1)S(1)}, u32[]{:S(2)}, u32[]{:S(2)}) collective-permute-start(bf16[2,5,64,512]{3,2,1,0:T(8,128)(2,1)S(1)} %pad_maximum_fusion.3.refs_0_), channel_id=1, source_target_pairs={{0,4},{4,0},{8,12},{12,8},{1,5},{5,1},{9,13},{13,9},{2,6},{6,2},{1... | collective-permute-start | bytes 1966088 | tf_op jit(solution)/shard_map/ppermute | solution.py:90
  190.9 12.0 %collective-permute-start.36 = (bf16[2,5,64,512]{3,2,1,0:T(8,128)(2,1)S(1)}, bf16[2,5,64,512]{3,2,1,0:T(8,128)(2,1)}, u32[]{:S(2)}, u32[]{:S(2)}) collective-permute-start(bf16[2,5,64,512]{3,2,1,0:T(8,128)(2,1)S(1)} %pad_maximum_fusion.3.refs_0_), channel_id=1, source_target_pairs={{0,1},{1,0},{2,3},{3,2},{4,5},{5,4},{6,7},{7,6},{8,9},{9,8},{10,11... | collective-permute-start | bytes 1966088 | tf_op jit(solution)/shard_map/ppermute | solution.py:98
  190.9 12.8 %collective-permute-start.37 = (bf16[2,5,64,512]{3,2,1,0:T(8,128)(2,1)S(1)}, bf16[2,5,64,512]{3,2,1,0:T(8,128)(2,1)}, u32[]{:S(2)}, u32[]{:S(2)}) collective-permute-start(bf16[2,5,64,512]{3,2,1,0:T(8,128)(2,1)S(1)} %pad_maximum_fusion.4.refs_1_), channel_id=1, source_target_pairs={{0,8},{4,12},{8,0},{12,4},{1,9},{5,13},{9,1},{13,5},{2,10},{6,14},... | collective-permute-start | bytes 1966088 | tf_op jit(solution)/shard_map/ppermute | solution.py:86
  191.1 10.8 %collective-permute-start.38 = (bf16[2,4,64,512]{3,2,1,0:T(8,128)(2,1)S(1)}, bf16[2,4,64,512]{3,2,1,0:T(8,128)(2,1)S(1)}, u32[]{:S(2)}, u32[]{:S(2)}) collective-permute-start(bf16[2,4,64,512]{3,2,1,0:T(8,128)(2,1)S(1)} %pad_maximum_fusion.5.refs_2_), channel_id=1, source_target_pairs={{0,16},{16,0},{1,17},{17,1},{2,18},{18,2},{3,19},{19,3},{4,20},{20... | collective-permute-start | bytes 1572872 | tf_op jit(solution)/shard_map/ppermute | solution.py:94
  192.0 13.6 %collective-permute-start.44 = (bf16[2,4,64,512]{3,2,1,0:T(8,128)(2,1)S(1)}, bf16[2,4,64,512]{3,2,1,0:T(8,128)(2,1)S(1)}, u32[]{:S(2)}, u32[]{:S(2)}) collective-permute-start(bf16[2,4,64,512]{3,2,1,0:T(8,128)(2,1)S(1)} %collective-permute-done.35.refs_8_), channel_id=1, source_target_pairs={{0,4},{4,0},{8,12},{12,8},{1,5},{5,1},{9,13},{13,9},{2,6},{6,2},{1... | collective-permute-start | bytes 1572872 | tf_op jit(solution)/shard_map/ppermute | solution.py:90
  192.0 14.5 %collective-permute-start.42 = (bf16[2,5,64,512]{3,2,1,0:T(8,128)(2,1)S(1)}, bf16[2,5,64,512]{3,2,1,0:T(8,128)(2,1)S(1)}, u32[]{:S(2)}, u32[]{:S(2)}) collective-permute-start(bf16[2,5,64,512]{3,2,1,0:T(8,128)(2,1)S(1)} %collective-permute-done.33.refs_6_), channel_id=1, source_target_pairs={{0,4},{4,0},{8,12},{12,8},{1,5},{5,1},{9,13},{13,9},{2,6},{6,2},{1... | collective-permute-start | bytes 1966088 | tf_op jit(solution)/shard_map/ppermute | solution.py:90
  201.9 4.7 %collective-permute-start.43 = (bf16[2,5,64,512]{3,2,1,0:T(8,128)(2,1)S(1)}, bf16[2,5,64,512]{3,2,1,0:T(8,128)(2,1)S(1)}, u32[]{:S(2)}, u32[]{:S(2)}) collective-permute-start(bf16[2,5,64,512]{3,2,1,0:T(8,128)(2,1)S(1)} %collective-permute-done.34.refs_7_), channel_id=1, source_target_pairs={{0,4},{4,0},{8,12},{12,8},{1,5},{5,1},{9,13},{13,9},{2,6},{6,2},{1... | collective-permute-start | bytes 1966088 | tf_op jit(solution)/shard_map/ppermute | solution.py:90
  203.8 15.4 %collective-permute-start.48 = (bf16[2,5,64,512]{3,2,1,0:T(8,128)(2,1)S(1)}, bf16[2,5,64,512]{3,2,1,0:T(8,128)(2,1)}, u32[]{:S(2)}, u32[]{:S(2)}) collective-permute-start(bf16[2,5,64,512]{3,2,1,0:T(8,128)(2,1)S(1)} %collective-permute-done.33.refs_6_), channel_id=1, source_target_pairs={{0,1},{1,0},{2,3},{3,2},{4,5},{5,4},{6,7},{7,6},{8,9},{9,8},{10,11... | collective-permute-start | bytes 1966088 | tf_op jit(solution)/shard_map/ppermute | solution.py:98
  204.6 14.8 %collective-permute-start.49 = (bf16[2,5,64,512]{3,2,1,0:T(8,128)(2,1)S(1)}, bf16[2,5,64,512]{3,2,1,0:T(8,128)(2,1)}, u32[]{:S(2)}, u32[]{:S(2)}) collective-permute-start(bf16[2,5,64,512]{3,2,1,0:T(8,128)(2,1)S(1)} %collective-permute-done.34.refs_7_), channel_id=1, source_target_pairs={{0,8},{4,12},{8,0},{12,4},{1,9},{5,13},{9,1},{13,5},{2,10},{6,14},... | collective-permute-start | bytes 1966088 | tf_op jit(solution)/shard_map/ppermute | solution.py:86
  205.6 12.4 %collective-permute-start.50 = (bf16[2,4,64,512]{3,2,1,0:T(8,128)(2,1)S(1)}, bf16[2,4,64,512]{3,2,1,0:T(8,128)(2,1)}, u32[]{:S(2)}, u32[]{:S(2)}) collective-permute-start(bf16[2,4,64,512]{3,2,1,0:T(8,128)(2,1)S(1)} %collective-permute-done.35.refs_8_), channel_id=1, source_target_pairs={{0,16},{16,0},{1,17},{17,1},{2,18},{18,2},{3,19},{19,3},{4,20},{20... | collective-permute-start | bytes 1572872 | tf_op jit(solution)/shard_map/ppermute | solution.py:94
  206.6 13.1 %collective-permute-start.47 = (bf16[2,4,64,512]{3,2,1,0:T(8,128)(2,1)S(1)}, bf16[2,4,64,512]{3,2,1,0:T(8,128)(2,1)S(1)}, u32[]{:S(2)}, u32[]{:S(2)}) collective-permute-start(bf16[2,4,64,512]{3,2,1,0:T(8,128)(2,1)S(1)} %collective-permute-done.38.refs_14_), channel_id=1, source_target_pairs={{0,4},{4,0},{8,12},{12,8},{1,5},{5,1},{9,13},{13,9},{2,6},{6,2},{1... | collective-permute-start | bytes 1572872 | tf_op jit(solution)/shard_map/ppermute | solution.py:90
  206.6 14.2 %collective-permute-start.45 = (bf16[2,5,64,512]{3,2,1,0:T(8,128)(2,1)}, bf16[2,5,64,512]{3,2,1,0:T(8,128)(2,1)}, u32[]{:S(2)}, u32[]{:S(2)}) collective-permute-start(bf16[2,5,64,512]{3,2,1,0:T(8,128)(2,1)} %collective-permute-done.36.refs_12_), channel_id=1, source_target_pairs={{0,4},{4,0},{8,12},{12,8},{1,5},{5,1},{9,13},{13,9},{2,6},{6,2},{1... | collective-permute-start | bytes 1966088 | tf_op jit(solution)/shard_map/ppermute | solution.py:90
  218.1 2.7 collective-permute-start.46
  219.2 4.1 %collective-permute-start.51 = (bf16[2,5,64,512]{3,2,1,0:T(8,128)(2,1)}, bf16[2,5,64,512]{3,2,1,0:T(8,128)(2,1)}, u32[]{:S(2)}, u32[]{:S(2)}) collective-permute-start(bf16[2,5,64,512]{3,2,1,0:T(8,128)(2,1)} %collective-permute-done.48.refs_18_), channel_id=1, source_target_pairs={{0,4},{4,0},{8,12},{12,8},{1,5},{5,1},{9,13},{13,9},{2,6},{6,2},{1... | collective-permute-start | bytes 1966088 | tf_op jit(solution)/shard_map/ppermute | solution.py:90
  219.4 3.9 %collective-permute-start.52 = (bf16[2,5,64,512]{3,2,1,0:T(8,128)(2,1)}, bf16[2,5,64,512]{3,2,1,0:T(8,128)(2,1)}, u32[]{:S(2)}, u32[]{:S(2)}) collective-permute-start(bf16[2,5,64,512]{3,2,1,0:T(8,128)(2,1)} %collective-permute-done.49.refs_19_), channel_id=1, source_target_pairs={{0,4},{4,0},{8,12},{12,8},{1,5},{5,1},{9,13},{13,9},{2,6},{6,2},{1... | collective-permute-start | bytes 1966088 | tf_op jit(solution)/shard_map/ppermute | solution.py:90
  220.5 2.8 collective-permute-start.53
  245.9 34.0 %collective-permute-start.54 = (bf16[7,128,256]{2,1,0:T(8,128)(2,1)}, bf16[7,128,256]{2,1,0:T(8,128)(2,1)S(1)}, u32[]{:S(2)}, u32[]{:S(2)}) collective-permute-start(bf16[7,128,256]{2,1,0:T(8,128)(2,1)} %get-tuple-element.227), channel_id=1, source_target_pairs={{0,0},{1,1},{2,16},{3,17},{16,2},{17,3},{18,18},{19,19},{4,4},{5,5... | collective-permute-start | bytes 1376264 | tf_op jit(solution)/shard_map/ppermute | solution.py:138
  249.2 42.3 %collective-permute-start.55 = (bf16[7,128,256]{2,1,0:T(8,128)(2,1)}, bf16[7,128,256]{2,1,0:T(8,128)(2,1)S(1)}, u32[]{:S(2)}, u32[]{:S(2)}) collective-permute-start(bf16[7,128,256]{2,1,0:T(8,128)(2,1)} %get-tuple-element.228), channel_id=1, source_target_pairs={{0,1},{1,0},{2,17},{3,16},{16,3},{17,2},{18,19},{19,18},{4,5},{5,4... | collective-permute-start | bytes 1376264 | tf_op jit(solution)/shard_map/ppermute | solution.py:138
  251.1 40.4 %collective-permute-start.56 = (bf16[7,128,256]{2,1,0:T(8,128)(2,1)}, bf16[7,128,256]{2,1,0:T(8,128)(2,1)S(1)}, u32[]{:S(2)}, u32[]{:S(2)}) collective-permute-start(bf16[7,128,256]{2,1,0:T(8,128)(2,1)} %get-tuple-element.229), channel_id=1, source_target_pairs={{0,2},{1,3},{2,18},{3,19},{16,0},{17,1},{18,16},{19,17},{4,6},{5,7... | collective-permute-start | bytes 1376264 | tf_op jit(solution)/shard_map/ppermute | solution.py:138
  251.1 43.2 %collective-permute-start.57 = (bf16[7,128,256]{2,1,0:T(8,128)(2,1)}, bf16[7,128,256]{2,1,0:T(8,128)(2,1)S(1)}, u32[]{:S(2)}, u32[]{:S(2)}) collective-permute-start(bf16[7,128,256]{2,1,0:T(8,128)(2,1)} %get-tuple-element.230), channel_id=1, source_target_pairs={{0,3},{1,2},{2,19},{3,18},{16,1},{17,0},{18,17},{19,16},{4,7},{5,6... | collective-permute-start | bytes 1376264 | tf_op jit(solution)/shard_map/ppermute | solution.py:138
  294.3 32.6 %collective-permute-start.58 = (bf16[7,128,256]{2,1,0:T(8,128)(2,1)}, bf16[7,128,256]{2,1,0:T(8,128)(2,1)S(1)}, u32[]{:S(2)}, u32[]{:S(2)}) collective-permute-start(bf16[7,128,256]{2,1,0:T(8,128)(2,1)} %get-tuple-element.235), channel_id=1, source_target_pairs={{0,0},{1,1},{2,16},{3,17},{16,2},{17,3},{18,18},{19,19},{4,4},{5,5... | collective-permute-start | bytes 1376264 | tf_op jit(solution)/shard_map/ppermute | solution.py:138
  296.2 40.2 %collective-permute-start.59 = (bf16[7,128,256]{2,1,0:T(8,128)(2,1)}, bf16[7,128,256]{2,1,0:T(8,128)(2,1)S(1)}, u32[]{:S(2)}, u32[]{:S(2)}) collective-permute-start(bf16[7,128,256]{2,1,0:T(8,128)(2,1)} %get-tuple-element.236), channel_id=1, source_target_pairs={{0,1},{1,0},{2,17},{3,16},{16,3},{17,2},{18,19},{19,18},{4,5},{5,4... | collective-permute-start | bytes 1376264 | tf_op jit(solution)/shard_map/ppermute | solution.py:138
  297.4 41.3 %collective-permute-start.60 = (bf16[7,128,256]{2,1,0:T(8,128)(2,1)}, bf16[7,128,256]{2,1,0:T(8,128)(2,1)S(1)}, u32[]{:S(2)}, u32[]{:S(2)}) collective-permute-start(bf16[7,128,256]{2,1,0:T(8,128)(2,1)} %get-tuple-element.237), channel_id=1, source_target_pairs={{0,2},{1,3},{2,18},{3,19},{16,0},{17,1},{18,16},{19,17},{4,6},{5,7... | collective-permute-start | bytes 1376264 | tf_op jit(solution)/shard_map/ppermute | solution.py:138
  297.4 43.9 %collective-permute-start.61 = (bf16[7,128,256]{2,1,0:T(8,128)(2,1)}, bf16[7,128,256]{2,1,0:T(8,128)(2,1)S(1)}, u32[]{:S(2)}, u32[]{:S(2)}) collective-permute-start(bf16[7,128,256]{2,1,0:T(8,128)(2,1)} %get-tuple-element.238), channel_id=1, source_target_pairs={{0,3},{1,2},{2,19},{3,18},{16,1},{17,0},{18,17},{19,16},{4,7},{5,6... | collective-permute-start | bytes 1376264 | tf_op jit(solution)/shard_map/ppermute | solution.py:138
  (17 other events, 438.7 us)

commit v8 on v7

--- a/solution.py
+++ b/solution.py
@@ -519,7 +519,7 @@
     keep, other = cast(0, y), over_y(cast(0, 1 - y))
     ahead = [(cast(n, y), cast(n, 1 - y)) for n in range(1, len(HOPS))]
     for n in range(len(HOPS) - 1):
-        ready, ahead, done = lax.optimization_barrier((chunks(keep, other), ahead, done))
+        ready, ahead = lax.optimization_barrier((chunks(keep, other), ahead))
         done.append(travel(ready))
         keep, other = ahead[n][0], over_y(ahead[n][1])
     ready = chunks(keep, other)

time: 344 us -> 355 us (1.032)
  waiting for transfers between devices: 196 us -> 207 us
    ppermute x20, waiting for transfers between devices: 76.7 us -> 86.1 us  [over_z(): return lax.ppermute(a, 'row', [(z, z ^ step) for z in range(4)])]
  transfers between devices with their start and end apart: 62 -> 62, of which waited for: 38 -> 35; matrix products, arithmetic and copies ran while one was open for 8% -> 7% of each run, Pallas kernels for 11% -> 10%
where the time goes in v8:
time: 355 us; the launch traced here: 354 us
  waiting for transfers between devices  207 us (58%)
  Pallas kernels  60.6 us (17%)
  starting transfers between devices  54.3 us (15%)
  other arithmetic  25.2 us (7%)
  local copies, waits for them, and re-layouts  6.7 us (2%)
    ppermute x20, waiting for transfers between devices, over_z(): return lax.ppermute(a, 'row', [(z, z ^ step) for z in range(4)])  86.1 us
    ppermute x11, waiting for transfers between devices, over_y(): return lax.ppermute(a, 'mats', [(0, 1), (1, 0)])  47.7 us
    pallas_call x2, Pallas kernels, step_call(): pl.pallas_call(functools.partial(step_kernel, keys, part), out_shape=[jax...  45 us
    ppermute x8, waiting for transfers between devices, home(): return lax.ppermute(a, ('mats', 'row'), pairs)  43.8 us
    ppermute x8, waiting for transfers between devices, over_x(): return lax.ppermute(a, 'col', [(0, 2), (1, 3), (2, 0), (3, 1)])  25.9 us
    ppermute x20, starting transfers between devices, over_z(): return lax.ppermute(a, 'row', [(z, z ^ step) for z in range(4)])  20.4 us
    dynamic_update_slice x8, other arithmetic, shards_cube(): lax.dynamic_update_slice_in_dim(out, pick(out, at, WIDE, 1) + piece, at, 1)  17.5 us
    ppermute x8, starting transfers between devices, home(): return lax.ppermute(a, ('mats', 'row'), pairs)  13.1 us
  transfers between devices with their start and end apart: 62, of which 35 were waited for; matrix products, arithmetic and copies ran while one was open for 7% of the time, Pallas kernels for 10%

profile of v8, /device:TPU:12, one launch (start us, length us, event | category | flops | bytes accessed | tf_op | source)
XLA Modules:
  0.0 354.4 jit_solution(16386877819954180905)
XLA Ops:
  1.6 1.7 dynamic-slice_convert_fusion.2
  3.3 2.5 dynamic-slice_convert_fusion
  5.9 3.3 collective-permute-done
  11.0 12.3 %collective-permute-done.1 = bf16[256,1024]{1,0:T(8,128)(2,1)S(1)} collective-permute-done((bf16[256,1024]{1,0:T(8,128)(2,1)S(1)}, bf16[256,1024]{1,0:T(8,128)(2,1)S(1)}, u32[]{:S(2)}, u32[]{:S(2)}) %collective-permute-start.1) | collective-permute-done | bytes 524320 | tf_op jit(solution)/shard_map/ppermute | solution.py:94
  24.6 1.5 collective-permute-start.3
  26.1 2.6 collective-permute-start.6
  29.0 9.9 %collective-permute-done.3 = bf16[128,512]{1,0:T(8,128)(2,1)S(1)} collective-permute-done((bf16[128,512]{1,0:T(8,128)(2,1)S(1)}, bf16[128,512]{1,0:T(8,128)(2,1)S(1)}, u32[]{:S(2)}, u32[]{:S(2)}) %collective-permute-start.3) | collective-permute-done | bytes 131104 | tf_op jit(solution)/shard_map/ppermute | solution.py:98
  39.4 1.6 collective-permute-start.7
  41.1 12.7 %collective-permute-done.5 = bf16[128,512]{1,0:T(8,128)(2,1)S(1)} collective-permute-done((bf16[128,512]{1,0:T(8,128)(2,1)S(1)}, bf16[128,512]{1,0:T(8,128)(2,1)S(1)}, u32[]{:S(2)}, u32[]{:S(2)}) %collective-permute-start.5) | collective-permute-done | bytes 131104 | tf_op jit(solution)/shard_map/ppermute | solution.py:98
  53.8 6.1 %collective-permute-done.7 = bf16[128,512]{1,0:T(8,128)(2,1)S(1)} collective-permute-done((bf16[128,512]{1,0:T(8,128)(2,1)S(1)}, bf16[128,512]{1,0:T(8,128)(2,1)S(1)}, u32[]{:S(2)}, u32[]{:S(2)}) %collective-permute-start.7) | collective-permute-done | bytes 131104 | tf_op jit(solution)/shard_map/ppermute | solution.py:98
  61.0 2.4 collective-permute-start.11
  63.3 2.0 collective-permute-start.9
  65.5 3.1 gram.2
  68.6 10.3 %collective-permute-done.10 = bf16[256,512]{1,0:T(8,128)(2,1)S(1)} collective-permute-done((bf16[256,512]{1,0:T(8,128)(2,1)S(1)}, bf16[256,512]{1,0:T(8,128)(2,1)S(1)}, u32[]{:S(2)}, u32[]{:S(2)}) %collective-permute-start.10) | collective-permute-done | bytes 262176 | tf_op jit(solution)/shard_map/ppermute | solution.py:98
  79.0 8.1 %collective-permute-done.11 = bf16[256,512]{1,0:T(8,128)(2,1)S(1)} collective-permute-done((bf16[256,512]{1,0:T(8,128)(2,1)S(1)}, bf16[256,512]{1,0:T(8,128)(2,1)S(1)}, u32[]{:S(2)}, u32[]{:S(2)}) %collective-permute-start.11) | collective-permute-done | bytes 262176 | tf_op jit(solution)/shard_map/ppermute | solution.py:98
  87.1 1.5 collective-permute-start.13
  89.6 2.5 collective-permute-start.16
  92.1 4.7 %fusion = f32[896,2048]{1,0:T(8,128)} fusion(f32[896,2048]{1,0:T(8,128)S(1)} %bitcast.38), kind=kLoop, calls=%fused_computation.1 | loop fusion | flops 5505024 | bytes 14680064 | tf_op jit(solution)/shard_map/mul | solution.py:542
  97.0 9.7 %collective-permute-done.13.refs_1_ = bf16[784,512]{1,0:T(8,128)(2,1)S(1)} collective-permute-done((bf16[784,512]{1,0:T(8,128)(2,1)S(1)}, bf16[784,512]{1,0:T(8,128)(2,1)S(1)}, u32[]{:S(2)}, u32[]{:S(2)}) %collective-permute-start.13) | collective-permute-done | bytes 802848 | tf_op jit(solution)/shard_map/ppermute | solution.py:86
  107.6 6.9 %collective-permute-done.16 = bf16[256,512]{1,0:T(8,128)(2,1)S(1)} collective-permute-done((bf16[256,512]{1,0:T(8,128)(2,1)S(1)}, bf16[256,512]{1,0:T(8,128)(2,1)S(1)}, u32[]{:S(2)}, u32[]{:S(2)}) %collective-permute-start.16) | collective-permute-done | bytes 262176 | tf_op jit(solution)/shard_map/ppermute | solution.py:98
  114.7 1.6 collective-permute-start.17
  117.3 10.0 %gram.3 = (f32[4,4,64,512]{3,2,1,0:T(8,128)S(1)}, bf16[1040,512]{1,0:T(8,128)(2,1)S(1)}, f32[4,4,64,512]{3,2,1,0:T(8,128)S(1)}, bf16[1040,512]{1,0:T(8,128)(2,1)...) custom-call(bf16[4,3,128,512]{3,2,1,0:T(8,128)(2,1)S(1)} %pad_maximum_fusion.refs_0_.refs_24_, ...), custom_call_target="tpu_custom_call" | custom-call | flops 7516192768 | bytes 458752 | tf_op jit(solution)/shard_map/gram/pallas_call | solution.py:296
  127.9 1.5 collective-permute-start.21
  129.7 2.1 collective-permute-start.23
  131.8 21.6 %collective-permute-done.23.refs_1_ = bf16[208,512]{1,0:T(8,128)(2,1)S(1)} collective-permute-done((bf16[208,512]{1,0:T(8,128)(2,1)S(1)}, bf16[208,512]{1,0:T(8,128)(2,1)S(1)}, u32[]{:S(2)}, u32[]{:S(2)}) %collective-permute-start.23) | collective-permute-done | bytes 213024 | tf_op jit(solution)/shard_map/ppermute | solution.py:98
  154.5 1.3 collective-permute-start.24
  155.8 1.5 collective-permute-start.26
  157.3 8.7 %collective-permute-done.26.refs_5_ = bf16[400,512]{1,0:T(8,128)(2,1)S(1)} collective-permute-done((bf16[400,512]{1,0:T(8,128)(2,1)S(1)}, bf16[400,512]{1,0:T(8,128)(2,1)S(1)}, u32[]{:S(2)}, u32[]{:S(2)}) %collective-permute-start.26) | collective-permute-done | bytes 409632 | tf_op jit(solution)/shard_map/ppermute | solution.py:86
  165.9 1.6 collective-permute-done.24.refs_1_
  169.5 1.4 collective-permute-start.28
  171.8 5.0 %collective-permute-done.29.refs_5_ = bf16[208,512]{1,0:T(8,128)(2,1)S(1)} collective-permute-done((bf16[208,512]{1,0:T(8,128)(2,1)S(1)}, bf16[208,512]{1,0:T(8,128)(2,1)S(1)}, u32[]{:S(2)}, u32[]{:S(2)}) %collective-permute-start.29) | collective-permute-done | bytes 213024 | tf_op jit(solution)/shard_map/ppermute | solution.py:94
  177.0 2.2 collective-permute-start.32
  180.0 4.0 %collective-permute-done.32 = bf16[1,4,64,512]{3,2,1,0:T(8,128)(2,1)S(1)} collective-permute-done((bf16[1,4,64,512]{3,2,1,0:T(8,128)(2,1)S(1)}, bf16[1,4,64,512]{3,2,1,0:T(8,128)(2,1)S(1)}, u32[]{:S(2)}, u32[]{:S(2)}) %collective-permute-start.32) | collective-permute-done | bytes 262176 | tf_op jit(solution)/shard_map/ppermute | solution.py:98
  184.3 3.8 %collective-permute-done.31 = bf16[1,5,64,512]{3,2,1,0:T(8,128)(2,1)S(1)} collective-permute-done((bf16[1,5,64,512]{3,2,1,0:T(8,128)(2,1)S(1)}, bf16[1,5,64,512]{3,2,1,0:T(8,128)(2,1)S(1)}, u32[]{:S(2)}, u32[]{:S(2)}) %collective-permute-start.31) | collective-permute-done | bytes 327712 | tf_op jit(solution)/shard_map/ppermute | solution.py:94
  188.2 2.1 collective-permute-done.30
  190.4 1.6 collective-permute-start.33
  192.5 3.9 %collective-permute-done.35.refs_8_ = bf16[2,4,64,512]{3,2,1,0:T(8,128)(2,1)S(1)} collective-permute-done((bf16[2,4,64,512]{3,2,1,0:T(8,128)(2,1)S(1)}, bf16[2,4,64,512]{3,2,1,0:T(8,128)(2,1)S(1)}, u32[]{:S(2)}, u32[]{:S(2)}) %collective-permute-start.35) | collective-permute-done | bytes 524320 | tf_op jit(solution)/shard_map/ppermute | solution.py:86
  196.4 2.4 collective-permute-done.34.refs_7_
  198.8 2.3 collective-permute-done.33.refs_6_
  201.9 1.3 collective-permute-start.38
  203.7 9.0 %collective-permute-done.38.refs_14_ = bf16[2,4,64,512]{3,2,1,0:T(8,128)(2,1)S(1)} collective-permute-done((bf16[2,4,64,512]{3,2,1,0:T(8,128)(2,1)S(1)}, bf16[2,4,64,512]{3,2,1,0:T(8,128)(2,1)S(1)}, u32[]{:S(2)}, u32[]{:S(2)}) %collective-permute-start.38) | collective-permute-done | bytes 524320 | tf_op jit(solution)/shard_map/ppermute | solution.py:94
  218.1 10.4 %collective-permute-done.50.refs_20_ = bf16[2,4,64,512]{3,2,1,0:T(8,128)(2,1)} collective-permute-done((bf16[2,4,64,512]{3,2,1,0:T(8,128)(2,1)S(1)}, bf16[2,4,64,512]{3,2,1,0:T(8,128)(2,1)}, u32[]{:S(2)}, u32[]{:S(2)}) %collective-permute-start.50) | collective-permute-done | bytes 524320 | tf_op jit(solution)/shard_map/ppermute | solution.py:94
  228.5 1.5 collective-permute-done.48.refs_18_
  231.7 2.5 collective-permute-done.53.refs_23_
  234.2 22.5 %step.2 = (bf16[7,128,256]{2,1,0:T(8,128)(2,1)}, bf16[7,128,256]{2,1,0:T(8,128)(2,1)}, bf16[7,128,256]{2,1,0:T(8,128)(2,1)}, bf16[7,128,256]{2,1,0:T(8,128)(2,1)}) custom-call(bf16[2,5,64,512]{3,2,1,0:T(8,128)(2,1)} %copy-done.4, bf16[2,5,64,512]{3,2,1,0:T(8,128)(2,1)} %copy-done.3, bf16[2,4,64,512]{3,2,1,0:T(8,128)(2,1)} %copy-done.5, ...), custom_call_target="tpu_custom_call" | custom-call | flops 13153337344 | bytes 20971520 | tf_op jit(solution)/shard_map/step/pallas_call | solution.py:469
  256.7 2.3 collective-permute-start.54
  259.0 2.9 collective-permute-start.55
  261.9 1.6 collective-permute-start.57
  263.5 22.4 %step.3 = (bf16[7,128,256]{2,1,0:T(8,128)(2,1)}, bf16[7,128,256]{2,1,0:T(8,128)(2,1)}, bf16[7,128,256]{2,1,0:T(8,128)(2,1)}, bf16[7,128,256]{2,1,0:T(8,128)(2,1)}) custom-call(bf16[2,5,64,512]{3,2,1,0:T(8,128)(2,1)} %copy-done.4, bf16[2,5,64,512]{3,2,1,0:T(8,128)(2,1)} %copy-done.3, bf16[2,4,64,512]{3,2,1,0:T(8,128)(2,1)} %copy-done.5, ...), custom_call_target="tpu_custom_call" | custom-call | flops 13153337344 | bytes 20971520 | tf_op jit(solution)/shard_map/step/pallas_call | solution.py:469
  285.9 3.8 %collective-permute-done.54 = bf16[7,128,256]{2,1,0:T(8,128)(2,1)S(1)} collective-permute-done((bf16[7,128,256]{2,1,0:T(8,128)(2,1)}, bf16[7,128,256]{2,1,0:T(8,128)(2,1)S(1)}, u32[]{:S(2)}, u32[]{:S(2)}) %collective-permute-start.54) | collective-permute-done | bytes 458784 | tf_op jit(solution)/shard_map/ppermute | solution.py:138
  289.8 12.5 %collective-permute-done.55 = bf16[7,128,256]{2,1,0:T(8,128)(2,1)S(1)} collective-permute-done((bf16[7,128,256]{2,1,0:T(8,128)(2,1)}, bf16[7,128,256]{2,1,0:T(8,128)(2,1)S(1)}, u32[]{:S(2)}, u32[]{:S(2)}) %collective-permute-start.55) | collective-permute-done | bytes 458784 | tf_op jit(solution)/shard_map/ppermute | solution.py:138
  302.3 2.8 collective-permute-done.57
  305.1 1.9 collective-permute-start.58
  307.3 4.2 %collective-permute-start.61 = (bf16[7,128,256]{2,1,0:T(8,128)(2,1)}, bf16[7,128,256]{2,1,0:T(8,128)(2,1)S(1)}, u32[]{:S(2)}, u32[]{:S(2)}) collective-permute-start(bf16[7,128,256]{2,1,0:T(8,128)(2,1)} %get-tuple-element.230), channel_id=1, source_target_pairs={{0,3},{1,2},{2,19},{3,18},{16,1},{17,0},{18,17},{19,16},{4,7},{5,6... | collective-permute-start | bytes 1376264 | tf_op jit(solution)/shard_map/ppermute | solution.py:138
  311.6 2.2 constant_dynamic-update-slice_fusion.7
  313.9 2.2 constant_dynamic-update-slice_fusion.6
  316.2 2.2 constant_dynamic-update-slice_fusion.5
  318.5 2.2 constant_dynamic-update-slice_fusion.4
  320.7 16.2 %collective-permute-done.58 = bf16[7,128,256]{2,1,0:T(8,128)(2,1)S(1)} collective-permute-done((bf16[7,128,256]{2,1,0:T(8,128)(2,1)}, bf16[7,128,256]{2,1,0:T(8,128)(2,1)S(1)}, u32[]{:S(2)}, u32[]{:S(2)}) %collective-permute-start.58) | collective-permute-done | bytes 458784 | tf_op jit(solution)/shard_map/ppermute | solution.py:138
  336.9 2.2 constant_dynamic-update-slice_fusion.3
  339.1 7.2 %collective-permute-done.59 = bf16[7,128,256]{2,1,0:T(8,128)(2,1)S(1)} collective-permute-done((bf16[7,128,256]{2,1,0:T(8,128)(2,1)}, bf16[7,128,256]{2,1,0:T(8,128)(2,1)S(1)}, u32[]{:S(2)}, u32[]{:S(2)}) %collective-permute-start.59) | collective-permute-done | bytes 458784 | tf_op jit(solution)/shard_map/ppermute | solution.py:138
  346.4 2.2 constant_dynamic-update-slice_fusion.2
  348.7 2.2 constant_dynamic-update-slice_fusion.1
  352.2 2.2 constant_dynamic-update-slice_fusion
  (153 shorter events, 27.2 us)
Async XLA Ops:
  1.1 8.1 %collective-permute-start = (bf16[128,1024]{1,0:T(8,128)(2,1)S(1)}, bf16[128,1024]{1,0:T(8,128)(2,1)S(1)}, u32[]{:S(2)}, u32[]{:S(2)}) collective-permute-start(bf16[128,1024]{1,0:T(8,128)(2,1)S(1)} %dynamic-slice_convert_fusion.4), channel_id=1, source_target_pairs={{0,16},{16,0},{1,17},{17,1},{2,18},{18,2},{3,19},{19,3},{4,20},{20... | collective-permute-start | bytes 786440 | tf_op jit(solution)/shard_map/ppermute | solution.py:94
  10.4 12.9 %collective-permute-start.1 = (bf16[256,1024]{1,0:T(8,128)(2,1)S(1)}, bf16[256,1024]{1,0:T(8,128)(2,1)S(1)}, u32[]{:S(2)}, u32[]{:S(2)}) collective-permute-start(bf16[256,1024]{1,0:T(8,128)(2,1)S(1)} %get-tuple-element.119), channel_id=1, source_target_pairs={{0,16},{16,0},{1,17},{17,1},{2,18},{18,2},{3,19},{19,3},{4,20},{20... | collective-permute-start | bytes 1572872 | tf_op jit(solution)/shard_map/ppermute | solution.py:94
  23.5 36.7 %collective-permute-start.2 = (bf16[512,1024]{1,0:T(8,128)(2,1)S(1)}, bf16[512,1024]{1,0:T(8,128)(2,1)S(1)}, u32[]{:S(2)}, u32[]{:S(2)}) collective-permute-start(bf16[512,1024]{1,0:T(8,128)(2,1)S(1)} %get-tuple-element.123), channel_id=1, source_target_pairs={{0,16},{16,0},{1,17},{17,1},{2,18},{18,2},{3,19},{19,3},{4,20},{20... | collective-permute-start | bytes 3145736 | tf_op jit(solution)/shard_map/ppermute | solution.py:94
  24.1 15.4 %collective-permute-start.4 = (bf16[256,512]{1,0:T(8,128)(2,1)S(1)}, bf16[256,512]{1,0:T(8,128)(2,1)S(1)}, u32[]{:S(2)}, u32[]{:S(2)}) collective-permute-start(bf16[256,512]{1,0:T(8,128)(2,1)S(1)} %get-tuple-element.127), channel_id=1, source_target_pairs={{0,1},{1,0},{2,3},{3,2},{4,5},{5,4},{6,7},{7,6},{8,9},{9,8},{10,11... | collective-permute-start | bytes 786440 | tf_op jit(solution)/shard_map/ppermute | solution.py:98
  24.6 14.3 %collective-permute-start.3 = (bf16[128,512]{1,0:T(8,128)(2,1)S(1)}, bf16[128,512]{1,0:T(8,128)(2,1)S(1)}, u32[]{:S(2)}, u32[]{:S(2)}) collective-permute-start(bf16[128,512]{1,0:T(8,128)(2,1)S(1)} %get-tuple-element.126), channel_id=1, source_target_pairs={{0,1},{1,0},{2,3},{3,2},{4,5},{5,4},{6,7},{7,6},{8,9},{9,8},{10,11... | collective-permute-start | bytes 393224 | tf_op jit(solution)/shard_map/ppermute | solution.py:98
  26.1 27.7 %collective-permute-start.6 = (bf16[256,512]{1,0:T(8,128)(2,1)S(1)}, bf16[256,512]{1,0:T(8,128)(2,1)S(1)}, u32[]{:S(2)}, u32[]{:S(2)}) collective-permute-start(bf16[256,512]{1,0:T(8,128)(2,1)S(1)} %get-tuple-element.129), channel_id=1, source_target_pairs={{0,2},{1,3},{2,0},{3,1},{4,6},{5,7},{6,4},{7,5},{8,10},{9,11},{10,... | collective-permute-start | bytes 786440 | tf_op jit(solution)/shard_map/ppermute | solution.py:98
  28.7 25.1 %collective-permute-start.5 = (bf16[128,512]{1,0:T(8,128)(2,1)S(1)}, bf16[128,512]{1,0:T(8,128)(2,1)S(1)}, u32[]{:S(2)}, u32[]{:S(2)}) collective-permute-start(bf16[128,512]{1,0:T(8,128)(2,1)S(1)} %get-tuple-element.128), channel_id=1, source_target_pairs={{0,2},{1,3},{2,0},{3,1},{4,6},{5,7},{6,4},{7,5},{8,10},{9,11},{10,... | collective-permute-start | bytes 393224 | tf_op jit(solution)/shard_map/ppermute | solution.py:98
  38.9 21.0 %collective-permute-start.8 = (bf16[256,512]{1,0:T(8,128)(2,1)S(1)}, bf16[256,512]{1,0:T(8,128)(2,1)S(1)}, u32[]{:S(2)}, u32[]{:S(2)}) collective-permute-start(bf16[256,512]{1,0:T(8,128)(2,1)S(1)} %get-tuple-element.131), channel_id=1, source_target_pairs={{0,3},{1,2},{2,1},{3,0},{4,7},{5,6},{6,5},{7,4},{8,11},{9,10},{10,... | collective-permute-start | bytes 786440 | tf_op jit(solution)/shard_map/ppermute | solution.py:98
  39.4 20.5 %collective-permute-start.7 = (bf16[128,512]{1,0:T(8,128)(2,1)S(1)}, bf16[128,512]{1,0:T(8,128)(2,1)S(1)}, u32[]{:S(2)}, u32[]{:S(2)}) collective-permute-start(bf16[128,512]{1,0:T(8,128)(2,1)S(1)} %get-tuple-element.130), channel_id=1, source_target_pairs={{0,3},{1,2},{2,1},{3,0},{4,7},{5,6},{6,5},{7,4},{8,11},{9,10},{10,... | collective-permute-start | bytes 393224 | tf_op jit(solution)/shard_map/ppermute | solution.py:98
  60.2 57.1 %copy-start = (bf16[4,3,128,512]{3,2,1,0:T(8,128)(2,1)}, bf16[4,3,128,512]{3,2,1,0:T(8,128)(2,1)S(1)}, u32[]{:S(2)}) copy-start(bf16[4,3,128,512]{3,2,1,0:T(8,128)(2,1)S(1)} %pad_maximum_fusion.refs_0_.refs_24_) | copy-start | bytes 4718596
  60.8 4.6 %collective-permute-start.12 = (bf16[4,3,128,512]{3,2,1,0:T(8,128)(2,1)S(1)}, bf16[4,3,128,512]{3,2,1,0:T(8,128)(2,1)S(1)}, u32[]{:S(2)}, u32[]{:S(2)}) collective-permute-start(bf16[4,3,128,512]{3,2,1,0:T(8,128)(2,1)S(1)} %pad_maximum_fusion.refs_0_.refs_24_), channel_id=1, source_target_pairs={{0,4},{4,0},{8,12},{12,8},{1,5},{5,1},{9,13},{13,9},{2,6},{6,2},{1... | collective-permute-start | bytes 4718600 | tf_op jit(solution)/shard_map/ppermute | solution.py:90
  60.9 18.0 %collective-permute-start.10 = (bf16[256,512]{1,0:T(8,128)(2,1)S(1)}, bf16[256,512]{1,0:T(8,128)(2,1)S(1)}, u32[]{:S(2)}, u32[]{:S(2)}) collective-permute-start(bf16[256,512]{1,0:T(8,128)(2,1)S(1)} %get-tuple-element.138), channel_id=1, source_target_pairs={{0,2},{1,3},{2,0},{3,1},{4,6},{5,7},{6,4},{7,5},{8,10},{9,11},{10,... | collective-permute-start | bytes 786440 | tf_op jit(solution)/shard_map/ppermute | solution.py:98
  61.0 26.1 %collective-permute-start.11 = (bf16[256,512]{1,0:T(8,128)(2,1)S(1)}, bf16[256,512]{1,0:T(8,128)(2,1)S(1)}, u32[]{:S(2)}, u32[]{:S(2)}) collective-permute-start(bf16[256,512]{1,0:T(8,128)(2,1)S(1)} %get-tuple-element.139), channel_id=1, source_target_pairs={{0,3},{1,2},{2,1},{3,0},{4,7},{5,6},{6,5},{7,4},{8,11},{9,10},{10,... | collective-permute-start | bytes 786440 | tf_op jit(solution)/shard_map/ppermute | solution.py:98
  63.3 23.7 %collective-permute-start.9 = (bf16[256,512]{1,0:T(8,128)(2,1)S(1)}, bf16[256,512]{1,0:T(8,128)(2,1)S(1)}, u32[]{:S(2)}, u32[]{:S(2)}) collective-permute-start(bf16[256,512]{1,0:T(8,128)(2,1)S(1)} %get-tuple-element.137), channel_id=1, source_target_pairs={{0,1},{1,0},{2,3},{3,2},{4,5},{5,4},{6,7},{7,6},{8,9},{9,8},{10,11... | collective-permute-start | bytes 786440 | tf_op jit(solution)/shard_map/ppermute | solution.py:98
  87.1 19.7 %collective-permute-start.13 = (bf16[784,512]{1,0:T(8,128)(2,1)S(1)}, bf16[784,512]{1,0:T(8,128)(2,1)S(1)}, u32[]{:S(2)}, u32[]{:S(2)}) collective-permute-start(bf16[784,512]{1,0:T(8,128)(2,1)S(1)} %get-tuple-element.144), channel_id=1, source_target_pairs={{0,8},{4,12},{8,0},{12,4},{1,9},{5,13},{9,1},{13,5},{2,10},{6,14},... | collective-permute-start | bytes 2408456 | tf_op jit(solution)/shard_map/ppermute | solution.py:86
  88.6 18.7 %collective-permute-start.14 = (bf16[256,512]{1,0:T(8,128)(2,1)S(1)}, bf16[256,512]{1,0:T(8,128)(2,1)S(1)}, u32[]{:S(2)}, u32[]{:S(2)}) collective-permute-start(bf16[256,512]{1,0:T(8,128)(2,1)S(1)} %slice.29), channel_id=1, source_target_pairs={{0,1},{1,0},{2,3},{3,2},{4,5},{5,4},{6,7},{7,6},{8,9},{9,8},{10,11... | collective-permute-start | bytes 786440 | tf_op jit(solution)/shard_map/ppermute | solution.py:98
  88.6 19.0 %collective-permute-start.15 = (bf16[256,512]{1,0:T(8,128)(2,1)S(1)}, bf16[256,512]{1,0:T(8,128)(2,1)S(1)}, u32[]{:S(2)}, u32[]{:S(2)}) collective-permute-start(bf16[256,512]{1,0:T(8,128)(2,1)S(1)} %slice.30), channel_id=1, source_target_pairs={{0,2},{1,3},{2,0},{3,1},{4,6},{5,7},{6,4},{7,5},{8,10},{9,11},{10,... | collective-permute-start | bytes 786440 | tf_op jit(solution)/shard_map/ppermute | solution.py:98
  89.6 24.9 %collective-permute-start.16 = (bf16[256,512]{1,0:T(8,128)(2,1)S(1)}, bf16[256,512]{1,0:T(8,128)(2,1)S(1)}, u32[]{:S(2)}, u32[]{:S(2)}) collective-permute-start(bf16[256,512]{1,0:T(8,128)(2,1)S(1)} %slice.31), channel_id=1, source_target_pairs={{0,3},{1,2},{2,1},{3,0},{4,7},{5,6},{6,5},{7,4},{8,11},{9,10},{10,... | collective-permute-start | bytes 786440 | tf_op jit(solution)/shard_map/ppermute | solution.py:98
  96.9 19.3 %collective-permute-start.18 = (bf16[4,2,128,512]{3,2,1,0:T(8,128)(2,1)S(1)}, bf16[4,2,128,512]{3,2,1,0:T(8,128)(2,1)S(1)}, u32[]{:S(2)}, u32[]{:S(2)}) collective-permute-start(bf16[4,2,128,512]{3,2,1,0:T(8,128)(2,1)S(1)} %pad_maximum_fusion.1.refs_1_.refs_25_), channel_id=1, source_target_pairs={{0,4},{4,0},{8,12},{12,8},{1,5},{5,1},{9,13},{13,9},{2,6},{6,2},{1... | collective-permute-start | bytes 3145736 | tf_op jit(solution)/shard_map/ppermute | solution.py:90
  114.6 2.7 collective-permute-start.19
  114.7 12.6 %collective-permute-start.17 = (bf16[400,512]{1,0:T(8,128)(2,1)S(1)}, bf16[400,512]{1,0:T(8,128)(2,1)S(1)}, u32[]{:S(2)}, u32[]{:S(2)}) collective-permute-start(bf16[400,512]{1,0:T(8,128)(2,1)S(1)} %get-tuple-element.157), channel_id=1, source_target_pairs={{0,16},{16,0},{1,17},{17,1},{2,18},{18,2},{3,19},{19,3},{4,20},{20... | collective-permute-start | bytes 1228808 | tf_op jit(solution)/shard_map/ppermute | solution.py:94
  127.3 26.2 %collective-permute-start.20 = (bf16[1040,512]{1,0:T(8,128)(2,1)S(1)}, bf16[1040,512]{1,0:T(8,128)(2,1)S(1)}, u32[]{:S(2)}, u32[]{:S(2)}) collective-permute-start(bf16[1040,512]{1,0:T(8,128)(2,1)S(1)} %get-tuple-element.170), channel_id=1, source_target_pairs={{0,8},{4,12},{8,0},{12,4},{1,9},{5,13},{9,1},{13,5},{2,10},{6,14},... | collective-permute-start | bytes 3194888 | tf_op jit(solution)/shard_map/ppermute | solution.py:86
  127.9 25.6 %collective-permute-start.21 = (bf16[1040,512]{1,0:T(8,128)(2,1)S(1)}, bf16[1040,512]{1,0:T(8,128)(2,1)S(1)}, u32[]{:S(2)}, u32[]{:S(2)}) collective-permute-start(bf16[1040,512]{1,0:T(8,128)(2,1)S(1)} %get-tuple-element.172), channel_id=1, source_target_pairs={{0,16},{16,0},{1,17},{17,1},{2,18},{18,2},{3,19},{19,3},{4,20},{20... | collective-permute-start | bytes 3194888 | tf_op jit(solution)/shard_map/ppermute | solution.py:94
  129.4 24.0 %collective-permute-start.22 = (bf16[784,512]{1,0:T(8,128)(2,1)S(1)}, bf16[784,512]{1,0:T(8,128)(2,1)S(1)}, u32[]{:S(2)}, u32[]{:S(2)}) collective-permute-start(bf16[784,512]{1,0:T(8,128)(2,1)S(1)} %get-tuple-element.174), channel_id=1, source_target_pairs={{0,1},{1,0},{2,3},{3,2},{4,5},{5,4},{6,7},{7,6},{8,9},{9,8},{10,11... | collective-permute-start | bytes 2408456 | tf_op jit(solution)/shard_map/ppermute | solution.py:98
  129.7 23.7 %collective-permute-start.23 = (bf16[208,512]{1,0:T(8,128)(2,1)S(1)}, bf16[208,512]{1,0:T(8,128)(2,1)S(1)}, u32[]{:S(2)}, u32[]{:S(2)}) collective-permute-start(bf16[208,512]{1,0:T(8,128)(2,1)S(1)} %get-tuple-element.184), channel_id=1, source_target_pairs={{0,1},{1,0},{2,3},{3,2},{4,5},{5,4},{6,7},{7,6},{8,9},{9,8},{10,11... | collective-permute-start | bytes 638984 | tf_op jit(solution)/shard_map/ppermute | solution.py:98
  154.5 13.0 %collective-permute-start.24 = (bf16[528,512]{1,0:T(8,128)(2,1)S(1)}, bf16[528,512]{1,0:T(8,128)(2,1)S(1)}, u32[]{:S(2)}, u32[]{:S(2)}) collective-permute-start(bf16[528,512]{1,0:T(8,128)(2,1)S(1)} %get-tuple-element.186), channel_id=1, source_target_pairs={{0,16},{16,0},{1,17},{17,1},{2,18},{18,2},{3,19},{19,3},{4,20},{20... | collective-permute-start | bytes 1622024 | tf_op jit(solution)/shard_map/ppermute | solution.py:94
  155.8 13.0 %collective-permute-start.25 = (bf16[528,512]{1,0:T(8,128)(2,1)S(1)}, bf16[528,512]{1,0:T(8,128)(2,1)S(1)}, u32[]{:S(2)}, u32[]{:S(2)}) collective-permute-start(bf16[528,512]{1,0:T(8,128)(2,1)S(1)} %get-tuple-element.188), channel_id=1, source_target_pairs={{0,1},{1,0},{2,3},{3,2},{4,5},{5,4},{6,7},{7,6},{8,9},{9,8},{10,11... | collective-permute-start | bytes 1622024 | tf_op jit(solution)/shard_map/ppermute | solution.py:98
  155.8 10.1 %collective-permute-start.26 = (bf16[400,512]{1,0:T(8,128)(2,1)S(1)}, bf16[400,512]{1,0:T(8,128)(2,1)S(1)}, u32[]{:S(2)}, u32[]{:S(2)}) collective-permute-start(bf16[400,512]{1,0:T(8,128)(2,1)S(1)} %get-tuple-element.190), channel_id=1, source_target_pairs={{0,8},{4,12},{8,0},{12,4},{1,9},{5,13},{9,1},{13,5},{2,10},{6,14},... | collective-permute-start | bytes 1228808 | tf_op jit(solution)/shard_map/ppermute | solution.py:86
  169.2 7.6 %collective-permute-start.27 = (bf16[272,512]{1,0:T(8,128)(2,1)S(1)}, bf16[272,512]{1,0:T(8,128)(2,1)S(1)}, u32[]{:S(2)}, u32[]{:S(2)}) collective-permute-start(bf16[272,512]{1,0:T(8,128)(2,1)S(1)} %get-tuple-element.192), channel_id=1, source_target_pairs={{0,1},{1,0},{2,3},{3,2},{4,5},{5,4},{6,7},{7,6},{8,9},{9,8},{10,11... | collective-permute-start | bytes 835592 | tf_op jit(solution)/shard_map/ppermute | solution.py:98
  169.5 7.3 %collective-permute-start.28 = (bf16[272,512]{1,0:T(8,128)(2,1)S(1)}, bf16[272,512]{1,0:T(8,128)(2,1)S(1)}, u32[]{:S(2)}, u32[]{:S(2)}) collective-permute-start(bf16[272,512]{1,0:T(8,128)(2,1)S(1)} %get-tuple-element.194), channel_id=1, source_target_pairs={{0,8},{4,12},{8,0},{12,4},{1,9},{5,13},{9,1},{13,5},{2,10},{6,14},... | collective-permute-start | bytes 835592 | tf_op jit(solution)/shard_map/ppermute | solution.py:86
  171.0 5.8 %collective-permute-start.29 = (bf16[208,512]{1,0:T(8,128)(2,1)S(1)}, bf16[208,512]{1,0:T(8,128)(2,1)S(1)}, u32[]{:S(2)}, u32[]{:S(2)}) collective-permute-start(bf16[208,512]{1,0:T(8,128)(2,1)S(1)} %get-tuple-element.196), channel_id=1, source_target_pairs={{0,16},{16,0},{1,17},{17,1},{2,18},{18,2},{3,19},{19,3},{4,20},{20... | collective-permute-start | bytes 638984 | tf_op jit(solution)/shard_map/ppermute | solution.py:94
  177.0 7.0 %collective-permute-start.32 = (bf16[1,4,64,512]{3,2,1,0:T(8,128)(2,1)S(1)}, bf16[1,4,64,512]{3,2,1,0:T(8,128)(2,1)S(1)}, u32[]{:S(2)}, u32[]{:S(2)}) collective-permute-start(bf16[1,4,64,512]{3,2,1,0:T(8,128)(2,1)S(1)} %bitcast.35), channel_id=1, source_target_pairs={{0,1},{1,0},{2,3},{3,2},{4,5},{5,4},{6,7},{7,6},{8,9},{9,8},{10,11... | collective-permute-start | bytes 786440 | tf_op jit(solution)/shard_map/ppermute | solution.py:98
  179.2 8.8 %collective-permute-start.31 = (bf16[1,5,64,512]{3,2,1,0:T(8,128)(2,1)S(1)}, bf16[1,5,64,512]{3,2,1,0:T(8,128)(2,1)S(1)}, u32[]{:S(2)}, u32[]{:S(2)}) collective-permute-start(bf16[1,5,64,512]{3,2,1,0:T(8,128)(2,1)S(1)} %bitcast.33), channel_id=1, source_target_pairs={{0,16},{16,0},{1,17},{17,1},{2,18},{18,2},{3,19},{19,3},{4,20},{20... | collective-permute-start | bytes 983048 | tf_op jit(solution)/shard_map/ppermute | solution.py:94
  179.7 10.7 %collective-permute-start.30 = (bf16[1,5,64,512]{3,2,1,0:T(8,128)(2,1)S(1)}, bf16[1,5,64,512]{3,2,1,0:T(8,128)(2,1)S(1)}, u32[]{:S(2)}, u32[]{:S(2)}) collective-permute-start(bf16[1,5,64,512]{3,2,1,0:T(8,128)(2,1)S(1)} %bitcast.31), channel_id=1, source_target_pairs={{0,8},{4,12},{8,0},{12,4},{1,9},{5,13},{9,1},{13,5},{2,10},{6,14},... | collective-permute-start | bytes 983048 | tf_op jit(solution)/shard_map/ppermute | solution.py:86
  184.1 50.0 %copy-start.5 = (bf16[2,4,64,512]{3,2,1,0:T(8,128)(2,1)}, bf16[2,4,64,512]{3,2,1,0:T(8,128)(2,1)S(1)}, u32[]{:S(2)}) copy-start(bf16[2,4,64,512]{3,2,1,0:T(8,128)(2,1)S(1)} %pad_maximum_fusion.5.refs_2_) | copy-start | bytes 1572868
  184.1 12.3 %collective-permute-start.35 = (bf16[2,4,64,512]{3,2,1,0:T(8,128)(2,1)S(1)}, bf16[2,4,64,512]{3,2,1,0:T(8,128)(2,1)S(1)}, u32[]{:S(2)}, u32[]{:S(2)}) collective-permute-start(bf16[2,4,64,512]{3,2,1,0:T(8,128)(2,1)S(1)} %pad_maximum_fusion.5.refs_2_), channel_id=1, source_target_pairs={{0,8},{4,12},{8,0},{12,4},{1,9},{5,13},{9,1},{13,5},{2,10},{6,14},... | collective-permute-start | bytes 1572872 | tf_op jit(solution)/shard_map/ppermute | solution.py:86
  188.1 10.7 %collective-permute-start.34 = (bf16[2,5,64,512]{3,2,1,0:T(8,128)(2,1)S(1)}, bf16[2,5,64,512]{3,2,1,0:T(8,128)(2,1)S(1)}, u32[]{:S(2)}, u32[]{:S(2)}) collective-permute-start(bf16[2,5,64,512]{3,2,1,0:T(8,128)(2,1)S(1)} %pad_maximum_fusion.4.refs_1_), channel_id=1, source_target_pairs={{0,1},{1,0},{2,3},{3,2},{4,5},{5,4},{6,7},{7,6},{8,9},{9,8},{10,11... | collective-permute-start | bytes 1966088 | tf_op jit(solution)/shard_map/ppermute | solution.py:98
  190.4 10.7 %collective-permute-start.33 = (bf16[2,5,64,512]{3,2,1,0:T(8,128)(2,1)S(1)}, bf16[2,5,64,512]{3,2,1,0:T(8,128)(2,1)S(1)}, u32[]{:S(2)}, u32[]{:S(2)}) collective-permute-start(bf16[2,5,64,512]{3,2,1,0:T(8,128)(2,1)S(1)} %pad_maximum_fusion.3.refs_0_), channel_id=1, source_target_pairs={{0,16},{16,0},{1,17},{17,1},{2,18},{18,2},{3,19},{19,3},{4,20},{20... | collective-permute-start | bytes 1966088 | tf_op jit(solution)/shard_map/ppermute | solution.py:94
  192.0 9.9 %collective-permute-start.41 = (bf16[2,4,64,512]{3,2,1,0:T(8,128)(2,1)S(1)}, bf16[2,4,64,512]{3,2,1,0:T(8,128)(2,1)S(1)}, u32[]{:S(2)}, u32[]{:S(2)}) collective-permute-start(bf16[2,4,64,512]{3,2,1,0:T(8,128)(2,1)S(1)} %pad_maximum_fusion.5.refs_2_), channel_id=1, source_target_pairs={{0,4},{4,0},{8,12},{12,8},{1,5},{5,1},{9,13},{13,9},{2,6},{6,2},{1... | collective-permute-start | bytes 1572872 | tf_op jit(solution)/shard_map/ppermute | solution.py:90
  192.0 11.2 %collective-permute-start.40 = (bf16[2,5,64,512]{3,2,1,0:T(8,128)(2,1)S(1)}, bf16[2,5,64,512]{3,2,1,0:T(8,128)(2,1)S(1)}, u32[]{:S(2)}, u32[]{:S(2)}) collective-permute-start(bf16[2,5,64,512]{3,2,1,0:T(8,128)(2,1)S(1)} %pad_maximum_fusion.4.refs_1_), channel_id=1, source_target_pairs={{0,4},{4,0},{8,12},{12,8},{1,5},{5,1},{9,13},{13,9},{2,6},{6,2},{1... | collective-permute-start | bytes 1966088 | tf_op jit(solution)/shard_map/ppermute | solution.py:90
  196.4 6.8 %collective-permute-start.39 = (bf16[2,5,64,512]{3,2,1,0:T(8,128)(2,1)S(1)}, bf16[2,5,64,512]{3,2,1,0:T(8,128)(2,1)S(1)}, u32[]{:S(2)}, u32[]{:S(2)}) collective-permute-start(bf16[2,5,64,512]{3,2,1,0:T(8,128)(2,1)S(1)} %pad_maximum_fusion.3.refs_0_), channel_id=1, source_target_pairs={{0,4},{4,0},{8,12},{12,8},{1,5},{5,1},{9,13},{13,9},{2,6},{6,2},{1... | collective-permute-start | bytes 1966088 | tf_op jit(solution)/shard_map/ppermute | solution.py:90
  201.1 12.7 %collective-permute-start.36 = (bf16[2,5,64,512]{3,2,1,0:T(8,128)(2,1)S(1)}, bf16[2,5,64,512]{3,2,1,0:T(8,128)(2,1)}, u32[]{:S(2)}, u32[]{:S(2)}) collective-permute-start(bf16[2,5,64,512]{3,2,1,0:T(8,128)(2,1)S(1)} %pad_maximum_fusion.3.refs_0_), channel_id=1, source_target_pairs={{0,1},{1,0},{2,3},{3,2},{4,5},{5,4},{6,7},{7,6},{8,9},{9,8},{10,11... | collective-permute-start | bytes 1966088 | tf_op jit(solution)/shard_map/ppermute | solution.py:98
  201.2 13.7 %collective-permute-start.37 = (bf16[2,5,64,512]{3,2,1,0:T(8,128)(2,1)S(1)}, bf16[2,5,64,512]{3,2,1,0:T(8,128)(2,1)}, u32[]{:S(2)}, u32[]{:S(2)}) collective-permute-start(bf16[2,5,64,512]{3,2,1,0:T(8,128)(2,1)S(1)} %pad_maximum_fusion.4.refs_1_), channel_id=1, source_target_pairs={{0,8},{4,12},{8,0},{12,4},{1,9},{5,13},{9,1},{13,5},{2,10},{6,14},... | collective-permute-start | bytes 1966088 | tf_op jit(solution)/shard_map/ppermute | solution.py:86
  201.9 10.8 %collective-permute-start.38 = (bf16[2,4,64,512]{3,2,1,0:T(8,128)(2,1)S(1)}, bf16[2,4,64,512]{3,2,1,0:T(8,128)(2,1)S(1)}, u32[]{:S(2)}, u32[]{:S(2)}) collective-permute-start(bf16[2,4,64,512]{3,2,1,0:T(8,128)(2,1)S(1)} %pad_maximum_fusion.5.refs_2_), channel_id=1, source_target_pairs={{0,16},{16,0},{1,17},{17,1},{2,18},{18,2},{3,19},{19,3},{4,20},{20... | collective-permute-start | bytes 1572872 | tf_op jit(solution)/shard_map/ppermute | solution.py:94
  203.2 13.3 %collective-permute-start.44 = (bf16[2,4,64,512]{3,2,1,0:T(8,128)(2,1)S(1)}, bf16[2,4,64,512]{3,2,1,0:T(8,128)(2,1)S(1)}, u32[]{:S(2)}, u32[]{:S(2)}) collective-permute-start(bf16[2,4,64,512]{3,2,1,0:T(8,128)(2,1)S(1)} %collective-permute-done.35.refs_8_), channel_id=1, source_target_pairs={{0,4},{4,0},{8,12},{12,8},{1,5},{5,1},{9,13},{13,9},{2,6},{6,2},{1... | collective-permute-start | bytes 1572872 | tf_op jit(solution)/shard_map/ppermute | solution.py:90
  203.2 14.3 %collective-permute-start.42 = (bf16[2,5,64,512]{3,2,1,0:T(8,128)(2,1)S(1)}, bf16[2,5,64,512]{3,2,1,0:T(8,128)(2,1)S(1)}, u32[]{:S(2)}, u32[]{:S(2)}) collective-permute-start(bf16[2,5,64,512]{3,2,1,0:T(8,128)(2,1)S(1)} %collective-permute-done.33.refs_6_), channel_id=1, source_target_pairs={{0,4},{4,0},{8,12},{12,8},{1,5},{5,1},{9,13},{13,9},{2,6},{6,2},{1... | collective-permute-start | bytes 1966088 | tf_op jit(solution)/shard_map/ppermute | solution.py:90
  212.7 4.9 %collective-permute-start.43 = (bf16[2,5,64,512]{3,2,1,0:T(8,128)(2,1)S(1)}, bf16[2,5,64,512]{3,2,1,0:T(8,128)(2,1)S(1)}, u32[]{:S(2)}, u32[]{:S(2)}) collective-permute-start(bf16[2,5,64,512]{3,2,1,0:T(8,128)(2,1)S(1)} %collective-permute-done.34.refs_7_), channel_id=1, source_target_pairs={{0,4},{4,0},{8,12},{12,8},{1,5},{5,1},{9,13},{13,9},{2,6},{6,2},{1... | collective-permute-start | bytes 1966088 | tf_op jit(solution)/shard_map/ppermute | solution.py:90
  214.9 15.0 %collective-permute-start.48 = (bf16[2,5,64,512]{3,2,1,0:T(8,128)(2,1)S(1)}, bf16[2,5,64,512]{3,2,1,0:T(8,128)(2,1)}, u32[]{:S(2)}, u32[]{:S(2)}) collective-permute-start(bf16[2,5,64,512]{3,2,1,0:T(8,128)(2,1)S(1)} %collective-permute-done.33.refs_6_), channel_id=1, source_target_pairs={{0,1},{1,0},{2,3},{3,2},{4,5},{5,4},{6,7},{7,6},{8,9},{9,8},{10,11... | collective-permute-start | bytes 1966088 | tf_op jit(solution)/shard_map/ppermute | solution.py:98
  215.5 14.8 %collective-permute-start.49 = (bf16[2,5,64,512]{3,2,1,0:T(8,128)(2,1)S(1)}, bf16[2,5,64,512]{3,2,1,0:T(8,128)(2,1)}, u32[]{:S(2)}, u32[]{:S(2)}) collective-permute-start(bf16[2,5,64,512]{3,2,1,0:T(8,128)(2,1)S(1)} %collective-permute-done.34.refs_7_), channel_id=1, source_target_pairs={{0,8},{4,12},{8,0},{12,4},{1,9},{5,13},{9,1},{13,5},{2,10},{6,14},... | collective-permute-start | bytes 1966088 | tf_op jit(solution)/shard_map/ppermute | solution.py:86
  216.5 12.0 %collective-permute-start.50 = (bf16[2,4,64,512]{3,2,1,0:T(8,128)(2,1)S(1)}, bf16[2,4,64,512]{3,2,1,0:T(8,128)(2,1)}, u32[]{:S(2)}, u32[]{:S(2)}) collective-permute-start(bf16[2,4,64,512]{3,2,1,0:T(8,128)(2,1)S(1)} %collective-permute-done.35.refs_8_), channel_id=1, source_target_pairs={{0,16},{16,0},{1,17},{17,1},{2,18},{18,2},{3,19},{19,3},{4,20},{20... | collective-permute-start | bytes 1572872 | tf_op jit(solution)/shard_map/ppermute | solution.py:94
  217.6 12.9 %collective-permute-start.47 = (bf16[2,4,64,512]{3,2,1,0:T(8,128)(2,1)S(1)}, bf16[2,4,64,512]{3,2,1,0:T(8,128)(2,1)S(1)}, u32[]{:S(2)}, u32[]{:S(2)}) collective-permute-start(bf16[2,4,64,512]{3,2,1,0:T(8,128)(2,1)S(1)} %collective-permute-done.38.refs_14_), channel_id=1, source_target_pairs={{0,4},{4,0},{8,12},{12,8},{1,5},{5,1},{9,13},{13,9},{2,6},{6,2},{1... | collective-permute-start | bytes 1572872 | tf_op jit(solution)/shard_map/ppermute | solution.py:90
  217.6 14.0 %collective-permute-start.45 = (bf16[2,5,64,512]{3,2,1,0:T(8,128)(2,1)}, bf16[2,5,64,512]{3,2,1,0:T(8,128)(2,1)}, u32[]{:S(2)}, u32[]{:S(2)}) collective-permute-start(bf16[2,5,64,512]{3,2,1,0:T(8,128)(2,1)} %collective-permute-done.36.refs_12_), channel_id=1, source_target_pairs={{0,4},{4,0},{8,12},{12,8},{1,5},{5,1},{9,13},{13,9},{2,6},{6,2},{1... | collective-permute-start | bytes 1966088 | tf_op jit(solution)/shard_map/ppermute | solution.py:90
  228.5 3.1 collective-permute-start.46
  230.0 4.1 %collective-permute-start.51 = (bf16[2,5,64,512]{3,2,1,0:T(8,128)(2,1)}, bf16[2,5,64,512]{3,2,1,0:T(8,128)(2,1)}, u32[]{:S(2)}, u32[]{:S(2)}) collective-permute-start(bf16[2,5,64,512]{3,2,1,0:T(8,128)(2,1)} %collective-permute-done.48.refs_18_), channel_id=1, source_target_pairs={{0,4},{4,0},{8,12},{12,8},{1,5},{5,1},{9,13},{13,9},{2,6},{6,2},{1... | collective-permute-start | bytes 1966088 | tf_op jit(solution)/shard_map/ppermute | solution.py:90
  230.3 3.8 %collective-permute-start.52 = (bf16[2,5,64,512]{3,2,1,0:T(8,128)(2,1)}, bf16[2,5,64,512]{3,2,1,0:T(8,128)(2,1)}, u32[]{:S(2)}, u32[]{:S(2)}) collective-permute-start(bf16[2,5,64,512]{3,2,1,0:T(8,128)(2,1)} %collective-permute-done.49.refs_19_), channel_id=1, source_target_pairs={{0,4},{4,0},{8,12},{12,8},{1,5},{5,1},{9,13},{13,9},{2,6},{6,2},{1... | collective-permute-start | bytes 1966088 | tf_op jit(solution)/shard_map/ppermute | solution.py:90
  231.4 2.8 collective-permute-start.53
  256.7 33.1 %collective-permute-start.54 = (bf16[7,128,256]{2,1,0:T(8,128)(2,1)}, bf16[7,128,256]{2,1,0:T(8,128)(2,1)S(1)}, u32[]{:S(2)}, u32[]{:S(2)}) collective-permute-start(bf16[7,128,256]{2,1,0:T(8,128)(2,1)} %get-tuple-element.219), channel_id=1, source_target_pairs={{0,0},{1,1},{2,16},{3,17},{16,2},{17,3},{18,18},{19,19},{4,4},{5,5... | collective-permute-start | bytes 1376264 | tf_op jit(solution)/shard_map/ppermute | solution.py:138
  259.0 43.3 %collective-permute-start.55 = (bf16[7,128,256]{2,1,0:T(8,128)(2,1)}, bf16[7,128,256]{2,1,0:T(8,128)(2,1)S(1)}, u32[]{:S(2)}, u32[]{:S(2)}) collective-permute-start(bf16[7,128,256]{2,1,0:T(8,128)(2,1)} %get-tuple-element.220), channel_id=1, source_target_pairs={{0,1},{1,0},{2,17},{3,16},{16,3},{17,2},{18,19},{19,18},{4,5},{5,4... | collective-permute-start | bytes 1376264 | tf_op jit(solution)/shard_map/ppermute | solution.py:138
  261.9 40.4 %collective-permute-start.56 = (bf16[7,128,256]{2,1,0:T(8,128)(2,1)}, bf16[7,128,256]{2,1,0:T(8,128)(2,1)S(1)}, u32[]{:S(2)}, u32[]{:S(2)}) collective-permute-start(bf16[7,128,256]{2,1,0:T(8,128)(2,1)} %get-tuple-element.221), channel_id=1, source_target_pairs={{0,2},{1,3},{2,18},{3,19},{16,0},{17,1},{18,16},{19,17},{4,6},{5,7... | collective-permute-start | bytes 1376264 | tf_op jit(solution)/shard_map/ppermute | solution.py:138
  261.9 43.2 %collective-permute-start.57 = (bf16[7,128,256]{2,1,0:T(8,128)(2,1)}, bf16[7,128,256]{2,1,0:T(8,128)(2,1)S(1)}, u32[]{:S(2)}, u32[]{:S(2)}) collective-permute-start(bf16[7,128,256]{2,1,0:T(8,128)(2,1)} %get-tuple-element.222), channel_id=1, source_target_pairs={{0,3},{1,2},{2,19},{3,18},{16,1},{17,0},{18,17},{19,16},{4,7},{5,6... | collective-permute-start | bytes 1376264 | tf_op jit(solution)/shard_map/ppermute | solution.py:138
  305.1 31.7 %collective-permute-start.58 = (bf16[7,128,256]{2,1,0:T(8,128)(2,1)}, bf16[7,128,256]{2,1,0:T(8,128)(2,1)S(1)}, u32[]{:S(2)}, u32[]{:S(2)}) collective-permute-start(bf16[7,128,256]{2,1,0:T(8,128)(2,1)} %get-tuple-element.227), channel_id=1, source_target_pairs={{0,0},{1,1},{2,16},{3,17},{16,2},{17,3},{18,18},{19,19},{4,4},{5,5... | collective-permute-start | bytes 1376264 | tf_op jit(solution)/shard_map/ppermute | solution.py:138
  307.1 39.2 %collective-permute-start.59 = (bf16[7,128,256]{2,1,0:T(8,128)(2,1)}, bf16[7,128,256]{2,1,0:T(8,128)(2,1)S(1)}, u32[]{:S(2)}, u32[]{:S(2)}) collective-permute-start(bf16[7,128,256]{2,1,0:T(8,128)(2,1)} %get-tuple-element.228), channel_id=1, source_target_pairs={{0,1},{1,0},{2,17},{3,16},{16,3},{17,2},{18,19},{19,18},{4,5},{5,4... | collective-permute-start | bytes 1376264 | tf_op jit(solution)/shard_map/ppermute | solution.py:138
  307.3 41.3 %collective-permute-start.60 = (bf16[7,128,256]{2,1,0:T(8,128)(2,1)}, bf16[7,128,256]{2,1,0:T(8,128)(2,1)S(1)}, u32[]{:S(2)}, u32[]{:S(2)}) collective-permute-start(bf16[7,128,256]{2,1,0:T(8,128)(2,1)} %get-tuple-element.229), channel_id=1, source_target_pairs={{0,2},{1,3},{2,18},{3,19},{16,0},{17,1},{18,16},{19,17},{4,6},{5,7... | collective-permute-start | bytes 1376264 | tf_op jit(solution)/shard_map/ppermute | solution.py:138
  307.3 44.8 %collective-permute-start.61 = (bf16[7,128,256]{2,1,0:T(8,128)(2,1)}, bf16[7,128,256]{2,1,0:T(8,128)(2,1)S(1)}, u32[]{:S(2)}, u32[]{:S(2)}) collective-permute-start(bf16[7,128,256]{2,1,0:T(8,128)(2,1)} %get-tuple-element.230), channel_id=1, source_target_pairs={{0,3},{1,2},{2,19},{3,18},{16,1},{17,0},{18,17},{19,16},{4,7},{5,6... | collective-permute-start | bytes 1376264 | tf_op jit(solution)/shard_map/ppermute | solution.py:138
  (17 other events, 440.2 us)
